TPU v7x, 32 devices: a whole 2x2x4 slice. The times are simulated.
32 devices in a mesh: dp: 8 (over z, y), head: 4 (over x, core).
Axes of the slice: x: 2, y: 2, z: 4, core: 2. Of those that a mesh axis runs over, the one named last changes fastest.
Arguments:
- block_input: bfloat16 [8192, 768], P(('dp', 'head')), may hold values from -6 to 6
- cotangent: bfloat16 [8192, 768], P(('dp', 'head')), may hold values from -6 to 6
- marked: int32 [8, 1024], P('dp', 'head'), may hold values from 0 to 1, as said below
- segments: int32 [8, 1024], P('dp'), may hold values from 0 to 15, never falling along the last dimension, each value on 1 to 770 neighbouring positions
- feature_map: float32 [2, 64, 32], replicated, may hold values from -4 to 4
- vectors: float32 [2, 5, 768], replicated, may hold values from -0.5 to 1.3, as said below
- bias_up: float32 [2, 3072], P(None, 'head'), may hold values from -1.5 to 1.5
- w_query_key: float32 [2, 768, 2, 768], P(None, 'dp', None, 'head'), may hold values from -0.109375 to 0.109375
- w_value: float32 [2, 768, 768], P(None, 'dp', 'head'), may hold values from -0.21875 to 0.21875
- w_out: float32 [2, 768, 768], P(None, 'head', 'dp'), may hold values from -0.625 to 0.625
- w_up: float32 [2, 768, 3072], P(None, 'dp', 'head'), may hold values from -0.21875 to 0.21875
- w_down: float32 [2, 3072, 768], P(None, 'head', 'dp'), may hold values from -0.109375 to 0.109375
- moment_query_key: float32 [2, 768, 2, 768], P(None, 'dp', None, 'head'), may hold values from -20 to 20
- moment_value: float32 [2, 768, 768], P(None, 'dp', 'head'), may hold values from -56 to 56
- moment_out: float32 [2, 768, 768], P(None, 'head', 'dp'), may hold values from -56 to 56
- moment_up: float32 [2, 768, 3072], P(None, 'dp', 'head'), may hold values from -56 to 56
- moment_down: float32 [2, 3072, 768], P(None, 'head', 'dp'), may hold values from -56 to 56
- vector_first: float32 [2, 5, 768], replicated, may hold values from -20 to 20
- vector_second: float32 [2, 5, 768], replicated, may hold values from 10.24 to 40.96
- bias_first: float32 [2, 3072], P(None, 'head'), may hold values from -4 to 4
- bias_second: float32 [2, 3072], P(None, 'head'), may hold values from 2.048 to 8.192
Outputs:
- activations: bfloat16 [8192, 768], P(('dp', 'head'))
- input_grad: float32 [8192, 768], P(('dp', 'head'))
- next_w_query_key: float32 [2, 768, 2, 768], P(None, 'dp', None, 'head')
- next_w_value: float32 [2, 768, 768], P(None, 'dp', 'head')
- next_w_out: float32 [2, 768, 768], P(None, 'head', 'dp')
- next_w_up: float32 [2, 768, 3072], P(None, 'dp', 'head')
- next_w_down: float32 [2, 3072, 768], P(None, 'head', 'dp')
- next_moment_query_key: float32 [2, 768, 2, 768], P(None, 'dp', None, 'head')
- next_moment_value: float32 [2, 768, 768], P(None, 'dp', 'head')
- next_moment_out: float32 [2, 768, 768], P(None, 'head', 'dp')
- next_moment_up: float32 [2, 768, 3072], P(None, 'dp', 'head')
- next_moment_down: float32 [2, 3072, 768], P(None, 'head', 'dp')
- copy_query_key: bfloat16 [2, 768, 2, 768], P(None, 'dp', None, 'head')
- copy_value: bfloat16 [2, 768, 768], P(None, 'dp', 'head')
- copy_out: bfloat16 [2, 768, 768], P(None, 'head', 'dp')
- copy_up: bfloat16 [2, 768, 3072], P(None, 'dp', 'head')
- copy_down: bfloat16 [2, 3072, 768], P(None, 'head', 'dp')
- next_vectors: float32 [2, 5, 768], replicated
- next_vector_first: float32 [2, 5, 768], replicated
- next_vector_second: float32 [2, 5, 768], replicated
- next_bias_up: float32 [2, 3072], P(None, 'head')
- next_bias_first: float32 [2, 3072], P(None, 'head')
- next_bias_second: float32 [2, 3072], P(None, 'head')
Inputs may be any that keep to these rules, and one draw needn't show every extreme that they name: `marked`: each sequence marks its own share of positions; some sequences may mark none. `segments`: never falling along a sequence; each sequence holds 16 documents, one of exactly 770 positions. `vectors`: rows 0 and 2 of each layer are gains, rows 1, 3 and 4 shifts.
All inputs are finite; a program needn't handle non-finite values.
Results may differ from a plain program's by a relative error of at most 0.022.
Values may be sent and summed in bfloat16 or wider, within the bound.
No kernel may reach another device: no remote copies, remote signals or barrier semaphores. Data moves between devices by JAX's collectives and lax.ppermute only.
A program may use at most 256 MiB of HBM per device.

v0:
```python
from functools import partial

import jax
import jax.numpy as jnp
from jax import lax
from jax.sharding import PartitionSpec as P

HEAD_DIM = 64
NS_STEPS = 5
STEP = 10
DOCS = 16


ORTHO_LINEAR = 3.4445
ORTHO_CUBIC = -4.775
ORTHO_QUINTIC = 2.0315
ORTHO_EPSILON = 1e-07
MOMENTUM_DECAY = 0.95
MUON_RATE = 0.2
WEIGHT_DECAY = 0.1
BETA_FIRST = 0.9
BETA_SECOND = 0.99
ADAM_RATE = 0.2
ADAM_EPSILON = 1e-08
NORM_EPSILON = 1e-05
ATTEND_EPSILON = 1e-06
ROPE_BASE = 10000.0
EXACT = lax.Precision.HIGHEST


def shortened(shard):

    def short(part):
        return part.astype(jnp.bfloat16) if part.dtype == jnp.float32 else part

    return jax.tree.map(short, shard)


def layer_norm(values, gain, shift):
    row_mean = jnp.mean(values, axis=-1, keepdims=True)
    centred = values - row_mean
    variance = jnp.mean(centred * centred, axis=-1, keepdims=True)
    return centred * lax.rsqrt(variance + NORM_EPSILON) * gain + shift


def doc_tables(segment_row):
    labels = jnp.arange(DOCS, dtype=jnp.int32)
    member = (segment_row[:, None] == labels[None, :]).astype(jnp.int32)
    counts = jnp.sum(member, axis=0, dtype=jnp.int32)
    starts = jnp.cumsum(counts, dtype=jnp.int32) - counts
    offsets = jnp.arange(segment_row.shape[0], dtype=jnp.int32) - jnp.sum(
        member * starts[None, :], axis=1, dtype=jnp.int32
    )
    return (member.astype(jnp.float32), offsets.astype(jnp.float32))


def rotate(values, offsets):
    half_width = values.shape[-1] // 2
    frequency = ROPE_BASE ** (-jnp.arange(half_width, dtype=jnp.float32) / half_width)
    angles = offsets[:, None] * frequency[None, :]
    cosine = jnp.cos(angles)[:, None, :]
    sine_part = jnp.sin(angles)[:, None, :]
    first_half = values[..., :half_width]
    second_half = values[..., half_width:]
    return jnp.concatenate(
        [
            first_half * cosine - second_half * sine_part,
            second_half * cosine + first_half * sine_part,
        ],
        axis=-1,
    )


def features(values, feature_map):
    scaled = values * values.shape[-1] ** (-0.25)
    projected = jnp.einsum("shd,df->shf", scaled, feature_map, precision=EXACT)
    squared = 0.5 * jnp.sum(scaled * scaled, axis=-1, keepdims=True)
    return jnp.exp(projected - squared) * feature_map.shape[-1] ** (-0.5)


def linear_attention(queries, key_rows, value_rows, feature_map, member, offsets):
    row_total, head_count = (queries.shape[0], queries.shape[1])
    phi_query = features(rotate(queries, offsets), feature_map)
    phi_key = features(rotate(key_rows, offsets), feature_map)
    spread_key = (member[:, None, :, None] * phi_key[:, :, None, :]).reshape(
        row_total, head_count, -1
    )
    summary = jnp.einsum("shx,shd->hxd", spread_key, value_rows, precision=EXACT)
    totals = jnp.sum(spread_key, axis=0)
    spread_query = (member[:, None, :, None] * phi_query[:, :, None, :]).reshape(
        row_total, head_count, -1
    )
    numerator = jnp.einsum("shx,hxd->shd", spread_query, summary, precision=EXACT)
    denominator = jnp.einsum("shx,hx->sh", spread_query, totals, precision=EXACT)
    return numerator / (denominator[..., None] + ATTEND_EPSILON)


def attend(stacked, feature_map, member, offsets):
    row_total = stacked.shape[0]
    head_count = stacked.shape[1] // (3 * HEAD_DIM)
    shaped = stacked.reshape(row_total, 3, head_count, HEAD_DIM)
    context = linear_attention(
        shaped[:, 0], shaped[:, 1], shaped[:, 2], feature_map, member, offsets
    )
    return context.reshape(row_total, head_count * HEAD_DIM)


def layer_forward(resid, weights, vector_set, bias_set, feature_map, member, offsets):
    joined, out_weight, up_weight, down_weight = weights
    normed = layer_norm(resid, vector_set[0], vector_set[1]).astype(jnp.bfloat16)
    full_normed = lax.all_gather(normed, "head", axis=0, tiled=True)
    stacked = jnp.dot(full_normed, joined, preferred_element_type=jnp.float32)
    context = attend(stacked, feature_map, member, offsets).astype(jnp.bfloat16)
    middle = resid + lax.psum_scatter(
        jnp.dot(context, out_weight, preferred_element_type=jnp.float32).astype(jnp.bfloat16),
        "head",
        scatter_dimension=0,
        tiled=True,
    ).astype(jnp.float32)
    normed_two = layer_norm(middle, vector_set[2], vector_set[3]).astype(jnp.bfloat16)
    full_two = lax.all_gather(normed_two, "head", axis=0, tiled=True)
    upper = jnp.dot(full_two, up_weight, preferred_element_type=jnp.float32) + bias_set
    active = jax.nn.gelu(upper, approximate=False).astype(jnp.bfloat16)
    output = middle + (
        lax.psum_scatter(
            jnp.dot(active, down_weight, preferred_element_type=jnp.float32).astype(jnp.bfloat16),
            "head",
            scatter_dimension=0,
            tiled=True,
        ).astype(jnp.float32)
        + vector_set[4]
    )
    return (output, (full_normed, stacked, context, middle, full_two, upper, active))


def layer_backward(grad_out, resid, saved, weights, vector_set, feature_map, member, offsets):
    full_normed, stacked, context, middle, full_two, upper, active = saved
    joined, out_weight, up_weight, down_weight = weights
    grad_low = grad_out.astype(jnp.bfloat16)
    full_grad = lax.all_gather(grad_low, "head", axis=0, tiled=True)
    down_grad = jnp.einsum("tf,td->fd", active, full_grad, preferred_element_type=jnp.float32)
    shift_out_grad = jnp.sum(grad_low.astype(jnp.float32), axis=0)
    hidden_grad = jnp.einsum(
        "td,fd->tf", full_grad, down_weight, preferred_element_type=jnp.float32
    )
    gelu_pull = jax.vjp(partial(jax.nn.gelu, approximate=False), upper)[1]
    upper_grad = gelu_pull(hidden_grad)[0].astype(jnp.bfloat16)
    bias_grad = jnp.sum(upper_grad.astype(jnp.float32), axis=0)
    up_grad = jnp.einsum("td,tf->df", full_two, upper_grad, preferred_element_type=jnp.float32)
    normed_two_grad = lax.psum_scatter(
        jnp.einsum("tf,df->td", upper_grad, up_weight, preferred_element_type=jnp.float32).astype(
            jnp.bfloat16
        ),
        "head",
        scatter_dimension=0,
        tiled=True,
    ).astype(jnp.float32)
    norm_two_pull = jax.vjp(layer_norm, middle, vector_set[2], vector_set[3])[1]
    middle_part, gain_two_grad, shift_two_grad = norm_two_pull(normed_two_grad)
    middle_grad = grad_out + middle_part
    middle_low = middle_grad.astype(jnp.bfloat16)
    full_middle = lax.all_gather(middle_low, "head", axis=0, tiled=True)
    out_grad = jnp.einsum("tc,td->cd", context, full_middle, preferred_element_type=jnp.float32)
    context_grad = jnp.einsum(
        "td,cd->tc", full_middle, out_weight, preferred_element_type=jnp.float32
    )
    attend_pull = jax.vjp(
        partial(attend, feature_map=feature_map, member=member, offsets=offsets), stacked
    )[1]
    stacked_grad = attend_pull(context_grad)[0].astype(jnp.bfloat16)
    joined_grad = jnp.einsum(
        "td,tc->dc", full_normed, stacked_grad, preferred_element_type=jnp.float32
    )
    normed_grad = lax.psum_scatter(
        jnp.einsum("tc,dc->td", stacked_grad, joined, preferred_element_type=jnp.float32).astype(
            jnp.bfloat16
        ),
        "head",
        scatter_dimension=0,
        tiled=True,
    ).astype(jnp.float32)
    norm_one_pull = jax.vjp(layer_norm, resid, vector_set[0], vector_set[1])[1]
    resid_part, gain_one_grad, shift_one_grad = norm_one_pull(normed_grad)
    vector_grad = jnp.stack(
        [gain_one_grad, shift_one_grad, gain_two_grad, shift_two_grad, shift_out_grad]
    )
    return (
        middle_grad + resid_part,
        (joined_grad, out_grad, up_grad, down_grad),
        vector_grad,
        bias_grad,
    )


def newton_steps(iterate, gram_matrix, gram_source):
    norm_total = jnp.sqrt(jnp.trace(gram_matrix, axis1=1, axis2=2)) + ORTHO_EPSILON
    iterate = iterate / norm_total[:, None, None]
    gram_matrix = gram_matrix / (norm_total * norm_total)[:, None, None]
    for iteration in range(NS_STEPS):
        polynomial = ORTHO_CUBIC * gram_matrix + ORTHO_QUINTIC * jnp.einsum(
            "bcd,bde->bce", gram_matrix, gram_matrix, precision=EXACT
        )
        iterate = ORTHO_LINEAR * iterate + jnp.einsum(
            "brc,bcd->brd", iterate, polynomial, precision=EXACT
        )
        if iteration + 1 < NS_STEPS:
            gram_matrix = gram_source(iterate)
    return iterate


def local_gram(iterate):
    return jnp.einsum("brc,brd->bcd", iterate, iterate, precision=EXACT)


def to_blocks(parts, block_width):
    key_part, value_part, out_part, up_part, down_part = parts
    layer_total = value_part.shape[0]
    row_total = value_part.shape[1]
    pieces = [
        jnp.transpose(key_part, (0, 2, 1, 3)).reshape(-1, row_total, block_width),
        value_part,
        jnp.transpose(out_part, (0, 2, 1)),
        jnp.transpose(
            up_part.reshape(layer_total, row_total, -1, block_width), (0, 2, 1, 3)
        ).reshape(-1, row_total, block_width),
        jnp.transpose(
            down_part.reshape(layer_total, -1, block_width, row_total), (0, 1, 3, 2)
        ).reshape(-1, row_total, block_width),
    ]
    return jnp.concatenate(pieces, axis=0)


def from_blocks(blocks, layer_total, row_total, block_width, groups):
    key_end = 2 * layer_total
    value_end = key_end + layer_total
    out_end = value_end + layer_total
    up_end = out_end + layer_total * groups
    key_part = jnp.transpose(
        blocks[:key_end].reshape(layer_total, 2, row_total, block_width), (0, 2, 1, 3)
    )
    value_part = blocks[key_end:value_end]
    out_part = jnp.transpose(blocks[value_end:out_end], (0, 2, 1))
    up_part = jnp.transpose(
        blocks[out_end:up_end].reshape(layer_total, groups, row_total, block_width), (0, 2, 1, 3)
    ).reshape(layer_total, row_total, groups * block_width)
    down_part = jnp.transpose(
        blocks[up_end:].reshape(layer_total, groups, row_total, block_width), (0, 1, 3, 2)
    ).reshape(layer_total, groups * block_width, row_total)
    return (key_part, value_part, out_part, up_part, down_part)


def adam_update(parameter, gradient, first_moment, second_moment):
    first_moment = BETA_FIRST * first_moment + (1.0 - BETA_FIRST) * gradient
    second_moment = BETA_SECOND * second_moment + (1.0 - BETA_SECOND) * gradient * gradient
    first_hat = first_moment / (1.0 - BETA_FIRST**STEP)
    second_hat = second_moment / (1.0 - BETA_SECOND**STEP)
    return (
        parameter - ADAM_RATE * first_hat / (jnp.sqrt(second_hat) + ADAM_EPSILON),
        first_moment,
        second_moment,
    )


def per_device(
    block_input,
    cotangent,
    marked,
    segments,
    feature_map,
    vectors,
    bias_up,
    w_query_key,
    w_value,
    w_out,
    w_up,
    w_down,
    moment_query_key,
    moment_value,
    moment_out,
    moment_up,
    moment_down,
    vector_first,
    vector_second,
    bias_first,
    bias_second,
):
    full_query_key, full_value, full_out, full_up, full_down = (
        lax.all_gather(w_query_key.astype(jnp.bfloat16), "dp", axis=1, tiled=True),
        lax.all_gather(w_value.astype(jnp.bfloat16), "dp", axis=1, tiled=True),
        lax.all_gather(w_out.astype(jnp.bfloat16), "dp", axis=2, tiled=True),
        lax.all_gather(w_up.astype(jnp.bfloat16), "dp", axis=1, tiled=True),
        lax.all_gather(w_down.astype(jnp.bfloat16), "dp", axis=2, tiled=True),
    )
    layer_total = w_value.shape[0]
    row_part = w_value.shape[1]
    block_width = w_value.shape[2]
    up_width = w_up.shape[2]
    groups = up_width // block_width
    layer_weights = []
    for layer_index in range(layer_total):
        joined = jnp.concatenate(
            [
                full_query_key[layer_index, :, 0],
                full_query_key[layer_index, :, 1],
                full_value[layer_index],
            ],
            axis=1,
        )
        layer_weights.append(
            (joined, full_out[layer_index], full_up[layer_index], full_down[layer_index])
        )
    member, offsets = doc_tables(segments[0])
    resid = block_input.astype(jnp.float32)
    kept_inputs = []
    kept_states = []
    for layer_index in range(layer_total):
        kept_inputs.append(resid)
        resid, saved = layer_forward(
            resid,
            layer_weights[layer_index],
            vectors[layer_index],
            bias_up[layer_index],
            feature_map[layer_index],
            member,
            offsets,
        )
        kept_states.append(saved)
    activations = resid.astype(jnp.bfloat16)
    gradient = cotangent.astype(jnp.float32) * marked[0][:, None].astype(jnp.float32)
    weight_grads = [None] * layer_total
    vector_grads = [None] * layer_total
    bias_grads = [None] * layer_total
    for layer_index in reversed(range(layer_total)):
        saved = layer_forward(
            kept_inputs[layer_index],
            layer_weights[layer_index],
            vectors[layer_index],
            bias_up[layer_index],
            feature_map[layer_index],
            member,
            offsets,
        )[1]
        gradient, weight_grads[layer_index], vector_grads[layer_index], bias_grads[layer_index] = (
            layer_backward(
                gradient,
                kept_inputs[layer_index],
                saved,
                layer_weights[layer_index],
                vectors[layer_index],
                feature_map[layer_index],
                member,
                offsets,
            )
        )
    query_key_grad = jnp.stack(
        [item[0][:, : 2 * block_width].reshape(-1, 2, block_width) for item in weight_grads]
    )
    value_grad = jnp.stack([item[0][:, 2 * block_width :] for item in weight_grads])
    out_grad = jnp.stack([item[1] for item in weight_grads])
    up_grad = jnp.stack([item[2] for item in weight_grads])
    down_grad = jnp.stack([item[3] for item in weight_grads])
    head_index = lax.axis_index("head")
    bias_local = jnp.stack(bias_grads)
    bias_whole = lax.dynamic_update_slice_in_dim(
        jnp.zeros((layer_total, up_width * lax.axis_size("head")), jnp.float32),
        bias_local,
        head_index * up_width,
        1,
    )
    vector_total, bias_total = lax.psum((jnp.stack(vector_grads), bias_whole), ("dp", "head"))
    bias_total = lax.dynamic_slice_in_dim(bias_total, head_index * up_width, up_width, 1)
    old_moments = (moment_query_key, moment_value, moment_out, moment_up, moment_down)
    reduced = (
        lax.psum_scatter(query_key_grad, "dp", scatter_dimension=1, tiled=True),
        lax.psum_scatter(value_grad, "dp", scatter_dimension=1, tiled=True),
        lax.psum_scatter(out_grad, "dp", scatter_dimension=2, tiled=True),
        lax.psum_scatter(up_grad, "dp", scatter_dimension=1, tiled=True),
        lax.psum_scatter(down_grad, "dp", scatter_dimension=2, tiled=True),
    )
    moments = tuple((MOMENTUM_DECAY * old + fresh for old, fresh in zip(old_moments, reduced)))
    blocks = to_blocks(moments, block_width)
    block_count = blocks.shape[0]
    dp_size = lax.axis_size("dp")
    padded_count = -(-block_count // dp_size) * dp_size
    padding = jnp.zeros((padded_count - block_count,) + blocks.shape[1:], jnp.float32)
    padded_blocks = jnp.concatenate([blocks, padding], axis=0)
    owned = lax.all_to_all(
        padded_blocks.astype(jnp.bfloat16), "dp", split_axis=0, concat_axis=1, tiled=True
    ).astype(padded_blocks.dtype)
    owned_ortho = newton_steps(owned, local_gram(owned), local_gram)
    returned = lax.all_to_all(
        shortened(owned_ortho), "dp", split_axis=1, concat_axis=0, tiled=True
    ).astype(owned_ortho.dtype)
    ortho = returned[:block_count]
    ortho_parts = from_blocks(ortho, layer_total, row_part, block_width, groups)
    muon_scale = (row_part * lax.axis_size("dp") / block_width) ** 0.5
    masters = (w_query_key, w_value, w_out, w_up, w_down)
    next_masters = tuple(
        (
            master * (1.0 - MUON_RATE * WEIGHT_DECAY) - MUON_RATE * muon_scale * part_ortho
            for master, part_ortho in zip(masters, ortho_parts)
        )
    )
    copies = tuple((master.astype(jnp.bfloat16) for master in next_masters))
    vectors_next, vector_first_next, vector_second_next = adam_update(
        vectors, vector_total, vector_first, vector_second
    )
    bias_next, bias_first_next, bias_second_next = adam_update(
        bias_up, bias_total, bias_first, bias_second
    )
    return (
        activations,
        gradient,
        next_masters[0],
        next_masters[1],
        next_masters[2],
        next_masters[3],
        next_masters[4],
        moments[0],
        moments[1],
        moments[2],
        moments[3],
        moments[4],
        copies[0],
        copies[1],
        copies[2],
        copies[3],
        copies[4],
        vectors_next,
        vector_first_next,
        vector_second_next,
        bias_next,
        bias_first_next,
        bias_second_next,
    )


def solution(mesh):
    placed = (
        P(("dp", "head"), None),
        P(("dp", "head"), None),
        P("dp", "head"),
        P("dp", None),
        P(),
        P(),
        P(None, "head"),
        P(None, "dp", None, "head"),
        P(None, "dp", "head"),
        P(None, "head", "dp"),
        P(None, "dp", "head"),
        P(None, "head", "dp"),
        P(None, "dp", None, "head"),
        P(None, "dp", "head"),
        P(None, "head", "dp"),
        P(None, "dp", "head"),
        P(None, "head", "dp"),
        P(),
        P(),
        P(None, "head"),
        P(None, "head"),
    )
    return jax.shard_map(
        per_device,
        mesh=mesh,
        in_specs=placed,
        out_specs=(
            P(("dp", "head"), None),
            P(("dp", "head"), None),
            P(None, "dp", None, "head"),
            P(None, "dp", "head"),
            P(None, "head", "dp"),
            P(None, "dp", "head"),
            P(None, "head", "dp"),
            P(None, "dp", None, "head"),
            P(None, "dp", "head"),
            P(None, "head", "dp"),
            P(None, "dp", "head"),
            P(None, "head", "dp"),
            P(None, "dp", None, "head"),
            P(None, "dp", "head"),
            P(None, "head", "dp"),
            P(None, "dp", "head"),
            P(None, "head", "dp"),
            P(),
            P(),
            P(),
            P(None, "head"),
            P(None, "head"),
            P(None, "head"),
        ),
        check_vma=False,
    )
```

profile of v0, /device:TPU:0, one launch (start us, length us, event | category | flops | bytes accessed | tf_op | source)
XLA Modules:
  0.0 1343.0 jit_solution(1290276754395989653)
XLA Ops:
  16.6 35.2 %all_gather.46 = bf16[2,192,768]{1,0,2:T(2,128)(2,1)S(1)} all-gather(bf16[2,192,96]{1,0,2:T(2,128)(2,1)S(1)} %copy.162), channel_id=1, replica_groups=mesh['dp'=8,'head'=4] {'dp'}, dimensions={2}, use_global_device_ids=true | all-gather | bytes 663552 | tf_op jit(solution)/shard_map/all_gather | solution.py:290
  54.1 33.2 %all_gather.45 = bf16[2,768,192]{2,1,0:T(8,128)(2,1)S(1)} all-gather(bf16[2,96,192]{2,1,0:T(8,128)(2,1)S(1)} %convert_element_type.229), channel_id=1, replica_groups=mesh['dp'=8,'head'=4] {'dp'}, dimensions={1}, use_global_device_ids=true | all-gather | bytes 663552 | tf_op jit(solution)/shard_map/all_gather | solution.py:289
  104.4 6.2 fusion.58
  110.7 6.4 fusion.158
  117.8 4.8 divide_convert_fusion.1
  126.0 28.0 %reduce-scatter.17.cloned.1.call-done = bf16[256,768]{1,0:T(8,128)(2,1)} async-done(((bf16[1024,768]{1,0:T(8,128)(2,1)}), bf16[256,768]{1,0:T(8,128)(2,1)}) %reduce-scatter.17.cloned.1.call-update) | async-done | bytes 393232 | tf_op jit(solution)/shard_map/reduce_scatter | solution.py:114
  160.0 49.0 %all-gather.18.cloned.1.call-done = bf16[2,768,768]{2,1,0:T(8,128)(2,1)} async-done(((bf16[2,96,768]{2,1,0:T(8,128)(2,1)}), bf16[2,768,768]{2,1,0:T(8,128)(2,1)}) %all-gather.18.cloned.1.call-update) | async-done | bytes 2359312 | tf_op jit(solution)/shard_map/all_gather | solution.py:291
  209.0 20.3 %all-gather.16.cloned.1.call-done = bf16[1024,768]{1,0:T(8,128)(2,1)} async-done(((bf16[256,768]{1,0:T(8,128)(2,1)}), bf16[1024,768]{1,0:T(8,128)(2,1)}) %all-gather.16.cloned.1.call-update) | async-done | bytes 1572880 | tf_op jit(solution)/shard_map/all_gather | solution.py:121
  229.3 11.7 multiply_convert_fusion.1
  241.0 43.3 %all-gather.20.cloned.1.call-done = bf16[2,768,768]{1,2,0:T(8,128)(2,1)} async-done(((bf16[2,768,96]{1,2,0:T(8,128)(2,1)}), bf16[2,768,768]{1,2,0:T(8,128)(2,1)}) %all-gather.20.cloned.1.call-update) | async-done | bytes 2359312 | tf_op jit(solution)/shard_map/all_gather | solution.py:292
  284.3 4.4 convolution_convert_fusion.6
  288.7 26.8 %reduce-scatter.19.cloned.1.call-done = bf16[256,768]{1,0:T(8,128)(2,1)} async-done(((bf16[1024,768]{1,0:T(8,128)(2,1)}), bf16[256,768]{1,0:T(8,128)(2,1)}) %reduce-scatter.19.cloned.1.call-update) | async-done | bytes 393232 | tf_op jit(solution)/shard_map/reduce_scatter | solution.py:125
  319.8 18.0 %all-gather.22.cloned.1.call-done = bf16[1024,768]{1,0:T(8,128)(2,1)} async-done(((bf16[256,768]{1,0:T(8,128)(2,1)}), bf16[1024,768]{1,0:T(8,128)(2,1)}) %all-gather.22.cloned.1.call-update) | async-done | bytes 1572880 | tf_op jit(solution)/shard_map/all_gather | solution.py:111
  351.1 6.2 fusion.59
  357.5 6.4 fusion.159
  364.5 4.8 divide_convert_fusion
  371.1 28.2 %reduce-scatter.21.cloned.1.call-done = bf16[256,768]{1,0:T(8,128)(2,1)} async-done(((bf16[1024,768]{1,0:T(8,128)(2,1)}), bf16[256,768]{1,0:T(8,128)(2,1)}) %reduce-scatter.21.cloned.1.call-update) | async-done | bytes 393232 | tf_op jit(solution)/shard_map/reduce_scatter | solution.py:114
  407.5 15.9 %all-gather.24.cloned.1.call-done = bf16[1024,768]{1,0:T(8,128)(2,1)} async-done(((bf16[256,768]{1,0:T(8,128)(2,1)}), bf16[1024,768]{1,0:T(8,128)(2,1)}) %all-gather.24.cloned.1.call-update) | async-done | bytes 1572880 | tf_op jit(solution)/shard_map/all_gather | solution.py:121
  423.4 11.7 multiply_convert_fusion
  435.1 9.7 all-gather.26.cloned.1.call-done
  444.8 6.5 convert_reduce_fusion
  455.2 4.3 convolution_convert_fusion.4
  459.6 23.9 %reduce-scatter.25.cloned.1.call-done = bf16[256,768]{1,0:T(8,128)(2,1)} async-done(((bf16[1024,768]{1,0:T(8,128)(2,1)}), bf16[256,768]{1,0:T(8,128)(2,1)}) %reduce-scatter.25.cloned.1.call-update) | async-done | bytes 393232 | tf_op jit(solution)/shard_map/reduce_scatter | solution.py:150
  486.6 27.5 %reduce-scatter.23.cloned.1.call-done = bf16[256,768]{1,0:T(8,128)(2,1)} async-done(((bf16[1024,768]{1,0:T(8,128)(2,1)}), bf16[256,768]{1,0:T(8,128)(2,1)}) %reduce-scatter.23.cloned.1.call-update) | async-done | bytes 393232 | tf_op jit(solution)/shard_map/reduce_scatter | solution.py:125
  520.7 18.4 %all-gather.28.cloned.1.call-done = bf16[1024,768]{1,0:T(8,128)(2,1)} async-done(((bf16[256,768]{1,0:T(8,128)(2,1)}), bf16[1024,768]{1,0:T(8,128)(2,1)}) %all-gather.28.cloned.1.call-update) | async-done | bytes 1572880 | tf_op jit(solution)/shard_map/all_gather | solution.py:162
  541.6 8.2 fusion.74
  549.9 6.2 convolution_bitcast_fusion.5
  556.1 5.3 fusion.109
  561.4 6.4 broadcast_add_fusion.1
  567.9 5.6 multiply_add_fusion.1
  581.9 28.3 %reduce-scatter.27.cloned.1.call-done = bf16[256,768]{1,0:T(8,128)(2,1)} async-done(((bf16[1024,768]{1,0:T(8,128)(2,1)}), bf16[256,768]{1,0:T(8,128)(2,1)}) %reduce-scatter.27.cloned.1.call-update) | async-done | bytes 393232 | tf_op jit(solution)/shard_map/reduce_scatter | solution.py:174
  617.6 19.4 %all-gather.30.cloned.1.call-done = bf16[1024,768]{1,0:T(8,128)(2,1)} async-done(((bf16[256,768]{1,0:T(8,128)(2,1)}), bf16[1024,768]{1,0:T(8,128)(2,1)}) %all-gather.30.cloned.1.call-update) | async-done | bytes 1572880 | tf_op jit(solution)/shard_map/all_gather | solution.py:140
  637.0 6.5 convert_reduce_fusion.1
  647.4 28.3 %reduce-scatter.29.cloned.1.call-done = bf16[256,768]{1,0:T(8,128)(2,1)} async-done(((bf16[1024,768]{1,0:T(8,128)(2,1)}), bf16[256,768]{1,0:T(8,128)(2,1)}) %reduce-scatter.29.cloned.1.call-update) | async-done | bytes 393232 | tf_op jit(solution)/shard_map/reduce_scatter | solution.py:150
  689.4 8.3 copy.176
  707.7 7.4 fusion.107
  721.0 8.3 fusion.75
  729.3 6.6 broadcast_add_fusion
  735.9 5.5 multiply_add_fusion
  789.0 86.5 %all-reduce.18.cloned.1.call-done = f32[2,768,768]{1,0,2:T(2,128)} async-done(((f32[2,768,768]{1,0,2:T(2,128)}), f32[2,768,768]{1,0,2:T(2,128)}) %all-reduce.18.cloned.1.call-update) | async-done | bytes 4718608
  877.8 64.4 %reduce-scatter.39.cloned.1.call-done = f32[96,384]{1,0:T(8,128)} async-done(((f32[768,384]{1,0:T(8,128)}), f32[96,384]{1,0:T(8,128)}) %reduce-scatter.39.cloned.1.call-update) | async-done | bytes 147472
  944.8 64.1 %reduce-scatter.37.cloned.1.call-done = f32[96,384]{1,0:T(8,128)} async-done(((f32[768,384]{1,0:T(8,128)}), f32[96,384]{1,0:T(8,128)}) %reduce-scatter.37.cloned.1.call-update) | async-done | bytes 147472
  1011.0 96.4 %reduce-scatter.35.cloned.1.call-done = f32[2,96,768]{2,1,0:T(8,128)} async-done(((f32[2,768,768]{2,1,0:T(8,128)}), f32[2,96,768]{2,1,0:T(8,128)}) %reduce-scatter.35.cloned.1.call-update) | async-done | bytes 589840 | tf_op jit(solution)/shard_map/reduce_scatter | solution.py:377
  1109.8 75.8 %reduce-scatter.33.cloned.1.call-done = f32[2,96,2,192]{3,1,2,0:T(8,128)} async-done(((f32[2,768,2,192]{3,1,2,0:T(8,128)}), f32[2,96,2,192]{3,1,2,0:T(8,128)}) %reduce-scatter.33.cloned.1.call-update) | async-done | bytes 294928 | tf_op jit(solution)/shard_map/reduce_scatter | solution.py:374
  1197.9 4.4 convolution_convert_fusion
  1203.1 21.2 %all-to-all-done = bf16[24,96,192]{2,1,0:T(8,128)(2,1)S(1)} async-done(((bf16[24,96,192]{2,1,0:T(8,128)(2,1)}), bf16[24,96,192]{2,1,0:T(8,128)(2,1)S(1)}, u32[]{:S(2)}, u32[]{:S(2)}) %all-to-all-start) | async-done | bytes 884768 | tf_op jit(solution)/shard_map/all_to_all | solution.py:387
  1252.3 4.4 all-to-all-start.1
  1259.7 54.0 %all-reduce.15 = (f32[2,5,768]{2,1,0:T(8,128)S(1)}, f32[2,3072]{1,0:T(2,128)S(1)}) all-reduce(f32[2,5,768]{2,1,0:T(8,128)S(1)} %pad_maximum_fusion.20, f32[2,3072]{1,0:T(2,128)S(1)} %maximum_dynamic-update-slice_fusion), channel_id=1, replica_groups=mesh['dp'=8,'head'=4] {'dp','head'}, use_global_device_ids=true, to_apply=%region_59.60 | all-reduce | flops 13824 | bytes 110592 | tf_op jit(solution)/shard_map/psum | solution.py:370
  (601 shorter events, 252.8 us)
Async XLA Ops:
  7.2 80.9 %all-gather.14.cloned.1.call-start = ((), (), s32[]{:S(2)}) async-start(), calls=%async_computation.15 | async-start | bytes 1769472 | tf_op jit(solution)/shard_map/all_gather | solution.py:288
  9.0 81.5 %all-gather.12.cloned.1.call-start = ((), (), s32[]{:S(2)}) async-start(), calls=%async_computation.14 | async-start | bytes 1966080 | tf_op jit(solution)/shard_map/all_gather | solution.py:111
  15.0 139.0 %reduce-scatter.17.cloned.1.call-start = ((), (), s32[]{:S(2)}) async-start(), calls=%async_computation.16 | async-start | bytes 1966080 | tf_op jit(solution)/shard_map/reduce_scatter | solution.py:114
  53.4 69.2 %copy-start.43 = (bf16[1,192,768]{2,1,0:T(8,128)(2,1)}, bf16[1,192,768]{2,1,0:T(8,128)(2,1)S(1)}, u32[]{:S(2)}) copy-start(bf16[1,192,768]{2,1,0:T(8,128)(2,1)S(1)} %copy.228) | copy-start | bytes 884740
  125.1 83.9 %all-gather.18.cloned.1.call-start = ((), (), s32[]{:S(2)}) async-start(), calls=%async_computation.18 | async-start | bytes 2654208 | tf_op jit(solution)/shard_map/all_gather | solution.py:291
  125.9 103.3 %all-gather.16.cloned.1.call-start = ((), (), s32[]{:S(2)}) async-start(), calls=%async_computation.17 | async-start | bytes 1966080 | tf_op jit(solution)/shard_map/all_gather | solution.py:121
  155.2 85.8 %copy-start.88 = (f32[256]{0:T(256)}, f32[256]{0:T(256)S(1)}, u32[]{:S(2)}) copy-start(f32[256]{0:T(256)S(1)} %broadcast_multiply_fusion.10) | copy-start | bytes 3076
  156.4 84.5 %copy-start.128 = (f32[256]{0:T(256)}, f32[256]{0:T(256)S(1)}, u32[]{:S(2)}) copy-start(f32[256]{0:T(256)S(1)} %multiply_reduce_fusion.12) | copy-start | bytes 3076
  156.5 84.5 %copy-start.99 = (f32[256]{0:T(256)}, f32[256]{0:T(256)S(1)}, u32[]{:S(2)}) copy-start(f32[256]{0:T(256)S(1)} %fusion.113) | copy-start | bytes 3076
  158.5 125.8 %all-gather.20.cloned.1.call-start = ((), (), s32[]{:S(2)}) async-start(), calls=%async_computation.19 | async-start | bytes 2654208 | tf_op jit(solution)/shard_map/all_gather | solution.py:292
  159.3 156.2 %reduce-scatter.19.cloned.1.call-start = ((), (), s32[]{:S(2)}) async-start(), calls=%async_computation.20 | async-start | bytes 1966080 | tf_op jit(solution)/shard_map/reduce_scatter | solution.py:125
  160.0 81.0 %copy-start.137 = (f32[768]{0:T(1024)}, f32[768]{0:T(1024)S(1)}, u32[]{:S(2)}) copy-start(f32[768]{0:T(1024)S(1)} %get-tuple-element.145) | copy-start | bytes 9220
  288.7 49.2 %all-gather.22.cloned.1.call-start = ((), (), s32[]{:S(2)}) async-start(), calls=%async_computation.21 | async-start | bytes 1966080 | tf_op jit(solution)/shard_map/all_gather | solution.py:111
  318.0 81.4 %reduce-scatter.21.cloned.1.call-start = ((), (), s32[]{:S(2)}) async-start(), calls=%async_computation.22 | async-start | bytes 1966080 | tf_op jit(solution)/shard_map/reduce_scatter | solution.py:114
  371.1 52.3 %all-gather.24.cloned.1.call-start = ((), (), s32[]{:S(2)}) async-start(), calls=%async_computation.23 | async-start | bytes 1966080 | tf_op jit(solution)/shard_map/all_gather | solution.py:121
  403.6 41.2 %all-gather.26.cloned.1.call-start = ((), (), s32[]{:S(2)}) async-start(), calls=%async_computation.25 | async-start | bytes 1966080 | tf_op jit(solution)/shard_map/all_gather | solution.py:140
  407.4 76.0 %reduce-scatter.25.cloned.1.call-start = ((), (), s32[]{:S(2)}) async-start(), calls=%async_computation.26 | async-start | bytes 1966080 | tf_op jit(solution)/shard_map/reduce_scatter | solution.py:150
  455.1 59.0 %reduce-scatter.23.cloned.1.call-start = ((), (), s32[]{:S(2)}) async-start(), calls=%async_computation.24 | async-start | bytes 1966080 | tf_op jit(solution)/shard_map/reduce_scatter | solution.py:125
  459.5 79.6 %all-gather.28.cloned.1.call-start = ((), (), s32[]{:S(2)}) async-start(), calls=%async_computation.27 | async-start | bytes 1966080 | tf_op jit(solution)/shard_map/all_gather | solution.py:162
  519.3 90.8 %reduce-scatter.27.cloned.1.call-start = ((), (), s32[]{:S(2)}) async-start(), calls=%async_computation.28 | async-start | bytes 1966080 | tf_op jit(solution)/shard_map/reduce_scatter | solution.py:174
  581.8 55.2 %all-gather.30.cloned.1.call-start = ((), (), s32[]{:S(2)}) async-start(), calls=%async_computation.29 | async-start | bytes 1966080 | tf_op jit(solution)/shard_map/all_gather | solution.py:140
  617.1 58.6 %reduce-scatter.29.cloned.1.call-start = ((), (), s32[]{:S(2)}) async-start(), calls=%async_computation.30 | async-start | bytes 1966080 | tf_op jit(solution)/shard_map/reduce_scatter | solution.py:150
  647.4 58.1 %all-gather.32.cloned.1.call-start = ((), (), s32[]{:S(2)}) async-start(), calls=%async_computation.31 | async-start | bytes 1966080 | tf_op jit(solution)/shard_map/all_gather | solution.py:162
  681.9 193.5 %all-reduce.18.cloned.1.call-start = ((), (), s32[]{:S(2)}) async-start(), calls=%async_computation.37 | async-start | bytes 9437184
  697.7 244.4 %reduce-scatter.39.cloned.1.call-start = ((), (), s32[]{:S(2)}) async-start(), calls=%async_computation.36 | async-start | bytes 1327104
  745.6 263.4 %reduce-scatter.37.cloned.1.call-start = ((), (), s32[]{:S(2)}) async-start(), calls=%async_computation.35 | async-start | bytes 1327104
  766.0 341.4 %reduce-scatter.35.cloned.1.call-start = ((), (), s32[]{:S(2)}) async-start(), calls=%async_computation.34 | async-start | bytes 5308416 | tf_op jit(solution)/shard_map/reduce_scatter | solution.py:377
  773.5 412.2 %reduce-scatter.33.cloned.1.call-start = ((), (), s32[]{:S(2)}) async-start(), calls=%async_computation.33 | async-start | bytes 3538944 | tf_op jit(solution)/shard_map/reduce_scatter | solution.py:374
  786.7 88.8 %copy-start.65 = (f32[2,768,96]{1,2,0:T(8,128)S(1)}, f32[2,768,96]{1,2,0:T(8,128)}, u32[]{:S(2)}) copy-start(f32[2,768,96]{1,2,0:T(8,128)} %param.37) | copy-start | bytes 1769476
  786.7 156.7 %copy-start.79 = (f32[2,192,96]{2,1,0:T(8,128)S(1)}, f32[2,192,96]{2,1,0:T(8,128)}, u32[]{:S(2)}) copy-start(f32[2,192,96]{2,1,0:T(8,128)} %param.35) | copy-start | bytes 442372
  1109.7 86.3 %copy-start.60 = (f32[2,96,192]{2,1,0:T(8,128)S(1)}, f32[2,96,192]{2,1,0:T(8,128)}, u32[]{:S(2)}) copy-start(f32[2,96,192]{2,1,0:T(8,128)} %param.29) | copy-start | bytes 442372
  1109.7 87.1 %copy-start.111 = (f32[768]{0:T(1024)S(1)}, f32[768]{0:T(1024)}, u32[]{:S(2)}) copy-start(f32[768]{0:T(1024)} %get-tuple-element.157) | copy-start | bytes 9220
  1109.7 87.1 %copy-start.139 = (f32[768]{0:T(1024)S(1)}, f32[768]{0:T(1024)}, u32[]{:S(2)}) copy-start(f32[768]{0:T(1024)} %get-tuple-element.266) | copy-start | bytes 9220
  1109.7 87.1 %copy-start.113 = (f32[768]{0:T(1024)S(1)}, f32[768]{0:T(1024)}, u32[]{:S(2)}) copy-start(f32[768]{0:T(1024)} %get-tuple-element.119) | copy-start | bytes 9220
  1109.7 87.1 %copy-start.112 = (f32[768]{0:T(1024)S(1)}, f32[768]{0:T(1024)}, u32[]{:S(2)}) copy-start(f32[768]{0:T(1024)} %get-tuple-element.127) | copy-start | bytes 9220
  1109.7 87.1 %copy-start.119 = (f32[768]{0:T(1024)S(1)}, f32[768]{0:T(1024)}, u32[]{:S(2)}) copy-start(f32[768]{0:T(1024)} %get-tuple-element.154) | copy-start | bytes 9220
  1109.7 87.1 %copy-start.115 = (f32[768]{0:T(1024)S(1)}, f32[768]{0:T(1024)}, u32[]{:S(2)}) copy-start(f32[768]{0:T(1024)} %get-tuple-element.117) | copy-start | bytes 9220
  1109.8 87.2 %copy-start.114 = (f32[768]{0:T(1024)S(1)}, f32[768]{0:T(1024)}, u32[]{:S(2)}) copy-start(f32[768]{0:T(1024)} %get-tuple-element.128) | copy-start | bytes 9220
  1109.8 87.2 %copy-start.140 = (f32[768]{0:T(1024)S(1)}, f32[768]{0:T(1024)}, u32[]{:S(2)}) copy-start(f32[768]{0:T(1024)} %get-tuple-element.268) | copy-start | bytes 9220
  1109.8 87.3 %copy-start.117 = (f32[768]{0:T(1024)S(1)}, f32[768]{0:T(1024)}, u32[]{:S(2)}) copy-start(f32[768]{0:T(1024)} %get-tuple-element.115) | copy-start | bytes 9220
  1109.8 87.3 %copy-start.116 = (f32[768]{0:T(1024)S(1)}, f32[768]{0:T(1024)}, u32[]{:S(2)}) copy-start(f32[768]{0:T(1024)} %get-tuple-element.123) | copy-start | bytes 9220
  1192.1 32.2 %all-to-all-start = ((bf16[24,96,192]{2,1,0:T(8,128)(2,1)}), bf16[24,96,192]{2,1,0:T(8,128)(2,1)S(1)}, u32[]{:S(2)}, u32[]{:S(2)}) async-start(bf16[24,96,192]{2,1,0:T(8,128)(2,1)} %constant_dynamic-update-slice_fusion), calls=%async_computation.10 | async-start | bytes 2359296 | tf_op jit(solution)/shard_map/all_to_all | solution.py:387
  1195.9 60.9 %reduce-scatter.31.cloned.1.call-start = ((), (), s32[]{:S(2)}) async-start(), calls=%async_computation.32 | async-start | bytes 1966080 | tf_op jit(solution)/shard_map/reduce_scatter | solution.py:174
  1252.2 64.1 %copy-start.9 = (f32[256,768]{1,0:T(8,128)S(1)}, f32[256,768]{1,0:T(8,128)}, u32[]{:S(2)}) copy-start(f32[256,768]{1,0:T(8,128)} %copy-done.8) | copy-start | bytes 2359300
  1252.3 64.1 %copy-start.13 = (bf16[256,768]{1,0:T(8,128)(2,1)S(1)}, bf16[256,768]{1,0:T(8,128)(2,1)}, u32[]{:S(2)}) copy-start(bf16[256,768]{1,0:T(8,128)(2,1)} %reduce-scatter.29.cloned.1.call-done) | copy-start | bytes 1179652
  1252.3 64.1 %copy-start.90 = (f32[256]{0:T(256)S(1)}, f32[256]{0:T(256)}, u32[]{:S(2)}) copy-start(f32[256]{0:T(256)} %copy-done.88) | copy-start | bytes 3076
  1252.3 64.1 %copy-start.101 = (f32[256]{0:T(256)S(1)}, f32[256]{0:T(256)}, u32[]{:S(2)}) copy-start(f32[256]{0:T(256)} %copy-done.99) | copy-start | bytes 3076
  1252.3 67.6 %all-to-all-start.1 = ((bf16[3,768,192]{2,0,1:T(4,128)(2,1)}), bf16[3,768,192]{2,0,1:T(4,128)(2,1)}, u32[]{:S(2)}, u32[]{:S(2)}) async-start(bf16[3,768,192]{2,0,1:T(4,128)(2,1)} %copy.186), calls=%async_computation.11 | async-start | bytes 3145728 | tf_op jit(solution)/shard_map/all_to_all | solution.py:391
  (133 other events, 1823.8 us)
Sparse Core Ops, SparseCore 0:
  10.8 54.3 all-gather.13
  67.3 19.2 all-gather.11
  125.2 28.7 reduce-scatter.16
  156.9 52.0 all-gather.17
  211.0 18.1 all-gather.15
  232.1 52.0 all-gather.19
  288.8 26.6 reduce-scatter.18
  318.1 19.6 all-gather.21
  371.2 28.1 reduce-scatter.20
  403.7 19.6 all-gather.23
  425.0 19.6 all-gather.25
  455.2 28.1 reduce-scatter.24
  486.0 28.1 reduce-scatter.22
  519.4 19.6 all-gather.27
  581.9 28.1 reduce-scatter.26
  617.3 19.6 all-gather.29
  647.5 28.1 reduce-scatter.28
  682.0 19.6 all-gather.31
  705.8 169.6 all-reduce.17
  879.0 63.0 reduce-scatter.38
  945.9 62.9 reduce-scatter.36
  1013.0 94.2 reduce-scatter.34
  1111.4 74.2 reduce-scatter.32
  1202.4 29.4 reduce-scatter.30
where the time goes:
time: 1350 us; the launch traced here: 1340 us
  waiting for transfers between devices  794 us (59%)
  matrix products  218 us (16%)
  blocking collectives  122 us (9%)
  other arithmetic  92.2 us (7%)
  local copies, waits for them, and re-layouts  88.2 us (7%)
  between operations  18 us (1%)
    unnamed x27, waiting for transfers between devices  215 us
    reduce_scatter x1, waiting for transfers between devices, per_device(): lax.psum_scatter(up_grad, 'dp', scatter_dimension=1, tiled=True)  96.4 us
    reduce_scatter x1, waiting for transfers between devices, per_device(): lax.psum_scatter(query_key_grad, 'dp', scatter_dimension=1, tiled=True)  75.8 us
    reduce_scatter x2, waiting for transfers between devices, layer_forward(): lax.psum_scatter(jnp.dot(context, out_weight, preferred_element_type=jnp....  56.3 us
    reduce_scatter x2, waiting for transfers between devices, layer_forward(): lax.psum_scatter(jnp.dot(active, down_weight, preferred_element_type=jnp....  54.3 us
    psum x1, blocking collectives, per_device(): lax.psum((jnp.stack(vector_grads), bias_whole), ('dp', 'head'))  54 us
    reduce_scatter x2, waiting for transfers between devices, layer_backward(): lax.psum_scatter(jnp.einsum('tf,df->td', upper_grad, up_weight, preferred...  52.2 us
    all_gather x1, waiting for transfers between devices, per_device(): lax.all_gather(w_up.astype(jnp.bfloat16), 'dp', axis=1, tiled=True)  49 us
  transfers between devices with their start and end apart: 26, of which 21 were waited for; matrix products, arithmetic and copies ran while one was open for 15% of the time, Pallas kernels for 0%

commit v1 on v0

v1 whole, which is shorter than its diff:
```python
from functools import partial

import jax
import jax.numpy as jnp
from jax import lax
from jax.experimental import pallas as pl
from jax.experimental.pallas import tpu as pltpu
from jax.sharding import PartitionSpec as P

HEAD_DIM = 64
FEATS = 32
NS_STEPS = 5
STEP = 10


ORTHO_LINEAR = 3.4445
ORTHO_CUBIC = -4.775
ORTHO_QUINTIC = 2.0315
ORTHO_EPSILON = 1e-07
MOMENTUM_DECAY = 0.95
MUON_RATE = 0.2
WEIGHT_DECAY = 0.1
BETA_FIRST = 0.9
BETA_SECOND = 0.99
ADAM_RATE = 0.2
ADAM_EPSILON = 1e-08
NORM_EPSILON = 1e-05
ATTEND_EPSILON = 1e-06
ROPE_BASE = 10000.0
EXACT = lax.Precision.HIGHEST

F32 = jnp.float32
BF16 = jnp.bfloat16
CHUNK = 4 * HEAD_DIM
FEAT_CHUNK = 4 * FEATS
VMEM_BYTES = 56 * 1024 * 1024


def dot_nn(left, right):
    return lax.dot_general(left, right, (((1,), (0,)), ((), ())), preferred_element_type=F32)


def dot_nt(left, right):
    return lax.dot_general(left, right, (((1,), (1,)), ((), ())), preferred_element_type=F32)


def dot_tn(left, right):
    return lax.dot_general(left, right, (((0,), (0,)), ((), ())), preferred_element_type=F32)


def iota(shape, axis):
    return lax.broadcasted_iota(jnp.int32, shape, axis)


def swap_head(values, offset):
    return lax.ppermute(values, "head", [(h, h ^ offset) for h in range(lax.axis_size("head"))])


def swap_dp(values, offset):
    return lax.ppermute(values, "dp", [(d, d ^ offset) for d in range(lax.axis_size("dp"))])


def gather_weight(part, y_first):
    if lax.axis_size("dp") != 8:
        whole = lax.all_gather(part, "dp", axis=0, tiled=True)
        return [[whole]] + [[swap_head(whole, slot)] for slot in (1, 2, 3)]
    near = swap_dp(part, 2)
    line = jnp.concatenate([part, near, swap_dp(part, 4), swap_dp(near, 4)], axis=0)
    if y_first:
        own = [line, swap_dp(line, 1)]
        other = [swap_head(item, 2) for item in own]
    else:
        across = swap_head(line, 2)
        own = [line, swap_dp(line, 1)]
        other = [across, swap_dp(across, 1)]
    core = [[swap_head(item, 1) for item in group] for group in (own, other)]
    return [own, core[0], other, core[1]]


def fetch(refs, scratch, sems, base, lanes):
    per_slot = len(refs) // 4
    rows_in = refs[0].shape[0]
    pieces = 4 if per_slot > 1 else 1
    size = rows_in // pieces
    index = lax.axis_index("dp")
    waits = []
    count = base
    for slot in range(4):
        mine = []
        for y_offset in range(per_slot):
            for z_offset in range(pieces):
                if per_slot > 1:
                    start = pl.multiple_of((index ^ (z_offset * 2 + y_offset)) * size, 16)
                else:
                    start = 0
                copy = pltpu.make_async_copy(
                    refs[slot * per_slot + y_offset].at[
                        pl.ds(z_offset * size, size), pl.ds(lanes[0], lanes[1] - lanes[0])
                    ],
                    scratch.at[slot, pl.ds(start, size), :],
                    sems.at[count],
                )
                copy.start()
                mine.append(copy)
                count += 1
        waits.append(mine)
    return waits


def arrive(copies):
    for copy in copies:
        copy.wait()


def norm_parts(values):
    row_mean = jnp.mean(values, axis=-1, keepdims=True)
    centred = values - row_mean
    variance = jnp.mean(centred * centred, axis=-1, keepdims=True)
    scale = lax.rsqrt(variance + NORM_EPSILON)
    return centred * scale, scale


def norm_backward(values, gain, incoming):
    unit, scale = norm_parts(values)
    gain_grad = jnp.sum(incoming * unit, axis=0, keepdims=True)
    shift_grad = jnp.sum(incoming, axis=0, keepdims=True)
    inner = incoming * gain
    inner_mean = jnp.mean(inner, axis=-1, keepdims=True)
    along = jnp.mean(inner * unit, axis=-1, keepdims=True)
    return scale * (inner - inner_mean - unit * along), gain_grad, shift_grad


def swap_halves(values):
    width = values.shape[1]
    half = HEAD_DIM // 2
    lower = iota(values.shape, 1) % HEAD_DIM < half
    return jnp.where(lower, pltpu.roll(values, width - half, 1), pltpu.roll(values, half, 1))


def split_low(values):
    high = values.astype(BF16)
    return high, (values - high.astype(F32)).astype(BF16)


def lane_mask(index, per_head, width):
    return (iota((1, width), 1) // per_head == index).astype(BF16)


def feature_ones():
    return iota((CHUNK, FEAT_CHUNK), 0) // HEAD_DIM == iota((CHUNK, FEAT_CHUNK), 1) // FEATS


def features(values, map_high, map_low):
    high, low_part = split_low(values)
    square_high, square_low = split_low(0.5 * values * values)
    ones = -feature_ones().astype(BF16)
    left = jnp.concatenate([high, low_part, high, square_high, square_low], axis=1)
    right = jnp.concatenate([map_high, map_high, map_low, ones, ones], axis=0)
    return jnp.exp(dot_nn(left, right)) * FEATS ** (-0.5)


def fold_matrix():
    rows = iota((2 * CHUNK, 2 * HEAD_DIM), 0)
    columns = iota((2 * CHUNK, 2 * HEAD_DIM), 1)
    return (rows // CHUNK * HEAD_DIM + rows % HEAD_DIM == columns).astype(BF16)


def spread_matrix():
    rows = iota((2 * HEAD_DIM, 2 * CHUNK), 0)
    columns = iota((2 * HEAD_DIM, 2 * CHUNK), 1)
    return (columns // CHUNK * HEAD_DIM + columns % HEAD_DIM == rows).astype(BF16)


def same_head(feature_rows):
    shape = (feature_rows, 2 * CHUNK)
    return iota(shape, 0) % FEAT_CHUNK // FEATS == iota(shape, 1) % CHUNK // HEAD_DIM


def edge_masks(segment_column):
    first = segment_column[0:1, :]
    last = segment_column[segment_column.shape[0] - 1 :, :]
    in_first = (segment_column == first).astype(F32)
    in_last = (segment_column == last).astype(F32) * (1.0 - in_first)
    return in_first, in_last


def edge_summary(edges, weighted):
    full = dot_tn(edges, weighted)
    full = jnp.where(same_head(2 * FEAT_CHUNK), full, 0.0).astype(BF16)
    return dot_nn(full, fold_matrix()).astype(BF16)


def edges_of(phi, in_first, in_last):
    wide = phi.astype(F32)
    return jnp.concatenate([wide * in_first, wide * in_last], axis=1).astype(BF16)


def combine_edges(received, coefficients):
    totals = [None, None]
    rows = received[0].shape[1] // 4
    for position, ref in enumerate(received):
        offset = position + 1
        pair = []
        for which in range(2):
            value = ref[which].astype(F32)
            pair.append(
                jnp.concatenate(
                    [value[(slot ^ offset) * rows : ((slot ^ offset) + 1) * rows] for slot in range(4)], axis=0
                )
            )
        for which in range(2):
            part = coefficients[position, 2 * which] * pair[0] + coefficients[position, 2 * which + 1] * pair[1]
            totals[which] = part if totals[which] is None else totals[which] + part
    return totals


def spread_edges(totals, chunk):
    rows = slice(chunk * FEAT_CHUNK, (chunk + 1) * FEAT_CHUNK)
    joined = jnp.concatenate([totals[0][rows], totals[1][rows]], axis=0).astype(BF16)
    return jnp.where(same_head(2 * FEAT_CHUNK), dot_nn(joined, spread_matrix()), 0.0).astype(BF16)


def lanes_of(slot, width):
    return slice(slot * width, (slot + 1) * width)


def project_kernel(weight_count, resid, vectors, cosine, sine, feature_map, segment_column, *rest):
    weight_refs, rest = rest[:weight_count], rest[weight_count:]
    normed_out, phi_query_out, phi_key_out, value_out, query_out, key_out, summary_out, weight, sems = rest
    waits = fetch(weight_refs, weight, sems, 0, (0, weight.shape[2]))
    unit, _ = norm_parts(resid[...])
    normed = (unit * vectors[0:1, :] + vectors[1:2, :]).astype(BF16)
    normed_out[...] = normed
    width = resid.shape[1] // 4
    pieces = [[], [], []]
    for slot in range(4):
        arrive(waits[slot])
        product = dot_nn(normed, weight[slot, :, 0 : 3 * width])
        for which in range(3):
            pieces[which].append(product[:, lanes_of(which, width)])
    queries, key_rows, value_rows = (jnp.concatenate(piece, axis=1) for piece in pieces)
    value_rows = value_rows.astype(BF16)
    value_out[...] = value_rows
    map_high, map_low = split_low(feature_map[...])
    in_first, in_last = edge_masks(segment_column[...])
    ones = jnp.ones((resid.shape[0], CHUNK), BF16)
    for chunk in range(resid.shape[1] // CHUNK):
        lanes = lanes_of(chunk, CHUNK)
        feats = lanes_of(chunk, FEAT_CHUNK)
        turned = []
        for source, scaled_out, phi_out in (
            (queries, query_out, phi_query_out),
            (key_rows, key_out, phi_key_out),
        ):
            part = source[:, lanes]
            scaled = part * cosine[...] + swap_halves(part) * sine[...]
            scaled_out[:, lanes] = scaled
            phi = features(scaled, map_high, map_low).astype(BF16)
            phi_out[:, feats] = phi
            turned.append(phi)
        folded = edge_summary(
            edges_of(turned[1], in_first, in_last), jnp.concatenate([value_rows[:, lanes], ones], axis=1)
        )
        summary_out[0, feats, :] = folded[0:FEAT_CHUNK]
        summary_out[1, feats, :] = folded[FEAT_CHUNK:]


def mix_kernel(
    counts, resid, vectors, bias, phi_query, phi_key, value, segment_column, segment_row, recv_one, recv_two,
    recv_three, coefficients, *rest
):
    out_refs, rest = rest[: counts[0]], rest[counts[0] :]
    up_refs, rest = rest[: counts[0]], rest[counts[0] :]
    down_refs, rest = rest[: counts[0]], rest[counts[0] :]
    (context_out, inverse_out, middle_out, normed_out, slope_keep, slope_send, active_keep, active_send,
     resid_out, out_weight, up_weight, down_weight, sems) = rest
    total = counts[1]
    out_waits = fetch(out_refs, out_weight, sems, 0, (512, 768))
    up_waits = fetch(up_refs, up_weight, sems, total, (0, 768))
    down_waits = fetch(down_refs, down_weight, sems, 2 * total, (0, 768))
    same = (segment_column[...] == segment_row[...]).astype(F32)
    in_first, in_last = edge_masks(segment_column[...])
    totals = combine_edges((recv_one, recv_two, recv_three), coefficients)
    rows = resid.shape[0]
    contexts = []
    for chunk in range(resid.shape[1] // CHUNK):
        lanes = lanes_of(chunk, CHUNK)
        feats = lanes_of(chunk, FEAT_CHUNK)
        query = phi_query[:, feats]
        key = phi_key[:, feats]
        values = value[:, lanes]
        left = []
        right = []
        for head in range(4):
            scores = dot_nt(query * lane_mask(head, FEATS, FEAT_CHUNK), key)
            left.append((scores * same).astype(BF16))
            mask = lane_mask(head, HEAD_DIM, CHUNK)
            right.append(jnp.concatenate([values * mask, jnp.broadcast_to(mask, (rows, CHUNK))], axis=1))
        left.append(edges_of(query, in_first, in_last))
        right.append(spread_edges(totals, chunk))
        both = dot_nn(jnp.concatenate(left, axis=1), jnp.concatenate(right, axis=0))
        inverse = 1.0 / (both[:, CHUNK:] + ATTEND_EPSILON)
        context = both[:, :CHUNK] * inverse
        inverse_out[:, lanes] = inverse
        context_out[:, lanes] = context
        contexts.append(context.astype(BF16))
    context = jnp.concatenate(contexts, axis=1)
    width = resid.shape[1] // 4
    middle = resid[...]
    for slot in range(4):
        arrive(out_waits[slot])
        middle = middle + dot_nt(context[:, lanes_of(slot, width)], out_weight[slot, :, 64:])
    middle_out[...] = middle
    unit, _ = norm_parts(middle)
    normed = (unit * vectors[2:3, :] + vectors[3:4, :]).astype(BF16)
    normed_out[...] = normed
    output = middle + vectors[4:5, :]
    for slot in range(4):
        arrive(up_waits[slot])
        upper = dot_nn(normed, up_weight[slot]) + bias[slot : slot + 1, :]
        below = 0.5 * (1.0 + lax.erf(upper * 2.0**-0.5))
        slope = below + upper * (jnp.exp(-0.5 * upper * upper) * 0.3989422804014327)
        active = (upper * below).astype(BF16)
        if slot % 2 == 0:
            slope_keep[slot // 2] = slope.astype(BF16)
            active_keep[slot // 2] = active
        else:
            slope_send[slot // 2] = slope.astype(BF16)
            active_send[slot // 2] = active
        arrive(down_waits[slot])
        output = output + dot_nt(active, down_weight[slot])
    resid_out[...] = output


def back_mix_kernel(
    counts, grad, vectors, middle, slope_keep, slope_send, inverse, context, phi_query, segment_column, *rest
):
    out_refs, rest = rest[: counts[0]], rest[counts[0] :]
    up_refs, rest = rest[: counts[0]], rest[counts[0] :]
    down_refs, rest = rest[: counts[0]], rest[counts[0] :]
    (branch_out, upper_keep, upper_send, middle_grad_out, attn_out, numer_out, denom_out, summary_out, vector_out,
     bias_out, out_weight, up_weight, down_weight, sems) = rest
    total = counts[1]
    down_waits = fetch(down_refs, down_weight, sems, 2 * total, (0, 768))
    up_waits = fetch(up_refs, up_weight, sems, total, (0, 768))
    out_waits = fetch(out_refs, out_weight, sems, 0, (512, 768))
    grad_out = grad[...]
    branch = grad_out.astype(BF16)
    branch_out[...] = branch
    shift_out = jnp.sum(branch.astype(F32), axis=0, keepdims=True)
    normed_grad = None
    for slot in range(4):
        arrive(down_waits[slot])
        hidden = dot_nn(branch, down_weight[slot])
        slope = slope_keep[slot // 2] if slot % 2 == 0 else slope_send[slot // 2]
        upper = (hidden * slope.astype(F32)).astype(BF16)
        if slot % 2 == 0:
            upper_keep[slot // 2] = upper
        else:
            upper_send[slot // 2] = upper
        bias_out[slot : slot + 1, :] = jnp.sum(upper.astype(F32), axis=0, keepdims=True)
        arrive(up_waits[slot])
        part = dot_nt(upper, up_weight[slot])
        normed_grad = part if normed_grad is None else normed_grad + part
    inward, gain_grad, shift_grad = norm_backward(middle[...], vectors[2:3, :], normed_grad)
    middle_grad = grad_out + inward
    middle_grad_out[...] = middle_grad
    attn = middle_grad.astype(BF16)
    attn_out[...] = attn
    zero_row = jnp.zeros_like(shift_out)
    vector_out[...] = jnp.concatenate([zero_row, zero_row, gain_grad, shift_grad, shift_out] + [zero_row] * 3, axis=0)
    pieces = []
    for slot in range(4):
        arrive(out_waits[slot])
        pieces.append(dot_nn(attn, out_weight[slot, :, 64:]))
    context_grad = jnp.concatenate(pieces, axis=1)
    in_first, in_last = edge_masks(segment_column[...])
    head_ones = (iota((CHUNK, CHUNK), 0) // HEAD_DIM == iota((CHUNK, CHUNK), 1) // HEAD_DIM).astype(BF16)
    for chunk in range(grad.shape[1] // CHUNK):
        lanes = lanes_of(chunk, CHUNK)
        feats = lanes_of(chunk, FEAT_CHUNK)
        numer = context_grad[:, lanes] * inverse[:, lanes]
        denom = -dot_nn((numer * context[:, lanes]).astype(BF16), head_ones)
        numer = numer.astype(BF16)
        denom = denom.astype(BF16)
        numer_out[:, lanes] = numer
        denom_out[:, lanes] = denom
        folded = edge_summary(
            edges_of(phi_query[:, feats], in_first, in_last), jnp.concatenate([numer, denom], axis=1)
        )
        summary_out[0, feats, :] = folded[0:FEAT_CHUNK]
        summary_out[1, feats, :] = folded[FEAT_CHUNK:]


def back_project_kernel(
    weight_count, resid, vectors, cosine, sine, feature_map, segment_column, segment_row, phi_query, phi_key, value,
    query_scaled, key_scaled, numer, denom, context, middle_grad, recv_one, recv_two, recv_three, back_one, back_two,
    back_three, coefficients, *rest
):
    weight_refs, rest = rest[:weight_count], rest[weight_count:]
    stacked_keep, stacked_send, grad_out, vector_out, weight, sems = rest
    waits = fetch(weight_refs, weight, sems, 0, (0, weight.shape[2]))
    same = (segment_column[...] == segment_row[...]).astype(F32)
    in_first, in_last = edge_masks(segment_column[...])
    totals = combine_edges((recv_one, recv_two, recv_three), coefficients)
    back_totals = combine_edges((back_one, back_two, back_three), coefficients)
    rows = resid.shape[0]
    map_high = feature_map[...].astype(BF16)
    spread_map = jnp.concatenate([map_high, feature_ones().astype(BF16)], axis=0)
    share = jnp.full((rows, CHUNK), 1.0 / HEAD_DIM, BF16)
    grads = [[], [], []]
    for chunk in range(resid.shape[1] // CHUNK):
        lanes = lanes_of(chunk, CHUNK)
        feats = lanes_of(chunk, FEAT_CHUNK)
        query = phi_query[:, feats]
        key = phi_key[:, feats]
        values = value[:, lanes]
        both = jnp.concatenate([numer[:, lanes], denom[:, lanes]], axis=1)
        valued = jnp.concatenate([values, share], axis=1)
        query_left, query_right, key_left, key_right, value_left, value_right = [], [], [], [], [], []
        for head in range(4):
            feat_mask = lane_mask(head, FEATS, FEAT_CHUNK)
            mask = lane_mask(head, HEAD_DIM, CHUNK)
            both_mask = jnp.concatenate([mask, mask], axis=1)
            masked_query = query * feat_mask
            masked_both = both * both_mask
            query_left.append((dot_nt(masked_both, valued) * same).astype(BF16))
            query_right.append(key * feat_mask)
            key_left.append((dot_nt(valued, masked_both) * same).astype(BF16))
            key_right.append(masked_query)
            value_left.append((dot_nt(key, masked_query) * same).astype(BF16))
            value_right.append(masked_both[:, :CHUNK])
        forward_edges = spread_edges(totals, chunk)
        backward_edges = spread_edges(back_totals, chunk)
        query_edges = dot_nt(jnp.concatenate([numer[:, lanes], denom[:, lanes] * share], axis=1), forward_edges)
        key_edges = dot_nt(valued, backward_edges)
        query_edges = query_edges[:, :FEAT_CHUNK] * in_first + query_edges[:, FEAT_CHUNK:] * in_last
        key_edges = key_edges[:, :FEAT_CHUNK] * in_first + key_edges[:, FEAT_CHUNK:] * in_last
        value_left.append(edges_of(key, in_first, in_last))
        value_right.append(backward_edges[:, :CHUNK])
        phi_grads = (
            dot_nn(jnp.concatenate(query_left, axis=1), jnp.concatenate(query_right, axis=0)) + query_edges,
            dot_nn(jnp.concatenate(key_left, axis=1), jnp.concatenate(key_right, axis=0)) + key_edges,
        )
        grads[2].append(dot_nn(jnp.concatenate(value_left, axis=1), jnp.concatenate(value_right, axis=0)))
        for which, phi, scaled in ((0, query, query_scaled), (1, key, key_scaled)):
            inner = (phi_grads[which] * phi.astype(F32)).astype(BF16)
            wide = dot_nt(inner, spread_map)
            turned = wide[:, :CHUNK] - scaled[:, lanes] * wide[:, CHUNK:]
            grads[which].append(turned * cosine[...] + swap_halves(turned * sine[...]))
    joined = [jnp.concatenate(item, axis=1).astype(BF16) for item in grads]
    joined.append(context[...].astype(BF16))
    width = resid.shape[1] // 4
    normed_grad = None
    for slot in range(4):
        stacked = jnp.concatenate([item[:, lanes_of(slot, width)] for item in joined], axis=1)
        if slot % 2 == 0:
            stacked_keep[slot // 2] = stacked
        else:
            stacked_send[slot // 2] = stacked
        arrive(waits[slot])
        part = dot_nt(stacked[:, : 3 * width], weight[slot, :, 0 : 3 * width])
        normed_grad = part if normed_grad is None else normed_grad + part
    inward, gain_grad, shift_grad = norm_backward(resid[...], vectors[0:1, :], normed_grad)
    grad_out[...] = middle_grad[...] + inward
    zero_row = jnp.zeros_like(gain_grad)
    vector_out[...] = jnp.concatenate([gain_grad, shift_grad] + [zero_row] * 6, axis=0)


def hidden_grad_kernel(
    upper_own, upper_other, active_own, active_other, normed_own, normed_other, branch_own, branch_other, up_keep,
    up_send, down_keep, down_send
):
    normed = jnp.concatenate([normed_own[...], normed_other[...]], axis=0)
    branch = jnp.concatenate([branch_own[...], branch_other[...]], axis=0)
    for position, up_out, down_out in ((1, up_send, down_send), (0, up_keep, down_keep)):
        upper = jnp.concatenate([upper_own[position], upper_other[position]], axis=0)
        up_out[...] = dot_tn(upper, normed).astype(BF16)
        active = jnp.concatenate([active_own[position], active_other[position]], axis=0)
        down_out[...] = dot_tn(active, branch).astype(BF16)


def attend_grad_kernel(
    stacked_own, stacked_other, normed_own, normed_other, attn_own, attn_other, keep_out, send_out
):
    normed = jnp.concatenate([normed_own[...], normed_other[...]], axis=0)
    attn = jnp.concatenate([attn_own[...], attn_other[...]], axis=0)
    split = 3 * (normed.shape[1] // 4)
    for position, out in ((1, send_out), (0, keep_out)):
        stacked = jnp.concatenate([stacked_own[position], stacked_other[position]], axis=0)
        out[0:split, :] = dot_tn(stacked[:, :split], normed).astype(BF16)
        out[split:, :] = dot_tn(stacked[:, split:], attn).astype(BF16)


def ortho_kernel(pieces, grad_own, grad_other, moment, result, whole):
    index = lax.axis_index("dp")
    size = moment.shape[2]
    width = moment.shape[3]
    eye = (iota((width, width), 0) == iota((width, width), 1)).astype(F32)

    def exact(left, right, dims=(((1,), (0,)), ((), ()))):
        return lax.dot_general(left, right, dims, precision=EXACT, preferred_element_type=F32)

    count = grad_own.shape[0]
    grads, sources, grams, chains, norms = [], [], [], [], []
    for block in range(count):
        grad = grad_own[block].astype(F32) + grad_other[block].astype(F32)
        for piece in range(pieces):
            start = pl.multiple_of((index ^ piece) * size, size) if pieces > 1 else 0
            whole[block, pl.ds(start, size), :] = moment[piece, block].astype(F32)
        source = MOMENTUM_DECAY * whole[block].T + grad
        gram = exact(source, source, (((1,), (1,)), ((), ())))
        trace = jnp.sum(gram * eye)
        norm = jnp.sqrt(trace) + ORTHO_EPSILON
        grads.append(grad)
        sources.append(source)
        norms.append(norm)
        grams.append(gram / (norm * norm))
        chains.append(None)
    for iteration in range(NS_STEPS):
        steps = []
        for block in range(count):
            gram = grams[block]
            steps.append(ORTHO_LINEAR * eye + ORTHO_CUBIC * gram + ORTHO_QUINTIC * exact(gram, gram))
        for block in range(count):
            step = steps[block]
            chains[block] = step if iteration == 0 else exact(chains[block], step)
        if iteration + 1 < NS_STEPS:
            halves = [exact(steps[block], grams[block]) for block in range(count)]
            grams = [exact(halves[block], steps[block]) for block in range(count)]
    for block in range(count):
        ortho = dot_tn(sources[block].astype(BF16), (chains[block] / norms[block]).astype(BF16))
        for which, value in ((0, grads[block].T), (1, ortho)):
            if pieces == 1:
                result[0, block, which] = value.astype(BF16)
            else:
                whole[block] = value
                for piece in range(pieces):
                    start = pl.multiple_of((index ^ piece) * size, size)
                    result[piece, block, which] = whole[block, pl.ds(start, size), :].astype(BF16)


def vmem(count):
    return [pl.BlockSpec(memory_space=pltpu.VMEM)] * count


def anywhere(count):
    return [pl.BlockSpec(memory_space=pl.ANY)] * count


def scalars():
    return [pl.BlockSpec(memory_space=pltpu.SMEM)]


def shape(dims, dtype=F32):
    return jax.ShapeDtypeStruct(dims, dtype)


def call(kernel, name, in_specs, outs, scratch, flops, moved):
    return pl.pallas_call(
        kernel,
        name=name,
        out_shape=outs,
        in_specs=in_specs,
        out_specs=vmem(len(outs)),
        scratch_shapes=scratch,
        cost_estimate=pl.CostEstimate(flops=int(flops), bytes_accessed=int(moved), transcendentals=0),
        compiler_params=pltpu.CompilerParams(vmem_limit_bytes=VMEM_BYTES),
    )


def flat(weight):
    return [item for slot in weight for item in slot]


def copies_of(weight):
    return len(flat(weight)) * (4 if len(weight[0]) > 1 else 1)


def project(resid, vectors, tables, weight):
    rows, width = resid.shape
    refs = flat(weight)
    feats = width // HEAD_DIM * FEATS
    outs = [
        shape((rows, width), BF16),
        shape((rows, feats), BF16),
        shape((rows, feats), BF16),
        shape((rows, width), BF16),
        shape((rows, width)),
        shape((rows, width)),
        shape((2, feats, 2 * HEAD_DIM), BF16),
    ]
    return call(
        partial(project_kernel, len(refs)),
        "project",
        vmem(6) + anywhere(len(refs)),
        outs,
        [pltpu.VMEM((4, width, 640), BF16), pltpu.SemaphoreType.DMA((copies_of(weight),))],
        2 * rows * width * width * 3 * 1.5,
        8 * width * width,
    )(resid, vectors, tables["cosine"], tables["sine"], tables["map"], tables["column"], *refs)


def mix_scratch(width, weight):
    return [
        pltpu.VMEM((4, width, 256), BF16),
        pltpu.VMEM((4, width, width), BF16),
        pltpu.VMEM((4, width, width), BF16),
        pltpu.SemaphoreType.DMA((3 * copies_of(weight),)),
    ]


def mix(resid, vectors, bias, state, received, tables, weights):
    rows, width = resid.shape
    refs = [flat(weight) for weight in weights]
    counts = (len(refs[0]), copies_of(weights[0]))
    pair = (2, rows, width)
    outs = [
        shape((rows, width)),
        shape((rows, width)),
        shape((rows, width)),
        shape((rows, width), BF16),
        shape(pair, BF16),
        shape(pair, BF16),
        shape(pair, BF16),
        shape(pair, BF16),
        shape((rows, width)),
    ]
    return call(
        partial(mix_kernel, counts),
        "mix",
        vmem(11) + scalars() + anywhere(3 * counts[0]),
        outs,
        mix_scratch(width, weights[0]),
        2 * rows * width * width * 12,
        20 * width * width,
    )(
        resid, vectors, bias, state["phi_query"], state["phi_key"], state["value"], tables["column"], tables["row"],
        *received, tables["shares"], *refs[0], *refs[1], *refs[2],
    )


def back_mix(grad, vectors, state, tables, weights):
    rows, width = grad.shape
    refs = [flat(weight) for weight in weights]
    counts = (len(refs[0]), copies_of(weights[0]))
    pair = (2, rows, width)
    feats = width // HEAD_DIM * FEATS
    outs = [
        shape((rows, width), BF16),
        shape(pair, BF16),
        shape(pair, BF16),
        shape((rows, width)),
        shape((rows, width), BF16),
        shape((rows, width), BF16),
        shape((rows, width), BF16),
        shape((2, feats, 2 * HEAD_DIM), BF16),
        shape((8, width)),
        shape((4, width)),
    ]
    return call(
        partial(back_mix_kernel, counts),
        "back_mix",
        vmem(9) + anywhere(3 * counts[0]),
        outs,
        mix_scratch(width, weights[0]),
        2 * rows * width * width * 11,
        20 * width * width,
    )(
        grad, vectors, state["middle"], state["slope_keep"], state["slope_send"], state["inverse"], state["context"],
        state["phi_query"], tables["column"], *refs[0], *refs[1], *refs[2],
    )


def back_project(resid, vectors, state, back, received, back_received, tables, weight):
    rows, width = resid.shape
    refs = flat(weight)
    pair = (2, rows, width)
    outs = [shape(pair, BF16), shape(pair, BF16), shape((rows, width)), shape((8, width))]
    return call(
        partial(back_project_kernel, len(refs)),
        "back_project",
        vmem(22) + scalars() + anywhere(len(refs)),
        outs,
        [pltpu.VMEM((4, width, 640), BF16), pltpu.SemaphoreType.DMA((copies_of(weight),))],
        2 * rows * width * width * 8,
        8 * width * width,
    )(
        resid, vectors, tables["cosine"], tables["sine"], tables["map"], tables["column"], tables["row"],
        state["phi_query"], state["phi_key"], state["value"], state["query"], state["key"], back["numer"],
        back["denom"], state["context"], back["middle_grad"], *received, *back_received, tables["shares"], *refs,
    )


def hidden_grad(*operands):
    width = operands[4].shape[1]
    return call(
        hidden_grad_kernel, "hidden_grad", vmem(8), [shape((width, width), BF16)] * 4, [],
        2 * 512 * width * width * 4, 16 * width * width,
    )(*operands)


def attend_grad(*operands):
    width = operands[2].shape[1]
    return call(
        attend_grad_kernel, "attend_grad", vmem(6), [shape((width, width), BF16)] * 2, [],
        2 * 512 * width * width * 2, 8 * width * width,
    )(*operands)


def orthogonalize(grad_own, grad_other, moment):
    pieces, count, size, width = moment.shape
    return call(
        partial(ortho_kernel, pieces), "orthogonalize", vmem(3), [shape((pieces, count, 2, size, width), BF16)],
        [pltpu.VMEM((count, pieces * size, width), F32)],
        2 * 6 * 20 * count * width**3, 4 * count * width * pieces * size,
    )(grad_own, grad_other, moment)[0]


def doc_tables(segment_row, feature_map, rows):
    index = lax.axis_index("head")
    own = lax.dynamic_slice_in_dim(segment_row, index * rows, rows, 0)
    starts = jnp.sum((segment_row[None, :] < own[:, None]).astype(jnp.int32), axis=1, dtype=jnp.int32)
    offsets = (index * rows + jnp.arange(rows, dtype=jnp.int32) - starts).astype(F32)
    half = HEAD_DIM // 2
    frequency = ROPE_BASE ** (-jnp.arange(half, dtype=F32) / half)
    angles = offsets[:, None] * frequency[None, :]
    scale = HEAD_DIM ** (-0.25)
    cosine = jnp.cos(angles) * scale
    sine = jnp.sin(angles) * scale
    shares = []
    for offset in (1, 2, 3):
        other = index ^ offset
        first = segment_row[other * rows]
        last = segment_row[other * rows + rows - 1]
        shares.append(
            jnp.stack([first == own[0], last == own[0], first == own[rows - 1], last == own[rows - 1]]).astype(F32)
        )
    return {
        "cosine": jnp.tile(cosine, (1, 2 * CHUNK // HEAD_DIM)),
        "sine": jnp.tile(jnp.concatenate([-sine, sine], axis=1), (1, CHUNK // HEAD_DIM)),
        "column": own[:, None],
        "row": own[None, :],
        "shares": jnp.stack(shares),
        "maps": [jnp.kron(jnp.eye(4, dtype=F32), feature_map[layer]) for layer in range(feature_map.shape[0])],
    }


def exchange_edges(summary):
    return [swap_head(summary, offset) for offset in (1, 2, 3)]


def added(left, right):
    return (left.astype(F32) + right.astype(F32)).astype(BF16)


def halve(blocks, bit):
    kept = lax.dynamic_index_in_dim(blocks, bit, 1, keepdims=False)
    sent = lax.dynamic_index_in_dim(blocks, 1 - bit, 1, keepdims=False)
    return kept, sent


def adam_update(parameter, gradient, first_moment, second_moment):
    first_moment = BETA_FIRST * first_moment + (1.0 - BETA_FIRST) * gradient
    second_moment = BETA_SECOND * second_moment + (1.0 - BETA_SECOND) * gradient * gradient
    first_hat = first_moment / (1.0 - BETA_FIRST**STEP)
    second_hat = second_moment / (1.0 - BETA_SECOND**STEP)
    return (
        parameter - ADAM_RATE * first_hat / (jnp.sqrt(second_hat) + ADAM_EPSILON),
        first_moment,
        second_moment,
    )


def split_columns(matrix, width):
    rows = matrix.shape[0]
    return jnp.transpose(matrix.reshape(rows, -1, width), (1, 0, 2))


def join_columns(blocks):
    count, rows, width = blocks.shape
    return jnp.transpose(blocks, (1, 0, 2)).reshape(rows, count * width)


def per_device(
    block_input,
    cotangent,
    marked,
    segments,
    feature_map,
    vectors,
    bias_up,
    w_query_key,
    w_value,
    w_out,
    w_up,
    w_down,
    moment_query_key,
    moment_value,
    moment_out,
    moment_up,
    moment_down,
    vector_first,
    vector_second,
    bias_first,
    bias_second,
):
    layers = w_value.shape[0]
    block = w_value.shape[2]
    rows = block_input.shape[0]
    dp_size = lax.axis_size("dp")
    dp_index = lax.axis_index("dp")
    quick = dp_size == 8

    gathered = []
    for layer in range(layers):
        attend_part = jnp.concatenate(
            [w_query_key[layer, :, 0], w_query_key[layer, :, 1], w_value[layer], w_out[layer].T], axis=1
        ).astype(BF16)
        up_part = w_up[layer].astype(BF16)
        down_part = w_down[layer].T.astype(BF16)
        gathered.append(
            (
                gather_weight(attend_part, layer % 2 == 0),
                gather_weight(up_part, True),
                gather_weight(down_part, False),
            )
        )
    bias_slots = [bias_up] + [swap_head(bias_up, offset) for offset in (1, 2, 3)]
    biases = [jnp.stack([item[layer] for item in bias_slots]) for layer in range(layers)]

    moments = (moment_query_key, moment_value, moment_out, moment_up, moment_down)
    old_blocks = []
    for layer in range(layers):
        attend_blocks = jnp.stack(
            [
                moment_query_key[layer, :, 0],
                moment_query_key[layer, :, 1],
                moment_value[layer],
                moment_out[layer].T,
            ]
        )
        hidden_blocks = jnp.concatenate(
            [split_columns(moment_up[layer], block), split_columns(moment_down[layer].T, block)]
        )
        old_blocks.append((attend_blocks.astype(BF16), hidden_blocks.astype(BF16)))

    tables = doc_tables(segments[0], feature_map, rows)
    resid = block_input.astype(F32)
    inputs = []
    states = []
    summaries = []
    for layer in range(layers):
        own = dict(tables, map=tables["maps"][layer])
        inputs.append(resid)
        normed, phi_query, phi_key, value, query, key, summary = project(
            resid, vectors[layer], own, gathered[layer][0]
        )
        state = {
            "normed": normed, "phi_query": phi_query, "phi_key": phi_key, "value": value, "query": query, "key": key
        }
        received = exchange_edges(summary)
        (state["context"], state["inverse"], state["middle"], state["normed_two"], state["slope_keep"],
         state["slope_send"], state["active_keep"], state["active_send"], resid) = mix(
            resid, vectors[layer], biases[layer], state, received, own, gathered[layer]
        )
        states.append(state)
        summaries.append(received)
    activations = resid.astype(BF16)

    if quick:
        payloads = []
        for offset in range(8):
            owner = dp_index ^ offset
            payloads.append(
                jnp.stack(
                    [
                        part
                        for layer in range(layers)
                        for part in (
                            lax.dynamic_index_in_dim(old_blocks[layer][0], owner & 3, 0, keepdims=False),
                            lax.dynamic_index_in_dim(old_blocks[layer][1], owner, 0, keepdims=False),
                        )
                    ]
                )
            )
        owned_moments = jnp.stack(
            [payloads[0]] + [swap_dp(payloads[offset], offset) for offset in range(1, 8)]
        )

    gradient = cotangent.astype(F32) * marked[0][:, None].astype(F32)
    vector_grads = [None] * layers
    bias_grads = [None] * layers
    results = [None] * layers
    raw = [None] * layers
    for layer in reversed(range(layers)):
        own = dict(tables, map=tables["maps"][layer])
        state = states[layer]
        (branch, upper_keep, upper_send, middle_grad, attn, numer, denom, back_summary, vector_two,
         bias_grads[layer]) = back_mix(gradient, vectors[layer], state, own, gathered[layer])
        back = {"numer": numer, "denom": denom, "middle_grad": middle_grad}
        back_received = exchange_edges(back_summary)
        stacked_keep, stacked_send, gradient, vector_one = back_project(
            inputs[layer], vectors[layer], state, back, summaries[layer], back_received, own, gathered[layer][0]
        )
        vector_grads[layer] = (vector_one + vector_two)[:5]
        up_keep, up_send, down_keep, down_send = hidden_grad(
            upper_keep, swap_head(upper_send, 1), state["active_keep"], swap_head(state["active_send"], 1),
            state["normed_two"], swap_head(state["normed_two"], 1), branch, swap_head(branch, 1),
        )
        attend_keep, attend_send = attend_grad(
            stacked_keep, swap_head(stacked_send, 1), state["normed"], swap_head(state["normed"], 1),
            attn, swap_head(attn, 1),
        )
        if not quick:
            attend_sum = added(attend_keep, swap_head(attend_send, 2))
            up_sum = added(up_keep, swap_head(up_send, 2))
            down_sum = added(down_keep, swap_head(down_send, 2))
            raw[layer] = jnp.concatenate([attend_sum, up_sum, down_sum]).reshape(-1, block, attend_sum.shape[1])
            continue
        y_bit, near_bit, far_bit = dp_index & 1, (dp_index >> 1) & 1, dp_index >> 2
        view = (2, 2, block, up_keep.shape[1])
        up_sum = added(up_keep, swap_head(up_send, 2)).reshape(view)
        kept, sent = halve(up_sum, y_bit)
        up_sum = added(kept, swap_dp(sent, 1))
        down_sums = []
        for part in (down_send, down_keep):
            kept, sent = halve(part.reshape(view), y_bit)
            down_sums.append(added(kept, swap_dp(sent, 1)))
        down_sum = added(down_sums[1], swap_head(down_sums[0], 2))
        hidden = jnp.stack([up_sum, down_sum])
        kept, sent = halve(hidden, near_bit)
        hidden = added(kept, swap_dp(sent, 2))
        hidden_own = lax.dynamic_index_in_dim(hidden, far_bit, 0, keepdims=False)
        hidden_other = swap_dp(lax.dynamic_index_in_dim(hidden, 1 - far_bit, 0, keepdims=False), 4)
        attend_sum = added(attend_keep, swap_head(attend_send, 2)).reshape(view)
        kept, sent = halve(attend_sum, y_bit)
        attend_sum = added(kept, swap_dp(sent, 1))[None]
        kept, sent = halve(attend_sum, near_bit)
        attend_own = added(kept, swap_dp(sent, 2))[0]
        attend_other = swap_dp(attend_own, 4)
        sent_back = orthogonalize(
            jnp.stack([attend_own, hidden_own]),
            jnp.stack([attend_other, hidden_other]),
            owned_moments[:, 2 * layer : 2 * layer + 2],
        )
        hidden_back = jnp.stack(
            [sent_back[0, 1]] + [swap_dp(sent_back[offset, 1], offset) for offset in range(1, 8)]
        )
        attend_back = jnp.stack(
            [sent_back[0, 0]] + [swap_dp(sent_back[offset, 0], offset) for offset in range(1, 4)]
        )
        results[layer] = jnp.stack(
            [lax.dynamic_index_in_dim(attend_back, position ^ (dp_index & 3), 0, keepdims=False) for position in range(4)]
            + [lax.dynamic_index_in_dim(hidden_back, position ^ dp_index, 0, keepdims=False) for position in range(8)]
        )
    if not quick:
        count = layers * raw[0].shape[0]
        padded = -(-count // dp_size) * dp_size
        grads = jnp.concatenate(raw)
        grads = jnp.concatenate([grads, jnp.zeros((padded - count,) + grads.shape[1:], grads.dtype)])
        grads = lax.psum_scatter(grads.astype(F32), "dp", scatter_dimension=0, tiled=True)
        old = jnp.concatenate([part for pair in old_blocks for part in pair])
        old = jnp.concatenate([old, jnp.zeros((padded - count,) + old.shape[1:], old.dtype)])
        old = lax.all_to_all(old, "dp", split_axis=0, concat_axis=1, tiled=True)
        back = orthogonalize(grads, jnp.zeros_like(grads), old[None])[0]
        back = lax.all_to_all(back, "dp", split_axis=2, concat_axis=0, tiled=True)
        results = [back[layer * 12 : (layer + 1) * 12] for layer in range(layers)]

    vector_stack = jnp.stack(vector_grads)
    bias_stack = jnp.stack(bias_grads)
    keep, send = bias_stack[:, 0::2], bias_stack[:, 1::2]
    vector_stack, keep = jax.tree.map(
        lambda mine, other: mine + swap_head(other, 1), (vector_stack, keep), (vector_stack, send)
    )
    keep, send = keep[:, 0], keep[:, 1]
    vector_total, bias_total = jax.tree.map(
        lambda mine, other: mine + swap_head(other, 2), (vector_stack, keep), (vector_stack, send)
    )
    if quick:
        packed = jnp.concatenate([vector_total.reshape(-1, vector_total.shape[2]), bias_total])
        for offset in (1, 2, 4):
            packed = packed + swap_dp(packed, offset)
        vector_total = packed[: 5 * layers].reshape(vector_total.shape)
        bias_total = packed[5 * layers :]
    else:
        vector_total, bias_total = lax.psum((vector_total, bias_total), "dp")

    fresh = []
    for which in range(2):
        parts = [result[:, which].astype(F32) for result in results]
        fresh.append(
            (
                jnp.stack([jnp.stack([part[0], part[1]], axis=1) for part in parts]),
                jnp.stack([part[2] for part in parts]),
                jnp.stack([part[3].T for part in parts]),
                jnp.stack([join_columns(part[4:8]) for part in parts]),
                jnp.stack([join_columns(part[8:12]).T for part in parts]),
            )
        )
    next_moments = tuple(MOMENTUM_DECAY * old + grad for old, grad in zip(moments, fresh[0]))
    muon_scale = (w_value.shape[1] * dp_size / block) ** 0.5
    masters = (w_query_key, w_value, w_out, w_up, w_down)
    next_masters = tuple(
        master * (1.0 - MUON_RATE * WEIGHT_DECAY) - MUON_RATE * muon_scale * ortho
        for master, ortho in zip(masters, fresh[1])
    )
    copies = tuple(master.astype(BF16) for master in next_masters)
    vectors_next, vector_first_next, vector_second_next = adam_update(
        vectors, vector_total, vector_first, vector_second
    )
    bias_next, bias_first_next, bias_second_next = adam_update(bias_up, bias_total, bias_first, bias_second)
    return (
        (activations, gradient)
        + next_masters
        + next_moments
        + copies
        + (vectors_next, vector_first_next, vector_second_next, bias_next, bias_first_next, bias_second_next)
    )


def solution(mesh):
    shards = (
        P(None, "dp", None, "head"),
        P(None, "dp", "head"),
        P(None, "head", "dp"),
        P(None, "dp", "head"),
        P(None, "head", "dp"),
    )
    rows = P(("dp", "head"), None)
    placed = (
        (rows, rows, P("dp", "head"), P("dp", None), P(), P(), P(None, "head"))
        + shards
        + shards
        + (P(), P(), P(None, "head"), P(None, "head"))
    )
    return jax.shard_map(
        per_device,
        mesh=mesh,
        in_specs=placed,
        out_specs=(rows, rows) + shards + shards + shards + (P(), P(), P()) + (P(None, "head"),) * 3,
        check_vma=False,
    )
```

time: 1350 us -> 750 us (0.56)
  waiting for transfers between devices: 794 us -> 340 us
  matrix products: 218 us -> 0 us
  Pallas kernels: 0 us -> 144 us
  blocking collectives: 122 us -> 0 us
  starting transfers between devices: 9.92 us -> 122 us
  other arithmetic: 92.2 us -> 49.7 us
  local copies, waits for them, and re-layouts: 88.2 us -> 65.4 us
    reduce_scatter x10 -> x0, waiting for transfers between devices: 363 us -> none  [the longest x1 96.4 us: per_device(): lax.psum_scatter(up_grad, 'dp', scatter_dimension=1, tiled=True)]
    ppermute x0 -> x145, waiting for transfers between devices: none -> 340 us  [the longest x73 182 us: swap_dp(): lax.ppermute(values, 'dp', [(d, d ^ offset) for d in range(lax.axis_size(...]
    dot_general x63 -> x0, matrix products: 218 us -> none  [the longest x6 37.2 us: linear_attention(): jnp.einsum('shx,hxd->shd', spread_query, summary, precision=EXACT)]
    unnamed x27 -> x0, waiting for transfers between devices: 215 us -> none
    all_gather x11 -> x0, waiting for transfers between devices: 194 us -> none  [the longest x1 49 us: per_device(): lax.all_gather(w_up.astype(jnp.bfloat16), 'dp', axis=1, tiled=True)]
    pallas_call x0 -> x14, Pallas kernels: none -> 144 us  [the longest x2 28.2 us: back_project(): call(partial(back_project_kernel, len(refs)), 'back_project', vmem(22) +...]
    ppermute x0 -> x145, starting transfers between devices: none -> 122 us  [the longest x73 83.4 us: swap_dp(): lax.ppermute(values, 'dp', [(d, d ^ offset) for d in range(lax.axis_size(...]
    all_gather x2 -> x0, blocking collectives: 68.4 us -> none  [the longest x1 35.2 us: per_device(): lax.all_gather(w_out.astype(jnp.bfloat16), 'dp', axis=2, tiled=True)]
  transfers between devices with their start and end apart: 26 -> 145, of which waited for: 21 -> 63; matrix products, arithmetic and copies ran while one was open for 15% -> 10% of each run, Pallas kernels for 0% -> 18%
where the time goes in v1:
time: 750 us; the launch traced here: 739 us
  waiting for transfers between devices  340 us (45%)
  Pallas kernels  144 us (19%)
  starting transfers between devices  122 us (16%)
  local copies, waits for them, and re-layouts  65.4 us (9%)
  other arithmetic  49.7 us (7%)
  between operations  19 us (3%)
    ppermute x73, waiting for transfers between devices, swap_dp(): lax.ppermute(values, 'dp', [(d, d ^ offset) for d in range(lax.axis_size(...  182 us
    ppermute x72, waiting for transfers between devices, swap_head(): lax.ppermute(values, 'head', [(h, h ^ offset) for h in range(lax.axis_siz...  157 us
    ppermute x73, starting transfers between devices, swap_dp(): lax.ppermute(values, 'dp', [(d, d ^ offset) for d in range(lax.axis_size(...  83.4 us
    ppermute x72, starting transfers between devices, swap_head(): lax.ppermute(values, 'head', [(h, h ^ offset) for h in range(lax.axis_siz...  38.4 us
    pallas_call x2, Pallas kernels, back_project(): call(partial(back_project_kernel, len(refs)), 'back_project', vmem(22) +...  28.2 us
    pallas_call x2, Pallas kernels, back_mix(): call(partial(back_mix_kernel, counts), 'back_mix', vmem(9) + anywhere(3 *...  27.4 us
    unnamed x395, local copies, waits for them, and re-layouts  26.9 us
    pallas_call x2, Pallas kernels, mix(): call(partial(mix_kernel, counts), 'mix', vmem(11) + scalars() + anywhere(...  26.2 us
  transfers between devices with their start and end apart: 145, of which 63 were waited for; matrix products, arithmetic and copies ran while one was open for 10% of the time, Pallas kernels for 18%

profile of v1, /device:TPU:0, one launch (start us, length us, event | category | flops | bytes accessed | tf_op | source)
XLA Modules:
  0.0 739.1 jit_solution(3737595254458385991)
XLA Ops:
  27.0 4.4 collective-permute-done.17
  32.9 4.8 collective-permute-done.27
  39.3 7.9 %collective-permute-done.37 = bf16[96,768]{1,0:T(8,128)(2,1)S(1)} collective-permute-done((bf16[96,768]{1,0:T(8,128)(2,1)S(1)}, bf16[96,768]{1,0:T(8,128)(2,1)S(1)}, u32[]{:S(2)}, u32[]{:S(2)}) %collective-permute-start.37) | collective-permute-done | bytes 147488 | tf_op jit(solution)/shard_map/ppermute | solution.py:60
  49.5 4.1 collective-permute-done.50
  53.6 4.7 collective-permute-done.5
  65.6 4.8 collective-permute-done.95
  71.8 8.1 %collective-permute-done.18 = bf16[96,768]{1,0:T(8,128)(2,1)S(1)} collective-permute-done((bf16[96,768]{1,0:T(8,128)(2,1)}, bf16[96,768]{1,0:T(8,128)(2,1)S(1)}, u32[]{:S(2)}, u32[]{:S(2)}) %collective-permute-start.18) | collective-permute-done | bytes 147488 | tf_op jit(solution)/shard_map/ppermute | solution.py:60
  79.9 7.9 %collective-permute-done.28 = bf16[96,768]{1,0:T(8,128)(2,1)S(1)} collective-permute-done((bf16[96,768]{1,0:T(8,128)(2,1)}, bf16[96,768]{1,0:T(8,128)(2,1)S(1)}, u32[]{:S(2)}, u32[]{:S(2)}) %collective-permute-start.28) | collective-permute-done | bytes 147488 | tf_op jit(solution)/shard_map/ppermute | solution.py:60
  87.8 4.7 collective-permute-done.38
  101.7 7.2 collective-permute-done.9.rest_4_
  114.6 6.9 collective-permute-done.22.rest_12_
  129.8 4.3 collective-permute-done.32.rest_20_
  139.7 7.1 collective-permute-done.42.rest_4_
  152.9 6.5 collective-permute-done.55.rest_12_
  189.8 9.3 %collective-permute-done.23.rest_13_ = bf16[384,768]{1,0:T(8,128)(2,1)S(1)} collective-permute-done((bf16[384,768]{1,0:T(8,128)(2,1)}, bf16[384,768]{1,0:T(8,128)(2,1)S(1)}, u32[]{:S(2)}, u32[]{:S(2)}) %collective-permute-start.23) | collective-permute-done | bytes 589856 | tf_op jit(solution)/shard_map/ppermute | solution.py:56
  227.1 8.9 %project.2 = (bf16[256,768]{1,0:T(8,128)(2,1)}, bf16[256,384]{1,0:T(8,128)(2,1)}, bf16[256,384]{1,0:T(8,128)(2,1)}, bf16[256,768]{1,0:T(8,128)(2,1)}, f32[256,76...) custom-call(f32[256,768]{1,0:T(8,128)} %convert_element_type.319.resid, ...), custom_call_target="tpu_custom_call" | custom-call | flops 1358954496 | bytes 4718592 | tf_op jit(solution)/shard_map/project/pallas_call | solution.py:593
  242.9 5.4 collective-permute-done.14.recv_two
  252.3 13.0 %mix.2 = (f32[256,768]{1,0:T(8,128)}, f32[256,768]{1,0:T(8,128)}, f32[256,768]{1,0:T(8,128)}, bf16[256,768]{1,0:T(8,128)(2,1)}, bf16[2,256,768]{2,1,0:T(8,128)(2...) custom-call(f32[256,768]{1,0:T(8,128)} %convert_element_type.319.res, ...), custom_call_target="tpu_custom_call" | custom-call | flops 3623878656 | bytes 11796480 | tf_op jit(solution)/shard_map/mix/pallas_call | solution.py:629
  265.4 8.6 %project.3 = (bf16[256,768]{1,0:T(8,128)(2,1)}, bf16[256,384]{1,0:T(8,128)(2,1)}, bf16[256,384]{1,0:T(8,128)(2,1)}, bf16[256,768]{1,0:T(8,128)(2,1)}, f32[256,76...) custom-call(f32[256,768]{1,0:T(8,128)} %get-tuple-element.99.resid, ...), custom_call_target="tpu_custom_call" | custom-call | flops 1358954496 | bytes 4718592 | tf_op jit(solution)/shard_map/project/pallas_call | solution.py:593
  276.7 3.3 collective-permute-start.97
  285.8 13.2 %mix.3 = (f32[256,768]{1,0:T(8,128)}, f32[256,768]{1,0:T(8,128)}, f32[256,768]{1,0:T(8,128)}, bf16[256,768]{1,0:T(8,128)(2,1)}, bf16[2,256,768]{2,1,0:T(8,128)(2...) custom-call(f32[256,768]{1,0:T(8,128)} %get-tuple-element.99.resid, ...), custom_call_target="tpu_custom_call" | custom-call | flops 3623878656 | bytes 11796480 | tf_op jit(solution)/shard_map/mix/pallas_call | solution.py:629
  299.0 13.8 %back_mix.2 = (bf16[256,768]{1,0:T(8,128)(2,1)}, bf16[2,256,768]{2,1,0:T(8,128)(2,1)}, bf16[2,256,768]{2,1,0:T(8,128)(2,1)}, f32[256,768]{1,0:T(8,128)}, bf16[25...) custom-call(f32[256,768]{1,0:T(8,128)} %convert_multiply_fusion.grad, ...), custom_call_target="tpu_custom_call" | custom-call | flops 3321888768 | bytes 11796480 | tf_op jit(solution)/shard_map/back_mix/pallas_call | solution.py:661
  315.8 5.8 collective-permute-done.70.back_two
  324.8 14.0 %back_project.2 = (bf16[2,256,768]{2,1,0:T(8,128)(2,1)}, bf16[2,256,768]{2,1,0:T(8,128)(2,1)}, f32[256,768]{1,0:T(8,128)}, f32[8,768]{1,0:T(8,128)}) custom-call(f32[256,768]{1,0:T(8,128)} %get-tuple-element.99.resid, f32[5,768]{1,0:T(8,128)} %get-tuple-element.364.vectors, f32[256,256]{1,0:T(8,128)} %copy.132.cosine, f32[256,256]{1,0:T(8,128)} %copy.133.sine, ...), custom_call_target="tpu_custom_call" | custom-call | flops 2415919104 | bytes 4718592 | tf_op jit(solution)/shard_map/back_project/pallas_call | solution.py:680
  338.8 13.7 %back_mix.3 = (bf16[256,768]{1,0:T(8,128)(2,1)}, bf16[2,256,768]{2,1,0:T(8,128)(2,1)}, bf16[2,256,768]{2,1,0:T(8,128)(2,1)}, f32[256,768]{1,0:T(8,128)}, bf16[25...) custom-call(f32[256,768]{1,0:T(8,128)} %get-tuple-element.118.grad, ...), custom_call_target="tpu_custom_call" | custom-call | flops 3321888768 | bytes 11796480 | tf_op jit(solution)/shard_map/back_mix/pallas_call | solution.py:661
  364.4 14.2 %back_project.3 = (bf16[2,256,768]{2,1,0:T(8,128)(2,1)}, bf16[2,256,768]{2,1,0:T(8,128)(2,1)}, f32[256,768]{1,0:T(8,128)}, f32[8,768]{1,0:T(8,128)}) custom-call(f32[256,768]{1,0:T(8,128)} %convert_element_type.319.resid, f32[5,768]{1,0:T(8,128)} %get-tuple-element.365.vectors, f32[256,256]{1,0:T(8,128)} %copy.132.cosine, f32[256,256]{1,0:T(8,128)} %copy.133.sine, ...), custom_call_target="tpu_custom_call" | custom-call | flops 2415919104 | bytes 4718592 | tf_op jit(solution)/shard_map/back_project/pallas_call | solution.py:680
  389.9 4.0 collective-permute-done.143
  395.1 4.9 collective-permute-done.144
  403.6 6.1 hidden_grad.3
  416.9 6.0 hidden_grad.2
  432.1 4.4 attend_grad.3
  437.8 4.4 attend_grad.2
  446.4 10.9 %collective-permute-done.122 = bf16[2,192,768]{2,1,0:T(8,128)(2,1)S(1)} collective-permute-done((bf16[2,192,768]{2,1,0:T(8,128)(2,1)S(1)}, bf16[2,192,768]{2,1,0:T(8,128)(2,1)S(1)}, u32[]{:S(2)}, u32[]{:S(2)}) %collective-permute-start.122) | collective-permute-done | bytes 589856 | tf_op jit(solution)/shard_map/ppermute | solution.py:60
  458.2 6.3 collective-permute-done.124
  469.1 58.6 %collective-permute-done.89 = bf16[2,192,768]{2,1,0:T(8,128)(2,1)S(1)} collective-permute-done((bf16[2,192,768]{2,1,0:T(8,128)(2,1)S(1)}, bf16[2,192,768]{2,1,0:T(8,128)(2,1)S(1)}, u32[]{:S(2)}, u32[]{:S(2)}) %collective-permute-start.89) | collective-permute-done | bytes 589856 | tf_op jit(solution)/shard_map/ppermute | solution.py:56
  531.6 21.0 %collective-permute-done.78 = bf16[768,768]{1,0:T(8,128)(2,1)S(1)} collective-permute-done((bf16[768,768]{1,0:T(8,128)(2,1)S(1)}, bf16[768,768]{1,0:T(8,128)(2,1)S(1)}, u32[]{:S(2)}, u32[]{:S(2)}) %collective-permute-start.78) | collective-permute-done | bytes 1179680 | tf_op jit(solution)/shard_map/ppermute | solution.py:56
  557.5 10.7 %collective-permute-done.79 = bf16[2,192,768]{2,1,0:T(8,128)(2,1)S(1)} collective-permute-done((bf16[2,192,768]{2,1,0:T(8,128)(2,1)S(1)}, bf16[2,192,768]{2,1,0:T(8,128)(2,1)S(1)}, u32[]{:S(2)}, u32[]{:S(2)}) %collective-permute-start.79) | collective-permute-done | bytes 589856 | tf_op jit(solution)/shard_map/ppermute | solution.py:60
  568.5 21.6 %collective-permute-done.115 = bf16[1,192,768]{2,1,0:T(8,128)(2,1)S(1)} collective-permute-done((bf16[1,192,768]{2,1,0:T(8,128)(2,1)S(1)}, bf16[1,192,768]{2,1,0:T(8,128)(2,1)S(1)}, u32[]{:S(2)}, u32[]{:S(2)}) %collective-permute-start.115) | collective-permute-done | bytes 294944 | tf_op jit(solution)/shard_map/ppermute | solution.py:60
  594.3 5.0 collective-permute-done.80
  603.6 22.3 %collective-permute-done.126 = bf16[192,768]{1,0:T(8,128)(2,1)S(1)} collective-permute-done((bf16[192,768]{1,0:T(8,128)(2,1)S(1)}, bf16[192,768]{1,0:T(8,128)(2,1)S(1)}, u32[]{:S(2)}, u32[]{:S(2)}) %collective-permute-start.126) | collective-permute-done | bytes 294944 | tf_op jit(solution)/shard_map/ppermute | solution.py:60
  625.9 6.3 collective-permute-done.127
  633.1 12.0 %orthogonalize.3 = bf16[8,2,2,96,192]{4,3,2,1,0:T(8,128)(2,1)} custom-call(bf16[2,192,768]{2,1,0:T(8,128)(2,1)} %pad_maximum_fusion.8.grad_own, bf16[2,192,768]{2,1,0:T(8,128)(2,1)} %pad_maximum_fusion.9.grad_other, bf16[8,2,96,192]{3,2,1,0:T(8,128)(2,1)} %get-tuple-element.264.moment), custom_call_target="tpu_custom_call" | custom-call | flops 3397386240 | bytes 1179648 | tf_op jit(solution)/shard_map/orthogonalize/pallas_call | solution.py:713
  652.7 5.0 collective-permute-done.132
  659.4 4.8 collective-permute-start.134
  664.5 3.3 collective-permute-start.136
  671.4 3.9 collective-permute-done.137
  676.3 11.5 %orthogonalize.2 = bf16[8,2,2,96,192]{4,3,2,1,0:T(8,128)(2,1)} custom-call(bf16[2,192,768]{2,1,0:T(8,128)(2,1)} %pad_maximum_fusion.6.grad_own, bf16[2,192,768]{2,1,0:T(8,128)(2,1)} %pad_maximum_fusion.7.grad_other, bf16[8,2,96,192]{3,2,1,0:T(8,128)(2,1)} %get-tuple-element.263.moment), custom_call_target="tpu_custom_call" | custom-call | flops 3397386240 | bytes 1179648 | tf_op jit(solution)/shard_map/orthogonalize/pallas_call | solution.py:713
  705.3 3.7 collective-permute-start.109
  (835 shorter events, 276.8 us)
Async XLA Ops:
  59.5 39.0 %collective-permute-start.6 = (bf16[384,768]{1,0:T(8,128)(2,1)S(1)}, bf16[384,768]{1,0:T(8,128)(2,1)S(1)}, u32[]{:S(2)}, u32[]{:S(2)}) collective-permute-start(bf16[384,768]{1,0:T(8,128)(2,1)S(1)} %pad_maximum_fusion.rest_0_), channel_id=1, source_target_pairs={{0,4},{4,0},{8,12},{12,8},{16,20},{20,16},{24,28},{28,24},{1,5},{5... | collective-permute-start | bytes 1769480 | tf_op jit(solution)/shard_map/ppermute | solution.py:60
  61.1 38.9 %collective-permute-start.7 = (bf16[384,768]{1,0:T(8,128)(2,1)S(1)}, bf16[384,768]{1,0:T(8,128)(2,1)S(1)}, u32[]{:S(2)}, u32[]{:S(2)}) collective-permute-start(bf16[384,768]{1,0:T(8,128)(2,1)S(1)} %pad_maximum_fusion.rest_0_), channel_id=1, source_target_pairs={{0,1},{1,0},{2,3},{3,2},{4,5},{5,4},{6,7},{7,6},{8,9},{9,8},{10,11... | collective-permute-start | bytes 1769480 | tf_op jit(solution)/shard_map/ppermute | solution.py:56
  64.9 22.9 %collective-permute-start.28 = (bf16[96,768]{1,0:T(8,128)(2,1)}, bf16[96,768]{1,0:T(8,128)(2,1)S(1)}, u32[]{:S(2)}, u32[]{:S(2)}) collective-permute-start(bf16[96,768]{1,0:T(8,128)(2,1)} %collective-permute-done.26), channel_id=1, source_target_pairs={{0,16},{4,20},{8,24},{12,28},{16,0},{20,4},{24,8},{28,12},{1,17},{... | collective-permute-start | bytes 442376 | tf_op jit(solution)/shard_map/ppermute | solution.py:60
  70.4 22.2 %collective-permute-start.38 = (bf16[96,768]{1,0:T(8,128)(2,1)}, bf16[96,768]{1,0:T(8,128)(2,1)S(1)}, u32[]{:S(2)}, u32[]{:S(2)}) collective-permute-start(bf16[96,768]{1,0:T(8,128)(2,1)} %copy-done.131), channel_id=1, source_target_pairs={{0,16},{4,20},{8,24},{12,28},{16,0},{20,4},{24,8},{28,12},{1,17},{... | collective-permute-start | bytes 442376 | tf_op jit(solution)/shard_map/ppermute | solution.py:60
  98.5 23.0 %collective-permute-start.22 = (bf16[384,768]{1,0:T(8,128)(2,1)S(1)}, bf16[384,768]{1,0:T(8,128)(2,1)S(1)}, u32[]{:S(2)}, u32[]{:S(2)}) collective-permute-start(bf16[384,768]{1,0:T(8,128)(2,1)S(1)} %pad_maximum_fusion.1.rest_8_), channel_id=1, source_target_pairs={{0,2},{1,3},{2,0},{3,1},{4,6},{5,7},{6,4},{7,5},{8,10},{9,11},{10,... | collective-permute-start | bytes 1769480 | tf_op jit(solution)/shard_map/ppermute | solution.py:56
  100.0 24.7 %collective-permute-start.29 = (bf16[384,768]{1,0:T(8,128)(2,1)S(1)}, bf16[384,768]{1,0:T(8,128)(2,1)S(1)}, u32[]{:S(2)}, u32[]{:S(2)}) collective-permute-start(bf16[384,768]{1,0:T(8,128)(2,1)S(1)} %pad_maximum_fusion.2.rest_16_), channel_id=1, source_target_pairs={{0,4},{4,0},{8,12},{12,8},{16,20},{20,16},{24,28},{28,24},{1,5},{5... | collective-permute-start | bytes 1769480 | tf_op jit(solution)/shard_map/ppermute | solution.py:60
  113.5 23.8 %collective-permute-start.39 = (bf16[384,768]{1,0:T(8,128)(2,1)S(1)}, bf16[384,768]{1,0:T(8,128)(2,1)S(1)}, u32[]{:S(2)}, u32[]{:S(2)}) collective-permute-start(bf16[384,768]{1,0:T(8,128)(2,1)S(1)} %pad_maximum_fusion.3.rest_0_), channel_id=1, source_target_pairs={{0,4},{4,0},{8,12},{12,8},{16,20},{20,16},{24,28},{28,24},{1,5},{5... | collective-permute-start | bytes 1769480 | tf_op jit(solution)/shard_map/ppermute | solution.py:60
  124.6 22.2 %collective-permute-start.42 = (bf16[384,768]{1,0:T(8,128)(2,1)S(1)}, bf16[384,768]{1,0:T(8,128)(2,1)}, u32[]{:S(2)}, u32[]{:S(2)}) collective-permute-start(bf16[384,768]{1,0:T(8,128)(2,1)S(1)} %pad_maximum_fusion.3.rest_0_), channel_id=1, source_target_pairs={{0,2},{1,3},{2,0},{3,1},{4,6},{5,7},{6,4},{7,5},{8,10},{9,11},{10,... | collective-permute-start | bytes 1769480 | tf_op jit(solution)/shard_map/ppermute | solution.py:56
  126.2 23.8 %collective-permute-start.52 = (bf16[384,768]{1,0:T(8,128)(2,1)S(1)}, bf16[384,768]{1,0:T(8,128)(2,1)}, u32[]{:S(2)}, u32[]{:S(2)}) collective-permute-start(bf16[384,768]{1,0:T(8,128)(2,1)S(1)} %pad_maximum_fusion.4.rest_8_), channel_id=1, source_target_pairs={{0,4},{4,0},{8,12},{12,8},{16,20},{20,16},{24,28},{28,24},{1,5},{5... | collective-permute-start | bytes 1769480 | tf_op jit(solution)/shard_map/ppermute | solution.py:60
  138.7 22.1 %collective-permute-start.62 = (bf16[384,768]{1,0:T(8,128)(2,1)}, bf16[384,768]{1,0:T(8,128)(2,1)S(1)}, u32[]{:S(2)}, u32[]{:S(2)}) collective-permute-start(bf16[384,768]{1,0:T(8,128)(2,1)} %pad_maximum_fusion.5.rest_16_), channel_id=1, source_target_pairs={{0,4},{4,0},{8,12},{12,8},{16,20},{20,16},{24,28},{28,24},{1,5},{5... | collective-permute-start | bytes 1769480 | tf_op jit(solution)/shard_map/ppermute | solution.py:60
  150.0 33.4 %collective-permute-start.65 = (bf16[384,768]{1,0:T(8,128)(2,1)}, bf16[384,768]{1,0:T(8,128)(2,1)}, u32[]{:S(2)}, u32[]{:S(2)}) collective-permute-start(bf16[384,768]{1,0:T(8,128)(2,1)} %pad_maximum_fusion.5.rest_16_), channel_id=1, source_target_pairs={{0,2},{1,3},{2,0},{3,1},{4,6},{5,7},{6,4},{7,5},{8,10},{9,11},{10,... | collective-permute-start | bytes 1769480 | tf_op jit(solution)/shard_map/ppermute | solution.py:56
  152.9 32.7 %collective-permute-start.8 = (bf16[384,768]{1,0:T(8,128)(2,1)S(1)}, bf16[384,768]{1,0:T(8,128)(2,1)S(1)}, u32[]{:S(2)}, u32[]{:S(2)}) collective-permute-start(bf16[384,768]{1,0:T(8,128)(2,1)S(1)} %collective-permute-done.6.rest_1_), channel_id=1, source_target_pairs={{0,1},{1,0},{2,3},{3,2},{4,5},{5,4},{6,7},{7,6},{8,9},{9,8},{10,11... | collective-permute-start | bytes 1769480 | tf_op jit(solution)/shard_map/ppermute | solution.py:56
  159.4 27.4 %collective-permute-start.10 = (bf16[384,768]{1,0:T(8,128)(2,1)S(1)}, bf16[384,768]{1,0:T(8,128)(2,1)S(1)}, u32[]{:S(2)}, u32[]{:S(2)}) collective-permute-start(bf16[384,768]{1,0:T(8,128)(2,1)S(1)} %collective-permute-done.6.rest_1_), channel_id=1, source_target_pairs={{0,2},{1,3},{2,0},{3,1},{4,6},{5,7},{6,4},{7,5},{8,10},{9,11},{10,... | collective-permute-start | bytes 1769480 | tf_op jit(solution)/shard_map/ppermute | solution.py:56
  160.8 25.9 %collective-permute-start.11 = (bf16[384,768]{1,0:T(8,128)(2,1)S(1)}, bf16[384,768]{1,0:T(8,128)(2,1)S(1)}, u32[]{:S(2)}, u32[]{:S(2)}) collective-permute-start(bf16[384,768]{1,0:T(8,128)(2,1)S(1)} %collective-permute-done.9.rest_4_), channel_id=1, source_target_pairs={{0,1},{1,0},{2,3},{3,2},{4,5},{5,4},{6,7},{7,6},{8,9},{9,8},{10,11... | collective-permute-start | bytes 1769480 | tf_op jit(solution)/shard_map/ppermute | solution.py:56
  160.9 26.4 %collective-permute-start.21 = (bf16[384,768]{1,0:T(8,128)(2,1)}, bf16[384,768]{1,0:T(8,128)(2,1)}, u32[]{:S(2)}, u32[]{:S(2)}) collective-permute-start(bf16[384,768]{1,0:T(8,128)(2,1)} %collective-permute-done.19.rest_9_), channel_id=1, source_target_pairs={{0,1},{1,0},{2,3},{3,2},{4,5},{5,4},{6,7},{7,6},{8,9},{9,8},{10,11... | collective-permute-start | bytes 1769480 | tf_op jit(solution)/shard_map/ppermute | solution.py:56
  199.2 22.7 %collective-permute-start.41 = (bf16[384,768]{1,0:T(8,128)(2,1)S(1)}, bf16[384,768]{1,0:T(8,128)(2,1)S(1)}, u32[]{:S(2)}, u32[]{:S(2)}) collective-permute-start(bf16[384,768]{1,0:T(8,128)(2,1)S(1)} %collective-permute-done.39.rest_1_), channel_id=1, source_target_pairs={{0,1},{1,0},{2,3},{3,2},{4,5},{5,4},{6,7},{7,6},{8,9},{9,8},{10,11... | collective-permute-start | bytes 1769480 | tf_op jit(solution)/shard_map/ppermute | solution.py:56
  200.7 23.5 %collective-permute-start.43 = (bf16[384,768]{1,0:T(8,128)(2,1)}, bf16[384,768]{1,0:T(8,128)(2,1)}, u32[]{:S(2)}, u32[]{:S(2)}) collective-permute-start(bf16[384,768]{1,0:T(8,128)(2,1)} %collective-permute-done.42.rest_4_), channel_id=1, source_target_pairs={{0,4},{4,0},{8,12},{12,8},{16,20},{20,16},{24,28},{28,24},{1,5},{5... | collective-permute-start | bytes 1769480 | tf_op jit(solution)/shard_map/ppermute | solution.py:60
  201.8 23.4 %collective-permute-start.44 = (bf16[384,768]{1,0:T(8,128)(2,1)}, bf16[384,768]{1,0:T(8,128)(2,1)}, u32[]{:S(2)}, u32[]{:S(2)}) collective-permute-start(bf16[384,768]{1,0:T(8,128)(2,1)} %collective-permute-done.42.rest_4_), channel_id=1, source_target_pairs={{0,1},{1,0},{2,3},{3,2},{4,5},{5,4},{6,7},{7,6},{8,9},{9,8},{10,11... | collective-permute-start | bytes 1769480 | tf_op jit(solution)/shard_map/ppermute | solution.py:56
  201.9 23.2 %collective-permute-start.54 = (bf16[384,768]{1,0:T(8,128)(2,1)}, bf16[384,768]{1,0:T(8,128)(2,1)}, u32[]{:S(2)}, u32[]{:S(2)}) collective-permute-start(bf16[384,768]{1,0:T(8,128)(2,1)} %collective-permute-done.52.rest_9_), channel_id=1, source_target_pairs={{0,1},{1,0},{2,3},{3,2},{4,5},{5,4},{6,7},{7,6},{8,9},{9,8},{10,11... | collective-permute-start | bytes 1769480 | tf_op jit(solution)/shard_map/ppermute | solution.py:56
  202.8 22.9 %collective-permute-start.12 = (bf16[384,768]{1,0:T(8,128)(2,1)S(1)}, bf16[384,768]{1,0:T(8,128)(2,1)S(1)}, u32[]{:S(2)}, u32[]{:S(2)}) collective-permute-start(bf16[384,768]{1,0:T(8,128)(2,1)S(1)} %collective-permute-done.10.rest_5_), channel_id=1, source_target_pairs={{0,1},{1,0},{2,3},{3,2},{4,5},{5,4},{6,7},{7,6},{8,9},{9,8},{10,11... | collective-permute-start | bytes 1769480 | tf_op jit(solution)/shard_map/ppermute | solution.py:56
  239.7 35.3 %collective-permute-start.67 = (bf16[384,768]{1,0:T(8,128)(2,1)}, bf16[384,768]{1,0:T(8,128)(2,1)S(1)}, u32[]{:S(2)}, u32[]{:S(2)}) collective-permute-start(bf16[384,768]{1,0:T(8,128)(2,1)} %collective-permute-done.65.rest_20_), channel_id=1, source_target_pairs={{0,1},{1,0},{2,3},{3,2},{4,5},{5,4},{6,7},{7,6},{8,9},{9,8},{10,11... | collective-permute-start | bytes 1769480 | tf_op jit(solution)/shard_map/ppermute | solution.py:56
  239.7 34.3 %collective-permute-start.57 = (bf16[384,768]{1,0:T(8,128)(2,1)S(1)}, bf16[384,768]{1,0:T(8,128)(2,1)S(1)}, u32[]{:S(2)}, u32[]{:S(2)}) collective-permute-start(bf16[384,768]{1,0:T(8,128)(2,1)S(1)} %copy-done.23), channel_id=1, source_target_pairs={{0,1},{1,0},{2,3},{3,2},{4,5},{5,4},{6,7},{7,6},{8,9},{9,8},{10,11... | collective-permute-start | bytes 1769480 | tf_op jit(solution)/shard_map/ppermute | solution.py:56
  240.3 34.1 %collective-permute-start.64 = (bf16[384,768]{1,0:T(8,128)(2,1)S(1)}, bf16[384,768]{1,0:T(8,128)(2,1)S(1)}, u32[]{:S(2)}, u32[]{:S(2)}) collective-permute-start(bf16[384,768]{1,0:T(8,128)(2,1)S(1)} %copy-done.25), channel_id=1, source_target_pairs={{0,1},{1,0},{2,3},{3,2},{4,5},{5,4},{6,7},{7,6},{8,9},{9,8},{10,11... | collective-permute-start | bytes 1769480 | tf_op jit(solution)/shard_map/ppermute | solution.py:56
  248.4 28.3 %collective-permute-start.58 = (bf16[384,768]{1,0:T(8,128)(2,1)S(1)}, bf16[384,768]{1,0:T(8,128)(2,1)S(1)}, u32[]{:S(2)}, u32[]{:S(2)}) collective-permute-start(bf16[384,768]{1,0:T(8,128)(2,1)S(1)} %collective-permute-done.56.rest_13_), channel_id=1, source_target_pairs={{0,1},{1,0},{2,3},{3,2},{4,5},{5,4},{6,7},{7,6},{8,9},{9,8},{10,11... | collective-permute-start | bytes 1769480 | tf_op jit(solution)/shard_map/ppermute | solution.py:56
  251.6 25.1 %collective-permute-start.68 = (bf16[384,768]{1,0:T(8,128)(2,1)S(1)}, bf16[384,768]{1,0:T(8,128)(2,1)S(1)}, u32[]{:S(2)}, u32[]{:S(2)}) collective-permute-start(bf16[384,768]{1,0:T(8,128)(2,1)S(1)} %collective-permute-done.66.rest_21_), channel_id=1, source_target_pairs={{0,1},{1,0},{2,3},{3,2},{4,5},{5,4},{6,7},{7,6},{8,9},{9,8},{10,11... | collective-permute-start | bytes 1769480 | tf_op jit(solution)/shard_map/ppermute | solution.py:56
  276.6 38.5 %collective-permute-start.96 = (bf16[4,96,192]{2,1,0:T(8,128)(2,1)S(1)}, bf16[4,96,192]{2,1,0:T(8,128)(2,1)S(1)}, u32[]{:S(2)}, u32[]{:S(2)}) collective-permute-start(bf16[4,96,192]{2,1,0:T(8,128)(2,1)S(1)} %copy-done.110), channel_id=1, source_target_pairs={{0,16},{4,20},{8,24},{12,28},{16,0},{20,4},{24,8},{28,12},{1,17},{... | collective-permute-start | bytes 442376 | tf_op jit(solution)/shard_map/ppermute | solution.py:60
  276.7 109.8 %collective-permute-start.97 = (bf16[4,96,192]{2,1,0:T(8,128)(2,1)S(1)}, bf16[4,96,192]{2,1,0:T(8,128)(2,1)S(1)}, u32[]{:S(2)}, u32[]{:S(2)}) collective-permute-start(bf16[4,96,192]{2,1,0:T(8,128)(2,1)S(1)} %copy-done.108), channel_id=1, source_target_pairs={{0,20},{4,16},{8,28},{12,24},{16,4},{20,0},{24,12},{28,8},{1,21},{... | collective-permute-start | bytes 442376 | tf_op jit(solution)/shard_map/ppermute | solution.py:60
  357.0 32.7 %collective-permute-start.98 = (bf16[4,96,192]{2,1,0:T(8,128)(2,1)S(1)}, bf16[4,96,192]{2,1,0:T(8,128)(2,1)S(1)}, u32[]{:S(2)}, u32[]{:S(2)}) collective-permute-start(bf16[4,96,192]{2,1,0:T(8,128)(2,1)S(1)} %copy-done.109), channel_id=1, source_target_pairs={{0,24},{4,28},{8,16},{12,20},{16,8},{20,12},{24,0},{28,4},{1,25},{... | collective-permute-start | bytes 442376 | tf_op jit(solution)/shard_map/ppermute | solution.py:60
  359.4 34.5 %collective-permute-start.99 = (bf16[4,96,192]{2,1,0:T(8,128)(2,1)S(1)}, bf16[4,96,192]{2,1,0:T(8,128)(2,1)S(1)}, u32[]{:S(2)}, u32[]{:S(2)}) collective-permute-start(bf16[4,96,192]{2,1,0:T(8,128)(2,1)S(1)} %copy-done.111), channel_id=1, source_target_pairs={{0,28},{4,24},{8,20},{12,16},{16,12},{20,8},{24,4},{28,0},{1,29},{... | collective-permute-start | bytes 442376 | tf_op jit(solution)/shard_map/ppermute | solution.py:60
  422.9 43.1 %collective-permute-start.120 = (bf16[768,768]{1,0:T(8,128)(2,1)}, bf16[768,768]{1,0:T(8,128)(2,1)S(1)}, u32[]{:S(2)}, u32[]{:S(2)}) collective-permute-start(bf16[768,768]{1,0:T(8,128)(2,1)} %get-tuple-element.158), channel_id=1, source_target_pairs={{0,2},{1,3},{2,0},{3,1},{4,6},{5,7},{6,4},{7,5},{8,10},{9,11},{10,... | collective-permute-start | bytes 3538952 | tf_op jit(solution)/shard_map/ppermute | solution.py:56
  429.6 27.7 %collective-permute-start.122 = (bf16[2,192,768]{2,1,0:T(8,128)(2,1)S(1)}, bf16[2,192,768]{2,1,0:T(8,128)(2,1)S(1)}, u32[]{:S(2)}, u32[]{:S(2)}) collective-permute-start(bf16[2,192,768]{2,1,0:T(8,128)(2,1)S(1)} %dynamic-slice_bitcast_fusion.1), channel_id=1, source_target_pairs={{0,4},{4,0},{8,12},{12,8},{16,20},{20,16},{24,28},{28,24},{1,5},{5... | collective-permute-start | bytes 1769480 | tf_op jit(solution)/shard_map/ppermute | solution.py:60
  431.2 33.4 %collective-permute-start.124 = (bf16[2,192,768]{2,1,0:T(8,128)(2,1)}, bf16[2,192,768]{2,1,0:T(8,128)(2,1)S(1)}, u32[]{:S(2)}, u32[]{:S(2)}) collective-permute-start(bf16[2,192,768]{2,1,0:T(8,128)(2,1)} %fusion.1), channel_id=1, source_target_pairs={{0,2},{1,3},{2,0},{3,1},{4,6},{5,7},{6,4},{7,5},{8,10},{9,11},{10,... | collective-permute-start | bytes 1769480 | tf_op jit(solution)/shard_map/ppermute | solution.py:56
  436.6 91.4 %collective-permute-start.85 = (bf16[768,768]{1,0:T(8,128)(2,1)}, bf16[768,768]{1,0:T(8,128)(2,1)S(1)}, u32[]{:S(2)}, u32[]{:S(2)}) collective-permute-start(bf16[768,768]{1,0:T(8,128)(2,1)} %get-tuple-element.142), channel_id=1, source_target_pairs={{0,2},{1,3},{2,0},{3,1},{4,6},{5,7},{6,4},{7,5},{8,10},{9,11},{10,... | collective-permute-start | bytes 3538952 | tf_op jit(solution)/shard_map/ppermute | solution.py:56
  444.7 23.4 %collective-permute-start.87 = (bf16[2,192,768]{2,1,0:T(8,128)(2,1)S(1)}, bf16[2,192,768]{2,1,0:T(8,128)(2,1)S(1)}, u32[]{:S(2)}, u32[]{:S(2)}) collective-permute-start(bf16[2,192,768]{2,1,0:T(8,128)(2,1)S(1)} %dynamic-slice_bitcast_fusion.5), channel_id=1, source_target_pairs={{0,4},{4,0},{8,12},{12,8},{16,20},{20,16},{24,28},{28,24},{1,5},{5... | collective-permute-start | bytes 1769480 | tf_op jit(solution)/shard_map/ppermute | solution.py:60
  457.3 72.7 %collective-permute-start.113 = (bf16[768,768]{1,0:T(8,128)(2,1)S(1)}, bf16[768,768]{1,0:T(8,128)(2,1)S(1)}, u32[]{:S(2)}, u32[]{:S(2)}) collective-permute-start(bf16[768,768]{1,0:T(8,128)(2,1)S(1)} %copy-done.156), channel_id=1, source_target_pairs={{0,2},{1,3},{2,0},{3,1},{4,6},{5,7},{6,4},{7,5},{8,10},{9,11},{10,... | collective-permute-start | bytes 3538952 | tf_op jit(solution)/shard_map/ppermute | solution.py:56
  464.5 63.2 %collective-permute-start.89 = (bf16[2,192,768]{2,1,0:T(8,128)(2,1)S(1)}, bf16[2,192,768]{2,1,0:T(8,128)(2,1)S(1)}, u32[]{:S(2)}, u32[]{:S(2)}) collective-permute-start(bf16[2,192,768]{2,1,0:T(8,128)(2,1)S(1)} %fusion.6), channel_id=1, source_target_pairs={{0,2},{1,3},{2,0},{3,1},{4,6},{5,7},{6,4},{7,5},{8,10},{9,11},{10,... | collective-permute-start | bytes 1769480 | tf_op jit(solution)/shard_map/ppermute | solution.py:56
  466.0 86.6 %collective-permute-start.78 = (bf16[768,768]{1,0:T(8,128)(2,1)S(1)}, bf16[768,768]{1,0:T(8,128)(2,1)S(1)}, u32[]{:S(2)}, u32[]{:S(2)}) collective-permute-start(bf16[768,768]{1,0:T(8,128)(2,1)S(1)} %copy-done.157), channel_id=1, source_target_pairs={{0,2},{1,3},{2,0},{3,1},{4,6},{5,7},{6,4},{7,5},{8,10},{9,11},{10,... | collective-permute-start | bytes 3538952 | tf_op jit(solution)/shard_map/ppermute | solution.py:56
  468.1 86.5 %collective-permute-start.121 = (bf16[2,192,768]{2,1,0:T(8,128)(2,1)S(1)}, bf16[2,192,768]{2,1,0:T(8,128)(2,1)S(1)}, u32[]{:S(2)}, u32[]{:S(2)}) collective-permute-start(bf16[2,192,768]{2,1,0:T(8,128)(2,1)S(1)} %dynamic-slice_bitcast_fusion.2), channel_id=1, source_target_pairs={{0,4},{4,0},{8,12},{12,8},{16,20},{20,16},{24,28},{28,24},{1,5},{5... | collective-permute-start | bytes 1769480 | tf_op jit(solution)/shard_map/ppermute | solution.py:60
  528.4 26.5 %collective-permute-start.86 = (bf16[2,192,768]{2,1,0:T(8,128)(2,1)S(1)}, bf16[2,192,768]{2,1,0:T(8,128)(2,1)S(1)}, u32[]{:S(2)}, u32[]{:S(2)}) collective-permute-start(bf16[2,192,768]{2,1,0:T(8,128)(2,1)S(1)} %dynamic-slice_bitcast_fusion.6), channel_id=1, source_target_pairs={{0,4},{4,0},{8,12},{12,8},{16,20},{20,16},{24,28},{28,24},{1,5},{5... | collective-permute-start | bytes 1769480 | tf_op jit(solution)/shard_map/ppermute | solution.py:60
  530.4 26.8 %collective-permute-start.114 = (bf16[2,192,768]{2,1,0:T(8,128)(2,1)S(1)}, bf16[2,192,768]{2,1,0:T(8,128)(2,1)S(1)}, u32[]{:S(2)}, u32[]{:S(2)}) collective-permute-start(bf16[2,192,768]{2,1,0:T(8,128)(2,1)S(1)} %dynamic-slice_bitcast_fusion.3), channel_id=1, source_target_pairs={{0,4},{4,0},{8,12},{12,8},{16,20},{20,16},{24,28},{28,24},{1,5},{5... | collective-permute-start | bytes 1769480 | tf_op jit(solution)/shard_map/ppermute | solution.py:60
  554.8 36.0 %collective-permute-start.125 = (bf16[2,192,768]{2,1,0:T(8,128)(2,1)S(1)}, bf16[2,192,768]{2,1,0:T(8,128)(2,1)S(1)}, u32[]{:S(2)}, u32[]{:S(2)}) collective-permute-start(bf16[2,192,768]{2,1,0:T(8,128)(2,1)S(1)} %fusion.15), channel_id=1, source_target_pairs={{0,8},{4,12},{8,0},{12,4},{16,24},{20,28},{24,16},{28,20},{1,9},{5... | collective-permute-start | bytes 1769480 | tf_op jit(solution)/shard_map/ppermute | solution.py:60
  555.1 44.4 %collective-permute-start.90 = (bf16[2,192,768]{2,1,0:T(8,128)(2,1)S(1)}, bf16[2,192,768]{2,1,0:T(8,128)(2,1)S(1)}, u32[]{:S(2)}, u32[]{:S(2)}) collective-permute-start(bf16[2,192,768]{2,1,0:T(8,128)(2,1)S(1)} %fusion.19), channel_id=1, source_target_pairs={{0,8},{4,12},{8,0},{12,4},{16,24},{20,28},{24,16},{28,20},{1,9},{5... | collective-permute-start | bytes 1769480 | tf_op jit(solution)/shard_map/ppermute | solution.py:60
  557.4 32.7 %collective-permute-start.115 = (bf16[1,192,768]{2,1,0:T(8,128)(2,1)S(1)}, bf16[1,192,768]{2,1,0:T(8,128)(2,1)S(1)}, u32[]{:S(2)}, u32[]{:S(2)}) collective-permute-start(bf16[1,192,768]{2,1,0:T(8,128)(2,1)S(1)} %constant_dynamic-slice_fusion.3), channel_id=1, source_target_pairs={{0,8},{4,12},{8,0},{12,4},{16,24},{20,28},{24,16},{28,20},{1,9},{5... | collective-permute-start | bytes 884744 | tf_op jit(solution)/shard_map/ppermute | solution.py:60
  568.4 31.0 %collective-permute-start.80 = (bf16[1,192,768]{2,1,0:T(8,128)(2,1)S(1)}, bf16[1,192,768]{2,1,0:T(8,128)(2,1)S(1)}, u32[]{:S(2)}, u32[]{:S(2)}) collective-permute-start(bf16[1,192,768]{2,1,0:T(8,128)(2,1)S(1)} %constant_dynamic-slice_fusion.21), channel_id=1, source_target_pairs={{0,8},{4,12},{8,0},{12,4},{16,24},{20,28},{24,16},{28,20},{1,9},{5... | collective-permute-start | bytes 884744 | tf_op jit(solution)/shard_map/ppermute | solution.py:60
  590.2 35.7 %collective-permute-start.126 = (bf16[192,768]{1,0:T(8,128)(2,1)S(1)}, bf16[192,768]{1,0:T(8,128)(2,1)S(1)}, u32[]{:S(2)}, u32[]{:S(2)}) collective-permute-start(bf16[192,768]{1,0:T(8,128)(2,1)S(1)} %bitcast.426), channel_id=1, source_target_pairs={{0,16},{4,20},{8,24},{12,28},{16,0},{20,4},{24,8},{28,12},{1,17},{... | collective-permute-start | bytes 884744 | tf_op jit(solution)/shard_map/ppermute | solution.py:60
  591.1 41.2 %collective-permute-start.127 = (bf16[192,768]{1,0:T(8,128)(2,1)S(1)}, bf16[192,768]{1,0:T(8,128)(2,1)S(1)}, u32[]{:S(2)}, u32[]{:S(2)}) collective-permute-start(bf16[192,768]{1,0:T(8,128)(2,1)S(1)} %get-tuple-element.306), channel_id=1, source_target_pairs={{0,16},{4,20},{8,24},{12,28},{16,0},{20,4},{24,8},{28,12},{1,17},{... | collective-permute-start | bytes 884744 | tf_op jit(solution)/shard_map/ppermute | solution.py:60
  599.5 76.0 %collective-permute-start.91 = (bf16[192,768]{1,0:T(8,128)(2,1)S(1)}, bf16[192,768]{1,0:T(8,128)(2,1)S(1)}, u32[]{:S(2)}, u32[]{:S(2)}) collective-permute-start(bf16[192,768]{1,0:T(8,128)(2,1)S(1)} %bitcast.425), channel_id=1, source_target_pairs={{0,16},{4,20},{8,24},{12,28},{16,0},{20,4},{24,8},{28,12},{1,17},{... | collective-permute-start | bytes 884744 | tf_op jit(solution)/shard_map/ppermute | solution.py:60
  599.8 75.6 %collective-permute-start.92 = (bf16[192,768]{1,0:T(8,128)(2,1)S(1)}, bf16[192,768]{1,0:T(8,128)(2,1)S(1)}, u32[]{:S(2)}, u32[]{:S(2)}) collective-permute-start(bf16[192,768]{1,0:T(8,128)(2,1)S(1)} %get-tuple-element.304), channel_id=1, source_target_pairs={{0,16},{4,20},{8,24},{12,28},{16,0},{20,4},{24,8},{28,12},{1,17},{... | collective-permute-start | bytes 884744 | tf_op jit(solution)/shard_map/ppermute | solution.py:60
  (266 other events, 3451.9 us)

commit v2 on v1

v2 whole, which is shorter than its diff:
```python
from functools import partial

import jax
import jax.numpy as jnp
from jax import lax
from jax.experimental import pallas as pl
from jax.experimental.pallas import tpu as pltpu
from jax.sharding import PartitionSpec as P

HEAD_DIM = 64
FEATS = 32
NS_STEPS = 5
STEP = 10


ORTHO_LINEAR = 3.4445
ORTHO_CUBIC = -4.775
ORTHO_QUINTIC = 2.0315
ORTHO_EPSILON = 1e-07
MOMENTUM_DECAY = 0.95
MUON_RATE = 0.2
WEIGHT_DECAY = 0.1
BETA_FIRST = 0.9
BETA_SECOND = 0.99
ADAM_RATE = 0.2
ADAM_EPSILON = 1e-08
NORM_EPSILON = 1e-05
ATTEND_EPSILON = 1e-06
ROPE_BASE = 10000.0
EXACT = lax.Precision.HIGHEST

F32 = jnp.float32
BF16 = jnp.bfloat16
CHUNK = 4 * HEAD_DIM
FEAT_CHUNK = 4 * FEATS
TOTAL_ROWS = 16
VMEM_BYTES = 56 * 1024 * 1024


def dot_nn(left, right):
    return lax.dot_general(left, right, (((1,), (0,)), ((), ())), preferred_element_type=F32)


def dot_nt(left, right):
    return lax.dot_general(left, right, (((1,), (1,)), ((), ())), preferred_element_type=F32)


def dot_tn(left, right):
    return lax.dot_general(left, right, (((0,), (0,)), ((), ())), preferred_element_type=F32)


def iota(shape, axis):
    return lax.broadcasted_iota(jnp.int32, shape, axis)


def swap_head(values, offset):
    return lax.ppermute(values, "head", [(h, h ^ offset) for h in range(lax.axis_size("head"))])


def swap_dp(values, offset):
    return lax.ppermute(values, "dp", [(d, d ^ offset) for d in range(lax.axis_size("dp"))])


def swap_all(items, swap, offset):
    return [swap(item, offset) for item in items]


def swap_line(parts):
    groups = [[z * 2 + y for z in range(4)] for y in range(2)]
    return lax.all_to_all(parts, "dp", split_axis=0, concat_axis=0, axis_index_groups=groups, tiled=True)


def gather_line(part):
    return swap_line(jnp.broadcast_to(part[None], (4,) + part.shape))


def swap_owners(parts):
    return lax.all_to_all(parts, "dp", split_axis=0, concat_axis=0, tiled=True)


def hold(*values):
    return lax.optimization_barrier(values)


def sources(kind, slot, rows):
    core, across = slot & 1, slot >> 1
    if kind == "whole":
        return [(slot, 0, 1, 0)]
    if "up" in kind:
        return [(slot, 0, 4, 0), (slot, rows // 2, 4, 1)]
    return [(core, across * rows // 2, 4, 0), (2 + core, across * rows // 2, 4, 1)]


def fetch(refs, plan, scratch, sems, base, lanes):
    index = lax.axis_index("dp")
    waits = [[], [], [], []]
    count = base
    for position, (kind, source_lane, lane, width) in enumerate(plan):
        first, last = max(lane, lanes[0]), min(lane + width, lanes[1])
        if first >= last:
            continue
        for slot in range(4):
            for array, row, pieces, y_offset in sources(kind, slot, scratch.shape[1]):
                ref = refs[4 * position + array]
                size = scratch.shape[1] // (2 * pieces) if pieces > 1 else scratch.shape[1]
                for piece in range(pieces):
                    start = 0
                    if pieces > 1:
                        place = 2 * piece + ((index & 1) ^ y_offset)
                        if "near" in kind:
                            place = index ^ (2 * piece + y_offset)
                        start = pl.multiple_of(place * size, 16)
                    copy = pltpu.make_async_copy(
                        ref.at[pl.ds(row + piece * size, size), pl.ds(source_lane + first - lane, last - first)],
                        scratch.at[slot, pl.ds(start, size), pl.ds(first - lanes[0], last - first)],
                        sems.at[count],
                    )
                    copy.start()
                    waits[slot].append(copy)
                    count += 1
    return waits


def ref_count(plan):
    return 4 * len(plan)


def copy_count(plan):
    return sum(4 if run[0] == "whole" else 32 for run in plan)


def take(refs, *plans):
    taken = []
    for plan in plans:
        taken.append(refs[: ref_count(plan)])
        refs = refs[ref_count(plan) :]
    return (*taken, refs)


def arrive(copies):
    for copy in copies:
        copy.wait()


def norm_parts(values):
    row_mean = jnp.mean(values, axis=-1, keepdims=True)
    centred = values - row_mean
    variance = jnp.mean(centred * centred, axis=-1, keepdims=True)
    scale = lax.rsqrt(variance + NORM_EPSILON)
    return centred * scale, scale


def norm_backward(values, gain, incoming):
    unit, scale = norm_parts(values)
    gain_grad = jnp.sum(incoming * unit, axis=0, keepdims=True)
    shift_grad = jnp.sum(incoming, axis=0, keepdims=True)
    inner = incoming * gain
    inner_mean = jnp.mean(inner, axis=-1, keepdims=True)
    along = jnp.mean(inner * unit, axis=-1, keepdims=True)
    return scale * (inner - inner_mean - unit * along), gain_grad, shift_grad


def swap_halves(values):
    width = values.shape[1]
    half = HEAD_DIM // 2
    lower = iota(values.shape, 1) % HEAD_DIM < half
    return jnp.where(lower, pltpu.roll(values, width - half, 1), pltpu.roll(values, half, 1))


def split_low(values):
    high = values.astype(BF16)
    return high, (values - high.astype(F32)).astype(BF16)


def lane_mask(index, per_head, width):
    return (iota((1, width), 1) // per_head == index).astype(BF16)


def turn_tables(cosine, sine):
    part, other = cosine[...], sine[...]
    return (
        jnp.concatenate([part] * (2 * CHUNK // HEAD_DIM), axis=1),
        jnp.concatenate([-other, other] * (CHUNK // HEAD_DIM), axis=1),
    )


def wide_map(feature_map):
    tall = jnp.concatenate([feature_map[...]] * 4, axis=0)
    return jnp.where(feature_ones(), jnp.concatenate([tall] * 4, axis=1), 0.0)


def feature_ones():
    return iota((CHUNK, FEAT_CHUNK), 0) // HEAD_DIM == iota((CHUNK, FEAT_CHUNK), 1) // FEATS


def features(values, map_high, map_low):
    high, low_part = split_low(values)
    square_high, square_low = split_low(0.5 * values * values)
    ones = -feature_ones().astype(BF16)
    left = jnp.concatenate([high, low_part, high, square_high, square_low], axis=1)
    right = jnp.concatenate([map_high, map_high, map_low, ones, ones], axis=0)
    return jnp.exp(dot_nn(left, right)) * FEATS ** (-0.5)


def fold_matrix():
    rows, columns = iota((CHUNK, HEAD_DIM), 0), iota((CHUNK, HEAD_DIM), 1)
    return (rows % HEAD_DIM == columns).astype(BF16)


def spread_matrix():
    rows = iota((2 * HEAD_DIM, 2 * CHUNK), 0)
    columns = iota((2 * HEAD_DIM, 2 * CHUNK), 1)
    return (columns // CHUNK * HEAD_DIM + columns % HEAD_DIM == rows).astype(BF16)


def same_head(feature_rows):
    shape = (feature_rows, 2 * CHUNK)
    return iota(shape, 0) % FEAT_CHUNK // FEATS == iota(shape, 1) % CHUNK // HEAD_DIM


def edge_masks(segment_column):
    first = segment_column[0:1, :]
    last = segment_column[segment_column.shape[0] - 1 :, :]
    in_first = (segment_column == first).astype(F32)
    in_last = (segment_column == last).astype(F32) * (1.0 - in_first)
    return in_first, in_last


def edge_summary(edges, weighted):
    full = dot_tn(edges, weighted)
    full = jnp.where(same_head(2 * FEAT_CHUNK)[:, :CHUNK], full, 0.0).astype(BF16)
    folded = dot_nn(full, fold_matrix())
    return jnp.concatenate([folded[:FEAT_CHUNK], folded[FEAT_CHUNK:]], axis=1).astype(BF16)


def store_totals(summary_out, rows):
    pieces = [piece for row in rows for piece in (row[:, :FEAT_CHUNK], row[:, FEAT_CHUNK:])]
    pieces.append(jnp.zeros((TOTAL_ROWS - len(pieces), FEAT_CHUNK), F32))
    summary_out[summary_out.shape[0] - TOTAL_ROWS :, :] = jnp.concatenate(pieces, axis=0).astype(BF16)


def edges_of(phi, in_first, in_last):
    wide = phi.astype(F32)
    return jnp.concatenate([wide * in_first, wide * in_last], axis=1).astype(BF16)


def open_edges(ref, which):
    feats = ref.shape[0] - TOTAL_ROWS
    totals = ref[feats:, :]
    columns = []
    for chunk in range(feats // FEAT_CHUNK):
        pick = (iota((TOTAL_ROWS, HEAD_DIM), 0) == 2 * chunk + which).astype(BF16)
        columns.append(dot_tn(totals, pick))
    sums = ref[:feats, lanes_of(which, HEAD_DIM)].astype(F32)
    return jnp.concatenate([sums, jnp.concatenate(columns, axis=0)], axis=1)


def combine_edges(received, coefficients):
    totals = [None, None]
    rows = (received[0].shape[0] - TOTAL_ROWS) // 4
    for position, ref in enumerate(received):
        offset = position + 1
        pair = []
        for which in range(2):
            value = open_edges(ref, which)
            pair.append(
                jnp.concatenate(
                    [value[(slot ^ offset) * rows : ((slot ^ offset) + 1) * rows] for slot in range(4)], axis=0
                )
            )
        for which in range(2):
            part = coefficients[position, 2 * which] * pair[0] + coefficients[position, 2 * which + 1] * pair[1]
            totals[which] = part if totals[which] is None else totals[which] + part
    return totals


def spread_edges(totals, chunk):
    rows = slice(chunk * FEAT_CHUNK, (chunk + 1) * FEAT_CHUNK)
    joined = jnp.concatenate([totals[0][rows], totals[1][rows]], axis=0).astype(BF16)
    return jnp.where(same_head(2 * FEAT_CHUNK), dot_nn(joined, spread_matrix()), 0.0).astype(BF16)


def lanes_of(slot, width):
    return slice(slot * width, (slot + 1) * width)


def project_kernel(plan, resid, vectors, cosine_part, sine_part, feature_map, segment_column, *rest):
    weight_refs, rest = take(rest, plan)
    phi_query_out, phi_key_out, value_out, query_out, key_out, summary_out, weight, sems = rest
    waits = fetch(weight_refs, plan, weight, sems, 0, (0, weight.shape[2]))
    cosine, sine = turn_tables(cosine_part, sine_part)
    unit, _ = norm_parts(resid[...])
    normed = (unit * vectors[0:1, :] + vectors[1:2, :]).astype(BF16)
    width = resid.shape[1] // 4
    pieces = [[], [], []]
    for slot in range(4):
        arrive(waits[slot])
        product = dot_nn(normed, weight[slot, :, 0 : 3 * width])
        for which in range(3):
            pieces[which].append(product[:, lanes_of(which, width)])
    queries, key_rows, value_rows = (jnp.concatenate(piece, axis=1) for piece in pieces)
    value_rows = value_rows.astype(BF16)
    value_out[...] = value_rows
    map_high, map_low = split_low(wide_map(feature_map))
    in_first, in_last = edge_masks(segment_column[...])
    totals = []
    for chunk in range(resid.shape[1] // CHUNK):
        lanes = lanes_of(chunk, CHUNK)
        feats = lanes_of(chunk, FEAT_CHUNK)
        turned = []
        for source, scaled_out, phi_out in (
            (queries, query_out, phi_query_out),
            (key_rows, key_out, phi_key_out),
        ):
            part = source[:, lanes]
            scaled = part * cosine + swap_halves(part) * sine
            scaled_out[:, lanes] = scaled
            phi = features(scaled, map_high, map_low).astype(BF16)
            phi_out[:, feats] = phi
            turned.append(phi)
        edges = edges_of(turned[1], in_first, in_last)
        summary_out[feats, :] = edge_summary(edges, value_rows[:, lanes])
        totals.append(jnp.sum(edges.astype(F32), axis=0, keepdims=True))
    store_totals(summary_out, totals)


def mix_kernel(
    plans, resid, vectors, bias, phi_query, phi_key, value, segment_column, segment_row, recv_one, recv_two,
    recv_three, coefficients, *rest
):
    out_refs, up_refs, down_refs, rest = take(rest, *plans)
    (context_out, inverse_out, middle_out, slope_out, active_keep, pack_out, resid_out, out_weight, up_weight,
     down_weight, sems) = rest
    bases = [0, copy_count(plans[0]), copy_count(plans[0]) + copy_count(plans[1])]
    out_waits = fetch(out_refs, plans[0], out_weight, sems, bases[0], (512, 768))
    up_waits = fetch(up_refs, plans[1], up_weight, sems, bases[1], (0, 768))
    down_waits = fetch(down_refs, plans[2], down_weight, sems, bases[2], (0, 768))
    same = (segment_column[...] == segment_row[...]).astype(F32)
    in_first, in_last = edge_masks(segment_column[...])
    totals = combine_edges((recv_one, recv_two, recv_three), coefficients)
    rows = resid.shape[0]
    contexts = []
    for chunk in range(resid.shape[1] // CHUNK):
        lanes = lanes_of(chunk, CHUNK)
        feats = lanes_of(chunk, FEAT_CHUNK)
        query = phi_query[:, feats]
        key = phi_key[:, feats]
        values = value[:, lanes]
        left = []
        right = []
        for head in range(4):
            scores = dot_nt(query * lane_mask(head, FEATS, FEAT_CHUNK), key)
            left.append((scores * same).astype(BF16))
            mask = lane_mask(head, HEAD_DIM, CHUNK)
            right.append(jnp.concatenate([values * mask, jnp.broadcast_to(mask, (rows, CHUNK))], axis=1))
        left.append(edges_of(query, in_first, in_last))
        right.append(spread_edges(totals, chunk))
        both = dot_nn(jnp.concatenate(left, axis=1), jnp.concatenate(right, axis=0))
        inverse = 1.0 / (both[:, CHUNK:] + ATTEND_EPSILON)
        context = both[:, :CHUNK] * inverse
        inverse_out[:, lanes] = inverse
        context_out[:, lanes] = context
        contexts.append(context.astype(BF16))
    context = jnp.concatenate(contexts, axis=1)
    width = resid.shape[1] // 4
    middle = resid[...]
    for slot in range(4):
        arrive(out_waits[slot])
        middle = middle + dot_nt(context[:, lanes_of(slot, width)], out_weight[slot, :, 64:])
    middle_out[...] = middle
    unit, _ = norm_parts(middle)
    normed = (unit * vectors[2:3, :] + vectors[3:4, :]).astype(BF16)
    pack_out[2] = normed
    output = middle + vectors[4:5, :]
    for slot in range(4):
        arrive(up_waits[slot])
        upper = dot_nn(normed, up_weight[slot]) + bias[slot : slot + 1, :]
        below = 0.5 * (1.0 + lax.erf(upper * 2.0**-0.5))
        slope = below + upper * (jnp.exp(-0.5 * upper * upper) * 0.3989422804014327)
        active = (upper * below).astype(BF16)
        slope_out[slot] = slope.astype(BF16)
        if slot % 2 == 0:
            active_keep[slot // 2] = active
        else:
            pack_out[slot // 2] = active
        arrive(down_waits[slot])
        output = output + dot_nt(active, down_weight[slot])
    resid_out[...] = output


def back_mix_kernel(
    plans, grad, vectors, middle, slope, inverse, context, phi_query, segment_column, *rest
):
    out_refs, up_refs, down_refs, rest = take(rest, *plans)
    (upper_keep, pack_out, middle_grad_out, numer_out, denom_out, summary_out, vector_out,
     bias_out, out_weight, up_weight, down_weight, sems) = rest
    bases = [0, copy_count(plans[0]), copy_count(plans[0]) + copy_count(plans[1])]
    down_waits = fetch(down_refs, plans[2], down_weight, sems, bases[2], (0, 768))
    up_waits = fetch(up_refs, plans[1], up_weight, sems, bases[1], (0, 768))
    out_waits = fetch(out_refs, plans[0], out_weight, sems, bases[0], (512, 768))
    grad_out = grad[...]
    branch = grad_out.astype(BF16)
    shift_out = jnp.sum(branch.astype(F32), axis=0, keepdims=True)
    normed_grad = None
    for slot in range(4):
        arrive(down_waits[slot])
        hidden = dot_nn(branch, down_weight[slot])
        upper = (hidden * slope[slot].astype(F32)).astype(BF16)
        if slot % 2 == 0:
            upper_keep[slot // 2] = upper
        else:
            pack_out[slot // 2] = upper
        bias_out[slot : slot + 1, :] = jnp.sum(upper.astype(F32), axis=0, keepdims=True)
        arrive(up_waits[slot])
        part = dot_nt(upper, up_weight[slot])
        normed_grad = part if normed_grad is None else normed_grad + part
    inward, gain_grad, shift_grad = norm_backward(middle[...], vectors[2:3, :], normed_grad)
    middle_grad = grad_out + inward
    middle_grad_out[...] = middle_grad
    attn = middle_grad.astype(BF16)
    pack_out[2] = attn
    zero_row = jnp.zeros_like(shift_out)
    vector_out[...] = jnp.concatenate([zero_row, zero_row, gain_grad, shift_grad, shift_out] + [zero_row] * 3, axis=0)
    pieces = []
    for slot in range(4):
        arrive(out_waits[slot])
        pieces.append(dot_nn(attn, out_weight[slot, :, 64:]))
    context_grad = jnp.concatenate(pieces, axis=1)
    in_first, in_last = edge_masks(segment_column[...])
    head_ones = (iota((CHUNK, CHUNK), 0) // HEAD_DIM == iota((CHUNK, CHUNK), 1) // HEAD_DIM).astype(BF16)
    one_lane = (iota((CHUNK, FEAT_CHUNK), 0) == iota((CHUNK, FEAT_CHUNK), 1) // FEATS * HEAD_DIM).astype(BF16)
    totals = []
    for chunk in range(grad.shape[1] // CHUNK):
        lanes = lanes_of(chunk, CHUNK)
        feats = lanes_of(chunk, FEAT_CHUNK)
        numer = context_grad[:, lanes] * inverse[:, lanes]
        denom = -dot_nn((numer * context[:, lanes]).astype(BF16), head_ones)
        numer = numer.astype(BF16)
        denom = denom.astype(BF16)
        numer_out[:, lanes] = numer
        denom_out[:, lanes] = denom
        edges = edges_of(phi_query[:, feats], in_first, in_last)
        summary_out[feats, :] = edge_summary(edges, numer)
        heads = dot_nn(denom, one_lane)
        weighted = edges.astype(F32) * jnp.concatenate([heads, heads], axis=1)
        totals.append(jnp.sum(weighted, axis=0, keepdims=True))
    store_totals(summary_out, totals)


def back_project_kernel(
    plan, resid, vectors, cosine_part, sine_part, feature_map, segment_column, segment_row, phi_query, phi_key, value,
    query_scaled, key_scaled, numer, denom, context, middle_grad, recv_one, recv_two, recv_three, back_one,
    back_two, back_three, coefficients, *rest
):
    weight_refs, rest = take(rest, plan)
    stacked_keep, pack_out, grad_out, vector_out, weight, sems = rest
    waits = fetch(weight_refs, plan, weight, sems, 0, (0, weight.shape[2]))
    cosine, sine = turn_tables(cosine_part, sine_part)
    unit, _ = norm_parts(resid[...])
    pack_out[2] = (unit * vectors[0:1, :] + vectors[1:2, :]).astype(BF16)
    same = (segment_column[...] == segment_row[...]).astype(F32)
    in_first, in_last = edge_masks(segment_column[...])
    totals = combine_edges((recv_one, recv_two, recv_three), coefficients)
    back_totals = combine_edges((back_one, back_two, back_three), coefficients)
    rows = resid.shape[0]
    map_high, map_low = split_low(wide_map(feature_map))
    spread_high = jnp.concatenate([map_high, feature_ones().astype(BF16)], axis=0)
    spread_low = jnp.concatenate([map_low, jnp.zeros_like(map_low)], axis=0)
    spread_map = jnp.concatenate([spread_high, spread_high, spread_low], axis=1)
    share = jnp.full((rows, CHUNK), 1.0 / HEAD_DIM, BF16)
    grads = [[], [], []]
    for chunk in range(resid.shape[1] // CHUNK):
        lanes = lanes_of(chunk, CHUNK)
        feats = lanes_of(chunk, FEAT_CHUNK)
        query = phi_query[:, feats]
        key = phi_key[:, feats]
        values = value[:, lanes]
        both = jnp.concatenate([numer[:, lanes], denom[:, lanes]], axis=1)
        valued = jnp.concatenate([values, share], axis=1)
        query_left, query_right, key_left, key_right, value_left, value_right = [], [], [], [], [], []
        for head in range(4):
            feat_mask = lane_mask(head, FEATS, FEAT_CHUNK)
            mask = lane_mask(head, HEAD_DIM, CHUNK)
            both_mask = jnp.concatenate([mask, mask], axis=1)
            masked_query = query * feat_mask
            masked_both = both * both_mask
            query_left.append((dot_nt(masked_both, valued) * same).astype(BF16))
            query_right.append(key * feat_mask)
            key_left.append((dot_nt(valued, masked_both) * same).astype(BF16))
            key_right.append(masked_query)
            value_left.append((dot_nt(key, masked_query) * same).astype(BF16))
            value_right.append(masked_both[:, :CHUNK])
        forward_edges = spread_edges(totals, chunk)
        backward_edges = spread_edges(back_totals, chunk)
        query_edges = dot_nt(jnp.concatenate([numer[:, lanes], denom[:, lanes] * share], axis=1), forward_edges)
        key_edges = dot_nt(valued, backward_edges)
        query_edges = query_edges[:, :FEAT_CHUNK] * in_first + query_edges[:, FEAT_CHUNK:] * in_last
        key_edges = key_edges[:, :FEAT_CHUNK] * in_first + key_edges[:, FEAT_CHUNK:] * in_last
        value_left.append(edges_of(key, in_first, in_last))
        value_right.append(backward_edges[:, :CHUNK])
        phi_grads = (
            dot_nn(jnp.concatenate(query_left, axis=1), jnp.concatenate(query_right, axis=0)) + query_edges,
            dot_nn(jnp.concatenate(key_left, axis=1), jnp.concatenate(key_right, axis=0)) + key_edges,
        )
        grads[2].append(dot_nn(jnp.concatenate(value_left, axis=1), jnp.concatenate(value_right, axis=0)))
        for which, phi, scaled in ((0, query, query_scaled), (1, key, key_scaled)):
            high, low_part = split_low(phi_grads[which] * phi.astype(F32))
            wide = dot_nt(jnp.concatenate([high, low_part, high], axis=1), spread_map)
            turned = wide[:, :CHUNK] - scaled[:, lanes] * wide[:, CHUNK:]
            grads[which].append(turned * cosine + swap_halves(turned * sine))
    joined = [jnp.concatenate(item, axis=1).astype(BF16) for item in grads]
    joined.append(context[...].astype(BF16))
    width = resid.shape[1] // 4
    normed_grad = None
    for slot in range(4):
        stacked = jnp.concatenate([item[:, lanes_of(slot, width)] for item in joined], axis=1)
        if slot % 2 == 0:
            stacked_keep[slot // 2] = stacked
        else:
            pack_out[slot // 2] = stacked
        arrive(waits[slot])
        part = dot_nt(stacked[:, : 3 * width], weight[slot, :, 0 : 3 * width])
        normed_grad = part if normed_grad is None else normed_grad + part
    inward, gain_grad, shift_grad = norm_backward(resid[...], vectors[0:1, :], normed_grad)
    below = middle_grad[...] + inward
    grad_out[...] = below
    pack_out[3] = below.astype(BF16)
    zero_row = jnp.zeros_like(gain_grad)
    vector_out[...] = jnp.concatenate([gain_grad, shift_grad] + [zero_row] * 6, axis=0)


def grad_kernel(quick, splits, right_own, right_other, *rest):
    lefts, (up_keep, up_send, down_keep, down_send, whole) = rest[: 2 * len(splits)], rest[2 * len(splits) :]
    y_bit = lax.axis_index("dp") & 1
    size = up_keep.shape[1]
    joined = []
    for position, (_, own_entry, other_entry) in enumerate(splits):
        own, other = lefts[2 * position], lefts[2 * position + 1]
        own = own[...] if own_entry is None else own[own_entry]
        other = other[...] if other_entry is None else other[other_entry]
        joined.append(jnp.concatenate([own, other], axis=0))
    for position, up_out, down_out in ((1, up_send, down_send), (0, up_keep, down_keep)):
        right = jnp.concatenate([right_own[position], right_other[position]], axis=0)
        start = 0
        for (columns, _, _), left in zip(splits, joined):
            whole[start : start + columns] = dot_tn(right[:, start : start + columns], left).astype(BF16)
            start += columns
        for part in range(2):
            up_out[part] = whole[part * size : (part + 1) * size]
        if not quick:
            for part in range(2):
                down_out[part] = whole[(2 + part) * size : (3 + part) * size]
            continue
        for bit, out in ((y_bit, down_keep), (1 - y_bit, down_send)):
            out[position] = whole[pl.ds(pl.multiple_of((2 + bit) * size, size), size), :]


def sum_of(left, right):
    return (left.astype(F32) + right.astype(F32)).astype(BF16)


def merge_first_kernel(up, up_other, down, down_other, up_keep, up_send, down_keep, down_send):
    y_bit = lax.axis_index("dp") & 1
    up_keep[...] = sum_of(up[y_bit], up_other[y_bit])
    up_send[...] = sum_of(up[1 - y_bit], up_other[1 - y_bit])
    down_keep[...] = sum_of(down[0], down_other[0])
    down_send[...] = sum_of(down[1], down_other[1])


def merge_second_kernel(up, up_other, down, down_other, *rest):
    other, out = rest[:-1], rest[-1]
    for blocks in other:
        out[:2] = blocks[...]
    base = 2 * len(other)
    out[base] = sum_of(up[...], up_other[...])
    out[base + 1] = sum_of(down[...], down_other[...])


def update_hidden_kernel(layers, *refs):
    up_pieces, down_pieces, rest = refs[:layers], refs[layers : 2 * layers], refs[2 * layers :]
    up, up_moment, down, down_moment, up_out, up_moment_out, up_copy, down_out, down_moment_out, down_copy = rest
    width = up_pieces[0].shape[2] // 2
    scale = MUON_RATE * (up.shape[2] // width) ** 0.5
    for old, moment, pieces, out, moment_out, copy in (
        (up, up_moment, up_pieces, up_out, up_moment_out, up_copy),
        (down, down_moment, down_pieces, down_out, down_moment_out, down_copy),
    ):
        for layer in range(layers):
            for block in range(4):
                lanes = lanes_of(block, width)
                both = pieces[layer][block].astype(F32)
                moment_out[layer, :, lanes] = MOMENTUM_DECAY * moment[layer, :, lanes] + both[:, :width]
                master = old[layer, :, lanes] * (1.0 - MUON_RATE * WEIGHT_DECAY) - scale * both[:, width:]
                out[layer, :, lanes] = master
                copy[layer, :, lanes] = master.astype(BF16)


def ortho_kernel(place, terms, moment, result, whole):
    pieces, size, _ = moment.shape
    width = whole.shape[1]
    eye = (iota((width, width), 0) == iota((width, width), 1)).astype(F32)

    def exact(left, right, dims=(((1,), (0,)), ((), ()))):
        return lax.dot_general(left, right, dims, precision=EXACT, preferred_element_type=F32)

    grad = terms[0].astype(F32)
    for term in range(1, terms.shape[0]):
        grad = grad + terms[term].astype(F32)
    for piece in range(pieces):
        whole[piece * size : (piece + 1) * size, :] = moment[piece, :, lanes_of(place, width)].astype(F32)
    source = MOMENTUM_DECAY * whole[...].T + grad
    gram = exact(source, source, (((1,), (1,)), ((), ())))
    norm = jnp.sqrt(jnp.sum(gram * eye)) + ORTHO_EPSILON
    gram = gram / (norm * norm)
    chain = None
    for iteration in range(NS_STEPS):
        step = ORTHO_LINEAR * eye + ORTHO_CUBIC * gram + ORTHO_QUINTIC * exact(gram, gram)
        chain = step if iteration == 0 else exact(chain, step)
        if iteration + 1 < NS_STEPS:
            gram = exact(exact(step, gram), step)
    ortho = dot_tn(source.astype(BF16), (chain / norm).astype(BF16))
    for which, value in ((0, grad.T), (1, ortho)):
        for piece in range(pieces):
            result[piece, :, lanes_of(which, width)] = value[piece * size : (piece + 1) * size].astype(BF16)


def vmem(count):
    return [pl.BlockSpec(memory_space=pltpu.VMEM)] * count


def anywhere(count):
    return [pl.BlockSpec(memory_space=pl.ANY)] * count


def scalars():
    return [pl.BlockSpec(memory_space=pltpu.SMEM)]


def shape(dims, dtype=F32):
    return jax.ShapeDtypeStruct(dims, dtype)


def call(kernel, name, in_specs, outs, scratch, flops, moved):
    return pl.pallas_call(
        kernel,
        name=name,
        out_shape=outs,
        in_specs=in_specs,
        out_specs=vmem(len(outs)),
        scratch_shapes=scratch,
        cost_estimate=pl.CostEstimate(flops=int(flops), bytes_accessed=int(moved), transcendentals=0),
        compiler_params=pltpu.CompilerParams(vmem_limit_bytes=VMEM_BYTES),
    )


def flat(weight):
    return [item for run in weight for item in run[0]]


def plan_of(weight):
    return tuple(tuple(run[1:]) for run in weight)


def project(resid, vectors, tables, feature_map, weight):
    rows, width = resid.shape
    plan = plan_of(weight)
    feats = width // HEAD_DIM * FEATS
    outs = [
        shape((rows, feats), BF16),
        shape((rows, feats), BF16),
        shape((rows, width), BF16),
        shape((rows, width)),
        shape((rows, width)),
        shape((feats + TOTAL_ROWS, 2 * HEAD_DIM), BF16),
    ]
    results = call(
        partial(project_kernel, plan),
        "project",
        vmem(6) + anywhere(ref_count(plan)),
        outs,
        [pltpu.VMEM((4, width, 640), BF16), pltpu.SemaphoreType.DMA((copy_count(plan),))],
        2 * rows * width * width * 3 * 1.5,
        8 * width * width,
    )(resid, vectors, tables["cosine"], tables["sine"], feature_map, tables["column"], *flat(weight))
    return dict(zip(("phi_query", "phi_key", "value", "query", "key", "summary"), results))


def mix_scratch(width, plans):
    return [
        pltpu.VMEM((4, width, 256), BF16),
        pltpu.VMEM((4, width, width), BF16),
        pltpu.VMEM((4, width, width), BF16),
        pltpu.SemaphoreType.DMA((sum(copy_count(plan) for plan in plans),)),
    ]


def mix(resid, vectors, bias, state, received, tables, weights):
    rows, width = resid.shape
    plans = [plan_of(weight) for weight in weights]
    refs = [item for weight in weights for item in flat(weight)]
    outs = [
        shape((rows, width)),
        shape((rows, width)),
        shape((rows, width)),
        shape((4, rows, width), BF16),
        shape((2, rows, width), BF16),
        shape((3, rows, width), BF16),
        shape((rows, width)),
    ]
    results = call(
        partial(mix_kernel, plans),
        "mix",
        vmem(11) + scalars() + anywhere(len(refs)),
        outs,
        mix_scratch(width, plans),
        2 * rows * width * width * 12,
        20 * width * width,
    )(
        resid, vectors, bias, state["phi_query"], state["phi_key"], state["value"], tables["column"], tables["row"],
        *received, tables["shares"], *refs,
    )
    return dict(zip(("context", "inverse", "middle", "slope", "active_keep", "mix_pack", "output"), results))


def back_mix(grad, vectors, state, tables, weights):
    rows, width = grad.shape
    plans = [plan_of(weight) for weight in weights]
    refs = [item for weight in weights for item in flat(weight)]
    feats = width // HEAD_DIM * FEATS
    outs = [
        shape((2, rows, width), BF16),
        shape((3, rows, width), BF16),
        shape((rows, width)),
        shape((rows, width), BF16),
        shape((rows, width), BF16),
        shape((feats + TOTAL_ROWS, 2 * HEAD_DIM), BF16),
        shape((8, width)),
        shape((4, width)),
    ]
    results = call(
        partial(back_mix_kernel, plans),
        "back_mix",
        vmem(8) + anywhere(len(refs)),
        outs,
        mix_scratch(width, plans),
        2 * rows * width * width * 11,
        20 * width * width,
    )(
        grad, vectors, state["middle"], state["slope"], state["inverse"], state["context"], state["phi_query"],
        tables["column"], *refs,
    )
    names = ("upper_keep", "back_pack", "middle_grad", "numer", "denom", "back_summary", "vector_two", "bias_grad")
    return dict(zip(names, results))


def back_project(resid, vectors, state, received, back_received, tables, feature_map, weight):
    rows, width = resid.shape
    plan = plan_of(weight)
    outs = [
        shape((2, rows, width), BF16),
        shape((4, rows, width), BF16),
        shape((rows, width)),
        shape((8, width)),
    ]
    results = call(
        partial(back_project_kernel, plan),
        "back_project",
        vmem(22) + scalars() + anywhere(ref_count(plan)),
        outs,
        [pltpu.VMEM((4, width, 640), BF16), pltpu.SemaphoreType.DMA((copy_count(plan),))],
        2 * rows * width * width * 8,
        8 * width * width,
    )(
        resid, vectors, tables["cosine"], tables["sine"], feature_map, tables["column"], tables["row"],
        state["phi_query"], state["phi_key"], state["value"], state["query"], state["key"], state["numer"],
        state["denom"], state["context"], state["middle_grad"], *received, *back_received, tables["shares"],
        *flat(weight),
    )
    return dict(zip(("stacked_keep", "stack_pack", "input_grad", "vector_one"), results))


def matrix_grad(quick, splits, right_own, right_other, *lefts):
    width = right_own.shape[2]
    block = shape((2, width // 4, width), BF16)
    return call(
        partial(grad_kernel, quick, splits), "matrix_grad", vmem(2 + len(lefts)), [block] * 4,
        [pltpu.VMEM((width, width), BF16)], 2 * 512 * width * width * 2, 8 * width * width,
    )(right_own, right_other, *lefts)


def down_grad(quick, state, mix_other, branch_own, branch_other, entries):
    splits = ((state["mix_pack"].shape[2], *entries),)
    return matrix_grad(quick, splits, state["active_keep"], mix_other, branch_own, branch_other)


def up_grad(quick, state, back_other, mix_other):
    splits = ((state["mix_pack"].shape[2], 2, 2),)
    return matrix_grad(quick, splits, state["upper_keep"], back_other, state["mix_pack"], mix_other)


def attend_grad(quick, state, stack_other, back_other):
    width = state["mix_pack"].shape[2]
    splits = ((width // 4 * 3, 2, 2), (width // 4, 2, 2))
    return matrix_grad(
        quick, splits, state["stacked_keep"], stack_other, state["stack_pack"], stack_other, state["back_pack"],
        back_other,
    )


def merge(kernel, outs, *operands):
    return call(kernel, "merge", vmem(len(operands)), outs, [], 1, 1)(*operands)


def merge_first(own, others):
    out = shape(own[0].shape[1:], BF16)
    return merge(merge_first_kernel, [out] * 4, own[0], others[0], own[2], others[1])


def merge_second(own, others, *other_blocks):
    out = shape((2 + 2 * len(other_blocks),) + own[0].shape, BF16)
    return merge(merge_second_kernel, [out], own[0], others[0], own[2], others[1], *other_blocks)[0]


def send_first(own):
    return swap_head(own[1], 2), swap_dp(own[3], 1)


def send_second(own):
    return swap_dp(own[1], 1), swap_head(own[3], 2)


def orthogonalize(place, terms, moment):
    pieces, size, _ = moment.shape
    width = terms.shape[1]
    return call(
        partial(ortho_kernel, place), "orthogonalize", vmem(2), [shape((pieces, size, 2 * width), BF16)],
        [pltpu.VMEM((pieces * size, width), F32)], 2 * 6 * 20 * width**3, 8 * width * pieces * size,
    )(terms, moment)[0]


def update_hidden(up_pieces, down_pieces, up, up_moment, down, down_moment):
    outs = [shape(up.shape), shape(up.shape), shape(up.shape, BF16)] * 2
    layers = up.shape[0]
    return call(
        partial(update_hidden_kernel, layers), "update_hidden", vmem(2 * layers + 4), outs, [], 8 * up.size,
        26 * up.size,
    )(*up_pieces, *down_pieces, up, up_moment, down, down_moment)


def doc_tables(segment_row, rows):
    index = lax.axis_index("head")
    own = lax.dynamic_slice_in_dim(segment_row, index * rows, rows, 0)
    starts = jnp.sum((segment_row[None, :] < own[:, None]).astype(jnp.int32), axis=1, dtype=jnp.int32)
    offsets = (index * rows + jnp.arange(rows, dtype=jnp.int32) - starts).astype(F32)
    half = HEAD_DIM // 2
    frequency = ROPE_BASE ** (-jnp.arange(half, dtype=F32) / half)
    angles = offsets[:, None] * frequency[None, :]
    scale = HEAD_DIM ** (-0.25)
    edges = segment_row.reshape(-1, rows)[:, :: rows - 1]
    others = jnp.stack([lax.dynamic_index_in_dim(edges, index ^ offset, 0, keepdims=False) for offset in (1, 2, 3)])
    mine = jnp.stack([own[0], own[rows - 1]])
    shares = (others[:, None, :] == mine[None, :, None]).astype(F32).reshape(3, 4)
    return {
        "cosine": jnp.cos(angles) * scale,
        "sine": jnp.sin(angles) * scale,
        "column": own[:, None],
        "row": own[None, :],
        "shares": shares,
    }


def cross_edges(summary, near):
    return swap_head(summary, 2), swap_head(near, 2)


def exchange_edges(summary):
    near = swap_head(summary, 1)
    return near, *cross_edges(summary, near)


def other_slots(values):
    return [swap_head(values, offset) for offset in (1, 2, 3)]


def adam_update(parameter, gradient, first_moment, second_moment):
    first_moment = BETA_FIRST * first_moment + (1.0 - BETA_FIRST) * gradient
    second_moment = BETA_SECOND * second_moment + (1.0 - BETA_SECOND) * gradient * gradient
    first_hat = first_moment / (1.0 - BETA_FIRST**STEP)
    second_hat = second_moment / (1.0 - BETA_SECOND**STEP)
    return (
        parameter - ADAM_RATE * first_hat / (jnp.sqrt(second_hat) + ADAM_EPSILON),
        first_moment,
        second_moment,
    )


def split_columns(matrix, width):
    rows = matrix.shape[0]
    return jnp.transpose(matrix.reshape(rows, -1, width), (1, 0, 2))


def join_columns(blocks):
    count, rows, width = blocks.shape
    return jnp.transpose(blocks, (1, 0, 2)).reshape(rows, count * width)


def attend_shard(query_key, value, out):
    return jnp.concatenate([query_key[:, 0], query_key[:, 1], value, out.T], axis=1).astype(BF16)


def old_blocks(layer, moments, block):
    query_key, value, out, up, down = (moment[layer] for moment in moments)
    return (
        jnp.stack([query_key[:, 0], query_key[:, 1], value, out.T]).astype(BF16),
        jnp.concatenate([split_columns(up, block), split_columns(down.T, block)]).astype(BF16),
    )


def line_parts(line, cuts):
    return [line[:, :, first:last].reshape(-1, last - first) for first, last in cuts]


def core_vectors(vector_grads, bias_grads):
    vectors = jnp.concatenate(vector_grads)
    biases = jnp.stack(bias_grads)
    keep, send = biases[:, 0::2], biases[:, 1::2]
    size = vectors.shape[0]
    sent = swap_head(jnp.concatenate([vectors, send.reshape(-1, vectors.shape[1])]), 1)
    biases = keep + sent[size:].reshape(keep.shape)
    return jnp.concatenate([vectors + sent[:size], biases[:, 1]]), biases[:, 0]


def across_vectors(packed, bias_keep):
    size = packed.shape[0] - bias_keep.shape[0]
    return jnp.concatenate([packed[:size], bias_keep]) + swap_head(packed, 2)


def hold_weight(weight, *values):
    arrays, *values = hold([run[0] for run in weight], *values)
    return [(items, *run[1:]) for items, run in zip(arrays, weight)], *values


def hold_runs(lines, received, *runs):
    arrays, lines, received = hold([run[0] for run in runs], lines, received)
    return lines, received, *[(items, *run[1:]) for items, run in zip(arrays, runs)]


def per_device(
    block_input,
    cotangent,
    marked,
    segments,
    feature_map,
    vectors,
    bias_up,
    w_query_key,
    w_value,
    w_out,
    w_up,
    w_down,
    moment_query_key,
    moment_value,
    moment_out,
    moment_up,
    moment_down,
    vector_first,
    vector_second,
    bias_first,
    bias_second,
):
    layers = w_value.shape[0]
    block = w_value.shape[2]
    rows, width = block_input.shape
    dp_size = lax.axis_size("dp")
    dp_index = lax.axis_index("dp")
    quick = dp_size == 8 and layers == 2
    masters = (w_query_key, w_value, w_out, w_up, w_down)
    moments = (moment_query_key, moment_value, moment_out, moment_up, moment_down)
    muon_scale = (w_value.shape[1] * dp_size / block) ** 0.5

    def attend_of(layer):
        return attend_shard(w_query_key[layer], w_value[layer], w_out[layer])

    def hidden_of(layer):
        return jnp.concatenate([w_up[layer], w_down[layer].T], axis=1).astype(BF16)

    tables = doc_tables(segments[0], rows)
    resid = block_input.astype(F32)
    bias_slots = [bias_up] + other_slots(bias_up)
    biases = [jnp.stack([item[layer] for item in bias_slots]) for layer in range(layers)]
    gradient = cotangent.astype(F32) * marked[0][:, None].astype(F32)
    states = [None] * layers

    def run_project(layer, resid, weight):
        states[layer] = project(resid, vectors[layer], tables, feature_map[layer], weight)
        states[layer]["input"] = resid

    def run_mix(layer, received, weights):
        state = states[layer]
        state["received"] = received
        state.update(mix(state["input"], vectors[layer], biases[layer], state, received, tables, weights))
        return state["output"]

    def run_back_mix(layer, gradient, weights):
        states[layer].update(back_mix(gradient, vectors[layer], states[layer], tables, weights))

    def run_back_project(layer, back_received, weight):
        state = states[layer]
        state.update(
            back_project(
                state["input"], vectors[layer], state, state["received"], back_received, tables, feature_map[layer],
                weight,
            )
        )
        return state["input_grad"]

    if quick:
        half = width // 2
        first = attend_of(0)
        hidden = hidden_of(0)
        second = jnp.concatenate([attend_of(1), hidden_of(1)], axis=1)
        line = [first] + [swap_dp(first, offset) for offset in (2, 4, 6)]

        line, hidden = hold(line, hidden)
        up_line, down_line = (jnp.concatenate([item[:, cut] for item in line]) for cut in (slice(half), slice(half, width)))
        up_y, down_x = swap_dp(up_line, 1), swap_head(down_line, 2)
        hidden_line = gather_line(hidden)

        up_line, down_line, up_y, down_x = hold(up_line, down_line, up_y, down_x)
        up, down = jnp.concatenate([up_line, up_y]), jnp.concatenate([down_line, down_x])
        up_other, down_other = swap_head(up, 2), swap_dp(down, 1)

        up, down, up_other, down_other, resid, tables, biases = hold(
            up, down, up_other, down_other, resid, tables, biases
        )
        cores = swap_all([up, up_other, down, down_other], swap_head, 1)
        weight_one = [
            ((up, cores[0], up_other, cores[1]), "up near", 0, 0, half),
            ((down, cores[2], down_other, cores[3]), "down near", 0, half, half),
        ]
        weight_one, hidden_line, second = hold_weight(weight_one, hidden_line, second)
        up_line, down_line = line_parts(hidden_line, ((0, width), (width, 2 * width)))
        up_y, down_x = swap_dp(up_line, 1), swap_head(down_line, 2)
        second_line = gather_line(second)
        run_project(0, resid, weight_one)
        near = swap_head(states[0]["summary"], 1)

        up_line, down_line, up_y, down_x, near, moments = hold(up_line, down_line, up_y, down_x, near, moments)
        up, down = jnp.concatenate([up_line, up_y]), jnp.concatenate([down_line, down_x])
        up_other, down_other = swap_head(up, 2), swap_dp(down, 1)
        both = cross_edges(states[0]["summary"], near)
        cores = swap_all([up, down], swap_head, 1)
        blocks = [old_blocks(layer, moments, block) for layer in (1, 0)]
        (attend_one, hidden_one), (attend_zero, hidden_zero) = blocks
        payload = jnp.concatenate(
            [
                jnp.concatenate([hidden_one[4:], hidden_one[:4]]),
                jnp.concatenate([attend_one, hidden_zero[4:]]),
            ],
            axis=2,
        )
        payload_late = jnp.concatenate([hidden_zero[:4], attend_zero])

        branch = gradient.astype(BF16)
        branch_other = swap_head(branch, 1)

        cores, up_other, down_other, received, payload, payload_late, second_line, branch_other = hold(
            cores, up_other, down_other, (near, *both), payload, payload_late, second_line, branch_other
        )
        cores += swap_all([up_other, down_other], swap_head, 1)
        weights = [
            (
                weight_one,
                [((up, cores[0], up_other, cores[2]), "up", 0, 0, width)],
                [((down, cores[1], down_other, cores[3]), "down", 0, 0, width)],
            )
        ]
        cuts = ((0, half), (half, width), (width, 2 * width), (2 * width, 3 * width))
        lines = line_parts(second_line, cuts)

        lines, received, weights[0][1][0], weights[0][2][0] = hold_runs(
            lines, received, weights[0][1][0], weights[0][2][0]
        )
        crossed = [swap_dp(lines[0], 1), swap_head(lines[1], 2), swap_dp(lines[2], 1), swap_head(lines[3], 2)]
        resid = run_mix(0, received, weights[0])

        lines, crossed, resid = hold(lines, crossed, resid)
        up, down, up_late, down_late = (jnp.concatenate(pair) for pair in zip(lines, crossed))
        up_other, down_other = swap_head(up, 2), swap_dp(down, 1)
        up_late_other, down_late_other = swap_head(up_late, 2), swap_dp(down_late, 1)

        up, down, up_other, down_other = hold(up, down, up_other, down_other)
        cores = swap_all([up, down, up_other, down_other], swap_head, 1)
        weight_one = [
            ((up, cores[0], up_other, cores[2]), "up", 0, 0, half),
            ((down, cores[1], down_other, cores[3]), "down", 0, half, half),
        ]
        run_project(1, resid, weight_one)
        late_cores = swap_all([up_late, down_late], swap_head, 1)
        near = swap_head(states[1]["summary"], 1)

        both = cross_edges(states[1]["summary"], near)
        received, late_cores, up_late_other, down_late_other, payload = hold(
            (near, *both), late_cores, up_late_other, down_late_other, payload
        )
        late_cores += swap_all([up_late_other, down_late_other], swap_head, 1)
        weights.append(
            (
                weight_one,
                [((up_late, late_cores[0], up_late_other, late_cores[2]), "up", 0, 0, width)],
                [((down_late, late_cores[1], down_late_other, late_cores[3]), "down", 0, 0, width)],
            )
        )
        moment = swap_owners(payload)
        activations = run_mix(1, received, weights[1])

        moment, mix_pack, activations = hold(moment, states[1]["mix_pack"], activations)
        mix_other = swap_head(mix_pack, 1)
        down_one = down_grad(quick, states[1], mix_other, branch, branch_other, (None, None))

        down_one, gradient = hold(down_one, gradient)
        down_others = send_first(down_one)
        run_back_mix(1, gradient, weights[1])

        down_others, summary, back_pack = hold(down_others, states[1]["back_summary"], states[1]["back_pack"])
        near, back_other = swap_all([summary, back_pack], swap_head, 1)
        down_one = merge_first(down_one, down_others)
        near, back_other, down_one = hold(near, back_other, down_one)
        both = cross_edges(summary, near)
        down_others = send_second(down_one)
        up_one = up_grad(quick, states[1], back_other, mix_other)

        back_received, up_one, down_others = hold((near, *both), up_one, down_others)
        up_others = send_first(up_one)
        moment_late = swap_owners(payload_late)
        gradient = run_back_project(1, back_received, weights[1][0])

        up_others, gradient, stack_pack, mix_pack, moment_late = hold(
            up_others, gradient, states[1]["stack_pack"], states[0]["mix_pack"], moment_late
        )
        stack_other, mix_other = swap_all([stack_pack, mix_pack], swap_head, 1)
        up_one = merge_first(up_one, up_others)
        stack_other, mix_other, up_one = hold(stack_other, mix_other, up_one)
        up_others = send_second(up_one)
        down_blocks = merge_second(down_one, down_others)
        attend_one = attend_grad(quick, states[1], stack_other, back_other)

        attend_one, up_others, gradient = hold(attend_one, up_others, gradient)
        attend_others = send_first(attend_one)
        pair_one = swap_line(merge_second(up_one, up_others, down_blocks))
        run_back_mix(0, gradient, weights[0])

        attend_others, summary, back_pack = hold(attend_others, states[0]["back_summary"], states[0]["back_pack"])
        near, back_other = swap_all([summary, back_pack], swap_head, 1)
        attend_one = merge_first(attend_one, attend_others)
        near, back_other, attend_one = hold(near, back_other, attend_one)
        both = cross_edges(summary, near)
        attend_others = send_second(attend_one)
        down_zero = down_grad(quick, states[0], mix_other, stack_pack, stack_other, (3, 3))

        back_received, down_zero, attend_others = hold((near, *both), down_zero, attend_others)
        down_others = send_first(down_zero)
        gradient = run_back_project(0, back_received, weights[0][0])

        down_others, stack_pack, pair_one = hold(down_others, states[0]["stack_pack"], pair_one)
        stack_other = swap_head(stack_pack, 1)
        up_zero = up_grad(quick, states[0], back_other, mix_other)
        down_zero = merge_first(down_zero, down_others)
        up_zero, down_zero, stack_other = hold(up_zero, down_zero, stack_other)
        down_others = send_second(down_zero)
        up_others = send_first(up_zero)
        attend_blocks = merge_second(attend_one, attend_others)
        attend_zero = attend_grad(quick, states[0], stack_other, back_other)

        attend_zero, down_others = hold(attend_zero, down_others)
        attend_others = send_first(attend_zero)
        pair_two = merge_second(down_zero, down_others, attend_blocks)
        pair_two, pair_one = hold(pair_two, pair_one)
        pair_two = swap_line(pair_two)
        back_one = orthogonalize(0, pair_one, moment)

        up_others, back_one = hold(up_others, back_one)
        up_zero = merge_first(up_zero, up_others)
        up_others = send_second(up_zero)
        vector_grads = [(state["vector_one"] + state["vector_two"])[:5] for state in states]
        vector_pack, bias_keep = core_vectors(vector_grads, [state["bias_grad"] for state in states])

        attend_others, vector_pack = hold(attend_others, vector_pack)
        attend_zero = merge_first(attend_zero, attend_others)
        attend_others = send_second(attend_zero)
        packed = across_vectors(vector_pack, bias_keep)

        up_others, packed, pair_two = hold(up_others, packed, pair_two)
        pieces_one = swap_owners(back_one)
        up_blocks = merge_second(up_zero, up_others)
        packed = packed + swap_dp(packed, 1)

        attend_others, up_blocks, pieces_one = hold(attend_others, up_blocks, pieces_one)
        pair_three = merge_second(attend_zero, attend_others, up_blocks)
        pair_three, pair_two = hold(pair_three, pair_two)
        pair_three = swap_line(pair_three)
        back_two = orthogonalize(1, pair_two, moment)

        pair_three, back_two, packed = hold(pair_three, back_two, packed)
        pieces_two = swap_owners(back_two)
        back_three = orthogonalize(0, pair_three, moment_late)

        pieces_two, back_three, packed = hold(pieces_two, back_three, packed)
        pieces_three = swap_owners(back_three)
        for offset in (2, 4):
            packed = packed + swap_dp(packed, offset)
        hidden_pieces = (pieces_three[:4], pieces_one[4:]), (pieces_two[4:], pieces_one[:4])
        attend_pieces = pieces_three[4:], pieces_two[:4]
    else:
        weights = []
        for layer in range(layers):
            parts = []
            for part in (attend_of(layer), w_up[layer].astype(BF16), w_down[layer].T.astype(BF16)):
                whole = lax.all_gather(part, "dp", axis=0, tiled=True)
                parts.append([([whole] + other_slots(whole), "whole", 0, 0, width)])
            weights.append(tuple(parts))
        for layer in range(layers):
            run_project(layer, resid, weights[layer][0])
            resid = run_mix(layer, exchange_edges(states[layer]["summary"]), weights[layer])
        activations = resid
        raw = []
        for layer in reversed(range(layers)):
            state = states[layer]
            branch = gradient.astype(BF16)
            run_back_mix(layer, gradient, weights[layer])
            gradient = run_back_project(layer, exchange_edges(state["back_summary"]), weights[layer][0])
            back_other, mix_other, stack_other, branch_other = swap_all(
                [state["back_pack"], state["mix_pack"], state["stack_pack"], branch], swap_head, 1
            )
            for own in (
                attend_grad(quick, state, stack_other, back_other),
                up_grad(quick, state, back_other, mix_other),
                down_grad(quick, state, mix_other, branch, branch_other, (None, None)),
            ):
                for keep, send in ((own[0], own[1]), (own[2], own[3])):
                    raw.append(keep.astype(F32) + swap_head(send, 2).astype(F32))
        count = layers * 12
        padded = -(-count // dp_size) * dp_size
        grads = jnp.concatenate(raw)
        grads = jnp.concatenate([grads, jnp.zeros((padded - count,) + grads.shape[1:], F32)])
        grads = lax.psum_scatter(grads, "dp", scatter_dimension=0, tiled=True)
        old = [part for layer in reversed(range(layers)) for part in old_blocks(layer, moments, block)]
        old = jnp.concatenate(old)
        old = jnp.concatenate([old, jnp.zeros((padded - count,) + old.shape[1:], old.dtype)])
        old = lax.all_to_all(old, "dp", split_axis=0, concat_axis=1, tiled=True)
        owned = padded // dp_size
        back = jnp.concatenate(
            [orthogonalize(0, grads[place : place + 1], old[place : place + 1]) for place in range(owned)]
        )
        back = jnp.stack([back[..., :block], back[..., block:]], axis=1)
        back = lax.all_to_all(back, "dp", split_axis=2, concat_axis=0, tiled=True)
        back = jnp.concatenate([back[:, 0], back[:, 1]], axis=2)
        ordered = [back[12 * place : 12 * (place + 1)] for place in reversed(range(layers))]
        attend_pieces = [part[:4] for part in ordered]
        hidden_pieces = [part[4:8] for part in ordered], [part[8:] for part in ordered]
        vector_grads = [(state["vector_one"] + state["vector_two"])[:5] for state in states]
        packed = across_vectors(*core_vectors(vector_grads, [state["bias_grad"] for state in states]))
        packed = lax.psum(packed, "dp")

    vector_total, bias_total = packed[: 5 * layers].reshape(vectors.shape), packed[5 * layers :]
    turned = [jnp.transpose(item, (0, 2, 1)) for item in (w_down, moment_down)]
    updated = list(update_hidden(*hidden_pieces, w_up, moment_up, *turned))
    updated[3:] = [jnp.transpose(item, (0, 2, 1)) for item in updated[3:]]
    fresh = []
    for which in range(2):
        parts = [pieces[:, :, lanes_of(which, block)].astype(F32) for pieces in attend_pieces]
        fresh.append(
            (
                jnp.stack([jnp.stack([part[0], part[1]], axis=1) for part in parts]),
                jnp.stack([part[2] for part in parts]),
                jnp.stack([part[3].T for part in parts]),
            )
        )
    next_moments = tuple(MOMENTUM_DECAY * old + grad for old, grad in zip(moments, fresh[0]))
    next_masters = tuple(
        master * (1.0 - MUON_RATE * WEIGHT_DECAY) - MUON_RATE * muon_scale * ortho
        for master, ortho in zip(masters, fresh[1])
    )
    copies = tuple(master.astype(BF16) for master in next_masters)
    vectors_next, vector_first_next, vector_second_next = adam_update(
        vectors, vector_total, vector_first, vector_second
    )
    bias_next, bias_first_next, bias_second_next = adam_update(bias_up, bias_total, bias_first, bias_second)
    return (
        (activations.astype(BF16), gradient)
        + (*next_masters, updated[0], updated[3])
        + (*next_moments, updated[1], updated[4])
        + (*copies, updated[2], updated[5])
        + (vectors_next, vector_first_next, vector_second_next, bias_next, bias_first_next, bias_second_next)
    )


def solution(mesh):
    shards = (
        P(None, "dp", None, "head"),
        P(None, "dp", "head"),
        P(None, "head", "dp"),
        P(None, "dp", "head"),
        P(None, "head", "dp"),
    )
    rows = P(("dp", "head"), None)
    placed = (
        (rows, rows, P("dp", "head"), P("dp", None), P(), P(), P(None, "head"))
        + shards
        + shards
        + (P(), P(), P(None, "head"), P(None, "head"))
    )
    return jax.shard_map(
        per_device,
        mesh=mesh,
        in_specs=placed,
        out_specs=(rows, rows) + shards + shards + shards + (P(), P(), P()) + (P(None, "head"),) * 3,
        check_vma=False,
    )
```

time: 750 us -> 553 us (0.74)
  waiting for transfers between devices: 340 us -> 147 us
  Pallas kernels: 144 us -> 200 us
  other arithmetic: 49.7 us -> 19.2 us
  between operations: 19 us -> 2.67 us
  starting transfers between devices: 122 us -> 114 us
    ppermute x73 -> x26, waiting for transfers between devices: 182 us -> 58.1 us  [swap_dp(): lax.ppermute(values, 'dp', [(d, d ^ offset) for d in range(lax.axis_size(...]
    ppermute x72 -> x60, waiting for transfers between devices: 157 us -> 46.9 us  [swap_head(): lax.ppermute(values, 'head', [(h, h ^ offset) for h in range(lax.axis_siz...]
    pallas_call x14 -> x30, Pallas kernels: 144 us -> 200 us  [the longest x6 32.8 us: matrix_grad(): call(partial(grad_kernel, quick, splits), 'matrix_grad', vmem(2 + len(lef...]
    ppermute x73 -> x26, starting transfers between devices: 83.4 us -> 33.8 us  [swap_dp(): lax.ppermute(values, 'dp', [(d, d ^ offset) for d in range(lax.axis_size(...]
    all_to_all x0 -> x10, starting transfers between devices: none -> 42.7 us  [the longest x5 23.9 us: swap_line(): lax.all_to_all(parts, 'dp', split_axis=0, concat_axis=0, axis_index_group...]
    all_to_all x0 -> x10, waiting for transfers between devices: none -> 42.1 us  [the longest x5 36.8 us: swap_line(): lax.all_to_all(parts, 'dp', split_axis=0, concat_axis=0, axis_index_group...]
    another operation x32 -> x11, other arithmetic: 14.8 us -> 5.83 us  [the longest x7 6.82 us: per_device(): jnp.stack([part for layer in range(layers) for part in (lax.dynamic_index...]
    mul x5 -> x0, local copies, waits for them, and re-layouts: 8.32 us -> none  [doc_tables(): jnp.kron(jnp.eye(4, dtype=F32), feature_map[layer])]
  transfers between devices with their start and end apart: 145 -> 96, of which waited for: 63 -> 39; matrix products, arithmetic and copies ran while one was open for 10% -> 11% of each run, Pallas kernels for 18% -> 34%
where the time goes in v2:
time: 553 us; the launch traced here: 544 us
  Pallas kernels  200 us (36%)
  waiting for transfers between devices  147 us (27%)
  starting transfers between devices  114 us (21%)
  local copies, waits for them, and re-layouts  61 us (11%)
  other arithmetic  19.2 us (3%)
    ppermute x26, waiting for transfers between devices, swap_dp(): lax.ppermute(values, 'dp', [(d, d ^ offset) for d in range(lax.axis_size(...  58.1 us
    ppermute x60, waiting for transfers between devices, swap_head(): lax.ppermute(values, 'head', [(h, h ^ offset) for h in range(lax.axis_siz...  46.9 us
    ppermute x60, starting transfers between devices, swap_head(): lax.ppermute(values, 'head', [(h, h ^ offset) for h in range(lax.axis_siz...  37 us
    all_to_all x5, waiting for transfers between devices, swap_line(): lax.all_to_all(parts, 'dp', split_axis=0, concat_axis=0, axis_index_group...  36.8 us
    ppermute x26, starting transfers between devices, swap_dp(): lax.ppermute(values, 'dp', [(d, d ^ offset) for d in range(lax.axis_size(...  33.8 us
    pallas_call x6, Pallas kernels, matrix_grad(): call(partial(grad_kernel, quick, splits), 'matrix_grad', vmem(2 + len(lef...  32.8 us
    pallas_call x2, Pallas kernels, back_project(): call(partial(back_project_kernel, plan), 'back_project', vmem(22) + scala...  31 us
    pallas_call x12, Pallas kernels, merge(): return call(kernel, 'merge', vmem(len(operands)), outs, [], 1, 1)(*operands)  30.9 us
  transfers between devices with their start and end apart: 96, of which 39 were waited for; matrix products, arithmetic and copies ran while one was open for 11% of the time, Pallas kernels for 34%

profile of v2, /device:TPU:0, one launch (start us, length us, event | category | flops | bytes accessed | tf_op | source)
XLA Modules:
  0.0 543.7 jit_solution(12565434676631058851)
XLA Ops:
  0.7 3.0 collective-permute-start.8
  6.5 3.7 collective-permute-start.2
  17.3 6.1 %collective-permute-done.1 = bf16[96,768]{1,0:T(8,128)(2,1)S(1)} collective-permute-done((bf16[96,768]{1,0:T(8,128)(2,1)S(1)}, bf16[96,768]{1,0:T(8,128)(2,1)S(1)}, u32[]{:S(2)}, u32[]{:S(2)}) %collective-permute-start.1) | collective-permute-done | bytes 147488 | tf_op jit(solution)/shard_map/ppermute | solution.py:61
  28.1 4.3 all-to-all-start
  35.6 11.8 %collective-permute-done.6.rest_6_ = bf16[768,384]{1,0:T(8,128)(2,1)S(1)} collective-permute-done((bf16[768,384]{1,0:T(8,128)(2,1)S(1)}, bf16[768,384]{1,0:T(8,128)(2,1)S(1)}, u32[]{:S(2)}, u32[]{:S(2)}) %collective-permute-start.6) | collective-permute-done | bytes 589856 | tf_op jit(solution)/shard_map/ppermute | solution.py:61
  52.5 8.1 %all-to-all-done = bf16[4,96,1536]{2,1,0:T(8,128)(2,1)} async-done(((bf16[4,96,1536]{2,1,0:T(8,128)(2,1)}), bf16[4,96,1536]{2,1,0:T(8,128)(2,1)}, u32[]{:S(2)}, u32[]{:S(2)}) %all-to-all-start) | async-done | bytes 1179680 | tf_op jit(solution)/shard_map/all_to_all | solution.py:70
  66.9 9.1 %project.2 = (bf16[256,384]{1,0:T(8,128)(2,1)}, bf16[256,384]{1,0:T(8,128)(2,1)}, bf16[256,768]{1,0:T(8,128)(2,1)}, f32[256,768]{1,0:T(8,128)}, f32[256,768]{1,0:T(8,128)}, /*index=5*/bf16[400,128]{1,0:T(8,128)(2,1)}) custom-call(f32[256,768]{1,0:T(8,128)} %convert_element_type.66.resid, f32[5,768]{1,0:T(8,128)} %get-tuple-element.767.vectors, ...), custom_call_target="tpu_custom_call" | custom-call | flops 1358954496 | bytes 4718592 | tf_op jit(solution)/shard_map/project/pallas_call | solution.py:676
  79.1 4.9 all-to-all-start.1
  113.0 4.4 collective-permute-done.21.recv_two
  134.0 13.5 %mix.2 = (f32[256,768]{1,0:T(8,128)}, f32[256,768]{1,0:T(8,128)}, f32[256,768]{1,0:T(8,128)}, bf16[4,256,768]{2,1,0:T(8,128)(2,1)}, bf16[2,256,768]{2,1,0:T(8,12...) custom-call(f32[256,768]{1,0:T(8,128)} %convert_element_type.66.resid, f32[5,768]{1,0:T(8,128)} %get-tuple-element.767.vectors, ...), custom_call_target="tpu_custom_call" | custom-call | flops 3623878656 | bytes 11796480 | tf_op jit(solution)/shard_map/mix/pallas_call | solution.py:710
  147.5 4.0 collective-permute-done.26
  154.2 13.0 %collective-permute-done.31.rest_6_ = bf16[768,384]{1,0:T(8,128)(2,1)S(1)} collective-permute-done((bf16[768,384]{1,0:T(8,128)(2,1)S(1)}, bf16[768,384]{1,0:T(8,128)(2,1)S(1)}, u32[]{:S(2)}, u32[]{:S(2)}) %collective-permute-start.31) | collective-permute-done | bytes 589856 | tf_op jit(solution)/shard_map/ppermute | solution.py:61
  178.4 9.2 %project.3 = (bf16[256,384]{1,0:T(8,128)(2,1)}, bf16[256,384]{1,0:T(8,128)(2,1)}, bf16[256,768]{1,0:T(8,128)(2,1)}, f32[256,768]{1,0:T(8,128)}, f32[256,768]{1,0:T(8,128)}, /*index=5*/bf16[400,128]{1,0:T(8,128)(2,1)}) custom-call(f32[256,768]{1,0:T(8,128)} %get-tuple-element.391.resid, f32[5,768]{1,0:T(8,128)} %get-tuple-element.766.vectors, ...), custom_call_target="tpu_custom_call" | custom-call | flops 1358954496 | bytes 4718592 | tf_op jit(solution)/shard_map/project/pallas_call | solution.py:676
  187.8 10.8 %collective-permute-done.42.rest_14_ = bf16[768,768]{1,0:T(8,128)(2,1)} collective-permute-done((bf16[768,768]{1,0:T(8,128)(2,1)}, bf16[768,768]{1,0:T(8,128)(2,1)}, u32[]{:S(2)}, u32[]{:S(2)}) %collective-permute-start.42) | collective-permute-done | bytes 1179680 | tf_op jit(solution)/shard_map/ppermute | solution.py:61
  206.6 3.5 all-to-all-start.2
  211.9 13.5 %mix.3 = (f32[256,768]{1,0:T(8,128)}, f32[256,768]{1,0:T(8,128)}, f32[256,768]{1,0:T(8,128)}, bf16[4,256,768]{2,1,0:T(8,128)(2,1)}, bf16[2,256,768]{2,1,0:T(8,12...) custom-call(f32[256,768]{1,0:T(8,128)} %get-tuple-element.391.resid, f32[5,768]{1,0:T(8,128)} %get-tuple-element.766.vectors, ...), custom_call_target="tpu_custom_call" | custom-call | flops 3623878656 | bytes 11796480 | tf_op jit(solution)/shard_map/mix/pallas_call | solution.py:710
  226.4 3.1 collective-permute-done.45.right_other.rest_1_
  230.5 4.4 matrix_grad.6
  236.9 14.1 %back_mix.2 = (bf16[2,256,768]{2,1,0:T(8,128)(2,1)}, bf16[3,256,768]{2,1,0:T(8,128)(2,1)}, f32[256,768]{1,0:T(8,128)}, bf16[256,768]{1,0:T(8,128)(2,1)}, bf16[25...) custom-call(f32[256,768]{1,0:T(8,128)} %get-tuple-element.432.grad, ...), custom_call_target="tpu_custom_call" | custom-call | flops 3321888768 | bytes 11796480 | tf_op jit(solution)/shard_map/back_mix/pallas_call | solution.py:740
  259.3 4.9 matrix_grad.7
  264.3 3.4 collective-permute-done.50.back_two
  272.0 4.3 all-to-all-start.3
  276.3 15.6 %back_project.2 = (bf16[2,256,768]{2,1,0:T(8,128)(2,1)}, bf16[4,256,768]{2,1,0:T(8,128)(2,1)}, f32[256,768]{1,0:T(8,128)}, f32[8,768]{1,0:T(8,128)}) custom-call(f32[256,768]{1,0:T(8,128)} %get-tuple-element.391.resid, f32[5,768]{1,0:T(8,128)} %get-tuple-element.766.vectors, f32[256,32]{1,0:T(8,128)} %get-tuple-element.338.cosine_part, ...), custom_call_target="tpu_custom_call" | custom-call | flops 2415919104 | bytes 4718592 | tf_op jit(solution)/shard_map/back_project/pallas_call | solution.py:765
  300.5 6.2 %matrix_grad.8 = (bf16[2,192,768]{2,1,0:T(8,128)(2,1)}, bf16[2,192,768]{2,1,0:T(8,128)(2,1)}, bf16[2,192,768]{2,1,0:T(8,128)(2,1)}, bf16[2,192,768]{2,1,0:T(8,128)(2,1)}) custom-call(bf16[2,256,768]{2,1,0:T(8,128)(2,1)} %get-tuple-element.466.right_own, bf16[4,256,768]{2,1,0:T(8,128)(2,1)} %copy-done, bf16[4,256,768]{2,1,0:T(8,128)(2,1)} %get-tuple-element.473.rest_0_, ...), custom_call_target="tpu_custom_call" | custom-call | flops 1207959552 | bytes 4718592 | tf_op jit(solution)/shard_map/matrix_grad/pallas_call | solution.py:785
  309.9 13.8 %back_mix.3 = (bf16[2,256,768]{2,1,0:T(8,128)(2,1)}, bf16[3,256,768]{2,1,0:T(8,128)(2,1)}, f32[256,768]{1,0:T(8,128)}, bf16[256,768]{1,0:T(8,128)(2,1)}, bf16[25...) custom-call(f32[256,768]{1,0:T(8,128)} %get-tuple-element.491.grad, ...), custom_call_target="tpu_custom_call" | custom-call | flops 3321888768 | bytes 11796480 | tf_op jit(solution)/shard_map/back_mix/pallas_call | solution.py:740
  329.0 4.8 all-to-all-start.4
  333.7 2.7 merge.14
  341.5 5.2 matrix_grad.9
  346.7 3.6 collective-permute-done.64.back_two
  353.9 15.4 %back_project.3 = (bf16[2,256,768]{2,1,0:T(8,128)(2,1)}, bf16[4,256,768]{2,1,0:T(8,128)(2,1)}, f32[256,768]{1,0:T(8,128)}, f32[8,768]{1,0:T(8,128)}) custom-call(f32[256,768]{1,0:T(8,128)} %convert_element_type.66.resid, f32[5,768]{1,0:T(8,128)} %get-tuple-element.767.vectors, f32[256,32]{1,0:T(8,128)} %get-tuple-element.338.cosine_part, ...), custom_call_target="tpu_custom_call" | custom-call | flops 2415919104 | bytes 4718592 | tf_op jit(solution)/shard_map/back_project/pallas_call | solution.py:765
  369.5 6.0 %matrix_grad.10 = (bf16[2,192,768]{2,1,0:T(8,128)(2,1)}, bf16[2,192,768]{2,1,0:T(8,128)(2,1)}, bf16[2,192,768]{2,1,0:T(8,128)(2,1)}, bf16[2,192,768]{2,1,0:T(8,128)(2,1)}) custom-call(bf16[2,256,768]{2,1,0:T(8,128)(2,1)} %get-tuple-element.527.right_own, bf16[3,256,768]{2,1,0:T(8,128)(2,1)} %copy-done.38, bf16[3,256,768]{2,1,0:T(8,128)(2,1)} %get-tuple-element.474.rest_0_, ...), custom_call_target="tpu_custom_call" | custom-call | flops 1207959552 | bytes 4718592 | tf_op jit(solution)/shard_map/matrix_grad/pallas_call | solution.py:785
  382.4 6.1 %matrix_grad.11 = (bf16[2,192,768]{2,1,0:T(8,128)(2,1)}, bf16[2,192,768]{2,1,0:T(8,128)(2,1)}, bf16[2,192,768]{2,1,0:T(8,128)(2,1)}, bf16[2,192,768]{2,1,0:T(8,128)(2,1)}) custom-call(bf16[2,256,768]{2,1,0:T(8,128)(2,1)} %get-tuple-element.526.right_own, bf16[4,256,768]{2,1,0:T(8,128)(2,1)} %copy-done.16, bf16[4,256,768]{2,1,0:T(8,128)(2,1)} %get-tuple-element.552.rest_0_, ...), custom_call_target="tpu_custom_call" | custom-call | flops 1207959552 | bytes 4718592 | tf_op jit(solution)/shard_map/matrix_grad/pallas_call | solution.py:785
  392.0 5.2 all-to-all-start.5
  403.6 9.5 %orthogonalize.3 = bf16[8,96,384]{2,1,0:T(8,128)(2,1)} custom-call(bf16[4,192,768]{2,1,0:T(8,128)(2,1)} %copy-done.35, bf16[8,96,384]{2,1,0:T(8,128)(2,1)} %copy-done.45), custom_call_target="tpu_custom_call" | custom-call | flops 1698693120 | bytes 1179648 | tf_op jit(solution)/shard_map/orthogonalize/pallas_call | solution.py:835
  415.4 9.8 %all-to-all-done.5.terms = bf16[4,192,768]{2,1,0:T(8,128)(2,1)S(1)} async-done(((bf16[4,192,768]{2,1,0:T(8,128)(2,1)}), bf16[4,192,768]{2,1,0:T(8,128)(2,1)S(1)}, u32[]{:S(2)}, u32[]{:S(2)}) %all-to-all-start.5) | async-done | bytes 1179680 | tf_op jit(solution)/shard_map/all_to_all | solution.py:70
  425.2 3.5 all-to-all-start.6
  430.3 2.7 merge.21
  442.1 7.9 %collective-permute-done.82 = f32[12,768]{1,0:T(8,128)S(1)} collective-permute-done((f32[12,768]{1,0:T(8,128)S(1)}, f32[12,768]{1,0:T(8,128)S(1)}, u32[]{:S(2)}, u32[]{:S(2)}) %collective-permute-start.82) | collective-permute-done | bytes 36896 | tf_op jit(solution)/shard_map/ppermute | solution.py:57
  456.4 4.7 all-to-all-start.7
  461.8 9.6 %orthogonalize.4 = bf16[8,96,384]{2,1,0:T(8,128)(2,1)} custom-call(bf16[4,192,768]{2,1,0:T(8,128)(2,1)} %copy-done.36, bf16[8,96,384]{2,1,0:T(8,128)(2,1)} %copy-done.45), custom_call_target="tpu_custom_call" | custom-call | flops 1698693120 | bytes 1179648 | tf_op jit(solution)/shard_map/orthogonalize/pallas_call | solution.py:835
  471.4 16.8 %all-to-all-done.7.terms = bf16[4,192,768]{2,1,0:T(8,128)(2,1)S(1)} async-done(((bf16[4,192,768]{2,1,0:T(8,128)(2,1)}), bf16[4,192,768]{2,1,0:T(8,128)(2,1)S(1)}, u32[]{:S(2)}, u32[]{:S(2)}) %all-to-all-start.7) | async-done | bytes 1179680 | tf_op jit(solution)/shard_map/all_to_all | solution.py:70
  488.2 3.5 all-to-all-start.8
  493.4 9.5 %orthogonalize.5 = bf16[8,96,384]{2,1,0:T(8,128)(2,1)} custom-call(bf16[4,192,768]{2,1,0:T(8,128)(2,1)} %copy-done.37, bf16[8,96,192]{2,1,0:T(8,128)(2,1)} %copy-done.65), custom_call_target="tpu_custom_call" | custom-call | flops 1698693120 | bytes 1179648 | tf_op jit(solution)/shard_map/orthogonalize/pallas_call | solution.py:835
  502.9 4.2 all-to-all-done.8
  507.1 3.9 all-to-all-start.9
  513.3 8.2 %collective-permute-done.84 = f32[12,768]{1,0:T(8,128)S(1)} collective-permute-done((f32[12,768]{1,0:T(8,128)S(1)}, f32[12,768]{1,0:T(8,128)S(1)}, u32[]{:S(2)}, u32[]{:S(2)}) %collective-permute-start.84) | collective-permute-done | bytes 36896 | tf_op jit(solution)/shard_map/ppermute | solution.py:61
  521.6 4.7 collective-permute-start.85
  539.7 3.8 update_hidden.1
  (555 shorter events, 197.0 us)
Async XLA Ops:
  0.7 34.2 %collective-permute-start.8 = (f32[2,768]{1,0:T(2,128)}, f32[2,768]{1,0:T(2,128)S(1)}, u32[]{:S(2)}, u32[]{:S(2)}) collective-permute-start(f32[2,768]{1,0:T(2,128)} %param.27), channel_id=1, source_target_pairs={{0,2},{1,3},{2,0},{3,1},{4,6},{5,7},{6,4},{7,5},{8,10},{9,11},{10,... | collective-permute-start | bytes 18440 | tf_op jit(solution)/shard_map/ppermute | solution.py:57
  3.7 31.3 %collective-permute-start.7 = (f32[2,768]{1,0:T(2,128)}, f32[2,768]{1,0:T(2,128)S(1)}, u32[]{:S(2)}, u32[]{:S(2)}) collective-permute-start(f32[2,768]{1,0:T(2,128)} %param.27), channel_id=1, source_target_pairs={{0,1},{1,0},{2,3},{3,2},{4,5},{5,4},{6,7},{7,6},{8,9},{9,8},{10,11... | collective-permute-start | bytes 18440 | tf_op jit(solution)/shard_map/ppermute | solution.py:57
  17.3 17.7 %collective-permute-start.9 = (f32[2,768]{1,0:T(2,128)S(1)}, f32[2,768]{1,0:T(2,128)S(1)}, u32[]{:S(2)}, u32[]{:S(2)}) collective-permute-start(f32[2,768]{1,0:T(2,128)S(1)} %copy-done.103), channel_id=1, source_target_pairs={{0,3},{1,2},{2,1},{3,0},{4,7},{5,6},{6,5},{7,4},{8,11},{9,10},{10,... | collective-permute-start | bytes 18440 | tf_op jit(solution)/shard_map/ppermute | solution.py:57
  28.1 32.5 %all-to-all-start = ((bf16[4,96,1536]{2,1,0:T(8,128)(2,1)}), bf16[4,96,1536]{2,1,0:T(8,128)(2,1)}, u32[]{:S(2)}, u32[]{:S(2)}) async-start(bf16[4,96,1536]{2,1,0:T(8,128)(2,1)} %broadcast_in_dim.7), calls=%async_computation | async-start | bytes 2359296 | tf_op jit(solution)/shard_map/all_to_all | solution.py:70
  33.6 13.8 %collective-permute-start.6 = (bf16[768,384]{1,0:T(8,128)(2,1)S(1)}, bf16[768,384]{1,0:T(8,128)(2,1)S(1)}, u32[]{:S(2)}, u32[]{:S(2)}) collective-permute-start(bf16[768,384]{1,0:T(8,128)(2,1)S(1)} %constant_dynamic-update-slice_fusion.2.rest_4_), channel_id=1, source_target_pairs={{0,4},{4,0},{8,12},{12,8},{16,20},{20,16},{24,28},{28,24},{1,5},{5... | collective-permute-start | bytes 1769480 | tf_op jit(solution)/shard_map/ppermute | solution.py:61
  62.0 22.0 %collective-permute-start.14 = (bf16[384,768]{1,0:T(8,128)(2,1)S(1)}, bf16[384,768]{1,0:T(8,128)(2,1)S(1)}, u32[]{:S(2)}, u32[]{:S(2)}) collective-permute-start(bf16[384,768]{1,0:T(8,128)(2,1)S(1)} %bitcast.175), channel_id=1, source_target_pairs={{0,4},{4,0},{8,12},{12,8},{16,20},{20,16},{24,28},{28,24},{1,5},{5... | collective-permute-start | bytes 1769480 | tf_op jit(solution)/shard_map/ppermute | solution.py:61
  62.6 22.3 %collective-permute-start.15 = (bf16[384,768]{1,0:T(8,128)(2,1)S(1)}, bf16[384,768]{1,0:T(8,128)(2,1)S(1)}, u32[]{:S(2)}, u32[]{:S(2)}) collective-permute-start(bf16[384,768]{1,0:T(8,128)(2,1)S(1)} %bitcast.177), channel_id=1, source_target_pairs={{0,2},{1,3},{2,0},{3,1},{4,6},{5,7},{6,4},{7,5},{8,10},{9,11},{10,... | collective-permute-start | bytes 1769480 | tf_op jit(solution)/shard_map/ppermute | solution.py:57
  77.2 27.4 %collective-permute-start.23 = (bf16[256,768]{1,0:T(8,128)(2,1)}, bf16[256,768]{1,0:T(8,128)(2,1)}, u32[]{:S(2)}, u32[]{:S(2)}) collective-permute-start(bf16[256,768]{1,0:T(8,128)(2,1)} %get-tuple-element.717.rest_0_), channel_id=1, source_target_pairs={{0,1},{1,0},{2,3},{3,2},{4,5},{5,4},{6,7},{7,6},{8,9},{9,8},{10,11... | collective-permute-start | bytes 1179656 | tf_op jit(solution)/shard_map/ppermute | solution.py:57
  79.1 46.1 %all-to-all-start.1 = ((bf16[4,96,2304]{2,1,0:T(8,128)(2,1)}), bf16[4,96,2304]{2,1,0:T(8,128)(2,1)}, u32[]{:S(2)}, u32[]{:S(2)}) async-start(bf16[4,96,2304]{2,1,0:T(8,128)(2,1)} %broadcast_in_dim.8), calls=%async_computation.1 | async-start | bytes 3538944 | tf_op jit(solution)/shard_map/all_to_all | solution.py:70
  85.0 37.3 %collective-permute-start.20 = (bf16[768,768]{1,0:T(8,128)(2,1)S(1)}, bf16[768,768]{1,0:T(8,128)(2,1)S(1)}, u32[]{:S(2)}, u32[]{:S(2)}) collective-permute-start(bf16[768,768]{1,0:T(8,128)(2,1)S(1)} %constant_dynamic-update-slice_fusion.6.rest_12_), channel_id=1, source_target_pairs={{0,4},{4,0},{8,12},{12,8},{16,20},{20,16},{24,28},{28,24},{1,5},{5... | collective-permute-start | bytes 3538952 | tf_op jit(solution)/shard_map/ppermute | solution.py:61
  86.6 35.8 %collective-permute-start.18 = (bf16[768,768]{1,0:T(8,128)(2,1)S(1)}, bf16[768,768]{1,0:T(8,128)(2,1)}, u32[]{:S(2)}, u32[]{:S(2)}) collective-permute-start(bf16[768,768]{1,0:T(8,128)(2,1)S(1)} %constant_dynamic-update-slice_fusion.6.rest_12_), channel_id=1, source_target_pairs={{0,1},{1,0},{2,3},{3,2},{4,5},{5,4},{6,7},{7,6},{8,9},{9,8},{10,11... | collective-permute-start | bytes 3538952 | tf_op jit(solution)/shard_map/ppermute | solution.py:57
  86.7 35.6 %collective-permute-start.19 = (bf16[768,768]{1,0:T(8,128)(2,1)S(1)}, bf16[768,768]{1,0:T(8,128)(2,1)}, u32[]{:S(2)}, u32[]{:S(2)}) collective-permute-start(bf16[768,768]{1,0:T(8,128)(2,1)S(1)} %constant_dynamic-update-slice_fusion.4.rest_8_), channel_id=1, source_target_pairs={{0,2},{1,3},{2,0},{3,1},{4,6},{5,7},{6,4},{7,5},{8,10},{9,11},{10,... | collective-permute-start | bytes 3538952 | tf_op jit(solution)/shard_map/ppermute | solution.py:57
  87.3 35.6 %collective-permute-start.17 = (bf16[768,768]{1,0:T(8,128)(2,1)S(1)}, bf16[768,768]{1,0:T(8,128)(2,1)}, u32[]{:S(2)}, u32[]{:S(2)}) collective-permute-start(bf16[768,768]{1,0:T(8,128)(2,1)S(1)} %constant_dynamic-update-slice_fusion.4.rest_8_), channel_id=1, source_target_pairs={{0,1},{1,0},{2,3},{3,2},{4,5},{5,4},{6,7},{7,6},{8,9},{9,8},{10,11... | collective-permute-start | bytes 3538952 | tf_op jit(solution)/shard_map/ppermute | solution.py:57
  129.9 22.9 %collective-permute-start.28 = (bf16[384,768]{1,0:T(8,128)(2,1)S(1)}, bf16[384,768]{1,0:T(8,128)(2,1)S(1)}, u32[]{:S(2)}, u32[]{:S(2)}) collective-permute-start(bf16[384,768]{1,0:T(8,128)(2,1)S(1)} %bitcast.171), channel_id=1, source_target_pairs={{0,4},{4,0},{8,12},{12,8},{16,20},{20,16},{24,28},{28,24},{1,5},{5... | collective-permute-start | bytes 1769480 | tf_op jit(solution)/shard_map/ppermute | solution.py:61
  131.5 21.4 %collective-permute-start.29 = (bf16[384,768]{1,0:T(8,128)(2,1)S(1)}, bf16[384,768]{1,0:T(8,128)(2,1)S(1)}, u32[]{:S(2)}, u32[]{:S(2)}) collective-permute-start(bf16[384,768]{1,0:T(8,128)(2,1)S(1)} %bitcast.173), channel_id=1, source_target_pairs={{0,2},{1,3},{2,0},{3,1},{4,6},{5,7},{6,4},{7,5},{8,10},{9,11},{10,... | collective-permute-start | bytes 1769480 | tf_op jit(solution)/shard_map/ppermute | solution.py:57
  132.0 19.6 %collective-permute-start.26 = (bf16[384,384]{1,0:T(8,128)(2,1)S(1)}, bf16[384,384]{1,0:T(8,128)(2,1)S(1)}, u32[]{:S(2)}, u32[]{:S(2)}) collective-permute-start(bf16[384,384]{1,0:T(8,128)(2,1)S(1)} %bitcast.181), channel_id=1, source_target_pairs={{0,4},{4,0},{8,12},{12,8},{16,20},{20,16},{24,28},{28,24},{1,5},{5... | collective-permute-start | bytes 884744 | tf_op jit(solution)/shard_map/ppermute | solution.py:61
  132.5 20.3 %collective-permute-start.27 = (bf16[384,384]{1,0:T(8,128)(2,1)S(1)}, bf16[384,384]{1,0:T(8,128)(2,1)S(1)}, u32[]{:S(2)}, u32[]{:S(2)}) collective-permute-start(bf16[384,384]{1,0:T(8,128)(2,1)S(1)} %bitcast.179), channel_id=1, source_target_pairs={{0,2},{1,3},{2,0},{3,1},{4,6},{5,7},{6,4},{7,5},{8,10},{9,11},{10,... | collective-permute-start | bytes 884744 | tf_op jit(solution)/shard_map/ppermute | solution.py:57
  153.0 14.2 %collective-permute-start.31 = (bf16[768,384]{1,0:T(8,128)(2,1)S(1)}, bf16[768,384]{1,0:T(8,128)(2,1)S(1)}, u32[]{:S(2)}, u32[]{:S(2)}) collective-permute-start(bf16[768,384]{1,0:T(8,128)(2,1)S(1)} %constant_dynamic-update-slice_fusion.18.rest_4_), channel_id=1, source_target_pairs={{0,4},{4,0},{8,12},{12,8},{16,20},{20,16},{24,28},{28,24},{1,5},{5... | collective-permute-start | bytes 1769480 | tf_op jit(solution)/shard_map/ppermute | solution.py:61
  153.6 14.0 %collective-permute-start.30 = (bf16[768,384]{1,0:T(8,128)(2,1)S(1)}, bf16[768,384]{1,0:T(8,128)(2,1)S(1)}, u32[]{:S(2)}, u32[]{:S(2)}) collective-permute-start(bf16[768,384]{1,0:T(8,128)(2,1)S(1)} %constant_dynamic-update-slice_fusion.16.rest_0_), channel_id=1, source_target_pairs={{0,2},{1,3},{2,0},{3,1},{4,6},{5,7},{6,4},{7,5},{8,10},{9,11},{10,... | collective-permute-start | bytes 1769480 | tf_op jit(solution)/shard_map/ppermute | solution.py:57
  169.9 28.8 %collective-permute-start.42 = (bf16[768,768]{1,0:T(8,128)(2,1)}, bf16[768,768]{1,0:T(8,128)(2,1)}, u32[]{:S(2)}, u32[]{:S(2)}) collective-permute-start(bf16[768,768]{1,0:T(8,128)(2,1)} %constant_dynamic-update-slice_fusion.22.rest_12_), channel_id=1, source_target_pairs={{0,4},{4,0},{8,12},{12,8},{16,20},{20,16},{24,28},{28,24},{1,5},{5... | collective-permute-start | bytes 3538952 | tf_op jit(solution)/shard_map/ppermute | solution.py:61
  171.4 29.3 %collective-permute-start.40 = (bf16[768,768]{1,0:T(8,128)(2,1)}, bf16[768,768]{1,0:T(8,128)(2,1)}, u32[]{:S(2)}, u32[]{:S(2)}) collective-permute-start(bf16[768,768]{1,0:T(8,128)(2,1)} %constant_dynamic-update-slice_fusion.22.rest_12_), channel_id=1, source_target_pairs={{0,1},{1,0},{2,3},{3,2},{4,5},{5,4},{6,7},{7,6},{8,9},{9,8},{10,11... | collective-permute-start | bytes 3538952 | tf_op jit(solution)/shard_map/ppermute | solution.py:57
  173.4 29.0 %collective-permute-start.41 = (bf16[768,768]{1,0:T(8,128)(2,1)}, bf16[768,768]{1,0:T(8,128)(2,1)}, u32[]{:S(2)}, u32[]{:S(2)}) collective-permute-start(bf16[768,768]{1,0:T(8,128)(2,1)} %constant_dynamic-update-slice_fusion.20.rest_8_), channel_id=1, source_target_pairs={{0,2},{1,3},{2,0},{3,1},{4,6},{5,7},{6,4},{7,5},{8,10},{9,11},{10,... | collective-permute-start | bytes 3538952 | tf_op jit(solution)/shard_map/ppermute | solution.py:57
  173.9 28.4 %collective-permute-start.39 = (bf16[768,768]{1,0:T(8,128)(2,1)}, bf16[768,768]{1,0:T(8,128)(2,1)}, u32[]{:S(2)}, u32[]{:S(2)}) collective-permute-start(bf16[768,768]{1,0:T(8,128)(2,1)} %constant_dynamic-update-slice_fusion.20.rest_8_), channel_id=1, source_target_pairs={{0,1},{1,0},{2,3},{3,2},{4,5},{5,4},{6,7},{7,6},{8,9},{9,8},{10,11... | collective-permute-start | bytes 3538952 | tf_op jit(solution)/shard_map/ppermute | solution.py:57
  206.6 19.8 %all-to-all-start.2 = ((bf16[8,96,384]{2,1,0:T(8,128)(2,1)}), bf16[8,96,384]{2,1,0:T(8,128)(2,1)S(1)}, u32[]{:S(2)}, u32[]{:S(2)}) async-start(bf16[8,96,384]{2,1,0:T(8,128)(2,1)} %pad_maximum_fusion), calls=%async_computation.2 | async-start | bytes 1179648 | tf_op jit(solution)/shard_map/all_to_all | solution.py:78
  234.9 16.1 %collective-permute-start.46 = (bf16[2,192,768]{2,1,0:T(8,128)(2,1)}, bf16[2,192,768]{2,1,0:T(8,128)(2,1)S(1)}, u32[]{:S(2)}, u32[]{:S(2)}) collective-permute-start(bf16[2,192,768]{2,1,0:T(8,128)(2,1)} %get-tuple-element.440), channel_id=1, source_target_pairs={{0,2},{1,3},{2,0},{3,1},{4,6},{5,7},{6,4},{7,5},{8,10},{9,11},{10,... | collective-permute-start | bytes 1769480 | tf_op jit(solution)/shard_map/ppermute | solution.py:57
  235.4 15.6 %collective-permute-start.47 = (bf16[2,192,768]{2,1,0:T(8,128)(2,1)}, bf16[2,192,768]{2,1,0:T(8,128)(2,1)S(1)}, u32[]{:S(2)}, u32[]{:S(2)}) collective-permute-start(bf16[2,192,768]{2,1,0:T(8,128)(2,1)} %get-tuple-element.441), channel_id=1, source_target_pairs={{0,4},{4,0},{8,12},{12,8},{16,20},{20,16},{24,28},{28,24},{1,5},{5... | collective-permute-start | bytes 1769480 | tf_op jit(solution)/shard_map/ppermute | solution.py:61
  254.7 14.1 %collective-permute-start.52 = (bf16[192,768]{1,0:T(8,128)(2,1)}, bf16[192,768]{1,0:T(8,128)(2,1)S(1)}, u32[]{:S(2)}, u32[]{:S(2)}) collective-permute-start(bf16[192,768]{1,0:T(8,128)(2,1)} %get-tuple-element.461), channel_id=1, source_target_pairs={{0,4},{4,0},{8,12},{12,8},{16,20},{20,16},{24,28},{28,24},{1,5},{5... | collective-permute-start | bytes 884744 | tf_op jit(solution)/shard_map/ppermute | solution.py:61
  269.5 22.4 %collective-permute-start.54 = (bf16[2,192,768]{2,1,0:T(8,128)(2,1)}, bf16[2,192,768]{2,1,0:T(8,128)(2,1)S(1)}, u32[]{:S(2)}, u32[]{:S(2)}) collective-permute-start(bf16[2,192,768]{2,1,0:T(8,128)(2,1)} %get-tuple-element.467), channel_id=1, source_target_pairs={{0,2},{1,3},{2,0},{3,1},{4,6},{5,7},{6,4},{7,5},{8,10},{9,11},{10,... | collective-permute-start | bytes 1769480 | tf_op jit(solution)/shard_map/ppermute | solution.py:57
  271.0 20.9 %collective-permute-start.55 = (bf16[2,192,768]{2,1,0:T(8,128)(2,1)}, bf16[2,192,768]{2,1,0:T(8,128)(2,1)S(1)}, u32[]{:S(2)}, u32[]{:S(2)}) collective-permute-start(bf16[2,192,768]{2,1,0:T(8,128)(2,1)} %get-tuple-element.468), channel_id=1, source_target_pairs={{0,4},{4,0},{8,12},{12,8},{16,20},{20,16},{24,28},{28,24},{1,5},{5... | collective-permute-start | bytes 1769480 | tf_op jit(solution)/shard_map/ppermute | solution.py:61
  272.0 19.9 %all-to-all-start.3 = ((bf16[8,96,192]{2,1,0:T(8,128)(2,1)}), bf16[8,96,192]{2,1,0:T(8,128)(2,1)S(1)}, u32[]{:S(2)}, u32[]{:S(2)}) async-start(bf16[8,96,192]{2,1,0:T(8,128)(2,1)} %get-tuple-element.472), calls=%async_computation.3 | async-start | bytes 786432 | tf_op jit(solution)/shard_map/all_to_all | solution.py:78
  309.0 14.7 %collective-permute-start.60 = (bf16[2,192,768]{2,1,0:T(8,128)(2,1)}, bf16[2,192,768]{2,1,0:T(8,128)(2,1)S(1)}, u32[]{:S(2)}, u32[]{:S(2)}) collective-permute-start(bf16[2,192,768]{2,1,0:T(8,128)(2,1)} %get-tuple-element.499), channel_id=1, source_target_pairs={{0,2},{1,3},{2,0},{3,1},{4,6},{5,7},{6,4},{7,5},{8,10},{9,11},{10,... | collective-permute-start | bytes 1769480 | tf_op jit(solution)/shard_map/ppermute | solution.py:57
  309.5 14.2 %collective-permute-start.61 = (bf16[2,192,768]{2,1,0:T(8,128)(2,1)}, bf16[2,192,768]{2,1,0:T(8,128)(2,1)S(1)}, u32[]{:S(2)}, u32[]{:S(2)}) collective-permute-start(bf16[2,192,768]{2,1,0:T(8,128)(2,1)} %get-tuple-element.500), channel_id=1, source_target_pairs={{0,4},{4,0},{8,12},{12,8},{16,20},{20,16},{24,28},{28,24},{1,5},{5... | collective-permute-start | bytes 1769480 | tf_op jit(solution)/shard_map/ppermute | solution.py:61
  329.0 40.4 %all-to-all-start.4 = ((bf16[4,192,768]{2,1,0:T(8,128)(2,1)}), bf16[4,192,768]{2,1,0:T(8,128)(2,1)S(1)}, u32[]{:S(2)}, u32[]{:S(2)}) async-start(bf16[4,192,768]{2,1,0:T(8,128)(2,1)} %merge.16), calls=%async_computation.4 | async-start | bytes 2359296 | tf_op jit(solution)/shard_map/all_to_all | solution.py:70
  336.5 15.2 %collective-permute-start.66 = (bf16[192,768]{1,0:T(8,128)(2,1)}, bf16[192,768]{1,0:T(8,128)(2,1)S(1)}, u32[]{:S(2)}, u32[]{:S(2)}) collective-permute-start(bf16[192,768]{1,0:T(8,128)(2,1)} %get-tuple-element.520), channel_id=1, source_target_pairs={{0,4},{4,0},{8,12},{12,8},{16,20},{20,16},{24,28},{28,24},{1,5},{5... | collective-permute-start | bytes 884744 | tf_op jit(solution)/shard_map/ppermute | solution.py:61
  338.0 13.7 %collective-permute-start.67 = (bf16[192,768]{1,0:T(8,128)(2,1)}, bf16[192,768]{1,0:T(8,128)(2,1)S(1)}, u32[]{:S(2)}, u32[]{:S(2)}) collective-permute-start(bf16[192,768]{1,0:T(8,128)(2,1)} %get-tuple-element.521), channel_id=1, source_target_pairs={{0,2},{1,3},{2,0},{3,1},{4,6},{5,7},{6,4},{7,5},{8,10},{9,11},{10,... | collective-permute-start | bytes 884744 | tf_op jit(solution)/shard_map/ppermute | solution.py:57
  351.7 17.6 %collective-permute-start.68 = (bf16[2,192,768]{2,1,0:T(8,128)(2,1)}, bf16[2,192,768]{2,1,0:T(8,128)(2,1)S(1)}, u32[]{:S(2)}, u32[]{:S(2)}) collective-permute-start(bf16[2,192,768]{2,1,0:T(8,128)(2,1)} %get-tuple-element.534), channel_id=1, source_target_pairs={{0,2},{1,3},{2,0},{3,1},{4,6},{5,7},{6,4},{7,5},{8,10},{9,11},{10,... | collective-permute-start | bytes 1769480 | tf_op jit(solution)/shard_map/ppermute | solution.py:57
  353.3 16.1 %collective-permute-start.69 = (bf16[2,192,768]{2,1,0:T(8,128)(2,1)}, bf16[2,192,768]{2,1,0:T(8,128)(2,1)S(1)}, u32[]{:S(2)}, u32[]{:S(2)}) collective-permute-start(bf16[2,192,768]{2,1,0:T(8,128)(2,1)} %get-tuple-element.535), channel_id=1, source_target_pairs={{0,4},{4,0},{8,12},{12,8},{16,20},{20,16},{24,28},{28,24},{1,5},{5... | collective-permute-start | bytes 1769480 | tf_op jit(solution)/shard_map/ppermute | solution.py:61
  392.0 33.1 %all-to-all-start.5 = ((bf16[4,192,768]{2,1,0:T(8,128)(2,1)}), bf16[4,192,768]{2,1,0:T(8,128)(2,1)S(1)}, u32[]{:S(2)}, u32[]{:S(2)}) async-start(bf16[4,192,768]{2,1,0:T(8,128)(2,1)} %merge.20), calls=%async_computation.5 | async-start | bytes 2359296 | tf_op jit(solution)/shard_map/all_to_all | solution.py:70
  397.4 16.5 %collective-permute-start.78 = (bf16[2,192,768]{2,1,0:T(8,128)(2,1)}, bf16[2,192,768]{2,1,0:T(8,128)(2,1)S(1)}, u32[]{:S(2)}, u32[]{:S(2)}) collective-permute-start(bf16[2,192,768]{2,1,0:T(8,128)(2,1)} %get-tuple-element.576), channel_id=1, source_target_pairs={{0,2},{1,3},{2,0},{3,1},{4,6},{5,7},{6,4},{7,5},{8,10},{9,11},{10,... | collective-permute-start | bytes 1769480 | tf_op jit(solution)/shard_map/ppermute | solution.py:57
  398.9 16.5 %collective-permute-start.79 = (bf16[2,192,768]{2,1,0:T(8,128)(2,1)}, bf16[2,192,768]{2,1,0:T(8,128)(2,1)S(1)}, u32[]{:S(2)}, u32[]{:S(2)}) collective-permute-start(bf16[2,192,768]{2,1,0:T(8,128)(2,1)} %get-tuple-element.577), channel_id=1, source_target_pairs={{0,4},{4,0},{8,12},{12,8},{16,20},{20,16},{24,28},{28,24},{1,5},{5... | collective-permute-start | bytes 1769480 | tf_op jit(solution)/shard_map/ppermute | solution.py:61
  401.5 35.0 %collective-permute-start.73 = (bf16[2,192,768]{2,1,0:T(8,128)(2,1)}, bf16[2,192,768]{2,1,0:T(8,128)(2,1)S(1)}, u32[]{:S(2)}, u32[]{:S(2)}) collective-permute-start(bf16[2,192,768]{2,1,0:T(8,128)(2,1)} %get-tuple-element.561), channel_id=1, source_target_pairs={{0,2},{1,3},{2,0},{3,1},{4,6},{5,7},{6,4},{7,5},{8,10},{9,11},{10,... | collective-permute-start | bytes 1769480 | tf_op jit(solution)/shard_map/ppermute | solution.py:57
  402.1 34.4 %collective-permute-start.74 = (bf16[2,192,768]{2,1,0:T(8,128)(2,1)}, bf16[2,192,768]{2,1,0:T(8,128)(2,1)}, u32[]{:S(2)}, u32[]{:S(2)}) collective-permute-start(bf16[2,192,768]{2,1,0:T(8,128)(2,1)} %get-tuple-element.562), channel_id=1, source_target_pairs={{0,4},{4,0},{8,12},{12,8},{16,20},{20,16},{24,28},{28,24},{1,5},{5... | collective-permute-start | bytes 1769480 | tf_op jit(solution)/shard_map/ppermute | solution.py:61
  425.2 27.8 %all-to-all-start.6 = ((bf16[8,96,384]{2,1,0:T(8,128)(2,1)}), bf16[8,96,384]{2,1,0:T(8,128)(2,1)S(1)}, u32[]{:S(2)}, u32[]{:S(2)}) async-start(bf16[8,96,384]{2,1,0:T(8,128)(2,1)} %orthogonalize.3), calls=%async_computation.6 | async-start | bytes 1179648 | tf_op jit(solution)/shard_map/all_to_all | solution.py:78
  433.0 16.9 %collective-permute-start.80 = (bf16[192,768]{1,0:T(8,128)(2,1)}, bf16[192,768]{1,0:T(8,128)(2,1)S(1)}, u32[]{:S(2)}, u32[]{:S(2)}) collective-permute-start(bf16[192,768]{1,0:T(8,128)(2,1)} %get-tuple-element.593), channel_id=1, source_target_pairs={{0,4},{4,0},{8,12},{12,8},{16,20},{20,16},{24,28},{28,24},{1,5},{5... | collective-permute-start | bytes 884744 | tf_op jit(solution)/shard_map/ppermute | solution.py:61
  434.9 15.0 %collective-permute-start.81 = (bf16[192,768]{1,0:T(8,128)(2,1)}, bf16[192,768]{1,0:T(8,128)(2,1)S(1)}, u32[]{:S(2)}, u32[]{:S(2)}) collective-permute-start(bf16[192,768]{1,0:T(8,128)(2,1)} %get-tuple-element.594), channel_id=1, source_target_pairs={{0,2},{1,3},{2,0},{3,1},{4,6},{5,7},{6,4},{7,5},{8,10},{9,11},{10,... | collective-permute-start | bytes 884744 | tf_op jit(solution)/shard_map/ppermute | solution.py:57
  456.4 31.8 %all-to-all-start.7 = ((bf16[4,192,768]{2,1,0:T(8,128)(2,1)}), bf16[4,192,768]{2,1,0:T(8,128)(2,1)S(1)}, u32[]{:S(2)}, u32[]{:S(2)}) async-start(bf16[4,192,768]{2,1,0:T(8,128)(2,1)} %merge.23), calls=%async_computation.7 | async-start | bytes 2359296 | tf_op jit(solution)/shard_map/all_to_all | solution.py:70
  488.2 18.9 %all-to-all-start.8 = ((bf16[8,96,384]{2,1,0:T(8,128)(2,1)}), bf16[8,96,384]{2,1,0:T(8,128)(2,1)S(1)}, u32[]{:S(2)}, u32[]{:S(2)}) async-start(bf16[8,96,384]{2,1,0:T(8,128)(2,1)} %orthogonalize.4), calls=%async_computation.8 | async-start | bytes 1179648 | tf_op jit(solution)/shard_map/all_to_all | solution.py:78
  507.1 24.4 %all-to-all-start.9 = ((bf16[8,96,384]{2,1,0:T(8,128)(2,1)}), bf16[8,96,384]{2,1,0:T(8,128)(2,1)S(1)}, u32[]{:S(2)}, u32[]{:S(2)}) async-start(bf16[8,96,384]{2,1,0:T(8,128)(2,1)} %orthogonalize.5), calls=%async_computation.9 | async-start | bytes 1179648 | tf_op jit(solution)/shard_map/all_to_all | solution.py:78
  (163 other events, 1198.4 us)

commit v3 on v2

--- a/solution.py
+++ b/solution.py
@@ -70,8 +70,8 @@
     return lax.all_to_all(parts, "dp", split_axis=0, concat_axis=0, axis_index_groups=groups, tiled=True)
 
 
-def gather_line(part):
-    return swap_line(jnp.broadcast_to(part[None], (4,) + part.shape))
+def four_times(part):
+    return jnp.broadcast_to(part[None], (4,) + part.shape)
 
 
 def swap_owners(parts):
@@ -82,13 +82,13 @@
     return lax.optimization_barrier(values)
 
 
-def sources(kind, slot, rows):
+def sources(kind, slot):
     core, across = slot & 1, slot >> 1
     if kind == "whole":
-        return [(slot, 0, 1, 0)]
+        return [(slot, None, None)]
     if "up" in kind:
-        return [(slot, 0, 4, 0), (slot, rows // 2, 4, 1)]
-    return [(core, across * rows // 2, 4, 0), (2 + core, across * rows // 2, 4, 1)]
+        return [(slot, 0, 0), (slot, 1, 1)]
+    return [(core, across, 0), (2 + core, across, 1)]
 
 
 def fetch(refs, plan, scratch, sems, base, lanes):
@@ -99,34 +99,42 @@
         first, last = max(lane, lanes[0]), min(lane + width, lanes[1])
         if first >= last:
             continue
+        taken = pl.ds(source_lane + first - lane, last - first)
+        given = pl.ds(first - lanes[0], last - first)
         for slot in range(4):
-            for array, row, pieces, y_offset in sources(kind, slot, scratch.shape[1]):
+            for array, entry, y_offset in sources(kind, slot):
                 ref = refs[4 * position + array]
-                size = scratch.shape[1] // (2 * pieces) if pieces > 1 else scratch.shape[1]
-                for piece in range(pieces):
-                    start = 0
-                    if pieces > 1:
-                        place = 2 * piece + ((index & 1) ^ y_offset)
-                        if "near" in kind:
-                            place = index ^ (2 * piece + y_offset)
-                        start = pl.multiple_of(place * size, 16)
-                    copy = pltpu.make_async_copy(
-                        ref.at[pl.ds(row + piece * size, size), pl.ds(source_lane + first - lane, last - first)],
-                        scratch.at[slot, pl.ds(start, size), pl.ds(first - lanes[0], last - first)],
-                        sems.at[count],
-                    )
+                if kind == "whole":
+                    pairs = [(ref.at[:, :, :, taken], scratch.at[slot, :, :, :, given])]
+                elif "near" in kind:
+                    pairs = [
+                        (
+                            ref.at[entry, offset, :, taken],
+                            scratch.at[slot, (index >> 1) ^ offset, (index & 1) ^ y_offset, :, given],
+                        )
+                        for offset in range(4)
+                    ]
+                else:
+                    pairs = [(ref.at[entry, :, :, taken], scratch.at[slot, :, (index & 1) ^ y_offset, :, given])]
+                for source, target in pairs:
+                    copy = pltpu.make_async_copy(source, target, sems.at[count])
                     copy.start()
                     waits[slot].append(copy)
                     count += 1
     return waits
 
 
+def matrix(scratch, slot, first, last):
+    value = scratch[slot]
+    return value.reshape(-1, value.shape[-1])[:, first:last]
+
+
 def ref_count(plan):
     return 4 * len(plan)
 
 
 def copy_count(plan):
-    return sum(4 if run[0] == "whole" else 32 for run in plan)
+    return sum(4 if run[0] == "whole" else 32 if "near" in run[0] else 8 for run in plan)
 
 
 def take(refs, *plans):
@@ -216,6 +224,10 @@
 def same_head(feature_rows):
     shape = (feature_rows, 2 * CHUNK)
     return iota(shape, 0) % FEAT_CHUNK // FEATS == iota(shape, 1) % CHUNK // HEAD_DIM
+
+
+def column_of(segment_row):
+    return jnp.broadcast_to(segment_row[...], (8, segment_row.shape[1])).T[:, 0:1]
 
 
 def edge_masks(segment_column):
@@ -284,10 +296,10 @@
     return slice(slot * width, (slot + 1) * width)
 
 
-def project_kernel(plan, resid, vectors, cosine_part, sine_part, feature_map, segment_column, *rest):
+def project_kernel(plan, resid, vectors, cosine_part, sine_part, feature_map, segment_row, *rest):
     weight_refs, rest = take(rest, plan)
     phi_query_out, phi_key_out, value_out, query_out, key_out, summary_out, weight, sems = rest
-    waits = fetch(weight_refs, plan, weight, sems, 0, (0, weight.shape[2]))
+    waits = fetch(weight_refs, plan, weight, sems, 0, (0, weight.shape[4]))
     cosine, sine = turn_tables(cosine_part, sine_part)
     unit, _ = norm_parts(resid[...])
     normed = (unit * vectors[0:1, :] + vectors[1:2, :]).astype(BF16)
@@ -295,14 +307,14 @@
     pieces = [[], [], []]
     for slot in range(4):
         arrive(waits[slot])
-        product = dot_nn(normed, weight[slot, :, 0 : 3 * width])
+        product = dot_nn(normed, matrix(weight, slot, 0, 3 * width))
         for which in range(3):
             pieces[which].append(product[:, lanes_of(which, width)])
     queries, key_rows, value_rows = (jnp.concatenate(piece, axis=1) for piece in pieces)
     value_rows = value_rows.astype(BF16)
     value_out[...] = value_rows
     map_high, map_low = split_low(wide_map(feature_map))
-    in_first, in_last = edge_masks(segment_column[...])
+    in_first, in_last = edge_masks(column_of(segment_row))
     totals = []
     for chunk in range(resid.shape[1] // CHUNK):
         lanes = lanes_of(chunk, CHUNK)
@@ -325,7 +337,7 @@
 
 
 def mix_kernel(
-    plans, resid, vectors, bias, phi_query, phi_key, value, segment_column, segment_row, recv_one, recv_two,
+    plans, resid, vectors, bias, phi_query, phi_key, value, segment_row, recv_one, recv_two,
     recv_three, coefficients, *rest
 ):
     out_refs, up_refs, down_refs, rest = take(rest, *plans)
@@ -335,8 +347,9 @@
     out_waits = fetch(out_refs, plans[0], out_weight, sems, bases[0], (512, 768))
     up_waits = fetch(up_refs, plans[1], up_weight, sems, bases[1], (0, 768))
     down_waits = fetch(down_refs, plans[2], down_weight, sems, bases[2], (0, 768))
-    same = (segment_column[...] == segment_row[...]).astype(F32)
-    in_first, in_last = edge_masks(segment_column[...])
+    segment_column = column_of(segment_row)
+    same = (segment_column == segment_row[...]).astype(F32)
+    in_first, in_last = edge_masks(segment_column)
     totals = combine_edges((recv_one, recv_two, recv_three), coefficients)
     rows = resid.shape[0]
     contexts = []
@@ -366,7 +379,7 @@
     middle = resid[...]
     for slot in range(4):
         arrive(out_waits[slot])
-        middle = middle + dot_nt(context[:, lanes_of(slot, width)], out_weight[slot, :, 64:])
+        middle = middle + dot_nt(context[:, lanes_of(slot, width)], matrix(out_weight, slot, 64, 256))
     middle_out[...] = middle
     unit, _ = norm_parts(middle)
     normed = (unit * vectors[2:3, :] + vectors[3:4, :]).astype(BF16)
@@ -374,7 +387,7 @@
     output = middle + vectors[4:5, :]
     for slot in range(4):
         arrive(up_waits[slot])
-        upper = dot_nn(normed, up_weight[slot]) + bias[slot : slot + 1, :]
+        upper = dot_nn(normed, matrix(up_weight, slot, 0, 768)) + bias[slot : slot + 1, :]
         below = 0.5 * (1.0 + lax.erf(upper * 2.0**-0.5))
         slope = below + upper * (jnp.exp(-0.5 * upper * upper) * 0.3989422804014327)
         active = (upper * below).astype(BF16)
@@ -384,12 +397,12 @@
         else:
             pack_out[slot // 2] = active
         arrive(down_waits[slot])
-        output = output + dot_nt(active, down_weight[slot])
+        output = output + dot_nt(active, matrix(down_weight, slot, 0, 768))
     resid_out[...] = output
 
 
 def back_mix_kernel(
-    plans, grad, vectors, middle, slope, inverse, context, phi_query, segment_column, *rest
+    plans, grad, vectors, middle, slope, inverse, context, phi_query, segment_row, *rest
 ):
     out_refs, up_refs, down_refs, rest = take(rest, *plans)
     (upper_keep, pack_out, middle_grad_out, numer_out, denom_out, summary_out, vector_out,
@@ -404,7 +417,7 @@
     normed_grad = None
     for slot in range(4):
         arrive(down_waits[slot])
-        hidden = dot_nn(branch, down_weight[slot])
+        hidden = dot_nn(branch, matrix(down_weight, slot, 0, 768))
         upper = (hidden * slope[slot].astype(F32)).astype(BF16)
         if slot % 2 == 0:
             upper_keep[slot // 2] = upper
@@ -412,7 +425,7 @@
             pack_out[slot // 2] = upper
         bias_out[slot : slot + 1, :] = jnp.sum(upper.astype(F32), axis=0, keepdims=True)
         arrive(up_waits[slot])
-        part = dot_nt(upper, up_weight[slot])
+        part = dot_nt(upper, matrix(up_weight, slot, 0, 768))
         normed_grad = part if normed_grad is None else normed_grad + part
     inward, gain_grad, shift_grad = norm_backward(middle[...], vectors[2:3, :], normed_grad)
     middle_grad = grad_out + inward
@@ -424,9 +437,9 @@
     pieces = []
     for slot in range(4):
         arrive(out_waits[slot])
-        pieces.append(dot_nn(attn, out_weight[slot, :, 64:]))
+        pieces.append(dot_nn(attn, matrix(out_weight, slot, 64, 256)))
     context_grad = jnp.concatenate(pieces, axis=1)
-    in_first, in_last = edge_masks(segment_column[...])
+    in_first, in_last = edge_masks(column_of(segment_row))
     head_ones = (iota((CHUNK, CHUNK), 0) // HEAD_DIM == iota((CHUNK, CHUNK), 1) // HEAD_DIM).astype(BF16)
     one_lane = (iota((CHUNK, FEAT_CHUNK), 0) == iota((CHUNK, FEAT_CHUNK), 1) // FEATS * HEAD_DIM).astype(BF16)
     totals = []
@@ -448,18 +461,19 @@
 
 
 def back_project_kernel(
-    plan, resid, vectors, cosine_part, sine_part, feature_map, segment_column, segment_row, phi_query, phi_key, value,
+    plan, resid, vectors, cosine_part, sine_part, feature_map, segment_row, phi_query, phi_key, value,
     query_scaled, key_scaled, numer, denom, context, middle_grad, recv_one, recv_two, recv_three, back_one,
     back_two, back_three, coefficients, *rest
 ):
     weight_refs, rest = take(rest, plan)
     stacked_keep, pack_out, grad_out, vector_out, weight, sems = rest
-    waits = fetch(weight_refs, plan, weight, sems, 0, (0, weight.shape[2]))
+    waits = fetch(weight_refs, plan, weight, sems, 0, (0, weight.shape[4]))
     cosine, sine = turn_tables(cosine_part, sine_part)
     unit, _ = norm_parts(resid[...])
     pack_out[2] = (unit * vectors[0:1, :] + vectors[1:2, :]).astype(BF16)
-    same = (segment_column[...] == segment_row[...]).astype(F32)
-    in_first, in_last = edge_masks(segment_column[...])
+    segment_column = column_of(segment_row)
+    same = (segment_column == segment_row[...]).astype(F32)
+    in_first, in_last = edge_masks(segment_column)
     totals = combine_edges((recv_one, recv_two, recv_three), coefficients)
     back_totals = combine_edges((back_one, back_two, back_three), coefficients)
     rows = resid.shape[0]
@@ -519,7 +533,7 @@
         else:
             pack_out[slot // 2] = stacked
         arrive(waits[slot])
-        part = dot_nt(stacked[:, : 3 * width], weight[slot, :, 0 : 3 * width])
+        part = dot_nt(stacked[:, : 3 * width], matrix(weight, slot, 0, 3 * width))
         normed_grad = part if normed_grad is None else normed_grad + part
     inward, gain_grad, shift_grad = norm_backward(resid[...], vectors[0:1, :], normed_grad)
     below = middle_grad[...] + inward
@@ -576,26 +590,35 @@
     out[base + 1] = sum_of(down[...], down_other[...])
 
 
-def update_hidden_kernel(layers, *refs):
-    up_pieces, down_pieces, rest = refs[:layers], refs[layers : 2 * layers], refs[2 * layers :]
-    up, up_moment, down, down_moment, up_out, up_moment_out, up_copy, down_out, down_moment_out, down_copy = rest
-    width = up_pieces[0].shape[2] // 2
-    scale = MUON_RATE * (up.shape[2] // width) ** 0.5
-    for old, moment, pieces, out, moment_out, copy in (
-        (up, up_moment, up_pieces, up_out, up_moment_out, up_copy),
-        (down, down_moment, down_pieces, down_out, down_moment_out, down_copy),
-    ):
-        for layer in range(layers):
-            for block in range(4):
-                lanes = lanes_of(block, width)
-                both = pieces[layer][block].astype(F32)
-                moment_out[layer, :, lanes] = MOMENTUM_DECAY * moment[layer, :, lanes] + both[:, :width]
-                master = old[layer, :, lanes] * (1.0 - MUON_RATE * WEIGHT_DECAY) - scale * both[:, width:]
-                out[layer, :, lanes] = master
-                copy[layer, :, lanes] = master.astype(BF16)
-
-
-def ortho_kernel(place, terms, moment, result, whole):
+def update_kernel(ratio, items, aliased, pieces, *refs):
+    width = pieces.shape[2] // 2
+    scale = MUON_RATE * ratio**0.5
+    olds, news = refs[: 2 * len(items)], refs[2 * len(items) + aliased :]
+    for position, (name, base) in enumerate(items):
+        old, moment = olds[2 * position : 2 * position + 2]
+        new, new_moment, copy = news[3 * position : 3 * position + 3]
+        rows = old.shape[2] if name == "out" else old.shape[1]
+        for block in range({"query_key": 2, "value": 1, "out": 1}.get(name, 4)):
+            both = pieces[base + block, 0:rows].astype(F32)
+            if name == "out":
+                both = both.T
+                grad, ortho = both[:width], both[width:]
+            else:
+                grad, ortho = both[:, :width], both[:, width:]
+            if name == "query_key":
+                place = (0, slice(None), block)
+            elif name in ("value", "out"):
+                place = (0,)
+            else:
+                place = (0, slice(None), lanes_of(block, width))
+            new_moment[place] = MOMENTUM_DECAY * moment[place] + grad
+            master = old[place] * (1.0 - MUON_RATE * WEIGHT_DECAY) - scale * ortho
+            new[place] = master
+            copy[place] = master.astype(BF16)
+
+
+def ortho_kernel(place, terms, moment, *rest):
+    extra, (result, whole) = rest[:-2], rest[-2:]
     pieces, size, _ = moment.shape
     width = whole.shape[1]
     eye = (iota((width, width), 0) == iota((width, width), 1)).astype(F32)
@@ -621,7 +644,14 @@
     ortho = dot_tn(source.astype(BF16), (chain / norm).astype(BF16))
     for which, value in ((0, grad.T), (1, ortho)):
         for piece in range(pieces):
-            result[piece, :, lanes_of(which, width)] = value[piece * size : (piece + 1) * size].astype(BF16)
+            result[piece, 0:size, lanes_of(which, width)] = value[piece * size : (piece + 1) * size].astype(BF16)
+    for rows in extra:
+        half = rows.shape[1] // 2
+        spare = result.shape[1] - size
+        more = [rows[:, :half], rows[:, half:], jnp.zeros((spare - 2 * rows.shape[0], half), F32)]
+        more = jnp.concatenate(more, axis=0).astype(BF16)
+        for piece in range(pieces):
+            result[piece, size:, :] = more
 
 
 def vmem(count):
@@ -651,6 +681,10 @@
         cost_estimate=pl.CostEstimate(flops=int(flops), bytes_accessed=int(moved), transcendentals=0),
         compiler_params=pltpu.CompilerParams(vmem_limit_bytes=VMEM_BYTES),
     )
+
+
+def weight_scratch(width, lanes):
+    return pltpu.VMEM((4, 4, 2, width // 8, lanes), BF16)
 
 
 def flat(weight):
@@ -678,18 +712,18 @@
         "project",
         vmem(6) + anywhere(ref_count(plan)),
         outs,
-        [pltpu.VMEM((4, width, 640), BF16), pltpu.SemaphoreType.DMA((copy_count(plan),))],
+        [weight_scratch(width, 640), pltpu.SemaphoreType.DMA((copy_count(plan),))],
         2 * rows * width * width * 3 * 1.5,
         8 * width * width,
-    )(resid, vectors, tables["cosine"], tables["sine"], feature_map, tables["column"], *flat(weight))
+    )(resid, vectors, tables["cosine"], tables["sine"], feature_map, tables["row"], *flat(weight))
     return dict(zip(("phi_query", "phi_key", "value", "query", "key", "summary"), results))
 
 
 def mix_scratch(width, plans):
     return [
-        pltpu.VMEM((4, width, 256), BF16),
-        pltpu.VMEM((4, width, width), BF16),
-        pltpu.VMEM((4, width, width), BF16),
+        weight_scratch(width, 256),
+        weight_scratch(width, width),
+        weight_scratch(width, width),
         pltpu.SemaphoreType.DMA((sum(copy_count(plan) for plan in plans),)),
     ]
 
@@ -710,13 +744,13 @@
     results = call(
         partial(mix_kernel, plans),
         "mix",
-        vmem(11) + scalars() + anywhere(len(refs)),
+        vmem(10) + scalars() + anywhere(len(refs)),
         outs,
         mix_scratch(width, plans),
         2 * rows * width * width * 12,
         20 * width * width,
     )(
-        resid, vectors, bias, state["phi_query"], state["phi_key"], state["value"], tables["column"], tables["row"],
+        resid, vectors, bias, state["phi_query"], state["phi_key"], state["value"], tables["row"],
         *received, tables["shares"], *refs,
     )
     return dict(zip(("context", "inverse", "middle", "slope", "active_keep", "mix_pack", "output"), results))
@@ -747,7 +781,7 @@
         20 * width * width,
     )(
         grad, vectors, state["middle"], state["slope"], state["inverse"], state["context"], state["phi_query"],
-        tables["column"], *refs,
+        tables["row"], *refs,
     )
     names = ("upper_keep", "back_pack", "middle_grad", "numer", "denom", "back_summary", "vector_two", "bias_grad")
     return dict(zip(names, results))
@@ -765,13 +799,13 @@
     results = call(
         partial(back_project_kernel, plan),
         "back_project",
-        vmem(22) + scalars() + anywhere(ref_count(plan)),
+        vmem(21) + scalars() + anywhere(ref_count(plan)),
         outs,
-        [pltpu.VMEM((4, width, 640), BF16), pltpu.SemaphoreType.DMA((copy_count(plan),))],
+        [weight_scratch(width, 640), pltpu.SemaphoreType.DMA((copy_count(plan),))],
         2 * rows * width * width * 8,
         8 * width * width,
     )(
-        resid, vectors, tables["cosine"], tables["sine"], feature_map, tables["column"], tables["row"],
+        resid, vectors, tables["cosine"], tables["sine"], feature_map, tables["row"],
         state["phi_query"], state["phi_key"], state["value"], state["query"], state["key"], state["numer"],
         state["denom"], state["context"], state["middle_grad"], *received, *back_received, tables["shares"],
         *flat(weight),
@@ -829,22 +863,44 @@
     return swap_dp(own[1], 1), swap_head(own[3], 2)
 
 
-def orthogonalize(place, terms, moment):
+def orthogonalize(place, terms, moment, *extra):
     pieces, size, _ = moment.shape
     width = terms.shape[1]
+    spare = 32 if extra else 0
     return call(
-        partial(ortho_kernel, place), "orthogonalize", vmem(2), [shape((pieces, size, 2 * width), BF16)],
-        [pltpu.VMEM((pieces * size, width), F32)], 2 * 6 * 20 * width**3, 8 * width * pieces * size,
-    )(terms, moment)[0]
-
-
-def update_hidden(up_pieces, down_pieces, up, up_moment, down, down_moment):
-    outs = [shape(up.shape), shape(up.shape), shape(up.shape, BF16)] * 2
-    layers = up.shape[0]
-    return call(
-        partial(update_hidden_kernel, layers), "update_hidden", vmem(2 * layers + 4), outs, [], 8 * up.size,
-        26 * up.size,
-    )(*up_pieces, *down_pieces, up, up_moment, down, down_moment)
+        partial(ortho_kernel, place), "orthogonalize", vmem(2 + len(extra)),
+        [shape((pieces, size + spare, 2 * width), BF16)], [pltpu.VMEM((pieces * size, width), F32)], 1, 1,
+    )(terms, moment, *extra)[0]
+
+
+def update(ratio, pieces, items, olds, news):
+    def part_of(array, layer):
+        dims = array.shape[1:]
+        return pl.BlockSpec((1, *dims), lambda step: (layer,) + (0,) * len(dims))
+
+    in_specs, operands, out_specs, outs, before = vmem(1), [pieces], [], [], []
+    for name, layer, _ in items:
+        for array in olds[name]:
+            in_specs.append(part_of(array, layer))
+            operands.append(array)
+    for name, layer, _ in items:
+        for position, like in enumerate((olds[name][0], olds[name][0], olds[name][0])):
+            if name in news:
+                before.append((news[name][position], len(outs)))
+            outs.append(shape(like.shape, BF16 if position == 2 else F32))
+            out_specs.append(part_of(like, layer))
+    aliases = {len(operands) + position: out for position, (_, out) in enumerate(before)}
+    results = pl.pallas_call(
+        partial(update_kernel, ratio, [(name, base) for name, _, base in items], len(before)),
+        name="update",
+        grid=(1,),
+        out_shape=outs,
+        in_specs=in_specs + anywhere(len(before)),
+        out_specs=out_specs,
+        input_output_aliases=aliases,
+        compiler_params=pltpu.CompilerParams(vmem_limit_bytes=VMEM_BYTES),
+    )(*operands, *(array for array, _ in before))
+    return {name: results[3 * place : 3 * place + 3] for place, (name, _, _) in enumerate(items)}
 
 
 def doc_tables(segment_row, rows):
@@ -863,8 +919,7 @@
     return {
         "cosine": jnp.cos(angles) * scale,
         "sine": jnp.sin(angles) * scale,
-        "column": own[:, None],
-        "row": own[None, :],
+        "row": own[None, :].astype(F32),
         "shares": shares,
     }
 
@@ -917,32 +972,21 @@
 
 
 def line_parts(line, cuts):
-    return [line[:, :, first:last].reshape(-1, last - first) for first, last in cuts]
+    return [line[:, :, first:last] for first, last in cuts]
 
 
 def core_vectors(vector_grads, bias_grads):
     vectors = jnp.concatenate(vector_grads)
     biases = jnp.stack(bias_grads)
-    keep, send = biases[:, 0::2], biases[:, 1::2]
-    size = vectors.shape[0]
-    sent = swap_head(jnp.concatenate([vectors, send.reshape(-1, vectors.shape[1])]), 1)
-    biases = keep + sent[size:].reshape(keep.shape)
-    return jnp.concatenate([vectors + sent[:size], biases[:, 1]]), biases[:, 0]
-
-
-def across_vectors(packed, bias_keep):
-    size = packed.shape[0] - bias_keep.shape[0]
-    return jnp.concatenate([packed[:size], bias_keep]) + swap_head(packed, 2)
-
-
-def hold_weight(weight, *values):
-    arrays, *values = hold([run[0] for run in weight], *values)
-    return [(items, *run[1:]) for items, run in zip(arrays, weight)], *values
-
-
-def hold_runs(lines, received, *runs):
-    arrays, lines, received = hold([run[0] for run in runs], lines, received)
-    return lines, received, *[(items, *run[1:]) for items, run in zip(arrays, runs)]
+    width = vectors.shape[1]
+    keep, send = biases[:, 0::2].reshape(-1, width), biases[:, 1::2].reshape(-1, width)
+    return jnp.concatenate([vectors, keep]), jnp.concatenate([vectors, send])
+
+
+def across_vectors(total, layers):
+    size = total.shape[0] - 2 * layers
+    vectors, biases = total[:size], total[size:]
+    return jnp.concatenate([vectors, biases[0::2]]), jnp.concatenate([vectors, biases[1::2]])
 
 
 def per_device(
@@ -974,9 +1018,7 @@
     dp_size = lax.axis_size("dp")
     dp_index = lax.axis_index("dp")
     quick = dp_size == 8 and layers == 2
-    masters = (w_query_key, w_value, w_out, w_up, w_down)
     moments = (moment_query_key, moment_value, moment_out, moment_up, moment_down)
-    muon_scale = (w_value.shape[1] * dp_size / block) ** 0.5
 
     def attend_of(layer):
         return attend_shard(w_query_key[layer], w_value[layer], w_out[layer])
@@ -1017,36 +1059,40 @@
     if quick:
         half = width // 2
         first = attend_of(0)
-        hidden = hidden_of(0)
-        second = jnp.concatenate([attend_of(1), hidden_of(1)], axis=1)
+        hidden, second_attend, second_hidden = (
+            four_times(part) for part in (hidden_of(0), attend_of(1), hidden_of(1))
+        )
         line = [first] + [swap_dp(first, offset) for offset in (2, 4, 6)]
 
         line, hidden = hold(line, hidden)
-        up_line, down_line = (jnp.concatenate([item[:, cut] for item in line]) for cut in (slice(half), slice(half, width)))
+        up_line, down_line = (jnp.stack([item[:, cut] for item in line]) for cut in (slice(half), slice(half, width)))
         up_y, down_x = swap_dp(up_line, 1), swap_head(down_line, 2)
-        hidden_line = gather_line(hidden)
+        hidden_line = swap_line(hidden)
 
         up_line, down_line, up_y, down_x = hold(up_line, down_line, up_y, down_x)
-        up, down = jnp.concatenate([up_line, up_y]), jnp.concatenate([down_line, down_x])
+        up, down = jnp.stack([up_line, up_y]), jnp.stack([down_line, down_x])
         up_other, down_other = swap_head(up, 2), swap_dp(down, 1)
 
-        up, down, up_other, down_other, resid, tables, biases = hold(
-            up, down, up_other, down_other, resid, tables, biases
+        up, down, up_other, down_other, resid, tables, biases, second_attend = hold(
+            up, down, up_other, down_other, resid, tables, biases, second_attend
         )
         cores = swap_all([up, up_other, down, down_other], swap_head, 1)
+        cores, hidden_line, second_attend = hold(cores, hidden_line, second_attend)
         weight_one = [
             ((up, cores[0], up_other, cores[1]), "up near", 0, 0, half),
             ((down, cores[2], down_other, cores[3]), "down near", 0, half, half),
         ]
-        weight_one, hidden_line, second = hold_weight(weight_one, hidden_line, second)
         up_line, down_line = line_parts(hidden_line, ((0, width), (width, 2 * width)))
         up_y, down_x = swap_dp(up_line, 1), swap_head(down_line, 2)
-        second_line = gather_line(second)
+        attend_line = swap_line(second_attend)
         run_project(0, resid, weight_one)
         near = swap_head(states[0]["summary"], 1)
 
-        up_line, down_line, up_y, down_x, near, moments = hold(up_line, down_line, up_y, down_x, near, moments)
-        up, down = jnp.concatenate([up_line, up_y]), jnp.concatenate([down_line, down_x])
+        up_line, down_line, up_y, down_x, near, attend_line, second_hidden, moments, gradient = hold(
+            up_line, down_line, up_y, down_x, near, attend_line, second_hidden, moments, gradient
+        )
+        second_line = swap_line(second_hidden)
+        up, down = jnp.stack([up_line, up_y]), jnp.stack([down_line, down_x])
         up_other, down_other = swap_head(up, 2), swap_dp(down, 1)
         both = cross_edges(states[0]["summary"], near)
         cores = swap_all([up, down], swap_head, 1)
@@ -1068,6 +1114,10 @@
             cores, up_other, down_other, (near, *both), payload, payload_late, second_line, branch_other
         )
         cores += swap_all([up_other, down_other], swap_head, 1)
+        lines = line_parts(attend_line, ((0, half), (half, width)))
+        lines += line_parts(second_line, ((0, width), (width, 2 * width)))
+
+        lines, received, cores = hold(lines, received, cores)
         weights = [
             (
                 weight_one,
@@ -1075,33 +1125,29 @@
                 [((down, cores[1], down_other, cores[3]), "down", 0, 0, width)],
             )
         ]
-        cuts = ((0, half), (half, width), (width, 2 * width), (2 * width, 3 * width))
-        lines = line_parts(second_line, cuts)
-
-        lines, received, weights[0][1][0], weights[0][2][0] = hold_runs(
-            lines, received, weights[0][1][0], weights[0][2][0]
-        )
         crossed = [swap_dp(lines[0], 1), swap_head(lines[1], 2), swap_dp(lines[2], 1), swap_head(lines[3], 2)]
         resid = run_mix(0, received, weights[0])
 
         lines, crossed, resid = hold(lines, crossed, resid)
-        up, down, up_late, down_late = (jnp.concatenate(pair) for pair in zip(lines, crossed))
+        up, down, up_late, down_late = (jnp.stack(pair) for pair in zip(lines, crossed))
         up_other, down_other = swap_head(up, 2), swap_dp(down, 1)
         up_late_other, down_late_other = swap_head(up_late, 2), swap_dp(down_late, 1)
 
         up, down, up_other, down_other = hold(up, down, up_other, down_other)
         cores = swap_all([up, down, up_other, down_other], swap_head, 1)
+        late_cores = swap_all([up_late, down_late], swap_head, 1)
+        cores, late_cores, resid = hold(cores, late_cores, resid)
         weight_one = [
             ((up, cores[0], up_other, cores[2]), "up", 0, 0, half),
             ((down, cores[1], down_other, cores[3]), "down", 0, half, half),
         ]
         run_project(1, resid, weight_one)
-        late_cores = swap_all([up_late, down_late], swap_head, 1)
-        near = swap_head(states[1]["summary"], 1)
-
-        both = cross_edges(states[1]["summary"], near)
-        received, late_cores, up_late_other, down_late_other, payload = hold(
-            (near, *both), late_cores, up_late_other, down_late_other, payload
+
+        summary = states[1]["summary"]
+        near = swap_head(summary, 1)
+        both = cross_edges(summary, near)
+        received, up_late_other, down_late_other, payload = hold(
+            (near, *both), up_late_other, down_late_other, payload
         )
         late_cores += swap_all([up_late_other, down_late_other], swap_head, 1)
         weights.append(
@@ -1164,59 +1210,64 @@
 
         down_others, stack_pack, pair_one = hold(down_others, states[0]["stack_pack"], pair_one)
         stack_other = swap_head(stack_pack, 1)
+        vector_grads = [(state["vector_one"] + state["vector_two"])[:5] for state in states]
+        kept, sent = core_vectors(vector_grads, [state["bias_grad"] for state in states])
+        came = swap_head(sent, 1)
         up_zero = up_grad(quick, states[0], back_other, mix_other)
         down_zero = merge_first(down_zero, down_others)
-        up_zero, down_zero, stack_other = hold(up_zero, down_zero, stack_other)
+        up_zero, down_zero, stack_other, one, one_others, came = hold(
+            up_zero, down_zero, stack_other, attend_one, attend_others, came
+        )
         down_others = send_second(down_zero)
         up_others = send_first(up_zero)
-        attend_blocks = merge_second(attend_one, attend_others)
+        attend_blocks = merge_second(one, one_others)
+        kept, sent = across_vectors(kept + came, layers)
+        came = swap_head(sent, 2)
         attend_zero = attend_grad(quick, states[0], stack_other, back_other)
 
-        attend_zero, down_others = hold(attend_zero, down_others)
+        attend_zero, down_others, came = hold(attend_zero, down_others, came)
         attend_others = send_first(attend_zero)
-        pair_two = merge_second(down_zero, down_others, attend_blocks)
-        pair_two, pair_one = hold(pair_two, pair_one)
-        pair_two = swap_line(pair_two)
-        back_one = orthogonalize(0, pair_one, moment)
+        pair_two = swap_line(merge_second(down_zero, down_others, attend_blocks))
+        back_one = orthogonalize(0, pair_one, moment, kept + came)
 
         up_others, back_one = hold(up_others, back_one)
         up_zero = merge_first(up_zero, up_others)
+        up_kept = up_zero[0], up_zero[2]
         up_others = send_second(up_zero)
-        vector_grads = [(state["vector_one"] + state["vector_two"])[:5] for state in states]
-        vector_pack, bias_keep = core_vectors(vector_grads, [state["bias_grad"] for state in states])
-
-        attend_others, vector_pack = hold(attend_others, vector_pack)
+
+        attend_others, pair_two, back_one, up_kept = hold(attend_others, pair_two, back_one, up_kept)
         attend_zero = merge_first(attend_zero, attend_others)
+        attend_kept = attend_zero[0], attend_zero[2]
         attend_others = send_second(attend_zero)
-        packed = across_vectors(vector_pack, bias_keep)
-
-        up_others, packed, pair_two = hold(up_others, packed, pair_two)
         pieces_one = swap_owners(back_one)
-        up_blocks = merge_second(up_zero, up_others)
-        packed = packed + swap_dp(packed, 1)
-
-        attend_others, up_blocks, pieces_one = hold(attend_others, up_blocks, pieces_one)
-        pair_three = merge_second(attend_zero, attend_others, up_blocks)
-        pair_three, pair_two = hold(pair_three, pair_two)
+        back_two = orthogonalize(1, pair_two, moment)
+
+        attend_others, up_others, back_two = hold(attend_others, up_others, back_two)
+        up_blocks = merge_second((up_kept[0], None, up_kept[1]), up_others)
+        pair_three = merge_second((attend_kept[0], None, attend_kept[1]), attend_others, up_blocks)
+        pair_three, pieces_one = hold(pair_three, pieces_one)
         pair_three = swap_line(pair_three)
-        back_two = orthogonalize(1, pair_two, moment)
-
-        pair_three, back_two, packed = hold(pair_three, back_two, packed)
+
+        pair_three, back_two = hold(pair_three, back_two)
         pieces_two = swap_owners(back_two)
         back_three = orthogonalize(0, pair_three, moment_late)
 
-        pieces_two, back_three, packed = hold(pieces_two, back_three, packed)
+        pieces_two, back_three = hold(pieces_two, back_three)
         pieces_three = swap_owners(back_three)
-        for offset in (2, 4):
-            packed = packed + swap_dp(packed, offset)
-        hidden_pieces = (pieces_three[:4], pieces_one[4:]), (pieces_two[4:], pieces_one[:4])
-        attend_pieces = pieces_three[4:], pieces_two[:4]
+        packed = jnp.sum(pieces_one[:, moments[1].shape[1] :].astype(F32), axis=0)
+        packed = packed[: 2 * kept.shape[0]]
+        packed = jnp.concatenate([packed[: kept.shape[0]], packed[kept.shape[0] :]], axis=1)
+        plan = [
+            (pieces_one, [("up", 1, 4), ("down", 1, 0)]),
+            (pieces_two, [("down", 0, 4), ("query_key", 1, 0), ("value", 1, 2), ("out", 1, 3)]),
+            (pieces_three, [("up", 0, 0), ("query_key", 0, 4), ("value", 0, 6), ("out", 0, 7)]),
+        ]
     else:
         weights = []
         for layer in range(layers):
             parts = []
             for part in (attend_of(layer), w_up[layer].astype(BF16), w_down[layer].T.astype(BF16)):
-                whole = lax.all_gather(part, "dp", axis=0, tiled=True)
+                whole = lax.all_gather(part, "dp", axis=0, tiled=True).reshape(4, 2, width // 8, -1)
                 parts.append([([whole] + other_slots(whole), "whole", 0, 0, width)])
             weights.append(tuple(parts))
         for layer in range(layers):
@@ -1256,41 +1307,37 @@
         back = lax.all_to_all(back, "dp", split_axis=2, concat_axis=0, tiled=True)
         back = jnp.concatenate([back[:, 0], back[:, 1]], axis=2)
         ordered = [back[12 * place : 12 * (place + 1)] for place in reversed(range(layers))]
-        attend_pieces = [part[:4] for part in ordered]
-        hidden_pieces = [part[4:8] for part in ordered], [part[8:] for part in ordered]
+        plan = [
+            (part, [("query_key", layer, 0), ("value", layer, 2), ("out", layer, 3), ("up", layer, 4), ("down", layer, 8)])
+            for layer, part in enumerate(ordered)
+        ]
         vector_grads = [(state["vector_one"] + state["vector_two"])[:5] for state in states]
-        packed = across_vectors(*core_vectors(vector_grads, [state["bias_grad"] for state in states]))
-        packed = lax.psum(packed, "dp")
+        kept, sent = core_vectors(vector_grads, [state["bias_grad"] for state in states])
+        kept, sent = across_vectors(kept + swap_head(sent, 1), layers)
+        packed = lax.psum(kept + swap_head(sent, 2), "dp")
 
     vector_total, bias_total = packed[: 5 * layers].reshape(vectors.shape), packed[5 * layers :]
-    turned = [jnp.transpose(item, (0, 2, 1)) for item in (w_down, moment_down)]
-    updated = list(update_hidden(*hidden_pieces, w_up, moment_up, *turned))
-    updated[3:] = [jnp.transpose(item, (0, 2, 1)) for item in updated[3:]]
-    fresh = []
-    for which in range(2):
-        parts = [pieces[:, :, lanes_of(which, block)].astype(F32) for pieces in attend_pieces]
-        fresh.append(
-            (
-                jnp.stack([jnp.stack([part[0], part[1]], axis=1) for part in parts]),
-                jnp.stack([part[2] for part in parts]),
-                jnp.stack([part[3].T for part in parts]),
-            )
-        )
-    next_moments = tuple(MOMENTUM_DECAY * old + grad for old, grad in zip(moments, fresh[0]))
-    next_masters = tuple(
-        master * (1.0 - MUON_RATE * WEIGHT_DECAY) - MUON_RATE * muon_scale * ortho
-        for master, ortho in zip(masters, fresh[1])
-    )
-    copies = tuple(master.astype(BF16) for master in next_masters)
+    olds = {
+        "query_key": (w_query_key, moment_query_key),
+        "value": (w_value, moment_value),
+        "out": (w_out, moment_out),
+        "up": (w_up, moment_up),
+        "down": tuple(jnp.transpose(item, (0, 2, 1)) for item in (w_down, moment_down)),
+    }
+    news = {}
+    for pieces, items in plan:
+        news.update(update(width // block, pieces, items, olds, news))
+    news["down"] = [jnp.transpose(item, (0, 2, 1)) for item in news["down"]]
+    next_masters, next_moments, copies = zip(*(news[name] for name in ("query_key", "value", "out", "up", "down")))
     vectors_next, vector_first_next, vector_second_next = adam_update(
         vectors, vector_total, vector_first, vector_second
     )
     bias_next, bias_first_next, bias_second_next = adam_update(bias_up, bias_total, bias_first, bias_second)
     return (
         (activations.astype(BF16), gradient)
-        + (*next_masters, updated[0], updated[3])
-        + (*next_moments, updated[1], updated[4])
-        + (*copies, updated[2], updated[5])
+        + next_masters
+        + next_moments
+        + copies
         + (vectors_next, vector_first_next, vector_second_next, bias_next, bias_first_next, bias_second_next)
     )
 

time: 553 us -> 530 us (0.958)
  blocking collectives: 0 us -> 31.3 us
  local copies, waits for them, and re-layouts: 61 us -> 34.4 us
  waiting for transfers between devices: 147 us -> 126 us
    all_to_all x5, waiting for transfers between devices: 36.8 us -> 0.78 us  [swap_line(): lax.all_to_all(parts, 'dp', split_axis=0, concat_axis=0, axis_index_group...]
    all_to_all x0 -> x1, blocking collectives: none -> 31.3 us  [swap_line(): lax.all_to_all(parts, 'dp', split_axis=0, concat_axis=0, axis_index_group...]
    unnamed x259 -> x218, local copies, waits for them, and re-layouts: 28.3 us -> 19 us
    ppermute x60, waiting for transfers between devices: 46.9 us -> 55.1 us  [swap_head(): lax.ppermute(values, 'head', [(h, h ^ offset) for h in range(lax.axis_siz...]
    all_to_all x5, waiting for transfers between devices: 5.24 us -> 12.7 us  [swap_owners(): return lax.all_to_all(parts, 'dp', split_axis=0, concat_axis=0, tiled=True)]
    ppermute x26 -> x23, starting transfers between devices: 33.8 us -> 27.7 us  [swap_dp(): lax.ppermute(values, 'dp', [(d, d ^ offset) for d in range(lax.axis_size(...]
    pallas_call x8 -> x10, Pallas kernels: 90.5 us -> 92.9 us  [the longest x2 29.1 us: back_project(): call(partial(back_project_kernel, plan), 'back_project', vmem(21) + scala...]
    ppermute x26 -> x23, waiting for transfers between devices: 58.1 us -> 57.4 us  [swap_dp(): lax.ppermute(values, 'dp', [(d, d ^ offset) for d in range(lax.axis_size(...]
  transfers between devices with their start and end apart: 96 -> 93, of which waited for: 39 -> 42; matrix products, arithmetic and copies ran while one was open for 11% -> 8% of each run, Pallas kernels for 34% -> 36%
where the time goes in v3:
time: 530 us; the launch traced here: 520 us
  Pallas kernels  199 us (38%)
  waiting for transfers between devices  126 us (24%)
  starting transfers between devices  109 us (21%)
  local copies, waits for them, and re-layouts  34.4 us (6%)
  blocking collectives  31.3 us (6%)
  other arithmetic  17.4 us (3%)
    ppermute x23, waiting for transfers between devices, swap_dp(): lax.ppermute(values, 'dp', [(d, d ^ offset) for d in range(lax.axis_size(...  57.4 us
    ppermute x60, waiting for transfers between devices, swap_head(): lax.ppermute(values, 'head', [(h, h ^ offset) for h in range(lax.axis_siz...  55.1 us
    ppermute x60, starting transfers between devices, swap_head(): lax.ppermute(values, 'head', [(h, h ^ offset) for h in range(lax.axis_siz...  36.7 us
    pallas_call x6, Pallas kernels, matrix_grad(): call(partial(grad_kernel, quick, splits), 'matrix_grad', vmem(2 + len(lef...  32.1 us
    all_to_all x1, blocking collectives, swap_line(): lax.all_to_all(parts, 'dp', split_axis=0, concat_axis=0, axis_index_group...  31.3 us
    pallas_call x12, Pallas kernels, merge(): return call(kernel, 'merge', vmem(len(operands)), outs, [], 1, 1)(*operands)  30.9 us
    pallas_call x2, Pallas kernels, back_project(): call(partial(back_project_kernel, plan), 'back_project', vmem(21) + scala...  29.1 us
    pallas_call x3, Pallas kernels, orthogonalize(): call(partial(ortho_kernel, place), 'orthogonalize', vmem(2 + len(extra)),...  28.8 us
  transfers between devices with their start and end apart: 93, of which 42 were waited for; matrix products, arithmetic and copies ran while one was open for 8% of the time, Pallas kernels for 36%

profile of v3, /device:TPU:0, one launch (start us, length us, event | category | flops | bytes accessed | tf_op | source)
XLA Modules:
  0.0 520.1 jit_solution(4223717455533214679)
XLA Ops:
  0.7 3.0 collective-permute-start.8
  7.1 3.7 collective-permute-start.2
  18.9 5.0 collective-permute-done.1
  25.0 3.8 all-to-all-start
  32.8 4.6 collective-permute-done.3
  40.8 11.7 %collective-permute-done.6.rest_6_ = bf16[2,4,96,384]{3,2,1,0:T(8,128)(2,1)S(1)} collective-permute-done((bf16[2,4,96,384]{3,2,1,0:T(8,128)(2,1)S(1)}, bf16[2,4,96,384]{3,2,1,0:T(8,128)(2,1)S(1)}, u32[]{:S(2)}, u32[]{:S(2)}) %collective-permute-start.6) | collective-permute-done | bytes 589856 | tf_op jit(solution)/shard_map/ppermute | solution.py:61
  59.2 4.4 all-to-all-start.1
  67.2 8.9 %project.2 = (bf16[256,384]{1,0:T(8,128)(2,1)}, bf16[256,384]{1,0:T(8,128)(2,1)}, bf16[256,768]{1,0:T(8,128)(2,1)}, f32[256,768]{1,0:T(8,128)}, f32[256,768]{1,0:T(8,128)}, /*index=5*/bf16[400,128]{1,0:T(8,128)(2,1)}) custom-call(f32[256,768]{1,0:T(8,128)} %convert_element_type.65.resid, f32[5,768]{1,0:T(8,128)} %get-tuple-element.770.vectors, ...), custom_call_target="tpu_custom_call" | custom-call | flops 1358954496 | bytes 4718592 | tf_op jit(solution)/shard_map/project/pallas_call | solution.py:710
  85.0 5.2 %all-to-all-start.2 = ((bf16[4,96,1536]{2,1,0:T(8,128)(2,1)}), bf16[4,96,1536]{2,1,0:T(8,128)(2,1)}, u32[]{:S(2)}, u32[]{:S(2)}) async-start(bf16[4,96,1536]{2,1,0:T(8,128)(2,1)} %broadcast_in_dim.8), calls=%async_computation.2 | async-start | bytes 2359296 | tf_op jit(solution)/shard_map/all_to_all | solution.py:70
  100.2 14.5 %collective-permute-done.22.recv_three = bf16[400,128]{1,0:T(8,128)(2,1)} collective-permute-done((bf16[400,128]{1,0:T(8,128)(2,1)}, bf16[400,128]{1,0:T(8,128)(2,1)}, u32[]{:S(2)}, u32[]{:S(2)}) %collective-permute-start.22) | collective-permute-done | bytes 102432 | tf_op jit(solution)/shard_map/ppermute | solution.py:57
  128.8 13.1 %mix.2 = (f32[256,768]{1,0:T(8,128)}, f32[256,768]{1,0:T(8,128)}, f32[256,768]{1,0:T(8,128)}, bf16[4,256,768]{2,1,0:T(8,128)(2,1)}, bf16[2,256,768]{2,1,0:T(8,12...) custom-call(f32[256,768]{1,0:T(8,128)} %convert_element_type.65.resid, f32[5,768]{1,0:T(8,128)} %get-tuple-element.770.vectors, ...), custom_call_target="tpu_custom_call" | custom-call | flops 3623878656 | bytes 11796480 | tf_op jit(solution)/shard_map/mix/pallas_call | solution.py:744
  141.9 4.7 collective-permute-done.26
  150.3 11.4 %collective-permute-done.31.rest_6_ = bf16[2,4,96,384]{3,2,1,0:T(8,128)(2,1)} collective-permute-done((bf16[2,4,96,384]{3,2,1,0:T(8,128)(2,1)S(1)}, bf16[2,4,96,384]{3,2,1,0:T(8,128)(2,1)}, u32[]{:S(2)}, u32[]{:S(2)}) %collective-permute-start.31) | collective-permute-done | bytes 589856 | tf_op jit(solution)/shard_map/ppermute | solution.py:61
  169.2 8.4 %project.3 = (bf16[256,384]{1,0:T(8,128)(2,1)}, bf16[256,384]{1,0:T(8,128)(2,1)}, bf16[256,768]{1,0:T(8,128)(2,1)}, f32[256,768]{1,0:T(8,128)}, f32[256,768]{1,0:T(8,128)}, /*index=5*/bf16[400,128]{1,0:T(8,128)(2,1)}) custom-call(f32[256,768]{1,0:T(8,128)} %get-tuple-element.425.resid, f32[5,768]{1,0:T(8,128)} %get-tuple-element.769.vectors, ...), custom_call_target="tpu_custom_call" | custom-call | flops 1358954496 | bytes 4718592 | tf_op jit(solution)/shard_map/project/pallas_call | solution.py:710
  180.6 10.9 %collective-permute-done.42.rest_14_ = bf16[2,4,96,768]{3,2,1,0:T(8,128)(2,1)} collective-permute-done((bf16[2,4,96,768]{3,2,1,0:T(8,128)(2,1)S(1)}, bf16[2,4,96,768]{3,2,1,0:T(8,128)(2,1)}, u32[]{:S(2)}, u32[]{:S(2)}) %collective-permute-start.42) | collective-permute-done | bytes 1179680 | tf_op jit(solution)/shard_map/ppermute | solution.py:61
  196.6 4.9 all-to-all-start.3
  203.0 12.6 %mix.3 = (f32[256,768]{1,0:T(8,128)}, f32[256,768]{1,0:T(8,128)}, f32[256,768]{1,0:T(8,128)}, bf16[4,256,768]{2,1,0:T(8,128)(2,1)}, bf16[2,256,768]{2,1,0:T(8,12...) custom-call(f32[256,768]{1,0:T(8,128)} %get-tuple-element.425.resid, f32[5,768]{1,0:T(8,128)} %get-tuple-element.769.vectors, ...), custom_call_target="tpu_custom_call" | custom-call | flops 3623878656 | bytes 11796480 | tf_op jit(solution)/shard_map/mix/pallas_call | solution.py:744
  217.6 3.1 collective-permute-done.45.right_other.rest_1_
  221.7 4.4 matrix_grad.6
  229.0 13.0 %back_mix.2 = (bf16[2,256,768]{2,1,0:T(8,128)(2,1)}, bf16[3,256,768]{2,1,0:T(8,128)(2,1)}, f32[256,768]{1,0:T(8,128)}, bf16[256,768]{1,0:T(8,128)(2,1)}, bf16[25...) custom-call(f32[256,768]{1,0:T(8,128)} %convert_multiply_fusion.grad, ...), custom_call_target="tpu_custom_call" | custom-call | flops 3321888768 | bytes 11796480 | tf_op jit(solution)/shard_map/back_mix/pallas_call | solution.py:774
  250.5 4.9 matrix_grad.7
  255.4 4.4 collective-permute-done.50.back_two
  262.8 4.1 all-to-all-start.4
  266.9 13.7 %back_project.2 = (bf16[2,256,768]{2,1,0:T(8,128)(2,1)}, bf16[4,256,768]{2,1,0:T(8,128)(2,1)}, f32[256,768]{1,0:T(8,128)}, f32[8,768]{1,0:T(8,128)}) custom-call(f32[256,768]{1,0:T(8,128)} %get-tuple-element.425.resid, f32[5,768]{1,0:T(8,128)} %get-tuple-element.769.vectors, f32[256,32]{1,0:T(8,128)} %get-tuple-element.365.cosine_part, ...), custom_call_target="tpu_custom_call" | custom-call | flops 2415919104 | bytes 4718592 | tf_op jit(solution)/shard_map/back_project/pallas_call | solution.py:799
  289.6 6.3 %matrix_grad.8 = (bf16[2,192,768]{2,1,0:T(8,128)(2,1)}, bf16[2,192,768]{2,1,0:T(8,128)(2,1)}, bf16[2,192,768]{2,1,0:T(8,128)(2,1)}, bf16[2,192,768]{2,1,0:T(8,128)(2,1)}) custom-call(bf16[2,256,768]{2,1,0:T(8,128)(2,1)} %get-tuple-element.492.right_own, bf16[4,256,768]{2,1,0:T(8,128)(2,1)} %copy-done.4, bf16[4,256,768]{2,1,0:T(8,128)(2,1)} %get-tuple-element.499.rest_0_, ...), custom_call_target="tpu_custom_call" | custom-call | flops 1207959552 | bytes 4718592 | tf_op jit(solution)/shard_map/matrix_grad/pallas_call | solution.py:819
  298.9 13.2 %back_mix.3 = (bf16[2,256,768]{2,1,0:T(8,128)(2,1)}, bf16[3,256,768]{2,1,0:T(8,128)(2,1)}, f32[256,768]{1,0:T(8,128)}, bf16[256,768]{1,0:T(8,128)(2,1)}, bf16[25...) custom-call(f32[256,768]{1,0:T(8,128)} %get-tuple-element.517.grad, ...), custom_call_target="tpu_custom_call" | custom-call | flops 3321888768 | bytes 11796480 | tf_op jit(solution)/shard_map/back_mix/pallas_call | solution.py:774
  317.6 4.5 all-to-all-start.5
  322.2 2.7 merge.14
  328.9 5.2 matrix_grad.9
  334.0 4.5 collective-permute-done.64.back_two
  341.4 15.5 %back_project.3 = (bf16[2,256,768]{2,1,0:T(8,128)(2,1)}, bf16[4,256,768]{2,1,0:T(8,128)(2,1)}, f32[256,768]{1,0:T(8,128)}, f32[8,768]{1,0:T(8,128)}) custom-call(f32[256,768]{1,0:T(8,128)} %convert_element_type.65.resid, f32[5,768]{1,0:T(8,128)} %get-tuple-element.770.vectors, f32[256,32]{1,0:T(8,128)} %get-tuple-element.365.cosine_part, ...), custom_call_target="tpu_custom_call" | custom-call | flops 2415919104 | bytes 4718592 | tf_op jit(solution)/shard_map/back_project/pallas_call | solution.py:799
  359.3 5.1 matrix_grad.10
  370.7 6.2 %matrix_grad.11 = (bf16[2,192,768]{2,1,0:T(8,128)(2,1)}, bf16[2,192,768]{2,1,0:T(8,128)(2,1)}, bf16[2,192,768]{2,1,0:T(8,128)(2,1)}, bf16[2,192,768]{2,1,0:T(8,128)(2,1)}) custom-call(bf16[2,256,768]{2,1,0:T(8,128)(2,1)} %get-tuple-element.552.right_own, bf16[4,256,768]{2,1,0:T(8,128)(2,1)} %copy-done.17, bf16[4,256,768]{2,1,0:T(8,128)(2,1)} %get-tuple-element.578.rest_0_, ...), custom_call_target="tpu_custom_call" | custom-call | flops 1207959552 | bytes 4718592 | tf_op jit(solution)/shard_map/matrix_grad/pallas_call | solution.py:819
  382.6 5.1 all-to-all-start.6
  392.4 9.7 %orthogonalize.3 = bf16[8,128,384]{2,1,0:T(8,128)(2,1)} custom-call(bf16[4,192,768]{2,1,0:T(8,128)(2,1)} %copy-done.28, bf16[8,96,384]{2,1,0:T(8,128)(2,1)} %copy-done.21, f32[12,768]{1,0:T(8,128)} %maximum_add_fusion.1.rest_0_), custom_call_target="tpu_custom_call" | custom-call | flops 1 | bytes 1 | tf_op jit(solution)/shard_map/orthogonalize/pallas_call | solution.py:870
  408.4 6.2 %collective-permute-done.75.up_other = bf16[2,192,768]{2,1,0:T(8,128)(2,1)S(1)} collective-permute-done((bf16[2,192,768]{2,1,0:T(8,128)(2,1)}, bf16[2,192,768]{2,1,0:T(8,128)(2,1)S(1)}, u32[]{:S(2)}, u32[]{:S(2)}) %collective-permute-start.75) | collective-permute-done | bytes 589856 | tf_op jit(solution)/shard_map/ppermute | solution.py:57
  415.9 5.4 %all-to-all-start.7 = ((bf16[8,128,384]{2,1,0:T(8,128)(2,1)}), bf16[8,128,384]{2,1,0:T(8,128)(2,1)S(1)}, u32[]{:S(2)}, u32[]{:S(2)}) async-start(bf16[8,128,384]{2,1,0:T(8,128)(2,1)} %orthogonalize.3), calls=%async_computation.7 | async-start | bytes 1572864 | tf_op jit(solution)/shard_map/all_to_all | solution.py:78
  428.1 9.6 %orthogonalize.4 = bf16[8,96,384]{2,1,0:T(8,128)(2,1)} custom-call(bf16[4,192,768]{2,1,0:T(8,128)(2,1)} %copy-done.29, bf16[8,96,384]{2,1,0:T(8,128)(2,1)} %copy-done.21), custom_call_target="tpu_custom_call" | custom-call | flops 1 | bytes 1 | tf_op jit(solution)/shard_map/orthogonalize/pallas_call | solution.py:870
  438.1 4.2 collective-permute-done.79.up_other
  447.3 31.3 %all_to_all.55.terms = bf16[4,192,768]{2,1,0:T(8,128)(2,1)} all-to-all(bf16[4,192,768]{2,1,0:T(8,128)(2,1)} %merge.23), channel_id=1, replica_groups={{0,8,16,24},{4,12,20,28},{1,9,17,25},{5,13,21,29},{2,10,18,26},{6,14,22..., dimensions={0} | all-to-all | bytes 2359296 | tf_op jit(solution)/shard_map/all_to_all | solution.py:70
  478.7 3.7 all-to-all-start.9
  482.4 9.5 %orthogonalize.5 = bf16[8,96,384]{2,1,0:T(8,128)(2,1)} custom-call(bf16[4,192,768]{2,1,0:T(8,128)(2,1)} %all_to_all.55.terms, bf16[8,96,192]{2,1,0:T(8,128)(2,1)} %copy-done.36), custom_call_target="tpu_custom_call" | custom-call | flops 1 | bytes 1 | tf_op jit(solution)/shard_map/orthogonalize/pallas_call | solution.py:870
  491.9 5.1 all-to-all-done.9.pieces
  497.0 3.7 all-to-all-start.10
  503.5 2.8 update.3
  506.9 3.2 update.4
  510.2 5.7 %all-to-all-done.10.pieces = bf16[8,96,384]{2,1,0:T(8,128)(2,1)S(1)} async-done(((bf16[8,96,384]{2,1,0:T(8,128)(2,1)}), bf16[8,96,384]{2,1,0:T(8,128)(2,1)S(1)}, u32[]{:S(2)}, u32[]{:S(2)}) %all-to-all-start.10) | async-done | bytes 589856 | tf_op jit(solution)/shard_map/all_to_all | solution.py:78
  516.7 3.2 update.5
  (491 shorter events, 167.7 us)
Async XLA Ops:
  0.7 39.5 %collective-permute-start.8 = (f32[2,768]{1,0:T(2,128)}, f32[2,768]{1,0:T(2,128)S(1)}, u32[]{:S(2)}, u32[]{:S(2)}) collective-permute-start(f32[2,768]{1,0:T(2,128)} %param.27), channel_id=1, source_target_pairs={{0,2},{1,3},{2,0},{3,1},{4,6},{5,7},{6,4},{7,5},{8,10},{9,11},{10,... | collective-permute-start | bytes 18440 | tf_op jit(solution)/shard_map/ppermute | solution.py:57
  3.7 36.5 %collective-permute-start.7 = (f32[2,768]{1,0:T(2,128)}, f32[2,768]{1,0:T(2,128)S(1)}, u32[]{:S(2)}, u32[]{:S(2)}) collective-permute-start(f32[2,768]{1,0:T(2,128)} %param.27), channel_id=1, source_target_pairs={{0,1},{1,0},{2,3},{3,2},{4,5},{5,4},{6,7},{7,6},{8,9},{9,8},{10,11... | collective-permute-start | bytes 18440 | tf_op jit(solution)/shard_map/ppermute | solution.py:57
  18.8 21.4 %collective-permute-start.9 = (f32[2,768]{1,0:T(2,128)S(1)}, f32[2,768]{1,0:T(2,128)S(1)}, u32[]{:S(2)}, u32[]{:S(2)}) collective-permute-start(f32[2,768]{1,0:T(2,128)S(1)} %copy-done.91), channel_id=1, source_target_pairs={{0,3},{1,2},{2,1},{3,0},{4,7},{5,6},{6,5},{7,4},{8,11},{9,10},{10,... | collective-permute-start | bytes 18440 | tf_op jit(solution)/shard_map/ppermute | solution.py:57
  25.0 34.2 %all-to-all-start = ((bf16[4,96,1536]{2,1,0:T(8,128)(2,1)}), bf16[4,96,1536]{2,1,0:T(8,128)(2,1)S(1)}, u32[]{:S(2)}, u32[]{:S(2)}) async-start(bf16[4,96,1536]{2,1,0:T(8,128)(2,1)} %broadcast_in_dim.6), calls=%async_computation | async-start | bytes 2359296 | tf_op jit(solution)/shard_map/all_to_all | solution.py:70
  59.2 20.7 %all-to-all-start.1 = ((bf16[4,96,768]{2,1,0:T(8,128)(2,1)}), bf16[4,96,768]{2,1,0:T(8,128)(2,1)}, u32[]{:S(2)}, u32[]{:S(2)}) async-start(bf16[4,96,768]{2,1,0:T(8,128)(2,1)} %broadcast_in_dim.7), calls=%async_computation.1 | async-start | bytes 1179648 | tf_op jit(solution)/shard_map/all_to_all | solution.py:70
  63.8 15.2 %collective-permute-start.15 = (bf16[4,96,768]{2,1,0:T(8,128)(2,1)S(1)}, bf16[4,96,768]{2,1,0:T(8,128)(2,1)S(1)}, u32[]{:S(2)}, u32[]{:S(2)}) collective-permute-start(bf16[4,96,768]{2,1,0:T(8,128)(2,1)S(1)} %get-tuple-element.377), channel_id=1, source_target_pairs={{0,2},{1,3},{2,0},{3,1},{4,6},{5,7},{6,4},{7,5},{8,10},{9,11},{10,... | collective-permute-start | bytes 1769480 | tf_op jit(solution)/shard_map/ppermute | solution.py:57
  64.4 14.8 %collective-permute-start.14 = (bf16[4,96,768]{2,1,0:T(8,128)(2,1)S(1)}, bf16[4,96,768]{2,1,0:T(8,128)(2,1)S(1)}, u32[]{:S(2)}, u32[]{:S(2)}) collective-permute-start(bf16[4,96,768]{2,1,0:T(8,128)(2,1)S(1)} %get-tuple-element.375), channel_id=1, source_target_pairs={{0,4},{4,0},{8,12},{12,8},{16,20},{20,16},{24,28},{28,24},{1,5},{5... | collective-permute-start | bytes 1769480 | tf_op jit(solution)/shard_map/ppermute | solution.py:61
  76.3 20.9 %collective-permute-start.21 = (bf16[400,128]{1,0:T(8,128)(2,1)}, bf16[400,128]{1,0:T(8,128)(2,1)}, u32[]{:S(2)}, u32[]{:S(2)}) collective-permute-start(bf16[400,128]{1,0:T(8,128)(2,1)} %get-tuple-element.372), channel_id=1, source_target_pairs={{0,2},{1,3},{2,0},{3,1},{4,6},{5,7},{6,4},{7,5},{8,10},{9,11},{10,... | collective-permute-start | bytes 307208 | tf_op jit(solution)/shard_map/ppermute | solution.py:57
  82.2 37.5 %collective-permute-start.20 = (bf16[2,4,96,768]{3,2,1,0:T(8,128)(2,1)S(1)}, bf16[2,4,96,768]{3,2,1,0:T(8,128)(2,1)}, u32[]{:S(2)}, u32[]{:S(2)}) collective-permute-start(bf16[2,4,96,768]{3,2,1,0:T(8,128)(2,1)S(1)} %pad_maximum_fusion.1.rest_12_), channel_id=1, source_target_pairs={{0,4},{4,0},{8,12},{12,8},{16,20},{20,16},{24,28},{28,24},{1,5},{5... | collective-permute-start | bytes 3538952 | tf_op jit(solution)/shard_map/ppermute | solution.py:61
  83.8 35.9 %collective-permute-start.18 = (bf16[2,4,96,768]{3,2,1,0:T(8,128)(2,1)S(1)}, bf16[2,4,96,768]{3,2,1,0:T(8,128)(2,1)}, u32[]{:S(2)}, u32[]{:S(2)}) collective-permute-start(bf16[2,4,96,768]{3,2,1,0:T(8,128)(2,1)S(1)} %pad_maximum_fusion.1.rest_12_), channel_id=1, source_target_pairs={{0,1},{1,0},{2,3},{3,2},{4,5},{5,4},{6,7},{7,6},{8,9},{9,8},{10,11... | collective-permute-start | bytes 3538952 | tf_op jit(solution)/shard_map/ppermute | solution.py:57
  84.0 35.8 %collective-permute-start.19 = (bf16[2,4,96,768]{3,2,1,0:T(8,128)(2,1)S(1)}, bf16[2,4,96,768]{3,2,1,0:T(8,128)(2,1)}, u32[]{:S(2)}, u32[]{:S(2)}) collective-permute-start(bf16[2,4,96,768]{3,2,1,0:T(8,128)(2,1)S(1)} %pad_maximum_fusion.rest_8_), channel_id=1, source_target_pairs={{0,2},{1,3},{2,0},{3,1},{4,6},{5,7},{6,4},{7,5},{8,10},{9,11},{10,... | collective-permute-start | bytes 3538952 | tf_op jit(solution)/shard_map/ppermute | solution.py:57
  84.8 35.0 %collective-permute-start.17 = (bf16[2,4,96,768]{3,2,1,0:T(8,128)(2,1)S(1)}, bf16[2,4,96,768]{3,2,1,0:T(8,128)(2,1)}, u32[]{:S(2)}, u32[]{:S(2)}) collective-permute-start(bf16[2,4,96,768]{3,2,1,0:T(8,128)(2,1)S(1)} %pad_maximum_fusion.rest_8_), channel_id=1, source_target_pairs={{0,1},{1,0},{2,3},{3,2},{4,5},{5,4},{6,7},{7,6},{8,9},{9,8},{10,11... | collective-permute-start | bytes 3538952 | tf_op jit(solution)/shard_map/ppermute | solution.py:57
  85.0 34.8 %all-to-all-start.2 = ((bf16[4,96,1536]{2,1,0:T(8,128)(2,1)}), bf16[4,96,1536]{2,1,0:T(8,128)(2,1)}, u32[]{:S(2)}, u32[]{:S(2)}) async-start(bf16[4,96,1536]{2,1,0:T(8,128)(2,1)} %broadcast_in_dim.8), calls=%async_computation.2 | async-start | bytes 2359296 | tf_op jit(solution)/shard_map/all_to_all | solution.py:70
  97.2 17.5 %collective-permute-start.22 = (bf16[400,128]{1,0:T(8,128)(2,1)}, bf16[400,128]{1,0:T(8,128)(2,1)}, u32[]{:S(2)}, u32[]{:S(2)}) collective-permute-start(bf16[400,128]{1,0:T(8,128)(2,1)} %collective-permute-done.16.recv_one), channel_id=1, source_target_pairs={{0,2},{1,3},{2,0},{3,1},{4,6},{5,7},{6,4},{7,5},{8,10},{9,11},{10,... | collective-permute-start | bytes 307208 | tf_op jit(solution)/shard_map/ppermute | solution.py:57
  124.7 22.2 %collective-permute-start.28 = (bf16[4,96,768]{2,1,0:T(8,128)(2,1)S(1)}, bf16[4,96,768]{2,1,0:T(8,128)(2,1)S(1)}, u32[]{:S(2)}, u32[]{:S(2)}) collective-permute-start(bf16[4,96,768]{2,1,0:T(8,128)(2,1)S(1)} %get-tuple-element.420), channel_id=1, source_target_pairs={{0,4},{4,0},{8,12},{12,8},{16,20},{20,16},{24,28},{28,24},{1,5},{5... | collective-permute-start | bytes 1769480 | tf_op jit(solution)/shard_map/ppermute | solution.py:61
  125.2 21.6 %collective-permute-start.29 = (bf16[4,96,768]{2,1,0:T(8,128)(2,1)S(1)}, bf16[4,96,768]{2,1,0:T(8,128)(2,1)S(1)}, u32[]{:S(2)}, u32[]{:S(2)}) collective-permute-start(bf16[4,96,768]{2,1,0:T(8,128)(2,1)S(1)} %get-tuple-element.422), channel_id=1, source_target_pairs={{0,2},{1,3},{2,0},{3,1},{4,6},{5,7},{6,4},{7,5},{8,10},{9,11},{10,... | collective-permute-start | bytes 1769480 | tf_op jit(solution)/shard_map/ppermute | solution.py:57
  126.0 20.7 %collective-permute-start.26 = (bf16[4,96,384]{2,1,0:T(8,128)(2,1)S(1)}, bf16[4,96,384]{2,1,0:T(8,128)(2,1)S(1)}, u32[]{:S(2)}, u32[]{:S(2)}) collective-permute-start(bf16[4,96,384]{2,1,0:T(8,128)(2,1)S(1)} %get-tuple-element.412), channel_id=1, source_target_pairs={{0,4},{4,0},{8,12},{12,8},{16,20},{20,16},{24,28},{28,24},{1,5},{5... | collective-permute-start | bytes 884744 | tf_op jit(solution)/shard_map/ppermute | solution.py:61
  127.5 19.4 %collective-permute-start.27 = (bf16[4,96,384]{2,1,0:T(8,128)(2,1)S(1)}, bf16[4,96,384]{2,1,0:T(8,128)(2,1)S(1)}, u32[]{:S(2)}, u32[]{:S(2)}) collective-permute-start(bf16[4,96,384]{2,1,0:T(8,128)(2,1)S(1)} %get-tuple-element.414), channel_id=1, source_target_pairs={{0,2},{1,3},{2,0},{3,1},{4,6},{5,7},{6,4},{7,5},{8,10},{9,11},{10,... | collective-permute-start | bytes 884744 | tf_op jit(solution)/shard_map/ppermute | solution.py:57
  147.0 14.7 %collective-permute-start.31 = (bf16[2,4,96,384]{3,2,1,0:T(8,128)(2,1)S(1)}, bf16[2,4,96,384]{3,2,1,0:T(8,128)(2,1)}, u32[]{:S(2)}, u32[]{:S(2)}) collective-permute-start(bf16[2,4,96,384]{3,2,1,0:T(8,128)(2,1)S(1)} %pad_maximum_fusion.8.rest_4_), channel_id=1, source_target_pairs={{0,4},{4,0},{8,12},{12,8},{16,20},{20,16},{24,28},{28,24},{1,5},{5... | collective-permute-start | bytes 1769480 | tf_op jit(solution)/shard_map/ppermute | solution.py:61
  149.5 14.9 %collective-permute-start.37 = (bf16[2,4,96,768]{3,2,1,0:T(8,128)(2,1)S(1)}, bf16[2,4,96,768]{3,2,1,0:T(8,128)(2,1)S(1)}, u32[]{:S(2)}, u32[]{:S(2)}) collective-permute-start(bf16[2,4,96,768]{3,2,1,0:T(8,128)(2,1)S(1)} %pad_maximum_fusion.3.rest_12_), channel_id=1, source_target_pairs={{0,1},{1,0},{2,3},{3,2},{4,5},{5,4},{6,7},{7,6},{8,9},{9,8},{10,11... | collective-permute-start | bytes 3538952 | tf_op jit(solution)/shard_map/ppermute | solution.py:57
  149.8 14.7 %collective-permute-start.36 = (bf16[2,4,96,768]{3,2,1,0:T(8,128)(2,1)S(1)}, bf16[2,4,96,768]{3,2,1,0:T(8,128)(2,1)S(1)}, u32[]{:S(2)}, u32[]{:S(2)}) collective-permute-start(bf16[2,4,96,768]{3,2,1,0:T(8,128)(2,1)S(1)} %pad_maximum_fusion.2.rest_8_), channel_id=1, source_target_pairs={{0,1},{1,0},{2,3},{3,2},{4,5},{5,4},{6,7},{7,6},{8,9},{9,8},{10,11... | collective-permute-start | bytes 3538952 | tf_op jit(solution)/shard_map/ppermute | solution.py:57
  163.0 28.5 %collective-permute-start.42 = (bf16[2,4,96,768]{3,2,1,0:T(8,128)(2,1)S(1)}, bf16[2,4,96,768]{3,2,1,0:T(8,128)(2,1)}, u32[]{:S(2)}, u32[]{:S(2)}) collective-permute-start(bf16[2,4,96,768]{3,2,1,0:T(8,128)(2,1)S(1)} %pad_maximum_fusion.3.rest_12_), channel_id=1, source_target_pairs={{0,4},{4,0},{8,12},{12,8},{16,20},{20,16},{24,28},{28,24},{1,5},{5... | collective-permute-start | bytes 3538952 | tf_op jit(solution)/shard_map/ppermute | solution.py:61
  163.7 28.9 %collective-permute-start.41 = (bf16[2,4,96,768]{3,2,1,0:T(8,128)(2,1)S(1)}, bf16[2,4,96,768]{3,2,1,0:T(8,128)(2,1)}, u32[]{:S(2)}, u32[]{:S(2)}) collective-permute-start(bf16[2,4,96,768]{3,2,1,0:T(8,128)(2,1)S(1)} %pad_maximum_fusion.2.rest_8_), channel_id=1, source_target_pairs={{0,2},{1,3},{2,0},{3,1},{4,6},{5,7},{6,4},{7,5},{8,10},{9,11},{10,... | collective-permute-start | bytes 3538952 | tf_op jit(solution)/shard_map/ppermute | solution.py:57
  177.9 16.8 %collective-permute-start.39 = (bf16[400,128]{1,0:T(8,128)(2,1)}, bf16[400,128]{1,0:T(8,128)(2,1)S(1)}, u32[]{:S(2)}, u32[]{:S(2)}) collective-permute-start(bf16[400,128]{1,0:T(8,128)(2,1)} %get-tuple-element.430), channel_id=1, source_target_pairs={{0,2},{1,3},{2,0},{3,1},{4,6},{5,7},{6,4},{7,5},{8,10},{9,11},{10,... | collective-permute-start | bytes 307208 | tf_op jit(solution)/shard_map/ppermute | solution.py:57
  179.3 16.8 %collective-permute-start.40 = (bf16[400,128]{1,0:T(8,128)(2,1)S(1)}, bf16[400,128]{1,0:T(8,128)(2,1)S(1)}, u32[]{:S(2)}, u32[]{:S(2)}) collective-permute-start(bf16[400,128]{1,0:T(8,128)(2,1)S(1)} %collective-permute-done.38.recv_one), channel_id=1, source_target_pairs={{0,2},{1,3},{2,0},{3,1},{4,6},{5,7},{6,4},{7,5},{8,10},{9,11},{10,... | collective-permute-start | bytes 307208 | tf_op jit(solution)/shard_map/ppermute | solution.py:57
  196.6 20.9 %all-to-all-start.3 = ((bf16[8,96,384]{2,1,0:T(8,128)(2,1)}), bf16[8,96,384]{2,1,0:T(8,128)(2,1)S(1)}, u32[]{:S(2)}, u32[]{:S(2)}) async-start(bf16[8,96,384]{2,1,0:T(8,128)(2,1)} %pad_maximum_fusion.6), calls=%async_computation.3 | async-start | bytes 1179648 | tf_op jit(solution)/shard_map/all_to_all | solution.py:78
  226.1 15.9 %collective-permute-start.46 = (bf16[2,192,768]{2,1,0:T(8,128)(2,1)}, bf16[2,192,768]{2,1,0:T(8,128)(2,1)S(1)}, u32[]{:S(2)}, u32[]{:S(2)}) collective-permute-start(bf16[2,192,768]{2,1,0:T(8,128)(2,1)} %get-tuple-element.466), channel_id=1, source_target_pairs={{0,2},{1,3},{2,0},{3,1},{4,6},{5,7},{6,4},{7,5},{8,10},{9,11},{10,... | collective-permute-start | bytes 1769480 | tf_op jit(solution)/shard_map/ppermute | solution.py:57
  227.6 15.3 %collective-permute-start.47 = (bf16[2,192,768]{2,1,0:T(8,128)(2,1)}, bf16[2,192,768]{2,1,0:T(8,128)(2,1)S(1)}, u32[]{:S(2)}, u32[]{:S(2)}) collective-permute-start(bf16[2,192,768]{2,1,0:T(8,128)(2,1)} %get-tuple-element.467), channel_id=1, source_target_pairs={{0,4},{4,0},{8,12},{12,8},{16,20},{20,16},{24,28},{28,24},{1,5},{5... | collective-permute-start | bytes 1769480 | tf_op jit(solution)/shard_map/ppermute | solution.py:61
  261.7 18.9 %collective-permute-start.54 = (bf16[2,192,768]{2,1,0:T(8,128)(2,1)}, bf16[2,192,768]{2,1,0:T(8,128)(2,1)S(1)}, u32[]{:S(2)}, u32[]{:S(2)}) collective-permute-start(bf16[2,192,768]{2,1,0:T(8,128)(2,1)} %get-tuple-element.493), channel_id=1, source_target_pairs={{0,2},{1,3},{2,0},{3,1},{4,6},{5,7},{6,4},{7,5},{8,10},{9,11},{10,... | collective-permute-start | bytes 1769480 | tf_op jit(solution)/shard_map/ppermute | solution.py:57
  262.2 18.4 %collective-permute-start.55 = (bf16[2,192,768]{2,1,0:T(8,128)(2,1)}, bf16[2,192,768]{2,1,0:T(8,128)(2,1)S(1)}, u32[]{:S(2)}, u32[]{:S(2)}) collective-permute-start(bf16[2,192,768]{2,1,0:T(8,128)(2,1)} %get-tuple-element.494), channel_id=1, source_target_pairs={{0,4},{4,0},{8,12},{12,8},{16,20},{20,16},{24,28},{28,24},{1,5},{5... | collective-permute-start | bytes 1769480 | tf_op jit(solution)/shard_map/ppermute | solution.py:61
  262.8 17.8 %all-to-all-start.4 = ((bf16[8,96,192]{2,1,0:T(8,128)(2,1)}), bf16[8,96,192]{2,1,0:T(8,128)(2,1)S(1)}, u32[]{:S(2)}, u32[]{:S(2)}) async-start(bf16[8,96,192]{2,1,0:T(8,128)(2,1)} %get-tuple-element.498), calls=%async_computation.4 | async-start | bytes 786432 | tf_op jit(solution)/shard_map/all_to_all | solution.py:78
  297.0 15.1 %collective-permute-start.60 = (bf16[2,192,768]{2,1,0:T(8,128)(2,1)}, bf16[2,192,768]{2,1,0:T(8,128)(2,1)S(1)}, u32[]{:S(2)}, u32[]{:S(2)}) collective-permute-start(bf16[2,192,768]{2,1,0:T(8,128)(2,1)} %get-tuple-element.525), channel_id=1, source_target_pairs={{0,2},{1,3},{2,0},{3,1},{4,6},{5,7},{6,4},{7,5},{8,10},{9,11},{10,... | collective-permute-start | bytes 1769480 | tf_op jit(solution)/shard_map/ppermute | solution.py:57
  317.6 39.2 %all-to-all-start.5 = ((bf16[4,192,768]{2,1,0:T(8,128)(2,1)}), bf16[4,192,768]{2,1,0:T(8,128)(2,1)S(1)}, u32[]{:S(2)}, u32[]{:S(2)}) async-start(bf16[4,192,768]{2,1,0:T(8,128)(2,1)} %merge.16), calls=%async_computation.5 | async-start | bytes 2359296 | tf_op jit(solution)/shard_map/all_to_all | solution.py:70
  324.9 15.1 %collective-permute-start.66 = (bf16[192,768]{1,0:T(8,128)(2,1)}, bf16[192,768]{1,0:T(8,128)(2,1)S(1)}, u32[]{:S(2)}, u32[]{:S(2)}) collective-permute-start(bf16[192,768]{1,0:T(8,128)(2,1)} %get-tuple-element.546), channel_id=1, source_target_pairs={{0,4},{4,0},{8,12},{12,8},{16,20},{20,16},{24,28},{28,24},{1,5},{5... | collective-permute-start | bytes 884744 | tf_op jit(solution)/shard_map/ppermute | solution.py:61
  340.1 16.8 %collective-permute-start.68 = (bf16[2,192,768]{2,1,0:T(8,128)(2,1)}, bf16[2,192,768]{2,1,0:T(8,128)(2,1)S(1)}, u32[]{:S(2)}, u32[]{:S(2)}) collective-permute-start(bf16[2,192,768]{2,1,0:T(8,128)(2,1)} %get-tuple-element.560), channel_id=1, source_target_pairs={{0,2},{1,3},{2,0},{3,1},{4,6},{5,7},{6,4},{7,5},{8,10},{9,11},{10,... | collective-permute-start | bytes 1769480 | tf_op jit(solution)/shard_map/ppermute | solution.py:57
  340.6 16.3 %collective-permute-start.69 = (bf16[2,192,768]{2,1,0:T(8,128)(2,1)}, bf16[2,192,768]{2,1,0:T(8,128)(2,1)S(1)}, u32[]{:S(2)}, u32[]{:S(2)}) collective-permute-start(bf16[2,192,768]{2,1,0:T(8,128)(2,1)} %get-tuple-element.561), channel_id=1, source_target_pairs={{0,4},{4,0},{8,12},{12,8},{16,20},{20,16},{24,28},{28,24},{1,5},{5... | collective-permute-start | bytes 1769480 | tf_op jit(solution)/shard_map/ppermute | solution.py:61
  382.6 33.3 %all-to-all-start.6 = ((bf16[4,192,768]{2,1,0:T(8,128)(2,1)}), bf16[4,192,768]{2,1,0:T(8,128)(2,1)S(1)}, u32[]{:S(2)}, u32[]{:S(2)}) async-start(bf16[4,192,768]{2,1,0:T(8,128)(2,1)} %merge.19), calls=%async_computation.6 | async-start | bytes 2359296 | tf_op jit(solution)/shard_map/all_to_all | solution.py:70
  387.7 16.5 %collective-permute-start.77 = (bf16[2,192,768]{2,1,0:T(8,128)(2,1)}, bf16[2,192,768]{2,1,0:T(8,128)(2,1)S(1)}, u32[]{:S(2)}, u32[]{:S(2)}) collective-permute-start(bf16[2,192,768]{2,1,0:T(8,128)(2,1)} %get-tuple-element.608), channel_id=1, source_target_pairs={{0,2},{1,3},{2,0},{3,1},{4,6},{5,7},{6,4},{7,5},{8,10},{9,11},{10,... | collective-permute-start | bytes 1769480 | tf_op jit(solution)/shard_map/ppermute | solution.py:57
  389.2 16.6 %collective-permute-start.78 = (bf16[2,192,768]{2,1,0:T(8,128)(2,1)}, bf16[2,192,768]{2,1,0:T(8,128)(2,1)}, u32[]{:S(2)}, u32[]{:S(2)}) collective-permute-start(bf16[2,192,768]{2,1,0:T(8,128)(2,1)} %get-tuple-element.609), channel_id=1, source_target_pairs={{0,4},{4,0},{8,12},{12,8},{16,20},{20,16},{24,28},{28,24},{1,5},{5... | collective-permute-start | bytes 1769480 | tf_op jit(solution)/shard_map/ppermute | solution.py:61
  389.8 24.8 %collective-permute-start.75 = (bf16[2,192,768]{2,1,0:T(8,128)(2,1)}, bf16[2,192,768]{2,1,0:T(8,128)(2,1)S(1)}, u32[]{:S(2)}, u32[]{:S(2)}) collective-permute-start(bf16[2,192,768]{2,1,0:T(8,128)(2,1)} %get-tuple-element.598), channel_id=1, source_target_pairs={{0,2},{1,3},{2,0},{3,1},{4,6},{5,7},{6,4},{7,5},{8,10},{9,11},{10,... | collective-permute-start | bytes 1769480 | tf_op jit(solution)/shard_map/ppermute | solution.py:57
  390.4 25.5 %collective-permute-start.76 = (bf16[2,192,768]{2,1,0:T(8,128)(2,1)}, bf16[2,192,768]{2,1,0:T(8,128)(2,1)S(1)}, u32[]{:S(2)}, u32[]{:S(2)}) collective-permute-start(bf16[2,192,768]{2,1,0:T(8,128)(2,1)} %get-tuple-element.599), channel_id=1, source_target_pairs={{0,4},{4,0},{8,12},{12,8},{16,20},{20,16},{24,28},{28,24},{1,5},{5... | collective-permute-start | bytes 1769480 | tf_op jit(solution)/shard_map/ppermute | solution.py:61
  415.9 31.5 %all-to-all-start.7 = ((bf16[8,128,384]{2,1,0:T(8,128)(2,1)}), bf16[8,128,384]{2,1,0:T(8,128)(2,1)S(1)}, u32[]{:S(2)}, u32[]{:S(2)}) async-start(bf16[8,128,384]{2,1,0:T(8,128)(2,1)} %orthogonalize.3), calls=%async_computation.7 | async-start | bytes 1572864 | tf_op jit(solution)/shard_map/all_to_all | solution.py:78
  421.2 16.8 %collective-permute-start.81 = (bf16[192,768]{1,0:T(8,128)(2,1)}, bf16[192,768]{1,0:T(8,128)(2,1)S(1)}, u32[]{:S(2)}, u32[]{:S(2)}) collective-permute-start(bf16[192,768]{1,0:T(8,128)(2,1)} %get-tuple-element.626), channel_id=1, source_target_pairs={{0,4},{4,0},{8,12},{12,8},{16,20},{20,16},{24,28},{28,24},{1,5},{5... | collective-permute-start | bytes 884744 | tf_op jit(solution)/shard_map/ppermute | solution.py:61
  423.3 14.7 %collective-permute-start.82 = (bf16[192,768]{1,0:T(8,128)(2,1)S(1)}, bf16[192,768]{1,0:T(8,128)(2,1)S(1)}, u32[]{:S(2)}, u32[]{:S(2)}) collective-permute-start(bf16[192,768]{1,0:T(8,128)(2,1)S(1)} %copy-done.99), channel_id=1, source_target_pairs={{0,2},{1,3},{2,0},{3,1},{4,6},{5,7},{6,4},{7,5},{8,10},{9,11},{10,... | collective-permute-start | bytes 884744 | tf_op jit(solution)/shard_map/ppermute | solution.py:57
  426.5 15.8 %collective-permute-start.79 = (bf16[192,768]{1,0:T(8,128)(2,1)}, bf16[192,768]{1,0:T(8,128)(2,1)S(1)}, u32[]{:S(2)}, u32[]{:S(2)}) collective-permute-start(bf16[192,768]{1,0:T(8,128)(2,1)} %get-tuple-element.624), channel_id=1, source_target_pairs={{0,4},{4,0},{8,12},{12,8},{16,20},{20,16},{24,28},{28,24},{1,5},{5... | collective-permute-start | bytes 884744 | tf_op jit(solution)/shard_map/ppermute | solution.py:61
  426.6 15.7 %collective-permute-start.80 = (bf16[192,768]{1,0:T(8,128)(2,1)}, bf16[192,768]{1,0:T(8,128)(2,1)S(1)}, u32[]{:S(2)}, u32[]{:S(2)}) collective-permute-start(bf16[192,768]{1,0:T(8,128)(2,1)} %get-tuple-element.625), channel_id=1, source_target_pairs={{0,2},{1,3},{2,0},{3,1},{4,6},{5,7},{6,4},{7,5},{8,10},{9,11},{10,... | collective-permute-start | bytes 884744 | tf_op jit(solution)/shard_map/ppermute | solution.py:57
  478.7 18.3 %all-to-all-start.9 = ((bf16[8,96,384]{2,1,0:T(8,128)(2,1)}), bf16[8,96,384]{2,1,0:T(8,128)(2,1)S(1)}, u32[]{:S(2)}, u32[]{:S(2)}) async-start(bf16[8,96,384]{2,1,0:T(8,128)(2,1)} %orthogonalize.4), calls=%async_computation.9 | async-start | bytes 1179648 | tf_op jit(solution)/shard_map/all_to_all | solution.py:78
  497.0 18.8 %all-to-all-start.10 = ((bf16[8,96,384]{2,1,0:T(8,128)(2,1)}), bf16[8,96,384]{2,1,0:T(8,128)(2,1)S(1)}, u32[]{:S(2)}, u32[]{:S(2)}) async-start(bf16[8,96,384]{2,1,0:T(8,128)(2,1)} %orthogonalize.5), calls=%async_computation.10 | async-start | bytes 1179648 | tf_op jit(solution)/shard_map/all_to_all | solution.py:78
  (147 other events, 1128.4 us)

commit v4 on v3

--- a/solution.py
+++ b/solution.py
@@ -1,4 +1,5 @@
 from functools import partial
+from types import SimpleNamespace
 
 import jax
 import jax.numpy as jnp
@@ -617,8 +618,8 @@
             copy[place] = master.astype(BF16)
 
 
-def ortho_kernel(place, terms, moment, *rest):
-    extra, (result, whole) = rest[:-2], rest[-2:]
+def ortho_kernel(place, count, moment, *rest):
+    terms, extra, (result, whole) = rest[:count], rest[count:-2], rest[-2:]
     pieces, size, _ = moment.shape
     width = whole.shape[1]
     eye = (iota((width, width), 0) == iota((width, width), 1)).astype(F32)
@@ -626,9 +627,10 @@
     def exact(left, right, dims=(((1,), (0,)), ((), ()))):
         return lax.dot_general(left, right, dims, precision=EXACT, preferred_element_type=F32)
 
-    grad = terms[0].astype(F32)
-    for term in range(1, terms.shape[0]):
-        grad = grad + terms[term].astype(F32)
+    pieces_of = [part[term].astype(F32) for part in terms for term in range(part.shape[0])]
+    grad = pieces_of[0]
+    for term in pieces_of[1:]:
+        grad = grad + term
     for piece in range(pieces):
         whole[piece * size : (piece + 1) * size, :] = moment[piece, :, lanes_of(place, width)].astype(F32)
     source = MOMENTUM_DECAY * whole[...].T + grad
@@ -715,8 +717,10 @@
         [weight_scratch(width, 640), pltpu.SemaphoreType.DMA((copy_count(plan),))],
         2 * rows * width * width * 3 * 1.5,
         8 * width * width,
-    )(resid, vectors, tables["cosine"], tables["sine"], feature_map, tables["row"], *flat(weight))
-    return dict(zip(("phi_query", "phi_key", "value", "query", "key", "summary"), results))
+    )(resid, vectors, tables.cosine, tables.sine, feature_map, tables.row, *flat(weight))
+    state = SimpleNamespace(input=resid)
+    state.phi_query, state.phi_key, state.value, state.query, state.key, state.summary = results
+    return state
 
 
 def mix_scratch(width, plans):
@@ -750,10 +754,11 @@
         2 * rows * width * width * 12,
         20 * width * width,
     )(
-        resid, vectors, bias, state["phi_query"], state["phi_key"], state["value"], tables["row"],
-        *received, tables["shares"], *refs,
+        resid, vectors, bias, state.phi_query, state.phi_key, state.value, tables.row,
+        *received, tables.shares, *refs,
     )
-    return dict(zip(("context", "inverse", "middle", "slope", "active_keep", "mix_pack", "output"), results))
+    (state.context, state.inverse, state.middle, state.slope, state.active_keep, state.mix_pack,
+     state.output) = results
 
 
 def back_mix(grad, vectors, state, tables, weights):
@@ -780,11 +785,11 @@
         2 * rows * width * width * 11,
         20 * width * width,
     )(
-        grad, vectors, state["middle"], state["slope"], state["inverse"], state["context"], state["phi_query"],
-        tables["row"], *refs,
+        grad, vectors, state.middle, state.slope, state.inverse, state.context, state.phi_query,
+        tables.row, *refs,
     )
-    names = ("upper_keep", "back_pack", "middle_grad", "numer", "denom", "back_summary", "vector_two", "bias_grad")
-    return dict(zip(names, results))
+    (state.upper_keep, state.back_pack, state.middle_grad, state.numer, state.denom, state.back_summary,
+     state.vector_two, state.bias_grad) = results
 
 
 def back_project(resid, vectors, state, received, back_received, tables, feature_map, weight):
@@ -805,12 +810,12 @@
         2 * rows * width * width * 8,
         8 * width * width,
     )(
-        resid, vectors, tables["cosine"], tables["sine"], feature_map, tables["row"],
-        state["phi_query"], state["phi_key"], state["value"], state["query"], state["key"], state["numer"],
-        state["denom"], state["context"], state["middle_grad"], *received, *back_received, tables["shares"],
+        resid, vectors, tables.cosine, tables.sine, feature_map, tables.row,
+        state.phi_query, state.phi_key, state.value, state.query, state.key, state.numer,
+        state.denom, state.context, state.middle_grad, *received, *back_received, tables.shares,
         *flat(weight),
     )
-    return dict(zip(("stacked_keep", "stack_pack", "input_grad", "vector_one"), results))
+    state.stacked_keep, state.stack_pack, state.input_grad, state.vector_one = results
 
 
 def matrix_grad(quick, splits, right_own, right_other, *lefts):
@@ -823,20 +828,20 @@
 
 
 def down_grad(quick, state, mix_other, branch_own, branch_other, entries):
-    splits = ((state["mix_pack"].shape[2], *entries),)
-    return matrix_grad(quick, splits, state["active_keep"], mix_other, branch_own, branch_other)
+    splits = ((state.mix_pack.shape[2], *entries),)
+    return matrix_grad(quick, splits, state.active_keep, mix_other, branch_own, branch_other)
 
 
 def up_grad(quick, state, back_other, mix_other):
-    splits = ((state["mix_pack"].shape[2], 2, 2),)
-    return matrix_grad(quick, splits, state["upper_keep"], back_other, state["mix_pack"], mix_other)
+    splits = ((state.mix_pack.shape[2], 2, 2),)
+    return matrix_grad(quick, splits, state.upper_keep, back_other, state.mix_pack, mix_other)
 
 
 def attend_grad(quick, state, stack_other, back_other):
-    width = state["mix_pack"].shape[2]
+    width = state.mix_pack.shape[2]
     splits = ((width // 4 * 3, 2, 2), (width // 4, 2, 2))
     return matrix_grad(
-        quick, splits, state["stacked_keep"], stack_other, state["stack_pack"], stack_other, state["back_pack"],
+        quick, splits, state.stacked_keep, stack_other, state.stack_pack, stack_other, state.back_pack,
         back_other,
     )
 
@@ -865,12 +870,13 @@
 
 def orthogonalize(place, terms, moment, *extra):
     pieces, size, _ = moment.shape
-    width = terms.shape[1]
+    terms = terms if isinstance(terms, tuple) else (terms,)
+    width = terms[0].shape[1]
     spare = 32 if extra else 0
     return call(
-        partial(ortho_kernel, place), "orthogonalize", vmem(2 + len(extra)),
+        partial(ortho_kernel, place, len(terms)), "ortho", vmem(1 + len(terms) + len(extra)),
         [shape((pieces, size + spare, 2 * width), BF16)], [pltpu.VMEM((pieces * size, width), F32)], 1, 1,
-    )(terms, moment, *extra)[0]
+    )(moment, *terms, *extra)[0]
 
 
 def update(ratio, pieces, items, olds, news):
@@ -916,12 +922,9 @@
     others = jnp.stack([lax.dynamic_index_in_dim(edges, index ^ offset, 0, keepdims=False) for offset in (1, 2, 3)])
     mine = jnp.stack([own[0], own[rows - 1]])
     shares = (others[:, None, :] == mine[None, :, None]).astype(F32).reshape(3, 4)
-    return {
-        "cosine": jnp.cos(angles) * scale,
-        "sine": jnp.sin(angles) * scale,
-        "row": own[None, :].astype(F32),
-        "shares": shares,
-    }
+    return SimpleNamespace(
+        cosine=jnp.cos(angles) * scale, sine=jnp.sin(angles) * scale, row=own[None, :].astype(F32), shares=shares
+    )
 
 
 def cross_edges(summary, near):
@@ -1028,33 +1031,32 @@
 
     tables = doc_tables(segments[0], rows)
     resid = block_input.astype(F32)
-    bias_slots = [bias_up] + other_slots(bias_up)
-    biases = [jnp.stack([item[layer] for item in bias_slots]) for layer in range(layers)]
+    biases = []
     gradient = cotangent.astype(F32) * marked[0][:, None].astype(F32)
     states = [None] * layers
 
+    def spread_biases(bias_up):
+        slots = [bias_up] + other_slots(bias_up)
+        biases.extend(jnp.stack([item[layer] for item in slots]) for layer in range(layers))
+
     def run_project(layer, resid, weight):
         states[layer] = project(resid, vectors[layer], tables, feature_map[layer], weight)
-        states[layer]["input"] = resid
 
     def run_mix(layer, received, weights):
         state = states[layer]
-        state["received"] = received
-        state.update(mix(state["input"], vectors[layer], biases[layer], state, received, tables, weights))
-        return state["output"]
+        state.received = received
+        mix(state.input, vectors[layer], biases[layer], state, received, tables, weights)
+        return state.output
 
     def run_back_mix(layer, gradient, weights):
-        states[layer].update(back_mix(gradient, vectors[layer], states[layer], tables, weights))
+        back_mix(gradient, vectors[layer], states[layer], tables, weights)
 
     def run_back_project(layer, back_received, weight):
         state = states[layer]
-        state.update(
-            back_project(
-                state["input"], vectors[layer], state, state["received"], back_received, tables, feature_map[layer],
-                weight,
-            )
+        back_project(
+            state.input, vectors[layer], state, state.received, back_received, tables, feature_map[layer], weight
         )
-        return state["input_grad"]
+        return state.input_grad
 
     if quick:
         half = width // 2
@@ -1064,7 +1066,16 @@
         )
         line = [first] + [swap_dp(first, offset) for offset in (2, 4, 6)]
 
-        line, hidden = hold(line, hidden)
+        blocks = [old_blocks(layer, moments, block) for layer in (1, 0)]
+        (attend_one, hidden_one), (attend_zero, hidden_zero) = blocks
+        payload = jnp.concatenate(
+            [
+                jnp.concatenate([hidden_one[4:], hidden_one[:4]]),
+                jnp.concatenate([attend_one, hidden_zero[4:]]),
+            ],
+            axis=2,
+        )
+        line, hidden, payload = hold(line, hidden, payload)
         up_line, down_line = (jnp.stack([item[:, cut] for item in line]) for cut in (slice(half), slice(half, width)))
         up_y, down_x = swap_dp(up_line, 1), swap_head(down_line, 2)
         hidden_line = swap_line(hidden)
@@ -1073,9 +1084,10 @@
         up, down = jnp.stack([up_line, up_y]), jnp.stack([down_line, down_x])
         up_other, down_other = swap_head(up, 2), swap_dp(down, 1)
 
-        up, down, up_other, down_other, resid, tables, biases, second_attend = hold(
-            up, down, up_other, down_other, resid, tables, biases, second_attend
+        up, down, up_other, down_other, resid, held, second_attend = hold(
+            up, down, up_other, down_other, resid, vars(tables), second_attend
         )
+        vars(tables).update(held)
         cores = swap_all([up, up_other, down, down_other], swap_head, 1)
         cores, hidden_line, second_attend = hold(cores, hidden_line, second_attend)
         weight_one = [
@@ -1086,38 +1098,30 @@
         up_y, down_x = swap_dp(up_line, 1), swap_head(down_line, 2)
         attend_line = swap_line(second_attend)
         run_project(0, resid, weight_one)
-        near = swap_head(states[0]["summary"], 1)
-
-        up_line, down_line, up_y, down_x, near, attend_line, second_hidden, moments, gradient = hold(
-            up_line, down_line, up_y, down_x, near, attend_line, second_hidden, moments, gradient
+        near = swap_head(states[0].summary, 1)
+
+        up_line, down_line, up_y, down_x, near, attend_line, second_hidden, moments, gradient, late_bias = hold(
+            up_line, down_line, up_y, down_x, near, attend_line, second_hidden, moments, gradient, bias_up
         )
         second_line = swap_line(second_hidden)
+        spread_biases(late_bias)
         up, down = jnp.stack([up_line, up_y]), jnp.stack([down_line, down_x])
         up_other, down_other = swap_head(up, 2), swap_dp(down, 1)
-        both = cross_edges(states[0]["summary"], near)
+        both = cross_edges(states[0].summary, near)
         cores = swap_all([up, down], swap_head, 1)
-        blocks = [old_blocks(layer, moments, block) for layer in (1, 0)]
-        (attend_one, hidden_one), (attend_zero, hidden_zero) = blocks
-        payload = jnp.concatenate(
-            [
-                jnp.concatenate([hidden_one[4:], hidden_one[:4]]),
-                jnp.concatenate([attend_one, hidden_zero[4:]]),
-            ],
-            axis=2,
-        )
+        attend_zero, hidden_zero = old_blocks(0, moments, block)
         payload_late = jnp.concatenate([hidden_zero[:4], attend_zero])
 
         branch = gradient.astype(BF16)
         branch_other = swap_head(branch, 1)
 
-        cores, up_other, down_other, received, payload, payload_late, second_line, branch_other = hold(
-            cores, up_other, down_other, (near, *both), payload, payload_late, second_line, branch_other
+        cores, up_other, down_other, received, payload_late, branch_other = hold(
+            cores, up_other, down_other, (near, *both), payload_late, branch_other
         )
         cores += swap_all([up_other, down_other], swap_head, 1)
-        lines = line_parts(attend_line, ((0, half), (half, width)))
-        lines += line_parts(second_line, ((0, width), (width, 2 * width)))
-
-        lines, received, cores = hold(lines, received, cores)
+        attend_up, attend_down = line_parts(attend_line, ((0, half), (half, width)))
+        attend_y, attend_x = swap_dp(attend_up, 1), swap_head(attend_down, 2)
+        cores, attend_y, attend_x, second_line, received = hold(cores, attend_y, attend_x, second_line, received)
         weights = [
             (
                 weight_one,
@@ -1125,15 +1129,15 @@
                 [((down, cores[1], down_other, cores[3]), "down", 0, 0, width)],
             )
         ]
-        crossed = [swap_dp(lines[0], 1), swap_head(lines[1], 2), swap_dp(lines[2], 1), swap_head(lines[3], 2)]
+        up, down = jnp.stack([attend_up, attend_y]), jnp.stack([attend_down, attend_x])
+        up_other, down_other = swap_head(up, 2), swap_dp(down, 1)
+        up_line, down_line = line_parts(second_line, ((0, width), (width, 2 * width)))
+        up_y, down_x = swap_dp(up_line, 1), swap_head(down_line, 2)
         resid = run_mix(0, received, weights[0])
 
-        lines, crossed, resid = hold(lines, crossed, resid)
-        up, down, up_late, down_late = (jnp.stack(pair) for pair in zip(lines, crossed))
-        up_other, down_other = swap_head(up, 2), swap_dp(down, 1)
+        up_other, down_other, up_y, down_x, resid = hold(up_other, down_other, up_y, down_x, resid)
+        up_late, down_late = jnp.stack([up_line, up_y]), jnp.stack([down_line, down_x])
         up_late_other, down_late_other = swap_head(up_late, 2), swap_dp(down_late, 1)
-
-        up, down, up_other, down_other = hold(up, down, up_other, down_other)
         cores = swap_all([up, down, up_other, down_other], swap_head, 1)
         late_cores = swap_all([up_late, down_late], swap_head, 1)
         cores, late_cores, resid = hold(cores, late_cores, resid)
@@ -1143,7 +1147,7 @@
         ]
         run_project(1, resid, weight_one)
 
-        summary = states[1]["summary"]
+        summary = states[1].summary
         near = swap_head(summary, 1)
         both = cross_edges(summary, near)
         received, up_late_other, down_late_other, payload = hold(
@@ -1160,7 +1164,7 @@
         moment = swap_owners(payload)
         activations = run_mix(1, received, weights[1])
 
-        moment, mix_pack, activations = hold(moment, states[1]["mix_pack"], activations)
+        moment, mix_pack, activations = hold(moment, states[1].mix_pack, activations)
         mix_other = swap_head(mix_pack, 1)
         down_one = down_grad(quick, states[1], mix_other, branch, branch_other, (None, None))
 
@@ -1168,7 +1172,7 @@
         down_others = send_first(down_one)
         run_back_mix(1, gradient, weights[1])
 
-        down_others, summary, back_pack = hold(down_others, states[1]["back_summary"], states[1]["back_pack"])
+        down_others, summary, back_pack = hold(down_others, states[1].back_summary, states[1].back_pack)
         near, back_other = swap_all([summary, back_pack], swap_head, 1)
         down_one = merge_first(down_one, down_others)
         near, back_other, down_one = hold(near, back_other, down_one)
@@ -1182,7 +1186,7 @@
         gradient = run_back_project(1, back_received, weights[1][0])
 
         up_others, gradient, stack_pack, mix_pack, moment_late = hold(
-            up_others, gradient, states[1]["stack_pack"], states[0]["mix_pack"], moment_late
+            up_others, gradient, states[1].stack_pack, states[0].mix_pack, moment_late
         )
         stack_other, mix_other = swap_all([stack_pack, mix_pack], swap_head, 1)
         up_one = merge_first(up_one, up_others)
@@ -1196,7 +1200,7 @@
         pair_one = swap_line(merge_second(up_one, up_others, down_blocks))
         run_back_mix(0, gradient, weights[0])
 
-        attend_others, summary, back_pack = hold(attend_others, states[0]["back_summary"], states[0]["back_pack"])
+        attend_others, summary, back_pack = hold(attend_others, states[0].back_summary, states[0].back_pack)
         near, back_other = swap_all([summary, back_pack], swap_head, 1)
         attend_one = merge_first(attend_one, attend_others)
         near, back_other, attend_one = hold(near, back_other, attend_one)
@@ -1208,10 +1212,10 @@
         down_others = send_first(down_zero)
         gradient = run_back_project(0, back_received, weights[0][0])
 
-        down_others, stack_pack, pair_one = hold(down_others, states[0]["stack_pack"], pair_one)
+        down_others, stack_pack, pair_one = hold(down_others, states[0].stack_pack, pair_one)
         stack_other = swap_head(stack_pack, 1)
-        vector_grads = [(state["vector_one"] + state["vector_two"])[:5] for state in states]
-        kept, sent = core_vectors(vector_grads, [state["bias_grad"] for state in states])
+        vector_grads = [(state.vector_one + state.vector_two)[:5] for state in states]
+        kept, sent = core_vectors(vector_grads, [state.bias_grad for state in states])
         came = swap_head(sent, 1)
         up_zero = up_grad(quick, states[0], back_other, mix_other)
         down_zero = merge_first(down_zero, down_others)
@@ -1263,6 +1267,7 @@
             (pieces_three, [("up", 0, 0), ("query_key", 0, 4), ("value", 0, 6), ("out", 0, 7)]),
         ]
     else:
+        spread_biases(bias_up)
         weights = []
         for layer in range(layers):
             parts = []
@@ -1272,16 +1277,16 @@
             weights.append(tuple(parts))
         for layer in range(layers):
             run_project(layer, resid, weights[layer][0])
-            resid = run_mix(layer, exchange_edges(states[layer]["summary"]), weights[layer])
+            resid = run_mix(layer, exchange_edges(states[layer].summary), weights[layer])
         activations = resid
         raw = []
         for layer in reversed(range(layers)):
             state = states[layer]
             branch = gradient.astype(BF16)
             run_back_mix(layer, gradient, weights[layer])
-            gradient = run_back_project(layer, exchange_edges(state["back_summary"]), weights[layer][0])
+            gradient = run_back_project(layer, exchange_edges(state.back_summary), weights[layer][0])
             back_other, mix_other, stack_other, branch_other = swap_all(
-                [state["back_pack"], state["mix_pack"], state["stack_pack"], branch], swap_head, 1
+                [state.back_pack, state.mix_pack, state.stack_pack, branch], swap_head, 1
             )
             for own in (
                 attend_grad(quick, state, stack_other, back_other),
@@ -1311,8 +1316,8 @@
             (part, [("query_key", layer, 0), ("value", layer, 2), ("out", layer, 3), ("up", layer, 4), ("down", layer, 8)])
             for layer, part in enumerate(ordered)
         ]
-        vector_grads = [(state["vector_one"] + state["vector_two"])[:5] for state in states]
-        kept, sent = core_vectors(vector_grads, [state["bias_grad"] for state in states])
+        vector_grads = [(state.vector_one + state.vector_two)[:5] for state in states]
+        kept, sent = core_vectors(vector_grads, [state.bias_grad for state in states])
         kept, sent = across_vectors(kept + swap_head(sent, 1), layers)
         packed = lax.psum(kept + swap_head(sent, 2), "dp")
 

time: 530 us -> 528 us (level)
  waiting for transfers between devices: 126 us -> 115 us
  local copies, waits for them, and re-layouts: 34.4 us -> 42.4 us
    ppermute x23, waiting for transfers between devices: 57.4 us -> 35.2 us  [swap_dp(): lax.ppermute(values, 'dp', [(d, d ^ offset) for d in range(lax.axis_size(...]
    ppermute x60, waiting for transfers between devices: 55.1 us -> 67.9 us  [swap_head(): lax.ppermute(values, 'head', [(h, h ^ offset) for h in range(lax.axis_siz...]
    unnamed x218 -> x238, local copies, waits for them, and re-layouts: 19 us -> 21.6 us
  transfers between devices with their start and end apart: 93 -> 93, of which waited for: 42 -> 38; matrix products, arithmetic and copies ran while one was open for 8% -> 9% of each run, Pallas kernels for 36% -> 36%
where the time goes in v4:
time: 528 us; the launch traced here: 518 us
  Pallas kernels  199 us (38%)
  waiting for transfers between devices  115 us (22%)
  starting transfers between devices  111 us (21%)
  local copies, waits for them, and re-layouts  42.4 us (8%)
  blocking collectives  31.3 us (6%)
  other arithmetic  16.8 us (3%)
    ppermute x60, waiting for transfers between devices, swap_head(): lax.ppermute(values, 'head', [(h, h ^ offset) for h in range(lax.axis_siz...  67.9 us
    ppermute x60, starting transfers between devices, swap_head(): lax.ppermute(values, 'head', [(h, h ^ offset) for h in range(lax.axis_siz...  37.4 us
    ppermute x23, waiting for transfers between devices, swap_dp(): lax.ppermute(values, 'dp', [(d, d ^ offset) for d in range(lax.axis_size(...  35.2 us
    pallas_call x6, Pallas kernels, matrix_grad(): call(partial(grad_kernel, quick, splits), 'matrix_grad', vmem(2 + len(lef...  32 us
    all_to_all x1, blocking collectives, swap_line(): lax.all_to_all(parts, 'dp', split_axis=0, concat_axis=0, axis_index_group...  31.3 us
    pallas_call x12, Pallas kernels, merge(): return call(kernel, 'merge', vmem(len(operands)), outs, [], 1, 1)(*operands)  30.9 us
    pallas_call x2, Pallas kernels, back_project(): call(partial(back_project_kernel, plan), 'back_project', vmem(21) + scala...  29.1 us
    pallas_call x3, Pallas kernels, orthogonalize(): call(partial(ortho_kernel, place, len(terms)), 'ortho', vmem(1 + len(term...  28.9 us
  transfers between devices with their start and end apart: 93, of which 38 were waited for; matrix products, arithmetic and copies ran while one was open for 9% of the time, Pallas kernels for 36%

profile of v4, /device:TPU:0, one launch (start us, length us, event | category | flops | bytes accessed | tf_op | source)
XLA Modules:
  0.0 518.0 jit_solution(1916920133649316861)
XLA Ops:
  4.1 5.1 collective-permute-start.2
  18.1 3.6 collective-permute-done.1
  22.8 4.3 all-to-all-start
  31.1 4.3 collective-permute-done.3
  44.6 5.6 %collective-permute-done.6.rest_6_ = bf16[2,4,96,384]{3,2,1,0:T(8,128)(2,1)S(1)} collective-permute-done((bf16[2,4,96,384]{3,2,1,0:T(8,128)(2,1)S(1)}, bf16[2,4,96,384]{3,2,1,0:T(8,128)(2,1)S(1)}, u32[]{:S(2)}, u32[]{:S(2)}) %collective-permute-start.6) | collective-permute-done | bytes 589856 | tf_op jit(solution)/shard_map/ppermute | solution.py:62
  57.8 4.5 all-to-all-start.1
  68.1 8.9 %project.2 = (bf16[256,384]{1,0:T(8,128)(2,1)}, bf16[256,384]{1,0:T(8,128)(2,1)}, bf16[256,768]{1,0:T(8,128)(2,1)}, f32[256,768]{1,0:T(8,128)}, f32[256,768]{1,0:T(8,128)}, /*index=5*/bf16[400,128]{1,0:T(8,128)(2,1)}) custom-call(f32[256,768]{1,0:T(8,128)} %convert_element_type.66.resid, f32[5,768]{1,0:T(8,128)} %get-tuple-element.742.vectors, ...), custom_call_target="tpu_custom_call" | custom-call | flops 1358954496 | bytes 4718592 | tf_op jit(solution)/shard_map/project/pallas_call | solution.py:712
  85.2 5.3 %all-to-all-start.2 = ((bf16[4,96,1536]{2,1,0:T(8,128)(2,1)}), bf16[4,96,1536]{2,1,0:T(8,128)(2,1)}, u32[]{:S(2)}, u32[]{:S(2)}) async-start(bf16[4,96,1536]{2,1,0:T(8,128)(2,1)} %broadcast_in_dim.8), calls=%async_computation.2 | async-start | bytes 2359296 | tf_op jit(solution)/shard_map/all_to_all | solution.py:71
  99.6 15.3 %collective-permute-done.19.recv_three = bf16[400,128]{1,0:T(8,128)(2,1)S(1)} collective-permute-done((bf16[400,128]{1,0:T(8,128)(2,1)}, bf16[400,128]{1,0:T(8,128)(2,1)S(1)}, u32[]{:S(2)}, u32[]{:S(2)}) %collective-permute-start.19) | collective-permute-done | bytes 102432 | tf_op jit(solution)/shard_map/ppermute | solution.py:58
  123.6 6.5 %collective-permute-done.24 = bf16[4,96,384]{2,1,0:T(8,128)(2,1)S(1)} collective-permute-done((bf16[4,96,384]{2,1,0:T(8,128)(2,1)S(1)}, bf16[4,96,384]{2,1,0:T(8,128)(2,1)S(1)}, u32[]{:S(2)}, u32[]{:S(2)}) %collective-permute-start.24) | collective-permute-done | bytes 294944 | tf_op jit(solution)/shard_map/ppermute | solution.py:58
  137.8 13.1 %mix.2 = (f32[256,768]{1,0:T(8,128)}, f32[256,768]{1,0:T(8,128)}, f32[256,768]{1,0:T(8,128)}, bf16[4,256,768]{2,1,0:T(8,128)(2,1)}, bf16[2,256,768]{2,1,0:T(8,12...) custom-call(f32[256,768]{1,0:T(8,128)} %convert_element_type.66.resid, f32[5,768]{1,0:T(8,128)} %get-tuple-element.742.vectors, ...), custom_call_target="tpu_custom_call" | custom-call | flops 3623878656 | bytes 11796480 | tf_op jit(solution)/shard_map/mix/pallas_call | solution.py:748
  151.5 6.9 %collective-permute-done.30 = bf16[4,96,768]{2,1,0:T(8,128)(2,1)S(1)} collective-permute-done((bf16[4,96,768]{2,1,0:T(8,128)(2,1)S(1)}, bf16[4,96,768]{2,1,0:T(8,128)(2,1)S(1)}, u32[]{:S(2)}, u32[]{:S(2)}) %collective-permute-start.30) | collective-permute-done | bytes 589856 | tf_op jit(solution)/shard_map/ppermute | solution.py:58
  165.6 8.5 %project.3 = (bf16[256,384]{1,0:T(8,128)(2,1)}, bf16[256,384]{1,0:T(8,128)(2,1)}, bf16[256,768]{1,0:T(8,128)(2,1)}, f32[256,768]{1,0:T(8,128)}, f32[256,768]{1,0:T(8,128)}, /*index=5*/bf16[400,128]{1,0:T(8,128)(2,1)}) custom-call(f32[256,768]{1,0:T(8,128)} %get-tuple-element.402.resid, f32[5,768]{1,0:T(8,128)} %get-tuple-element.741.vectors, ...), custom_call_target="tpu_custom_call" | custom-call | flops 1358954496 | bytes 4718592 | tf_op jit(solution)/shard_map/project/pallas_call | solution.py:712
  176.4 11.6 %collective-permute-done.42.rest_14_ = bf16[2,4,96,768]{3,2,1,0:T(8,128)(2,1)} collective-permute-done((bf16[2,4,96,768]{3,2,1,0:T(8,128)(2,1)S(1)}, bf16[2,4,96,768]{3,2,1,0:T(8,128)(2,1)}, u32[]{:S(2)}, u32[]{:S(2)}) %collective-permute-start.42) | collective-permute-done | bytes 1179680 | tf_op jit(solution)/shard_map/ppermute | solution.py:62
  193.2 5.7 %all-to-all-start.3 = ((bf16[8,96,384]{2,1,0:T(8,128)(2,1)}), bf16[8,96,384]{2,1,0:T(8,128)(2,1)S(1)}, u32[]{:S(2)}, u32[]{:S(2)}) async-start(bf16[8,96,384]{2,1,0:T(8,128)(2,1)} %pad_maximum_fusion.4), calls=%async_computation.3 | async-start | bytes 1179648 | tf_op jit(solution)/shard_map/all_to_all | solution.py:79
  201.0 12.6 %mix.3 = (f32[256,768]{1,0:T(8,128)}, f32[256,768]{1,0:T(8,128)}, f32[256,768]{1,0:T(8,128)}, bf16[4,256,768]{2,1,0:T(8,128)(2,1)}, bf16[2,256,768]{2,1,0:T(8,12...) custom-call(f32[256,768]{1,0:T(8,128)} %get-tuple-element.402.resid, f32[5,768]{1,0:T(8,128)} %get-tuple-element.741.vectors, ...), custom_call_target="tpu_custom_call" | custom-call | flops 3623878656 | bytes 11796480 | tf_op jit(solution)/shard_map/mix/pallas_call | solution.py:748
  214.9 3.1 collective-permute-done.45.right_other.rest_1_
  219.1 4.4 matrix_grad.6
  226.3 12.9 %back_mix.2 = (bf16[2,256,768]{2,1,0:T(8,128)(2,1)}, bf16[3,256,768]{2,1,0:T(8,128)(2,1)}, f32[256,768]{1,0:T(8,128)}, bf16[256,768]{1,0:T(8,128)(2,1)}, bf16[25...) custom-call(f32[256,768]{1,0:T(8,128)} %convert_multiply_fusion.grad, ...), custom_call_target="tpu_custom_call" | custom-call | flops 3321888768 | bytes 11796480 | tf_op jit(solution)/shard_map/back_mix/pallas_call | solution.py:779
  247.9 4.9 matrix_grad.7
  252.8 4.3 collective-permute-done.50.back_two
  260.2 4.7 all-to-all-start.4
  264.9 13.7 %back_project.2 = (bf16[2,256,768]{2,1,0:T(8,128)(2,1)}, bf16[4,256,768]{2,1,0:T(8,128)(2,1)}, f32[256,768]{1,0:T(8,128)}, f32[8,768]{1,0:T(8,128)}) custom-call(f32[256,768]{1,0:T(8,128)} %get-tuple-element.402.resid, f32[5,768]{1,0:T(8,128)} %get-tuple-element.741.vectors, f32[256,32]{1,0:T(8,128)} %get-tuple-element.353.cosine_part, ...), custom_call_target="tpu_custom_call" | custom-call | flops 2415919104 | bytes 4718592 | tf_op jit(solution)/shard_map/back_project/pallas_call | solution.py:804
  287.5 6.1 %matrix_grad.8 = (bf16[2,192,768]{2,1,0:T(8,128)(2,1)}, bf16[2,192,768]{2,1,0:T(8,128)(2,1)}, bf16[2,192,768]{2,1,0:T(8,128)(2,1)}, bf16[2,192,768]{2,1,0:T(8,128)(2,1)}) custom-call(bf16[2,256,768]{2,1,0:T(8,128)(2,1)} %get-tuple-element.468.right_own, bf16[4,256,768]{2,1,0:T(8,128)(2,1)} %copy-done.4, bf16[4,256,768]{2,1,0:T(8,128)(2,1)} %get-tuple-element.475.rest_0_, ...), custom_call_target="tpu_custom_call" | custom-call | flops 1207959552 | bytes 4718592 | tf_op jit(solution)/shard_map/matrix_grad/pallas_call | solution.py:824
  296.8 13.2 %back_mix.3 = (bf16[2,256,768]{2,1,0:T(8,128)(2,1)}, bf16[3,256,768]{2,1,0:T(8,128)(2,1)}, f32[256,768]{1,0:T(8,128)}, bf16[256,768]{1,0:T(8,128)(2,1)}, bf16[25...) custom-call(f32[256,768]{1,0:T(8,128)} %get-tuple-element.493.grad, ...), custom_call_target="tpu_custom_call" | custom-call | flops 3321888768 | bytes 11796480 | tf_op jit(solution)/shard_map/back_mix/pallas_call | solution.py:779
  315.5 4.5 all-to-all-start.5
  320.1 2.7 merge.14
  326.9 5.2 matrix_grad.9
  332.0 4.4 collective-permute-done.64.back_two
  339.4 15.4 %back_project.3 = (bf16[2,256,768]{2,1,0:T(8,128)(2,1)}, bf16[4,256,768]{2,1,0:T(8,128)(2,1)}, f32[256,768]{1,0:T(8,128)}, f32[8,768]{1,0:T(8,128)}) custom-call(f32[256,768]{1,0:T(8,128)} %convert_element_type.66.resid, f32[5,768]{1,0:T(8,128)} %get-tuple-element.742.vectors, f32[256,32]{1,0:T(8,128)} %get-tuple-element.353.cosine_part, ...), custom_call_target="tpu_custom_call" | custom-call | flops 2415919104 | bytes 4718592 | tf_op jit(solution)/shard_map/back_project/pallas_call | solution.py:804
  357.3 5.2 %matrix_grad.10 = (bf16[2,192,768]{2,1,0:T(8,128)(2,1)}, bf16[2,192,768]{2,1,0:T(8,128)(2,1)}, bf16[2,192,768]{2,1,0:T(8,128)(2,1)}, bf16[2,192,768]{2,1,0:T(8,128)(2,1)}) custom-call(bf16[2,256,768]{2,1,0:T(8,128)(2,1)} %get-tuple-element.529.right_own, bf16[3,256,768]{2,1,0:T(8,128)(2,1)} %copy-done.42, bf16[3,256,768]{2,1,0:T(8,128)(2,1)} %get-tuple-element.476.rest_0_, ...), custom_call_target="tpu_custom_call" | custom-call | flops 1207959552 | bytes 4718592 | tf_op jit(solution)/shard_map/matrix_grad/pallas_call | solution.py:824
  362.4 2.7 merge.17
  368.7 6.2 %matrix_grad.11 = (bf16[2,192,768]{2,1,0:T(8,128)(2,1)}, bf16[2,192,768]{2,1,0:T(8,128)(2,1)}, bf16[2,192,768]{2,1,0:T(8,128)(2,1)}, bf16[2,192,768]{2,1,0:T(8,128)(2,1)}) custom-call(bf16[2,256,768]{2,1,0:T(8,128)(2,1)} %get-tuple-element.528.right_own, bf16[4,256,768]{2,1,0:T(8,128)(2,1)} %copy-done.20, bf16[4,256,768]{2,1,0:T(8,128)(2,1)} %get-tuple-element.554.rest_0_, ...), custom_call_target="tpu_custom_call" | custom-call | flops 1207959552 | bytes 4718592 | tf_op jit(solution)/shard_map/matrix_grad/pallas_call | solution.py:824
  380.5 5.1 all-to-all-start.6
  390.4 9.6 %ortho.3 = bf16[8,128,384]{2,1,0:T(8,128)(2,1)} custom-call(bf16[8,96,384]{2,1,0:T(8,128)(2,1)} %copy-done.24, bf16[4,192,768]{2,1,0:T(8,128)(2,1)} %copy-done.29, f32[12,768]{1,0:T(8,128)} %maximum_add_fusion.1.rest_1_), custom_call_target="tpu_custom_call" | custom-call | flops 1 | bytes 1 | tf_op jit(solution)/shard_map/ortho/pallas_call | solution.py:876
  406.3 6.3 %collective-permute-done.75.up_other = bf16[2,192,768]{2,1,0:T(8,128)(2,1)S(1)} collective-permute-done((bf16[2,192,768]{2,1,0:T(8,128)(2,1)}, bf16[2,192,768]{2,1,0:T(8,128)(2,1)S(1)}, u32[]{:S(2)}, u32[]{:S(2)}) %collective-permute-start.75) | collective-permute-done | bytes 589856 | tf_op jit(solution)/shard_map/ppermute | solution.py:58
  413.7 5.4 %all-to-all-start.7 = ((bf16[8,128,384]{2,1,0:T(8,128)(2,1)}), bf16[8,128,384]{2,1,0:T(8,128)(2,1)S(1)}, u32[]{:S(2)}, u32[]{:S(2)}) async-start(bf16[8,128,384]{2,1,0:T(8,128)(2,1)} %ortho.3), calls=%async_computation.7 | async-start | bytes 1572864 | tf_op jit(solution)/shard_map/all_to_all | solution.py:79
  426.0 9.6 %ortho.4 = bf16[8,96,384]{2,1,0:T(8,128)(2,1)} custom-call(bf16[8,96,384]{2,1,0:T(8,128)(2,1)} %copy-done.24, bf16[4,192,768]{2,1,0:T(8,128)(2,1)} %copy-done.30), custom_call_target="tpu_custom_call" | custom-call | flops 1 | bytes 1 | tf_op jit(solution)/shard_map/ortho/pallas_call | solution.py:876
  436.0 4.2 collective-permute-done.79.up_other
  445.3 31.3 %all_to_all.55.rest_0_ = bf16[4,192,768]{2,1,0:T(8,128)(2,1)} all-to-all(bf16[4,192,768]{2,1,0:T(8,128)(2,1)} %merge.23), channel_id=1, replica_groups={{0,8,16,24},{4,12,20,28},{1,9,17,25},{5,13,21,29},{2,10,18,26},{6,14,22..., dimensions={0} | all-to-all | bytes 2359296 | tf_op jit(solution)/shard_map/all_to_all | solution.py:71
  476.6 3.7 all-to-all-start.9
  480.3 9.6 %ortho.5 = bf16[8,96,384]{2,1,0:T(8,128)(2,1)} custom-call(bf16[8,96,192]{2,1,0:T(8,128)(2,1)} %copy-done.40, bf16[4,192,768]{2,1,0:T(8,128)(2,1)} %all_to_all.55.rest_0_), custom_call_target="tpu_custom_call" | custom-call | flops 1 | bytes 1 | tf_op jit(solution)/shard_map/ortho/pallas_call | solution.py:876
  489.9 5.0 all-to-all-done.9.pieces
  495.0 3.7 all-to-all-start.10
  501.5 2.7 update.3
  505.6 3.2 update.4
  508.8 5.0 all-to-all-done.10.pieces
  514.6 3.2 update.5
  (512 shorter events, 172.6 us)
Async XLA Ops:
  4.1 14.0 %collective-permute-start.2 = (bf16[96,768]{1,0:T(8,128)(2,1)S(1)}, bf16[96,768]{1,0:T(8,128)(2,1)S(1)}, u32[]{:S(2)}, u32[]{:S(2)}) collective-permute-start(bf16[96,768]{1,0:T(8,128)(2,1)S(1)} %pad_maximum_fusion.13), channel_id=1, source_target_pairs={{0,24},{4,28},{8,16},{12,20},{16,8},{20,12},{24,0},{28,4},{1,25},{... | collective-permute-start | bytes 442376 | tf_op jit(solution)/shard_map/ppermute | solution.py:62
  22.8 35.0 %all-to-all-start = ((bf16[4,96,1536]{2,1,0:T(8,128)(2,1)}), bf16[4,96,1536]{2,1,0:T(8,128)(2,1)}, u32[]{:S(2)}, u32[]{:S(2)}) async-start(bf16[4,96,1536]{2,1,0:T(8,128)(2,1)} %broadcast_in_dim.6), calls=%async_computation | async-start | bytes 2359296 | tf_op jit(solution)/shard_map/all_to_all | solution.py:71
  57.8 22.2 %all-to-all-start.1 = ((bf16[4,96,768]{2,1,0:T(8,128)(2,1)}), bf16[4,96,768]{2,1,0:T(8,128)(2,1)S(1)}, u32[]{:S(2)}, u32[]{:S(2)}) async-start(bf16[4,96,768]{2,1,0:T(8,128)(2,1)} %broadcast_in_dim.7), calls=%async_computation.1 | async-start | bytes 1179648 | tf_op jit(solution)/shard_map/all_to_all | solution.py:71
  63.7 15.3 %collective-permute-start.12 = (bf16[4,96,768]{2,1,0:T(8,128)(2,1)S(1)}, bf16[4,96,768]{2,1,0:T(8,128)(2,1)}, u32[]{:S(2)}, u32[]{:S(2)}) collective-permute-start(bf16[4,96,768]{2,1,0:T(8,128)(2,1)S(1)} %get-tuple-element.365), channel_id=1, source_target_pairs={{0,2},{1,3},{2,0},{3,1},{4,6},{5,7},{6,4},{7,5},{8,10},{9,11},{10,... | collective-permute-start | bytes 1769480 | tf_op jit(solution)/shard_map/ppermute | solution.py:58
  65.2 14.8 %collective-permute-start.11 = (bf16[4,96,768]{2,1,0:T(8,128)(2,1)S(1)}, bf16[4,96,768]{2,1,0:T(8,128)(2,1)S(1)}, u32[]{:S(2)}, u32[]{:S(2)}) collective-permute-start(bf16[4,96,768]{2,1,0:T(8,128)(2,1)S(1)} %get-tuple-element.363), channel_id=1, source_target_pairs={{0,4},{4,0},{8,12},{12,8},{16,20},{20,16},{24,28},{28,24},{1,5},{5... | collective-permute-start | bytes 1769480 | tf_op jit(solution)/shard_map/ppermute | solution.py:62
  77.1 18.9 %collective-permute-start.18 = (bf16[400,128]{1,0:T(8,128)(2,1)}, bf16[400,128]{1,0:T(8,128)(2,1)}, u32[]{:S(2)}, u32[]{:S(2)}) collective-permute-start(bf16[400,128]{1,0:T(8,128)(2,1)} %get-tuple-element.360), channel_id=1, source_target_pairs={{0,2},{1,3},{2,0},{3,1},{4,6},{5,7},{6,4},{7,5},{8,10},{9,11},{10,... | collective-permute-start | bytes 307208 | tf_op jit(solution)/shard_map/ppermute | solution.py:58
  82.5 34.6 %collective-permute-start.17 = (bf16[2,4,96,768]{3,2,1,0:T(8,128)(2,1)S(1)}, bf16[2,4,96,768]{3,2,1,0:T(8,128)(2,1)}, u32[]{:S(2)}, u32[]{:S(2)}) collective-permute-start(bf16[2,4,96,768]{3,2,1,0:T(8,128)(2,1)S(1)} %pad_maximum_fusion.1.rest_12_), channel_id=1, source_target_pairs={{0,4},{4,0},{8,12},{12,8},{16,20},{20,16},{24,28},{28,24},{1,5},{5... | collective-permute-start | bytes 3538952 | tf_op jit(solution)/shard_map/ppermute | solution.py:62
  84.1 33.0 %collective-permute-start.15 = (bf16[2,4,96,768]{3,2,1,0:T(8,128)(2,1)S(1)}, bf16[2,4,96,768]{3,2,1,0:T(8,128)(2,1)}, u32[]{:S(2)}, u32[]{:S(2)}) collective-permute-start(bf16[2,4,96,768]{3,2,1,0:T(8,128)(2,1)S(1)} %pad_maximum_fusion.1.rest_12_), channel_id=1, source_target_pairs={{0,1},{1,0},{2,3},{3,2},{4,5},{5,4},{6,7},{7,6},{8,9},{9,8},{10,11... | collective-permute-start | bytes 3538952 | tf_op jit(solution)/shard_map/ppermute | solution.py:58
  84.2 32.8 %collective-permute-start.16 = (bf16[2,4,96,768]{3,2,1,0:T(8,128)(2,1)S(1)}, bf16[2,4,96,768]{3,2,1,0:T(8,128)(2,1)}, u32[]{:S(2)}, u32[]{:S(2)}) collective-permute-start(bf16[2,4,96,768]{3,2,1,0:T(8,128)(2,1)S(1)} %pad_maximum_fusion.rest_8_), channel_id=1, source_target_pairs={{0,2},{1,3},{2,0},{3,1},{4,6},{5,7},{6,4},{7,5},{8,10},{9,11},{10,... | collective-permute-start | bytes 3538952 | tf_op jit(solution)/shard_map/ppermute | solution.py:58
  84.9 32.2 %collective-permute-start.14 = (bf16[2,4,96,768]{3,2,1,0:T(8,128)(2,1)S(1)}, bf16[2,4,96,768]{3,2,1,0:T(8,128)(2,1)}, u32[]{:S(2)}, u32[]{:S(2)}) collective-permute-start(bf16[2,4,96,768]{3,2,1,0:T(8,128)(2,1)S(1)} %pad_maximum_fusion.rest_8_), channel_id=1, source_target_pairs={{0,1},{1,0},{2,3},{3,2},{4,5},{5,4},{6,7},{7,6},{8,9},{9,8},{10,11... | collective-permute-start | bytes 3538952 | tf_op jit(solution)/shard_map/ppermute | solution.py:58
  85.2 45.2 %all-to-all-start.2 = ((bf16[4,96,1536]{2,1,0:T(8,128)(2,1)}), bf16[4,96,1536]{2,1,0:T(8,128)(2,1)}, u32[]{:S(2)}, u32[]{:S(2)}) async-start(bf16[4,96,1536]{2,1,0:T(8,128)(2,1)} %broadcast_in_dim.8), calls=%async_computation.2 | async-start | bytes 2359296 | tf_op jit(solution)/shard_map/all_to_all | solution.py:71
  96.1 18.8 %collective-permute-start.19 = (bf16[400,128]{1,0:T(8,128)(2,1)}, bf16[400,128]{1,0:T(8,128)(2,1)S(1)}, u32[]{:S(2)}, u32[]{:S(2)}) collective-permute-start(bf16[400,128]{1,0:T(8,128)(2,1)} %copy-done.57), channel_id=1, source_target_pairs={{0,2},{1,3},{2,0},{3,1},{4,6},{5,7},{6,4},{7,5},{8,10},{9,11},{10,... | collective-permute-start | bytes 307208 | tf_op jit(solution)/shard_map/ppermute | solution.py:58
  123.0 13.4 %collective-permute-start.31 = (f32[2,768]{1,0:T(2,128)}, f32[2,768]{1,0:T(2,128)}, u32[]{:S(2)}, u32[]{:S(2)}) collective-permute-start(f32[2,768]{1,0:T(2,128)} %param.27), channel_id=1, source_target_pairs={{0,1},{1,0},{2,3},{3,2},{4,5},{5,4},{6,7},{7,6},{8,9},{9,8},{10,11... | collective-permute-start | bytes 18440 | tf_op jit(solution)/shard_map/ppermute | solution.py:58
  130.5 20.4 %collective-permute-start.28 = (bf16[2,4,96,384]{3,2,1,0:T(8,128)(2,1)S(1)}, bf16[2,4,96,384]{3,2,1,0:T(8,128)(2,1)}, u32[]{:S(2)}, u32[]{:S(2)}) collective-permute-start(bf16[2,4,96,384]{3,2,1,0:T(8,128)(2,1)S(1)} %pad_maximum_fusion.8.rest_4_), channel_id=1, source_target_pairs={{0,4},{4,0},{8,12},{12,8},{16,20},{20,16},{24,28},{28,24},{1,5},{5... | collective-permute-start | bytes 1769480 | tf_op jit(solution)/shard_map/ppermute | solution.py:62
  131.8 19.7 %collective-permute-start.27 = (bf16[2,4,96,384]{3,2,1,0:T(8,128)(2,1)S(1)}, bf16[2,4,96,384]{3,2,1,0:T(8,128)(2,1)S(1)}, u32[]{:S(2)}, u32[]{:S(2)}) collective-permute-start(bf16[2,4,96,384]{3,2,1,0:T(8,128)(2,1)S(1)} %pad_maximum_fusion.7.rest_0_), channel_id=1, source_target_pairs={{0,2},{1,3},{2,0},{3,1},{4,6},{5,7},{6,4},{7,5},{8,10},{9,11},{10,... | collective-permute-start | bytes 1769480 | tf_op jit(solution)/shard_map/ppermute | solution.py:58
  134.8 23.6 %collective-permute-start.30 = (bf16[4,96,768]{2,1,0:T(8,128)(2,1)S(1)}, bf16[4,96,768]{2,1,0:T(8,128)(2,1)S(1)}, u32[]{:S(2)}, u32[]{:S(2)}) collective-permute-start(bf16[4,96,768]{2,1,0:T(8,128)(2,1)S(1)} %get-tuple-element.707), channel_id=1, source_target_pairs={{0,2},{1,3},{2,0},{3,1},{4,6},{5,7},{6,4},{7,5},{8,10},{9,11},{10,... | collective-permute-start | bytes 1769480 | tf_op jit(solution)/shard_map/ppermute | solution.py:58
  135.5 22.9 %collective-permute-start.29 = (bf16[4,96,768]{2,1,0:T(8,128)(2,1)S(1)}, bf16[4,96,768]{2,1,0:T(8,128)(2,1)S(1)}, u32[]{:S(2)}, u32[]{:S(2)}) collective-permute-start(bf16[4,96,768]{2,1,0:T(8,128)(2,1)S(1)} %get-tuple-element.708), channel_id=1, source_target_pairs={{0,4},{4,0},{8,12},{12,8},{16,20},{20,16},{24,28},{28,24},{1,5},{5... | collective-permute-start | bytes 1769480 | tf_op jit(solution)/shard_map/ppermute | solution.py:62
  137.8 21.5 %collective-permute-start.26 = (bf16[2,4,96,384]{3,2,1,0:T(8,128)(2,1)S(1)}, bf16[2,4,96,384]{3,2,1,0:T(8,128)(2,1)S(1)}, u32[]{:S(2)}, u32[]{:S(2)}) collective-permute-start(bf16[2,4,96,384]{3,2,1,0:T(8,128)(2,1)S(1)} %pad_maximum_fusion.8.rest_4_), channel_id=1, source_target_pairs={{0,1},{1,0},{2,3},{3,2},{4,5},{5,4},{6,7},{7,6},{8,9},{9,8},{10,11... | collective-permute-start | bytes 1769480 | tf_op jit(solution)/shard_map/ppermute | solution.py:58
  159.6 28.5 %collective-permute-start.42 = (bf16[2,4,96,768]{3,2,1,0:T(8,128)(2,1)S(1)}, bf16[2,4,96,768]{3,2,1,0:T(8,128)(2,1)}, u32[]{:S(2)}, u32[]{:S(2)}) collective-permute-start(bf16[2,4,96,768]{3,2,1,0:T(8,128)(2,1)S(1)} %pad_maximum_fusion.3.rest_12_), channel_id=1, source_target_pairs={{0,4},{4,0},{8,12},{12,8},{16,20},{20,16},{24,28},{28,24},{1,5},{5... | collective-permute-start | bytes 3538952 | tf_op jit(solution)/shard_map/ppermute | solution.py:62
  160.2 28.9 %collective-permute-start.41 = (bf16[2,4,96,768]{3,2,1,0:T(8,128)(2,1)S(1)}, bf16[2,4,96,768]{3,2,1,0:T(8,128)(2,1)}, u32[]{:S(2)}, u32[]{:S(2)}) collective-permute-start(bf16[2,4,96,768]{3,2,1,0:T(8,128)(2,1)S(1)} %pad_maximum_fusion.2.rest_8_), channel_id=1, source_target_pairs={{0,2},{1,3},{2,0},{3,1},{4,6},{5,7},{6,4},{7,5},{8,10},{9,11},{10,... | collective-permute-start | bytes 3538952 | tf_op jit(solution)/shard_map/ppermute | solution.py:58
  174.4 16.8 %collective-permute-start.39 = (bf16[400,128]{1,0:T(8,128)(2,1)}, bf16[400,128]{1,0:T(8,128)(2,1)S(1)}, u32[]{:S(2)}, u32[]{:S(2)}) collective-permute-start(bf16[400,128]{1,0:T(8,128)(2,1)} %get-tuple-element.407), channel_id=1, source_target_pairs={{0,2},{1,3},{2,0},{3,1},{4,6},{5,7},{6,4},{7,5},{8,10},{9,11},{10,... | collective-permute-start | bytes 307208 | tf_op jit(solution)/shard_map/ppermute | solution.py:58
  175.7 16.9 %collective-permute-start.40 = (bf16[400,128]{1,0:T(8,128)(2,1)S(1)}, bf16[400,128]{1,0:T(8,128)(2,1)S(1)}, u32[]{:S(2)}, u32[]{:S(2)}) collective-permute-start(bf16[400,128]{1,0:T(8,128)(2,1)S(1)} %collective-permute-done.38.recv_one), channel_id=1, source_target_pairs={{0,2},{1,3},{2,0},{3,1},{4,6},{5,7},{6,4},{7,5},{8,10},{9,11},{10,... | collective-permute-start | bytes 307208 | tf_op jit(solution)/shard_map/ppermute | solution.py:58
  193.2 21.7 %all-to-all-start.3 = ((bf16[8,96,384]{2,1,0:T(8,128)(2,1)}), bf16[8,96,384]{2,1,0:T(8,128)(2,1)S(1)}, u32[]{:S(2)}, u32[]{:S(2)}) async-start(bf16[8,96,384]{2,1,0:T(8,128)(2,1)} %pad_maximum_fusion.4), calls=%async_computation.3 | async-start | bytes 1179648 | tf_op jit(solution)/shard_map/all_to_all | solution.py:79
  223.5 15.8 %collective-permute-start.46 = (bf16[2,192,768]{2,1,0:T(8,128)(2,1)}, bf16[2,192,768]{2,1,0:T(8,128)(2,1)S(1)}, u32[]{:S(2)}, u32[]{:S(2)}) collective-permute-start(bf16[2,192,768]{2,1,0:T(8,128)(2,1)} %get-tuple-element.442), channel_id=1, source_target_pairs={{0,2},{1,3},{2,0},{3,1},{4,6},{5,7},{6,4},{7,5},{8,10},{9,11},{10,... | collective-permute-start | bytes 1769480 | tf_op jit(solution)/shard_map/ppermute | solution.py:58
  224.8 15.3 %collective-permute-start.47 = (bf16[2,192,768]{2,1,0:T(8,128)(2,1)}, bf16[2,192,768]{2,1,0:T(8,128)(2,1)S(1)}, u32[]{:S(2)}, u32[]{:S(2)}) collective-permute-start(bf16[2,192,768]{2,1,0:T(8,128)(2,1)} %get-tuple-element.443), channel_id=1, source_target_pairs={{0,4},{4,0},{8,12},{12,8},{16,20},{20,16},{24,28},{28,24},{1,5},{5... | collective-permute-start | bytes 1769480 | tf_op jit(solution)/shard_map/ppermute | solution.py:62
  243.7 14.6 %collective-permute-start.52 = (bf16[192,768]{1,0:T(8,128)(2,1)}, bf16[192,768]{1,0:T(8,128)(2,1)S(1)}, u32[]{:S(2)}, u32[]{:S(2)}) collective-permute-start(bf16[192,768]{1,0:T(8,128)(2,1)} %get-tuple-element.463), channel_id=1, source_target_pairs={{0,4},{4,0},{8,12},{12,8},{16,20},{20,16},{24,28},{28,24},{1,5},{5... | collective-permute-start | bytes 884744 | tf_op jit(solution)/shard_map/ppermute | solution.py:62
  259.0 19.7 %collective-permute-start.54 = (bf16[2,192,768]{2,1,0:T(8,128)(2,1)}, bf16[2,192,768]{2,1,0:T(8,128)(2,1)S(1)}, u32[]{:S(2)}, u32[]{:S(2)}) collective-permute-start(bf16[2,192,768]{2,1,0:T(8,128)(2,1)} %get-tuple-element.469), channel_id=1, source_target_pairs={{0,2},{1,3},{2,0},{3,1},{4,6},{5,7},{6,4},{7,5},{8,10},{9,11},{10,... | collective-permute-start | bytes 1769480 | tf_op jit(solution)/shard_map/ppermute | solution.py:58
  259.6 19.0 %collective-permute-start.55 = (bf16[2,192,768]{2,1,0:T(8,128)(2,1)}, bf16[2,192,768]{2,1,0:T(8,128)(2,1)S(1)}, u32[]{:S(2)}, u32[]{:S(2)}) collective-permute-start(bf16[2,192,768]{2,1,0:T(8,128)(2,1)} %get-tuple-element.470), channel_id=1, source_target_pairs={{0,4},{4,0},{8,12},{12,8},{16,20},{20,16},{24,28},{28,24},{1,5},{5... | collective-permute-start | bytes 1769480 | tf_op jit(solution)/shard_map/ppermute | solution.py:62
  260.2 18.4 %all-to-all-start.4 = ((bf16[8,96,192]{2,1,0:T(8,128)(2,1)}), bf16[8,96,192]{2,1,0:T(8,128)(2,1)S(1)}, u32[]{:S(2)}, u32[]{:S(2)}) async-start(bf16[8,96,192]{2,1,0:T(8,128)(2,1)} %fusion.10), calls=%async_computation.4 | async-start | bytes 786432 | tf_op jit(solution)/shard_map/all_to_all | solution.py:79
  295.0 14.9 %collective-permute-start.60 = (bf16[2,192,768]{2,1,0:T(8,128)(2,1)}, bf16[2,192,768]{2,1,0:T(8,128)(2,1)S(1)}, u32[]{:S(2)}, u32[]{:S(2)}) collective-permute-start(bf16[2,192,768]{2,1,0:T(8,128)(2,1)} %get-tuple-element.501), channel_id=1, source_target_pairs={{0,2},{1,3},{2,0},{3,1},{4,6},{5,7},{6,4},{7,5},{8,10},{9,11},{10,... | collective-permute-start | bytes 1769480 | tf_op jit(solution)/shard_map/ppermute | solution.py:58
  296.4 14.1 %collective-permute-start.61 = (bf16[2,192,768]{2,1,0:T(8,128)(2,1)}, bf16[2,192,768]{2,1,0:T(8,128)(2,1)S(1)}, u32[]{:S(2)}, u32[]{:S(2)}) collective-permute-start(bf16[2,192,768]{2,1,0:T(8,128)(2,1)} %get-tuple-element.502), channel_id=1, source_target_pairs={{0,4},{4,0},{8,12},{12,8},{16,20},{20,16},{24,28},{28,24},{1,5},{5... | collective-permute-start | bytes 1769480 | tf_op jit(solution)/shard_map/ppermute | solution.py:62
  315.5 39.3 %all-to-all-start.5 = ((bf16[4,192,768]{2,1,0:T(8,128)(2,1)}), bf16[4,192,768]{2,1,0:T(8,128)(2,1)S(1)}, u32[]{:S(2)}, u32[]{:S(2)}) async-start(bf16[4,192,768]{2,1,0:T(8,128)(2,1)} %merge.16), calls=%async_computation.5 | async-start | bytes 2359296 | tf_op jit(solution)/shard_map/all_to_all | solution.py:71
  322.8 15.1 %collective-permute-start.66 = (bf16[192,768]{1,0:T(8,128)(2,1)}, bf16[192,768]{1,0:T(8,128)(2,1)S(1)}, u32[]{:S(2)}, u32[]{:S(2)}) collective-permute-start(bf16[192,768]{1,0:T(8,128)(2,1)} %get-tuple-element.522), channel_id=1, source_target_pairs={{0,4},{4,0},{8,12},{12,8},{16,20},{20,16},{24,28},{28,24},{1,5},{5... | collective-permute-start | bytes 884744 | tf_op jit(solution)/shard_map/ppermute | solution.py:62
  324.2 13.7 %collective-permute-start.67 = (bf16[192,768]{1,0:T(8,128)(2,1)}, bf16[192,768]{1,0:T(8,128)(2,1)S(1)}, u32[]{:S(2)}, u32[]{:S(2)}) collective-permute-start(bf16[192,768]{1,0:T(8,128)(2,1)} %get-tuple-element.523), channel_id=1, source_target_pairs={{0,2},{1,3},{2,0},{3,1},{4,6},{5,7},{6,4},{7,5},{8,10},{9,11},{10,... | collective-permute-start | bytes 884744 | tf_op jit(solution)/shard_map/ppermute | solution.py:58
  337.9 16.9 %collective-permute-start.68 = (bf16[2,192,768]{2,1,0:T(8,128)(2,1)}, bf16[2,192,768]{2,1,0:T(8,128)(2,1)S(1)}, u32[]{:S(2)}, u32[]{:S(2)}) collective-permute-start(bf16[2,192,768]{2,1,0:T(8,128)(2,1)} %get-tuple-element.536), channel_id=1, source_target_pairs={{0,2},{1,3},{2,0},{3,1},{4,6},{5,7},{6,4},{7,5},{8,10},{9,11},{10,... | collective-permute-start | bytes 1769480 | tf_op jit(solution)/shard_map/ppermute | solution.py:58
  338.6 16.2 %collective-permute-start.69 = (bf16[2,192,768]{2,1,0:T(8,128)(2,1)}, bf16[2,192,768]{2,1,0:T(8,128)(2,1)S(1)}, u32[]{:S(2)}, u32[]{:S(2)}) collective-permute-start(bf16[2,192,768]{2,1,0:T(8,128)(2,1)} %get-tuple-element.537), channel_id=1, source_target_pairs={{0,4},{4,0},{8,12},{12,8},{16,20},{20,16},{24,28},{28,24},{1,5},{5... | collective-permute-start | bytes 1769480 | tf_op jit(solution)/shard_map/ppermute | solution.py:62
  380.5 33.2 %all-to-all-start.6 = ((bf16[4,192,768]{2,1,0:T(8,128)(2,1)}), bf16[4,192,768]{2,1,0:T(8,128)(2,1)S(1)}, u32[]{:S(2)}, u32[]{:S(2)}) async-start(bf16[4,192,768]{2,1,0:T(8,128)(2,1)} %merge.19), calls=%async_computation.6 | async-start | bytes 2359296 | tf_op jit(solution)/shard_map/all_to_all | solution.py:71
  385.6 16.5 %collective-permute-start.77 = (bf16[2,192,768]{2,1,0:T(8,128)(2,1)}, bf16[2,192,768]{2,1,0:T(8,128)(2,1)S(1)}, u32[]{:S(2)}, u32[]{:S(2)}) collective-permute-start(bf16[2,192,768]{2,1,0:T(8,128)(2,1)} %get-tuple-element.584), channel_id=1, source_target_pairs={{0,2},{1,3},{2,0},{3,1},{4,6},{5,7},{6,4},{7,5},{8,10},{9,11},{10,... | collective-permute-start | bytes 1769480 | tf_op jit(solution)/shard_map/ppermute | solution.py:58
  387.0 16.6 %collective-permute-start.78 = (bf16[2,192,768]{2,1,0:T(8,128)(2,1)}, bf16[2,192,768]{2,1,0:T(8,128)(2,1)}, u32[]{:S(2)}, u32[]{:S(2)}) collective-permute-start(bf16[2,192,768]{2,1,0:T(8,128)(2,1)} %get-tuple-element.585), channel_id=1, source_target_pairs={{0,4},{4,0},{8,12},{12,8},{16,20},{20,16},{24,28},{28,24},{1,5},{5... | collective-permute-start | bytes 1769480 | tf_op jit(solution)/shard_map/ppermute | solution.py:62
  387.7 24.9 %collective-permute-start.75 = (bf16[2,192,768]{2,1,0:T(8,128)(2,1)}, bf16[2,192,768]{2,1,0:T(8,128)(2,1)S(1)}, u32[]{:S(2)}, u32[]{:S(2)}) collective-permute-start(bf16[2,192,768]{2,1,0:T(8,128)(2,1)} %get-tuple-element.574), channel_id=1, source_target_pairs={{0,2},{1,3},{2,0},{3,1},{4,6},{5,7},{6,4},{7,5},{8,10},{9,11},{10,... | collective-permute-start | bytes 1769480 | tf_op jit(solution)/shard_map/ppermute | solution.py:58
  388.3 25.4 %collective-permute-start.76 = (bf16[2,192,768]{2,1,0:T(8,128)(2,1)}, bf16[2,192,768]{2,1,0:T(8,128)(2,1)S(1)}, u32[]{:S(2)}, u32[]{:S(2)}) collective-permute-start(bf16[2,192,768]{2,1,0:T(8,128)(2,1)} %get-tuple-element.575), channel_id=1, source_target_pairs={{0,4},{4,0},{8,12},{12,8},{16,20},{20,16},{24,28},{28,24},{1,5},{5... | collective-permute-start | bytes 1769480 | tf_op jit(solution)/shard_map/ppermute | solution.py:62
  413.7 31.6 %all-to-all-start.7 = ((bf16[8,128,384]{2,1,0:T(8,128)(2,1)}), bf16[8,128,384]{2,1,0:T(8,128)(2,1)S(1)}, u32[]{:S(2)}, u32[]{:S(2)}) async-start(bf16[8,128,384]{2,1,0:T(8,128)(2,1)} %ortho.3), calls=%async_computation.7 | async-start | bytes 1572864 | tf_op jit(solution)/shard_map/all_to_all | solution.py:79
  419.1 17.0 %collective-permute-start.81 = (bf16[192,768]{1,0:T(8,128)(2,1)}, bf16[192,768]{1,0:T(8,128)(2,1)S(1)}, u32[]{:S(2)}, u32[]{:S(2)}) collective-permute-start(bf16[192,768]{1,0:T(8,128)(2,1)} %get-tuple-element.602), channel_id=1, source_target_pairs={{0,4},{4,0},{8,12},{12,8},{16,20},{20,16},{24,28},{28,24},{1,5},{5... | collective-permute-start | bytes 884744 | tf_op jit(solution)/shard_map/ppermute | solution.py:62
  421.2 14.9 %collective-permute-start.82 = (bf16[192,768]{1,0:T(8,128)(2,1)S(1)}, bf16[192,768]{1,0:T(8,128)(2,1)S(1)}, u32[]{:S(2)}, u32[]{:S(2)}) collective-permute-start(bf16[192,768]{1,0:T(8,128)(2,1)S(1)} %copy-done.107), channel_id=1, source_target_pairs={{0,2},{1,3},{2,0},{3,1},{4,6},{5,7},{6,4},{7,5},{8,10},{9,11},{10,... | collective-permute-start | bytes 884744 | tf_op jit(solution)/shard_map/ppermute | solution.py:58
  424.5 15.8 %collective-permute-start.79 = (bf16[192,768]{1,0:T(8,128)(2,1)}, bf16[192,768]{1,0:T(8,128)(2,1)S(1)}, u32[]{:S(2)}, u32[]{:S(2)}) collective-permute-start(bf16[192,768]{1,0:T(8,128)(2,1)} %get-tuple-element.600), channel_id=1, source_target_pairs={{0,4},{4,0},{8,12},{12,8},{16,20},{20,16},{24,28},{28,24},{1,5},{5... | collective-permute-start | bytes 884744 | tf_op jit(solution)/shard_map/ppermute | solution.py:62
  424.6 15.7 %collective-permute-start.80 = (bf16[192,768]{1,0:T(8,128)(2,1)}, bf16[192,768]{1,0:T(8,128)(2,1)S(1)}, u32[]{:S(2)}, u32[]{:S(2)}) collective-permute-start(bf16[192,768]{1,0:T(8,128)(2,1)} %get-tuple-element.601), channel_id=1, source_target_pairs={{0,2},{1,3},{2,0},{3,1},{4,6},{5,7},{6,4},{7,5},{8,10},{9,11},{10,... | collective-permute-start | bytes 884744 | tf_op jit(solution)/shard_map/ppermute | solution.py:58
  476.6 18.3 %all-to-all-start.9 = ((bf16[8,96,384]{2,1,0:T(8,128)(2,1)}), bf16[8,96,384]{2,1,0:T(8,128)(2,1)S(1)}, u32[]{:S(2)}, u32[]{:S(2)}) async-start(bf16[8,96,384]{2,1,0:T(8,128)(2,1)} %ortho.4), calls=%async_computation.9 | async-start | bytes 1179648 | tf_op jit(solution)/shard_map/all_to_all | solution.py:79
  495.0 18.8 %all-to-all-start.10 = ((bf16[8,96,384]{2,1,0:T(8,128)(2,1)}), bf16[8,96,384]{2,1,0:T(8,128)(2,1)S(1)}, u32[]{:S(2)}, u32[]{:S(2)}) async-start(bf16[8,96,384]{2,1,0:T(8,128)(2,1)} %ortho.5), calls=%async_computation.10 | async-start | bytes 1179648 | tf_op jit(solution)/shard_map/all_to_all | solution.py:79
  (155 other events, 1196.6 us)

commit v5 on v4

--- a/solution.py
+++ b/solution.py
@@ -299,12 +299,15 @@
 
 def project_kernel(plan, resid, vectors, cosine_part, sine_part, feature_map, segment_row, *rest):
     weight_refs, rest = take(rest, plan)
-    phi_query_out, phi_key_out, value_out, query_out, key_out, summary_out, weight, sems = rest
+    phi_query_out, phi_key_out, value_out, centre_out, query_out, key_out, summary_out, weight, sems = rest
     waits = fetch(weight_refs, plan, weight, sems, 0, (0, weight.shape[4]))
     cosine, sine = turn_tables(cosine_part, sine_part)
     unit, _ = norm_parts(resid[...])
     normed = (unit * vectors[0:1, :] + vectors[1:2, :]).astype(BF16)
     width = resid.shape[1] // 4
+    rows = resid.shape[0]
+    shift = jnp.broadcast_to(vectors[1:2, :], (16, resid.shape[1])).astype(BF16)
+    normed = jnp.concatenate([normed, shift], axis=0)
     pieces = [[], [], []]
     for slot in range(4):
         arrive(waits[slot])
@@ -312,7 +315,10 @@
         for which in range(3):
             pieces[which].append(product[:, lanes_of(which, width)])
     queries, key_rows, value_rows = (jnp.concatenate(piece, axis=1) for piece in pieces)
-    value_rows = value_rows.astype(BF16)
+    queries, key_rows = queries[:rows], key_rows[:rows]
+    centre = value_rows[rows : rows + 8]
+    centre_out[...] = centre
+    value_rows = (value_rows[:rows] - centre[0:1]).astype(BF16)
     value_out[...] = value_rows
     map_high, map_low = split_low(wide_map(feature_map))
     in_first, in_last = edge_masks(column_of(segment_row))
@@ -338,7 +344,7 @@
 
 
 def mix_kernel(
-    plans, resid, vectors, bias, phi_query, phi_key, value, segment_row, recv_one, recv_two,
+    plans, resid, vectors, bias, phi_query, phi_key, value, centre, segment_row, recv_one, recv_two,
     recv_three, coefficients, *rest
 ):
     out_refs, up_refs, down_refs, rest = take(rest, *plans)
@@ -371,7 +377,7 @@
         right.append(spread_edges(totals, chunk))
         both = dot_nn(jnp.concatenate(left, axis=1), jnp.concatenate(right, axis=0))
         inverse = 1.0 / (both[:, CHUNK:] + ATTEND_EPSILON)
-        context = both[:, :CHUNK] * inverse
+        context = (both[:, :CHUNK] + centre[0:1, lanes] * both[:, CHUNK:]) * inverse
         inverse_out[:, lanes] = inverse
         context_out[:, lanes] = context
         contexts.append(context.astype(BF16))
@@ -403,7 +409,7 @@
 
 
 def back_mix_kernel(
-    plans, grad, vectors, middle, slope, inverse, context, phi_query, segment_row, *rest
+    plans, grad, vectors, middle, slope, inverse, context, centre, phi_query, segment_row, *rest
 ):
     out_refs, up_refs, down_refs, rest = take(rest, *plans)
     (upper_keep, pack_out, middle_grad_out, numer_out, denom_out, summary_out, vector_out,
@@ -448,7 +454,7 @@
         lanes = lanes_of(chunk, CHUNK)
         feats = lanes_of(chunk, FEAT_CHUNK)
         numer = context_grad[:, lanes] * inverse[:, lanes]
-        denom = -dot_nn((numer * context[:, lanes]).astype(BF16), head_ones)
+        denom = -dot_nn((numer * (context[:, lanes] - centre[0:1, lanes])).astype(BF16), head_ones)
         numer = numer.astype(BF16)
         denom = denom.astype(BF16)
         numer_out[:, lanes] = numer
@@ -705,6 +711,7 @@
         shape((rows, feats), BF16),
         shape((rows, feats), BF16),
         shape((rows, width), BF16),
+        shape((8, width)),
         shape((rows, width)),
         shape((rows, width)),
         shape((feats + TOTAL_ROWS, 2 * HEAD_DIM), BF16),
@@ -719,7 +726,7 @@
         8 * width * width,
     )(resid, vectors, tables.cosine, tables.sine, feature_map, tables.row, *flat(weight))
     state = SimpleNamespace(input=resid)
-    state.phi_query, state.phi_key, state.value, state.query, state.key, state.summary = results
+    state.phi_query, state.phi_key, state.value, state.centre, state.query, state.key, state.summary = results
     return state
 
 
@@ -748,13 +755,13 @@
     results = call(
         partial(mix_kernel, plans),
         "mix",
-        vmem(10) + scalars() + anywhere(len(refs)),
+        vmem(11) + scalars() + anywhere(len(refs)),
         outs,
         mix_scratch(width, plans),
         2 * rows * width * width * 12,
         20 * width * width,
     )(
-        resid, vectors, bias, state.phi_query, state.phi_key, state.value, tables.row,
+        resid, vectors, bias, state.phi_query, state.phi_key, state.value, state.centre, tables.row,
         *received, tables.shares, *refs,
     )
     (state.context, state.inverse, state.middle, state.slope, state.active_keep, state.mix_pack,
@@ -779,13 +786,13 @@
     results = call(
         partial(back_mix_kernel, plans),
         "back_mix",
-        vmem(8) + anywhere(len(refs)),
+        vmem(9) + anywhere(len(refs)),
         outs,
         mix_scratch(width, plans),
         2 * rows * width * width * 11,
         20 * width * width,
     )(
-        grad, vectors, state.middle, state.slope, state.inverse, state.context, state.phi_query,
+        grad, vectors, state.middle, state.slope, state.inverse, state.context, state.centre, state.phi_query,
         tables.row, *refs,
     )
     (state.upper_keep, state.back_pack, state.middle_grad, state.numer, state.denom, state.back_summary,

time: 528 us -> 528 us (level)
  transfers between devices with their start and end apart: 93 -> 93, of which waited for: 38 -> 37; matrix products, arithmetic and copies ran while one was open for 9% -> 9% of each run, Pallas kernels for 36% -> 37%
where the time goes in v5:
time: 528 us; the launch traced here: 518 us
  Pallas kernels  200 us (38%)
  waiting for transfers between devices  114 us (22%)
  starting transfers between devices  111 us (21%)
  local copies, waits for them, and re-layouts  42.5 us (8%)
  blocking collectives  31.3 us (6%)
  other arithmetic  16.7 us (3%)
    ppermute x60, waiting for transfers between devices, swap_head(): lax.ppermute(values, 'head', [(h, h ^ offset) for h in range(lax.axis_siz...  67.7 us
    ppermute x60, starting transfers between devices, swap_head(): lax.ppermute(values, 'head', [(h, h ^ offset) for h in range(lax.axis_siz...  37.2 us
    ppermute x23, waiting for transfers between devices, swap_dp(): lax.ppermute(values, 'dp', [(d, d ^ offset) for d in range(lax.axis_size(...  34.8 us
    pallas_call x6, Pallas kernels, matrix_grad(): call(partial(grad_kernel, quick, splits), 'matrix_grad', vmem(2 + len(lef...  32 us
    all_to_all x1, blocking collectives, swap_line(): lax.all_to_all(parts, 'dp', split_axis=0, concat_axis=0, axis_index_group...  31.3 us
    pallas_call x12, Pallas kernels, merge(): return call(kernel, 'merge', vmem(len(operands)), outs, [], 1, 1)(*operands)  30.9 us
    pallas_call x2, Pallas kernels, back_project(): call(partial(back_project_kernel, plan), 'back_project', vmem(21) + scala...  29.1 us
    pallas_call x3, Pallas kernels, orthogonalize(): call(partial(ortho_kernel, place, len(terms)), 'ortho', vmem(1 + len(term...  28.9 us
  transfers between devices with their start and end apart: 93, of which 37 were waited for; matrix products, arithmetic and copies ran while one was open for 9% of the time, Pallas kernels for 37%

profile of v5, /device:TPU:0, one launch (start us, length us, event | category | flops | bytes accessed | tf_op | source)
XLA Modules:
  0.0 518.1 jit_solution(17462193814786530262)
XLA Ops:
  4.1 5.1 collective-permute-start.2
  18.1 3.6 collective-permute-done.1
  22.8 4.3 all-to-all-start
  31.1 4.3 collective-permute-done.3
  44.6 5.6 %collective-permute-done.6.rest_6_ = bf16[2,4,96,384]{3,2,1,0:T(8,128)(2,1)S(1)} collective-permute-done((bf16[2,4,96,384]{3,2,1,0:T(8,128)(2,1)S(1)}, bf16[2,4,96,384]{3,2,1,0:T(8,128)(2,1)S(1)}, u32[]{:S(2)}, u32[]{:S(2)}) %collective-permute-start.6) | collective-permute-done | bytes 589856 | tf_op jit(solution)/shard_map/ppermute | solution.py:62
  57.8 4.5 all-to-all-start.1
  68.1 9.3 %project.2 = (bf16[256,384]{1,0:T(8,128)(2,1)}, bf16[256,384]{1,0:T(8,128)(2,1)}, bf16[256,768]{1,0:T(8,128)(2,1)}, f32[8,768]{1,0:T(8,128)}, f32[256,768]{1,0:T...) custom-call(f32[256,768]{1,0:T(8,128)} %convert_element_type.66.resid, f32[5,768]{1,0:T(8,128)} %get-tuple-element.746.vectors, ...), custom_call_target="tpu_custom_call" | custom-call | flops 1358954496 | bytes 4718592 | tf_op jit(solution)/shard_map/project/pallas_call | solution.py:719
  85.2 5.3 %all-to-all-start.2 = ((bf16[4,96,1536]{2,1,0:T(8,128)(2,1)}), bf16[4,96,1536]{2,1,0:T(8,128)(2,1)}, u32[]{:S(2)}, u32[]{:S(2)}) async-start(bf16[4,96,1536]{2,1,0:T(8,128)(2,1)} %broadcast_in_dim.8), calls=%async_computation.2 | async-start | bytes 2359296 | tf_op jit(solution)/shard_map/all_to_all | solution.py:71
  99.6 15.3 %collective-permute-done.19.recv_three = bf16[400,128]{1,0:T(8,128)(2,1)S(1)} collective-permute-done((bf16[400,128]{1,0:T(8,128)(2,1)}, bf16[400,128]{1,0:T(8,128)(2,1)S(1)}, u32[]{:S(2)}, u32[]{:S(2)}) %collective-permute-start.19) | collective-permute-done | bytes 102432 | tf_op jit(solution)/shard_map/ppermute | solution.py:58
  123.6 6.5 %collective-permute-done.24 = bf16[4,96,384]{2,1,0:T(8,128)(2,1)S(1)} collective-permute-done((bf16[4,96,384]{2,1,0:T(8,128)(2,1)S(1)}, bf16[4,96,384]{2,1,0:T(8,128)(2,1)S(1)}, u32[]{:S(2)}, u32[]{:S(2)}) %collective-permute-start.24) | collective-permute-done | bytes 294944 | tf_op jit(solution)/shard_map/ppermute | solution.py:58
  137.8 13.1 %mix.2 = (f32[256,768]{1,0:T(8,128)}, f32[256,768]{1,0:T(8,128)}, f32[256,768]{1,0:T(8,128)}, bf16[4,256,768]{2,1,0:T(8,128)(2,1)}, bf16[2,256,768]{2,1,0:T(8,12...) custom-call(f32[256,768]{1,0:T(8,128)} %convert_element_type.66.resid, f32[5,768]{1,0:T(8,128)} %get-tuple-element.746.vectors, ...), custom_call_target="tpu_custom_call" | custom-call | flops 3623878656 | bytes 11796480 | tf_op jit(solution)/shard_map/mix/pallas_call | solution.py:755
  151.5 6.9 %collective-permute-done.30 = bf16[4,96,768]{2,1,0:T(8,128)(2,1)S(1)} collective-permute-done((bf16[4,96,768]{2,1,0:T(8,128)(2,1)S(1)}, bf16[4,96,768]{2,1,0:T(8,128)(2,1)S(1)}, u32[]{:S(2)}, u32[]{:S(2)}) %collective-permute-start.30) | collective-permute-done | bytes 589856 | tf_op jit(solution)/shard_map/ppermute | solution.py:58
  165.7 8.8 %project.3 = (bf16[256,384]{1,0:T(8,128)(2,1)}, bf16[256,384]{1,0:T(8,128)(2,1)}, bf16[256,768]{1,0:T(8,128)(2,1)}, f32[8,768]{1,0:T(8,128)}, f32[256,768]{1,0:T...) custom-call(f32[256,768]{1,0:T(8,128)} %get-tuple-element.405.resid, f32[5,768]{1,0:T(8,128)} %get-tuple-element.745.vectors, ...), custom_call_target="tpu_custom_call" | custom-call | flops 1358954496 | bytes 4718592 | tf_op jit(solution)/shard_map/project/pallas_call | solution.py:719
  176.8 11.3 %collective-permute-done.42.rest_14_ = bf16[2,4,96,768]{3,2,1,0:T(8,128)(2,1)} collective-permute-done((bf16[2,4,96,768]{3,2,1,0:T(8,128)(2,1)S(1)}, bf16[2,4,96,768]{3,2,1,0:T(8,128)(2,1)}, u32[]{:S(2)}, u32[]{:S(2)}) %collective-permute-start.42) | collective-permute-done | bytes 1179680 | tf_op jit(solution)/shard_map/ppermute | solution.py:62
  193.2 5.7 %all-to-all-start.3 = ((bf16[8,96,384]{2,1,0:T(8,128)(2,1)}), bf16[8,96,384]{2,1,0:T(8,128)(2,1)S(1)}, u32[]{:S(2)}, u32[]{:S(2)}) async-start(bf16[8,96,384]{2,1,0:T(8,128)(2,1)} %pad_maximum_fusion.4), calls=%async_computation.3 | async-start | bytes 1179648 | tf_op jit(solution)/shard_map/all_to_all | solution.py:79
  201.0 12.6 %mix.3 = (f32[256,768]{1,0:T(8,128)}, f32[256,768]{1,0:T(8,128)}, f32[256,768]{1,0:T(8,128)}, bf16[4,256,768]{2,1,0:T(8,128)(2,1)}, bf16[2,256,768]{2,1,0:T(8,12...) custom-call(f32[256,768]{1,0:T(8,128)} %get-tuple-element.405.resid, f32[5,768]{1,0:T(8,128)} %get-tuple-element.745.vectors, ...), custom_call_target="tpu_custom_call" | custom-call | flops 3623878656 | bytes 11796480 | tf_op jit(solution)/shard_map/mix/pallas_call | solution.py:755
  214.9 3.1 collective-permute-done.45.right_other.rest_1_
  219.0 4.4 matrix_grad.6
  226.3 13.0 %back_mix.2 = (bf16[2,256,768]{2,1,0:T(8,128)(2,1)}, bf16[3,256,768]{2,1,0:T(8,128)(2,1)}, f32[256,768]{1,0:T(8,128)}, bf16[256,768]{1,0:T(8,128)(2,1)}, bf16[25...) custom-call(f32[256,768]{1,0:T(8,128)} %convert_multiply_fusion.grad, ...), custom_call_target="tpu_custom_call" | custom-call | flops 3321888768 | bytes 11796480 | tf_op jit(solution)/shard_map/back_mix/pallas_call | solution.py:786
  247.9 4.9 matrix_grad.7
  252.8 4.3 collective-permute-done.50.back_two
  260.2 4.7 all-to-all-start.4
  264.9 13.7 %back_project.2 = (bf16[2,256,768]{2,1,0:T(8,128)(2,1)}, bf16[4,256,768]{2,1,0:T(8,128)(2,1)}, f32[256,768]{1,0:T(8,128)}, f32[8,768]{1,0:T(8,128)}) custom-call(f32[256,768]{1,0:T(8,128)} %get-tuple-element.405.resid, f32[5,768]{1,0:T(8,128)} %get-tuple-element.745.vectors, f32[256,32]{1,0:T(8,128)} %get-tuple-element.355.cosine_part, ...), custom_call_target="tpu_custom_call" | custom-call | flops 2415919104 | bytes 4718592 | tf_op jit(solution)/shard_map/back_project/pallas_call | solution.py:811
  287.5 6.1 %matrix_grad.8 = (bf16[2,192,768]{2,1,0:T(8,128)(2,1)}, bf16[2,192,768]{2,1,0:T(8,128)(2,1)}, bf16[2,192,768]{2,1,0:T(8,128)(2,1)}, bf16[2,192,768]{2,1,0:T(8,128)(2,1)}) custom-call(bf16[2,256,768]{2,1,0:T(8,128)(2,1)} %get-tuple-element.472.right_own, bf16[4,256,768]{2,1,0:T(8,128)(2,1)} %copy-done.4, bf16[4,256,768]{2,1,0:T(8,128)(2,1)} %get-tuple-element.479.rest_0_, ...), custom_call_target="tpu_custom_call" | custom-call | flops 1207959552 | bytes 4718592 | tf_op jit(solution)/shard_map/matrix_grad/pallas_call | solution.py:831
  296.8 13.2 %back_mix.3 = (bf16[2,256,768]{2,1,0:T(8,128)(2,1)}, bf16[3,256,768]{2,1,0:T(8,128)(2,1)}, f32[256,768]{1,0:T(8,128)}, bf16[256,768]{1,0:T(8,128)(2,1)}, bf16[25...) custom-call(f32[256,768]{1,0:T(8,128)} %get-tuple-element.497.grad, ...), custom_call_target="tpu_custom_call" | custom-call | flops 3321888768 | bytes 11796480 | tf_op jit(solution)/shard_map/back_mix/pallas_call | solution.py:786
  315.5 4.5 all-to-all-start.5
  320.1 2.7 merge.14
  326.9 5.1 matrix_grad.9
  332.1 4.4 collective-permute-done.64.back_two
  339.4 15.4 %back_project.3 = (bf16[2,256,768]{2,1,0:T(8,128)(2,1)}, bf16[4,256,768]{2,1,0:T(8,128)(2,1)}, f32[256,768]{1,0:T(8,128)}, f32[8,768]{1,0:T(8,128)}) custom-call(f32[256,768]{1,0:T(8,128)} %convert_element_type.66.resid, f32[5,768]{1,0:T(8,128)} %get-tuple-element.746.vectors, f32[256,32]{1,0:T(8,128)} %get-tuple-element.355.cosine_part, ...), custom_call_target="tpu_custom_call" | custom-call | flops 2415919104 | bytes 4718592 | tf_op jit(solution)/shard_map/back_project/pallas_call | solution.py:811
  357.3 5.2 %matrix_grad.10 = (bf16[2,192,768]{2,1,0:T(8,128)(2,1)}, bf16[2,192,768]{2,1,0:T(8,128)(2,1)}, bf16[2,192,768]{2,1,0:T(8,128)(2,1)}, bf16[2,192,768]{2,1,0:T(8,128)(2,1)}) custom-call(bf16[2,256,768]{2,1,0:T(8,128)(2,1)} %get-tuple-element.533.right_own, bf16[3,256,768]{2,1,0:T(8,128)(2,1)} %copy-done.42, bf16[3,256,768]{2,1,0:T(8,128)(2,1)} %get-tuple-element.480.rest_0_, ...), custom_call_target="tpu_custom_call" | custom-call | flops 1207959552 | bytes 4718592 | tf_op jit(solution)/shard_map/matrix_grad/pallas_call | solution.py:831
  368.8 6.2 %matrix_grad.11 = (bf16[2,192,768]{2,1,0:T(8,128)(2,1)}, bf16[2,192,768]{2,1,0:T(8,128)(2,1)}, bf16[2,192,768]{2,1,0:T(8,128)(2,1)}, bf16[2,192,768]{2,1,0:T(8,128)(2,1)}) custom-call(bf16[2,256,768]{2,1,0:T(8,128)(2,1)} %get-tuple-element.532.right_own, bf16[4,256,768]{2,1,0:T(8,128)(2,1)} %copy-done.20, bf16[4,256,768]{2,1,0:T(8,128)(2,1)} %get-tuple-element.558.rest_0_, ...), custom_call_target="tpu_custom_call" | custom-call | flops 1207959552 | bytes 4718592 | tf_op jit(solution)/shard_map/matrix_grad/pallas_call | solution.py:831
  380.6 5.1 all-to-all-start.6
  390.4 9.6 %ortho.3 = bf16[8,128,384]{2,1,0:T(8,128)(2,1)} custom-call(bf16[8,96,384]{2,1,0:T(8,128)(2,1)} %copy-done.24, bf16[4,192,768]{2,1,0:T(8,128)(2,1)} %copy-done.25, f32[12,768]{1,0:T(8,128)} %maximum_add_fusion.1.rest_1_), custom_call_target="tpu_custom_call" | custom-call | flops 1 | bytes 1 | tf_op jit(solution)/shard_map/ortho/pallas_call | solution.py:883
  403.7 2.7 merge.20
  406.4 6.3 %collective-permute-done.75.up_other = bf16[2,192,768]{2,1,0:T(8,128)(2,1)S(1)} collective-permute-done((bf16[2,192,768]{2,1,0:T(8,128)(2,1)}, bf16[2,192,768]{2,1,0:T(8,128)(2,1)S(1)}, u32[]{:S(2)}, u32[]{:S(2)}) %collective-permute-start.75) | collective-permute-done | bytes 589856 | tf_op jit(solution)/shard_map/ppermute | solution.py:58
  413.8 5.3 %all-to-all-start.7 = ((bf16[8,128,384]{2,1,0:T(8,128)(2,1)}), bf16[8,128,384]{2,1,0:T(8,128)(2,1)S(1)}, u32[]{:S(2)}, u32[]{:S(2)}) async-start(bf16[8,128,384]{2,1,0:T(8,128)(2,1)} %ortho.3), calls=%async_computation.7 | async-start | bytes 1572864 | tf_op jit(solution)/shard_map/all_to_all | solution.py:79
  426.0 9.6 %ortho.4 = bf16[8,96,384]{2,1,0:T(8,128)(2,1)} custom-call(bf16[8,96,384]{2,1,0:T(8,128)(2,1)} %copy-done.24, bf16[4,192,768]{2,1,0:T(8,128)(2,1)} %copy-done.26), custom_call_target="tpu_custom_call" | custom-call | flops 1 | bytes 1 | tf_op jit(solution)/shard_map/ortho/pallas_call | solution.py:883
  436.1 4.2 collective-permute-done.79.up_other
  445.3 31.3 %all_to_all.55.rest_0_ = bf16[4,192,768]{2,1,0:T(8,128)(2,1)} all-to-all(bf16[4,192,768]{2,1,0:T(8,128)(2,1)} %merge.23), channel_id=1, replica_groups={{0,8,16,24},{4,12,20,28},{1,9,17,25},{5,13,21,29},{2,10,18,26},{6,14,22..., dimensions={0} | all-to-all | bytes 2359296 | tf_op jit(solution)/shard_map/all_to_all | solution.py:71
  476.7 3.7 all-to-all-start.9
  480.4 9.6 %ortho.5 = bf16[8,96,384]{2,1,0:T(8,128)(2,1)} custom-call(bf16[8,96,192]{2,1,0:T(8,128)(2,1)} %copy-done.40, bf16[4,192,768]{2,1,0:T(8,128)(2,1)} %all_to_all.55.rest_0_), custom_call_target="tpu_custom_call" | custom-call | flops 1 | bytes 1 | tf_op jit(solution)/shard_map/ortho/pallas_call | solution.py:883
  490.0 5.0 all-to-all-done.9.pieces
  495.0 3.7 all-to-all-start.10
  501.5 2.7 update.3
  505.6 3.2 update.4
  508.9 5.0 all-to-all-done.10.pieces
  514.7 3.2 update.5
  (512 shorter events, 172.2 us)
Async XLA Ops:
  4.1 14.0 %collective-permute-start.2 = (bf16[96,768]{1,0:T(8,128)(2,1)S(1)}, bf16[96,768]{1,0:T(8,128)(2,1)S(1)}, u32[]{:S(2)}, u32[]{:S(2)}) collective-permute-start(bf16[96,768]{1,0:T(8,128)(2,1)S(1)} %pad_maximum_fusion.13), channel_id=1, source_target_pairs={{0,24},{4,28},{8,16},{12,20},{16,8},{20,12},{24,0},{28,4},{1,25},{... | collective-permute-start | bytes 442376 | tf_op jit(solution)/shard_map/ppermute | solution.py:62
  22.8 35.0 %all-to-all-start = ((bf16[4,96,1536]{2,1,0:T(8,128)(2,1)}), bf16[4,96,1536]{2,1,0:T(8,128)(2,1)}, u32[]{:S(2)}, u32[]{:S(2)}) async-start(bf16[4,96,1536]{2,1,0:T(8,128)(2,1)} %broadcast_in_dim.6), calls=%async_computation | async-start | bytes 2359296 | tf_op jit(solution)/shard_map/all_to_all | solution.py:71
  57.8 22.2 %all-to-all-start.1 = ((bf16[4,96,768]{2,1,0:T(8,128)(2,1)}), bf16[4,96,768]{2,1,0:T(8,128)(2,1)S(1)}, u32[]{:S(2)}, u32[]{:S(2)}) async-start(bf16[4,96,768]{2,1,0:T(8,128)(2,1)} %broadcast_in_dim.7), calls=%async_computation.1 | async-start | bytes 1179648 | tf_op jit(solution)/shard_map/all_to_all | solution.py:71
  63.7 15.3 %collective-permute-start.12 = (bf16[4,96,768]{2,1,0:T(8,128)(2,1)S(1)}, bf16[4,96,768]{2,1,0:T(8,128)(2,1)}, u32[]{:S(2)}, u32[]{:S(2)}) collective-permute-start(bf16[4,96,768]{2,1,0:T(8,128)(2,1)S(1)} %get-tuple-element.367), channel_id=1, source_target_pairs={{0,2},{1,3},{2,0},{3,1},{4,6},{5,7},{6,4},{7,5},{8,10},{9,11},{10,... | collective-permute-start | bytes 1769480 | tf_op jit(solution)/shard_map/ppermute | solution.py:58
  65.2 14.8 %collective-permute-start.11 = (bf16[4,96,768]{2,1,0:T(8,128)(2,1)S(1)}, bf16[4,96,768]{2,1,0:T(8,128)(2,1)S(1)}, u32[]{:S(2)}, u32[]{:S(2)}) collective-permute-start(bf16[4,96,768]{2,1,0:T(8,128)(2,1)S(1)} %get-tuple-element.365), channel_id=1, source_target_pairs={{0,4},{4,0},{8,12},{12,8},{16,20},{20,16},{24,28},{28,24},{1,5},{5... | collective-permute-start | bytes 1769480 | tf_op jit(solution)/shard_map/ppermute | solution.py:62
  77.5 18.6 %collective-permute-start.18 = (bf16[400,128]{1,0:T(8,128)(2,1)}, bf16[400,128]{1,0:T(8,128)(2,1)}, u32[]{:S(2)}, u32[]{:S(2)}) collective-permute-start(bf16[400,128]{1,0:T(8,128)(2,1)} %get-tuple-element.362), channel_id=1, source_target_pairs={{0,2},{1,3},{2,0},{3,1},{4,6},{5,7},{6,4},{7,5},{8,10},{9,11},{10,... | collective-permute-start | bytes 307208 | tf_op jit(solution)/shard_map/ppermute | solution.py:58
  82.5 34.6 %collective-permute-start.17 = (bf16[2,4,96,768]{3,2,1,0:T(8,128)(2,1)S(1)}, bf16[2,4,96,768]{3,2,1,0:T(8,128)(2,1)}, u32[]{:S(2)}, u32[]{:S(2)}) collective-permute-start(bf16[2,4,96,768]{3,2,1,0:T(8,128)(2,1)S(1)} %pad_maximum_fusion.1.rest_12_), channel_id=1, source_target_pairs={{0,4},{4,0},{8,12},{12,8},{16,20},{20,16},{24,28},{28,24},{1,5},{5... | collective-permute-start | bytes 3538952 | tf_op jit(solution)/shard_map/ppermute | solution.py:62
  84.1 33.0 %collective-permute-start.15 = (bf16[2,4,96,768]{3,2,1,0:T(8,128)(2,1)S(1)}, bf16[2,4,96,768]{3,2,1,0:T(8,128)(2,1)}, u32[]{:S(2)}, u32[]{:S(2)}) collective-permute-start(bf16[2,4,96,768]{3,2,1,0:T(8,128)(2,1)S(1)} %pad_maximum_fusion.1.rest_12_), channel_id=1, source_target_pairs={{0,1},{1,0},{2,3},{3,2},{4,5},{5,4},{6,7},{7,6},{8,9},{9,8},{10,11... | collective-permute-start | bytes 3538952 | tf_op jit(solution)/shard_map/ppermute | solution.py:58
  84.2 32.8 %collective-permute-start.16 = (bf16[2,4,96,768]{3,2,1,0:T(8,128)(2,1)S(1)}, bf16[2,4,96,768]{3,2,1,0:T(8,128)(2,1)}, u32[]{:S(2)}, u32[]{:S(2)}) collective-permute-start(bf16[2,4,96,768]{3,2,1,0:T(8,128)(2,1)S(1)} %pad_maximum_fusion.rest_8_), channel_id=1, source_target_pairs={{0,2},{1,3},{2,0},{3,1},{4,6},{5,7},{6,4},{7,5},{8,10},{9,11},{10,... | collective-permute-start | bytes 3538952 | tf_op jit(solution)/shard_map/ppermute | solution.py:58
  84.8 32.3 %collective-permute-start.14 = (bf16[2,4,96,768]{3,2,1,0:T(8,128)(2,1)S(1)}, bf16[2,4,96,768]{3,2,1,0:T(8,128)(2,1)}, u32[]{:S(2)}, u32[]{:S(2)}) collective-permute-start(bf16[2,4,96,768]{3,2,1,0:T(8,128)(2,1)S(1)} %pad_maximum_fusion.rest_8_), channel_id=1, source_target_pairs={{0,1},{1,0},{2,3},{3,2},{4,5},{5,4},{6,7},{7,6},{8,9},{9,8},{10,11... | collective-permute-start | bytes 3538952 | tf_op jit(solution)/shard_map/ppermute | solution.py:58
  85.2 45.1 %all-to-all-start.2 = ((bf16[4,96,1536]{2,1,0:T(8,128)(2,1)}), bf16[4,96,1536]{2,1,0:T(8,128)(2,1)}, u32[]{:S(2)}, u32[]{:S(2)}) async-start(bf16[4,96,1536]{2,1,0:T(8,128)(2,1)} %broadcast_in_dim.8), calls=%async_computation.2 | async-start | bytes 2359296 | tf_op jit(solution)/shard_map/all_to_all | solution.py:71
  96.1 18.8 %collective-permute-start.19 = (bf16[400,128]{1,0:T(8,128)(2,1)}, bf16[400,128]{1,0:T(8,128)(2,1)S(1)}, u32[]{:S(2)}, u32[]{:S(2)}) collective-permute-start(bf16[400,128]{1,0:T(8,128)(2,1)} %copy-done.57), channel_id=1, source_target_pairs={{0,2},{1,3},{2,0},{3,1},{4,6},{5,7},{6,4},{7,5},{8,10},{9,11},{10,... | collective-permute-start | bytes 307208 | tf_op jit(solution)/shard_map/ppermute | solution.py:58
  123.0 13.4 %collective-permute-start.31 = (f32[2,768]{1,0:T(2,128)}, f32[2,768]{1,0:T(2,128)}, u32[]{:S(2)}, u32[]{:S(2)}) collective-permute-start(f32[2,768]{1,0:T(2,128)} %param.27), channel_id=1, source_target_pairs={{0,1},{1,0},{2,3},{3,2},{4,5},{5,4},{6,7},{7,6},{8,9},{9,8},{10,11... | collective-permute-start | bytes 18440 | tf_op jit(solution)/shard_map/ppermute | solution.py:58
  130.5 20.4 %collective-permute-start.28 = (bf16[2,4,96,384]{3,2,1,0:T(8,128)(2,1)S(1)}, bf16[2,4,96,384]{3,2,1,0:T(8,128)(2,1)}, u32[]{:S(2)}, u32[]{:S(2)}) collective-permute-start(bf16[2,4,96,384]{3,2,1,0:T(8,128)(2,1)S(1)} %pad_maximum_fusion.8.rest_4_), channel_id=1, source_target_pairs={{0,4},{4,0},{8,12},{12,8},{16,20},{20,16},{24,28},{28,24},{1,5},{5... | collective-permute-start | bytes 1769480 | tf_op jit(solution)/shard_map/ppermute | solution.py:62
  131.8 19.7 %collective-permute-start.27 = (bf16[2,4,96,384]{3,2,1,0:T(8,128)(2,1)S(1)}, bf16[2,4,96,384]{3,2,1,0:T(8,128)(2,1)S(1)}, u32[]{:S(2)}, u32[]{:S(2)}) collective-permute-start(bf16[2,4,96,384]{3,2,1,0:T(8,128)(2,1)S(1)} %pad_maximum_fusion.7.rest_0_), channel_id=1, source_target_pairs={{0,2},{1,3},{2,0},{3,1},{4,6},{5,7},{6,4},{7,5},{8,10},{9,11},{10,... | collective-permute-start | bytes 1769480 | tf_op jit(solution)/shard_map/ppermute | solution.py:58
  134.8 23.6 %collective-permute-start.30 = (bf16[4,96,768]{2,1,0:T(8,128)(2,1)S(1)}, bf16[4,96,768]{2,1,0:T(8,128)(2,1)S(1)}, u32[]{:S(2)}, u32[]{:S(2)}) collective-permute-start(bf16[4,96,768]{2,1,0:T(8,128)(2,1)S(1)} %get-tuple-element.711), channel_id=1, source_target_pairs={{0,2},{1,3},{2,0},{3,1},{4,6},{5,7},{6,4},{7,5},{8,10},{9,11},{10,... | collective-permute-start | bytes 1769480 | tf_op jit(solution)/shard_map/ppermute | solution.py:58
  135.4 22.9 %collective-permute-start.29 = (bf16[4,96,768]{2,1,0:T(8,128)(2,1)S(1)}, bf16[4,96,768]{2,1,0:T(8,128)(2,1)S(1)}, u32[]{:S(2)}, u32[]{:S(2)}) collective-permute-start(bf16[4,96,768]{2,1,0:T(8,128)(2,1)S(1)} %get-tuple-element.712), channel_id=1, source_target_pairs={{0,4},{4,0},{8,12},{12,8},{16,20},{20,16},{24,28},{28,24},{1,5},{5... | collective-permute-start | bytes 1769480 | tf_op jit(solution)/shard_map/ppermute | solution.py:62
  137.8 21.5 %collective-permute-start.26 = (bf16[2,4,96,384]{3,2,1,0:T(8,128)(2,1)S(1)}, bf16[2,4,96,384]{3,2,1,0:T(8,128)(2,1)S(1)}, u32[]{:S(2)}, u32[]{:S(2)}) collective-permute-start(bf16[2,4,96,384]{3,2,1,0:T(8,128)(2,1)S(1)} %pad_maximum_fusion.8.rest_4_), channel_id=1, source_target_pairs={{0,1},{1,0},{2,3},{3,2},{4,5},{5,4},{6,7},{7,6},{8,9},{9,8},{10,11... | collective-permute-start | bytes 1769480 | tf_op jit(solution)/shard_map/ppermute | solution.py:58
  159.6 28.5 %collective-permute-start.42 = (bf16[2,4,96,768]{3,2,1,0:T(8,128)(2,1)S(1)}, bf16[2,4,96,768]{3,2,1,0:T(8,128)(2,1)}, u32[]{:S(2)}, u32[]{:S(2)}) collective-permute-start(bf16[2,4,96,768]{3,2,1,0:T(8,128)(2,1)S(1)} %pad_maximum_fusion.3.rest_12_), channel_id=1, source_target_pairs={{0,4},{4,0},{8,12},{12,8},{16,20},{20,16},{24,28},{28,24},{1,5},{5... | collective-permute-start | bytes 3538952 | tf_op jit(solution)/shard_map/ppermute | solution.py:62
  160.2 28.9 %collective-permute-start.41 = (bf16[2,4,96,768]{3,2,1,0:T(8,128)(2,1)S(1)}, bf16[2,4,96,768]{3,2,1,0:T(8,128)(2,1)}, u32[]{:S(2)}, u32[]{:S(2)}) collective-permute-start(bf16[2,4,96,768]{3,2,1,0:T(8,128)(2,1)S(1)} %pad_maximum_fusion.2.rest_8_), channel_id=1, source_target_pairs={{0,2},{1,3},{2,0},{3,1},{4,6},{5,7},{6,4},{7,5},{8,10},{9,11},{10,... | collective-permute-start | bytes 3538952 | tf_op jit(solution)/shard_map/ppermute | solution.py:58
  174.7 16.5 %collective-permute-start.39 = (bf16[400,128]{1,0:T(8,128)(2,1)}, bf16[400,128]{1,0:T(8,128)(2,1)S(1)}, u32[]{:S(2)}, u32[]{:S(2)}) collective-permute-start(bf16[400,128]{1,0:T(8,128)(2,1)} %get-tuple-element.410), channel_id=1, source_target_pairs={{0,2},{1,3},{2,0},{3,1},{4,6},{5,7},{6,4},{7,5},{8,10},{9,11},{10,... | collective-permute-start | bytes 307208 | tf_op jit(solution)/shard_map/ppermute | solution.py:58
  176.1 16.6 %collective-permute-start.40 = (bf16[400,128]{1,0:T(8,128)(2,1)S(1)}, bf16[400,128]{1,0:T(8,128)(2,1)S(1)}, u32[]{:S(2)}, u32[]{:S(2)}) collective-permute-start(bf16[400,128]{1,0:T(8,128)(2,1)S(1)} %collective-permute-done.38.recv_one), channel_id=1, source_target_pairs={{0,2},{1,3},{2,0},{3,1},{4,6},{5,7},{6,4},{7,5},{8,10},{9,11},{10,... | collective-permute-start | bytes 307208 | tf_op jit(solution)/shard_map/ppermute | solution.py:58
  193.2 21.7 %all-to-all-start.3 = ((bf16[8,96,384]{2,1,0:T(8,128)(2,1)}), bf16[8,96,384]{2,1,0:T(8,128)(2,1)S(1)}, u32[]{:S(2)}, u32[]{:S(2)}) async-start(bf16[8,96,384]{2,1,0:T(8,128)(2,1)} %pad_maximum_fusion.4), calls=%async_computation.3 | async-start | bytes 1179648 | tf_op jit(solution)/shard_map/all_to_all | solution.py:79
  223.4 15.9 %collective-permute-start.46 = (bf16[2,192,768]{2,1,0:T(8,128)(2,1)}, bf16[2,192,768]{2,1,0:T(8,128)(2,1)S(1)}, u32[]{:S(2)}, u32[]{:S(2)}) collective-permute-start(bf16[2,192,768]{2,1,0:T(8,128)(2,1)} %get-tuple-element.446), channel_id=1, source_target_pairs={{0,2},{1,3},{2,0},{3,1},{4,6},{5,7},{6,4},{7,5},{8,10},{9,11},{10,... | collective-permute-start | bytes 1769480 | tf_op jit(solution)/shard_map/ppermute | solution.py:58
  224.8 15.3 %collective-permute-start.47 = (bf16[2,192,768]{2,1,0:T(8,128)(2,1)}, bf16[2,192,768]{2,1,0:T(8,128)(2,1)S(1)}, u32[]{:S(2)}, u32[]{:S(2)}) collective-permute-start(bf16[2,192,768]{2,1,0:T(8,128)(2,1)} %get-tuple-element.447), channel_id=1, source_target_pairs={{0,4},{4,0},{8,12},{12,8},{16,20},{20,16},{24,28},{28,24},{1,5},{5... | collective-permute-start | bytes 1769480 | tf_op jit(solution)/shard_map/ppermute | solution.py:62
  243.7 14.6 %collective-permute-start.52 = (bf16[192,768]{1,0:T(8,128)(2,1)}, bf16[192,768]{1,0:T(8,128)(2,1)S(1)}, u32[]{:S(2)}, u32[]{:S(2)}) collective-permute-start(bf16[192,768]{1,0:T(8,128)(2,1)} %get-tuple-element.467), channel_id=1, source_target_pairs={{0,4},{4,0},{8,12},{12,8},{16,20},{20,16},{24,28},{28,24},{1,5},{5... | collective-permute-start | bytes 884744 | tf_op jit(solution)/shard_map/ppermute | solution.py:62
  259.0 19.6 %collective-permute-start.54 = (bf16[2,192,768]{2,1,0:T(8,128)(2,1)}, bf16[2,192,768]{2,1,0:T(8,128)(2,1)S(1)}, u32[]{:S(2)}, u32[]{:S(2)}) collective-permute-start(bf16[2,192,768]{2,1,0:T(8,128)(2,1)} %get-tuple-element.473), channel_id=1, source_target_pairs={{0,2},{1,3},{2,0},{3,1},{4,6},{5,7},{6,4},{7,5},{8,10},{9,11},{10,... | collective-permute-start | bytes 1769480 | tf_op jit(solution)/shard_map/ppermute | solution.py:58
  259.6 19.0 %collective-permute-start.55 = (bf16[2,192,768]{2,1,0:T(8,128)(2,1)}, bf16[2,192,768]{2,1,0:T(8,128)(2,1)S(1)}, u32[]{:S(2)}, u32[]{:S(2)}) collective-permute-start(bf16[2,192,768]{2,1,0:T(8,128)(2,1)} %get-tuple-element.474), channel_id=1, source_target_pairs={{0,4},{4,0},{8,12},{12,8},{16,20},{20,16},{24,28},{28,24},{1,5},{5... | collective-permute-start | bytes 1769480 | tf_op jit(solution)/shard_map/ppermute | solution.py:62
  260.2 18.4 %all-to-all-start.4 = ((bf16[8,96,192]{2,1,0:T(8,128)(2,1)}), bf16[8,96,192]{2,1,0:T(8,128)(2,1)S(1)}, u32[]{:S(2)}, u32[]{:S(2)}) async-start(bf16[8,96,192]{2,1,0:T(8,128)(2,1)} %fusion.10), calls=%async_computation.4 | async-start | bytes 786432 | tf_op jit(solution)/shard_map/all_to_all | solution.py:79
  295.0 15.0 %collective-permute-start.60 = (bf16[2,192,768]{2,1,0:T(8,128)(2,1)}, bf16[2,192,768]{2,1,0:T(8,128)(2,1)S(1)}, u32[]{:S(2)}, u32[]{:S(2)}) collective-permute-start(bf16[2,192,768]{2,1,0:T(8,128)(2,1)} %get-tuple-element.505), channel_id=1, source_target_pairs={{0,2},{1,3},{2,0},{3,1},{4,6},{5,7},{6,4},{7,5},{8,10},{9,11},{10,... | collective-permute-start | bytes 1769480 | tf_op jit(solution)/shard_map/ppermute | solution.py:58
  296.4 14.1 %collective-permute-start.61 = (bf16[2,192,768]{2,1,0:T(8,128)(2,1)}, bf16[2,192,768]{2,1,0:T(8,128)(2,1)S(1)}, u32[]{:S(2)}, u32[]{:S(2)}) collective-permute-start(bf16[2,192,768]{2,1,0:T(8,128)(2,1)} %get-tuple-element.506), channel_id=1, source_target_pairs={{0,4},{4,0},{8,12},{12,8},{16,20},{20,16},{24,28},{28,24},{1,5},{5... | collective-permute-start | bytes 1769480 | tf_op jit(solution)/shard_map/ppermute | solution.py:62
  315.5 39.3 %all-to-all-start.5 = ((bf16[4,192,768]{2,1,0:T(8,128)(2,1)}), bf16[4,192,768]{2,1,0:T(8,128)(2,1)S(1)}, u32[]{:S(2)}, u32[]{:S(2)}) async-start(bf16[4,192,768]{2,1,0:T(8,128)(2,1)} %merge.16), calls=%async_computation.5 | async-start | bytes 2359296 | tf_op jit(solution)/shard_map/all_to_all | solution.py:71
  322.8 15.2 %collective-permute-start.66 = (bf16[192,768]{1,0:T(8,128)(2,1)}, bf16[192,768]{1,0:T(8,128)(2,1)S(1)}, u32[]{:S(2)}, u32[]{:S(2)}) collective-permute-start(bf16[192,768]{1,0:T(8,128)(2,1)} %get-tuple-element.526), channel_id=1, source_target_pairs={{0,4},{4,0},{8,12},{12,8},{16,20},{20,16},{24,28},{28,24},{1,5},{5... | collective-permute-start | bytes 884744 | tf_op jit(solution)/shard_map/ppermute | solution.py:62
  324.3 13.7 %collective-permute-start.67 = (bf16[192,768]{1,0:T(8,128)(2,1)}, bf16[192,768]{1,0:T(8,128)(2,1)S(1)}, u32[]{:S(2)}, u32[]{:S(2)}) collective-permute-start(bf16[192,768]{1,0:T(8,128)(2,1)} %get-tuple-element.527), channel_id=1, source_target_pairs={{0,2},{1,3},{2,0},{3,1},{4,6},{5,7},{6,4},{7,5},{8,10},{9,11},{10,... | collective-permute-start | bytes 884744 | tf_op jit(solution)/shard_map/ppermute | solution.py:58
  338.0 16.9 %collective-permute-start.68 = (bf16[2,192,768]{2,1,0:T(8,128)(2,1)}, bf16[2,192,768]{2,1,0:T(8,128)(2,1)S(1)}, u32[]{:S(2)}, u32[]{:S(2)}) collective-permute-start(bf16[2,192,768]{2,1,0:T(8,128)(2,1)} %get-tuple-element.540), channel_id=1, source_target_pairs={{0,2},{1,3},{2,0},{3,1},{4,6},{5,7},{6,4},{7,5},{8,10},{9,11},{10,... | collective-permute-start | bytes 1769480 | tf_op jit(solution)/shard_map/ppermute | solution.py:58
  338.7 16.2 %collective-permute-start.69 = (bf16[2,192,768]{2,1,0:T(8,128)(2,1)}, bf16[2,192,768]{2,1,0:T(8,128)(2,1)S(1)}, u32[]{:S(2)}, u32[]{:S(2)}) collective-permute-start(bf16[2,192,768]{2,1,0:T(8,128)(2,1)} %get-tuple-element.541), channel_id=1, source_target_pairs={{0,4},{4,0},{8,12},{12,8},{16,20},{20,16},{24,28},{28,24},{1,5},{5... | collective-permute-start | bytes 1769480 | tf_op jit(solution)/shard_map/ppermute | solution.py:62
  380.6 33.2 %all-to-all-start.6 = ((bf16[4,192,768]{2,1,0:T(8,128)(2,1)}), bf16[4,192,768]{2,1,0:T(8,128)(2,1)S(1)}, u32[]{:S(2)}, u32[]{:S(2)}) async-start(bf16[4,192,768]{2,1,0:T(8,128)(2,1)} %merge.19), calls=%async_computation.6 | async-start | bytes 2359296 | tf_op jit(solution)/shard_map/all_to_all | solution.py:71
  385.7 16.5 %collective-permute-start.77 = (bf16[2,192,768]{2,1,0:T(8,128)(2,1)}, bf16[2,192,768]{2,1,0:T(8,128)(2,1)S(1)}, u32[]{:S(2)}, u32[]{:S(2)}) collective-permute-start(bf16[2,192,768]{2,1,0:T(8,128)(2,1)} %get-tuple-element.588), channel_id=1, source_target_pairs={{0,2},{1,3},{2,0},{3,1},{4,6},{5,7},{6,4},{7,5},{8,10},{9,11},{10,... | collective-permute-start | bytes 1769480 | tf_op jit(solution)/shard_map/ppermute | solution.py:58
  387.1 16.6 %collective-permute-start.78 = (bf16[2,192,768]{2,1,0:T(8,128)(2,1)}, bf16[2,192,768]{2,1,0:T(8,128)(2,1)}, u32[]{:S(2)}, u32[]{:S(2)}) collective-permute-start(bf16[2,192,768]{2,1,0:T(8,128)(2,1)} %get-tuple-element.589), channel_id=1, source_target_pairs={{0,4},{4,0},{8,12},{12,8},{16,20},{20,16},{24,28},{28,24},{1,5},{5... | collective-permute-start | bytes 1769480 | tf_op jit(solution)/shard_map/ppermute | solution.py:62
  387.7 24.9 %collective-permute-start.75 = (bf16[2,192,768]{2,1,0:T(8,128)(2,1)}, bf16[2,192,768]{2,1,0:T(8,128)(2,1)S(1)}, u32[]{:S(2)}, u32[]{:S(2)}) collective-permute-start(bf16[2,192,768]{2,1,0:T(8,128)(2,1)} %get-tuple-element.578), channel_id=1, source_target_pairs={{0,2},{1,3},{2,0},{3,1},{4,6},{5,7},{6,4},{7,5},{8,10},{9,11},{10,... | collective-permute-start | bytes 1769480 | tf_op jit(solution)/shard_map/ppermute | solution.py:58
  388.3 25.5 %collective-permute-start.76 = (bf16[2,192,768]{2,1,0:T(8,128)(2,1)}, bf16[2,192,768]{2,1,0:T(8,128)(2,1)S(1)}, u32[]{:S(2)}, u32[]{:S(2)}) collective-permute-start(bf16[2,192,768]{2,1,0:T(8,128)(2,1)} %get-tuple-element.579), channel_id=1, source_target_pairs={{0,4},{4,0},{8,12},{12,8},{16,20},{20,16},{24,28},{28,24},{1,5},{5... | collective-permute-start | bytes 1769480 | tf_op jit(solution)/shard_map/ppermute | solution.py:62
  413.8 31.5 %all-to-all-start.7 = ((bf16[8,128,384]{2,1,0:T(8,128)(2,1)}), bf16[8,128,384]{2,1,0:T(8,128)(2,1)S(1)}, u32[]{:S(2)}, u32[]{:S(2)}) async-start(bf16[8,128,384]{2,1,0:T(8,128)(2,1)} %ortho.3), calls=%async_computation.7 | async-start | bytes 1572864 | tf_op jit(solution)/shard_map/all_to_all | solution.py:79
  419.1 17.0 %collective-permute-start.81 = (bf16[192,768]{1,0:T(8,128)(2,1)}, bf16[192,768]{1,0:T(8,128)(2,1)S(1)}, u32[]{:S(2)}, u32[]{:S(2)}) collective-permute-start(bf16[192,768]{1,0:T(8,128)(2,1)} %get-tuple-element.606), channel_id=1, source_target_pairs={{0,4},{4,0},{8,12},{12,8},{16,20},{20,16},{24,28},{28,24},{1,5},{5... | collective-permute-start | bytes 884744 | tf_op jit(solution)/shard_map/ppermute | solution.py:62
  421.2 14.9 %collective-permute-start.82 = (bf16[192,768]{1,0:T(8,128)(2,1)S(1)}, bf16[192,768]{1,0:T(8,128)(2,1)S(1)}, u32[]{:S(2)}, u32[]{:S(2)}) collective-permute-start(bf16[192,768]{1,0:T(8,128)(2,1)S(1)} %copy-done.107), channel_id=1, source_target_pairs={{0,2},{1,3},{2,0},{3,1},{4,6},{5,7},{6,4},{7,5},{8,10},{9,11},{10,... | collective-permute-start | bytes 884744 | tf_op jit(solution)/shard_map/ppermute | solution.py:58
  424.5 15.8 %collective-permute-start.79 = (bf16[192,768]{1,0:T(8,128)(2,1)}, bf16[192,768]{1,0:T(8,128)(2,1)S(1)}, u32[]{:S(2)}, u32[]{:S(2)}) collective-permute-start(bf16[192,768]{1,0:T(8,128)(2,1)} %get-tuple-element.604), channel_id=1, source_target_pairs={{0,4},{4,0},{8,12},{12,8},{16,20},{20,16},{24,28},{28,24},{1,5},{5... | collective-permute-start | bytes 884744 | tf_op jit(solution)/shard_map/ppermute | solution.py:62
  424.6 15.7 %collective-permute-start.80 = (bf16[192,768]{1,0:T(8,128)(2,1)}, bf16[192,768]{1,0:T(8,128)(2,1)S(1)}, u32[]{:S(2)}, u32[]{:S(2)}) collective-permute-start(bf16[192,768]{1,0:T(8,128)(2,1)} %get-tuple-element.605), channel_id=1, source_target_pairs={{0,2},{1,3},{2,0},{3,1},{4,6},{5,7},{6,4},{7,5},{8,10},{9,11},{10,... | collective-permute-start | bytes 884744 | tf_op jit(solution)/shard_map/ppermute | solution.py:58
  476.7 18.3 %all-to-all-start.9 = ((bf16[8,96,384]{2,1,0:T(8,128)(2,1)}), bf16[8,96,384]{2,1,0:T(8,128)(2,1)S(1)}, u32[]{:S(2)}, u32[]{:S(2)}) async-start(bf16[8,96,384]{2,1,0:T(8,128)(2,1)} %ortho.4), calls=%async_computation.9 | async-start | bytes 1179648 | tf_op jit(solution)/shard_map/all_to_all | solution.py:79
  495.0 18.8 %all-to-all-start.10 = ((bf16[8,96,384]{2,1,0:T(8,128)(2,1)}), bf16[8,96,384]{2,1,0:T(8,128)(2,1)S(1)}, u32[]{:S(2)}, u32[]{:S(2)}) async-start(bf16[8,96,384]{2,1,0:T(8,128)(2,1)} %ortho.5), calls=%async_computation.10 | async-start | bytes 1179648 | tf_op jit(solution)/shard_map/all_to_all | solution.py:79
  (155 other events, 1195.5 us)

commit v6 on v5

--- a/solution.py
+++ b/solution.py
@@ -1236,12 +1236,10 @@
         came = swap_head(sent, 2)
         attend_zero = attend_grad(quick, states[0], stack_other, back_other)
 
-        attend_zero, down_others, came = hold(attend_zero, down_others, came)
+        attend_zero, down_others, came, up_others = hold(attend_zero, down_others, came, up_others)
         attend_others = send_first(attend_zero)
         pair_two = swap_line(merge_second(down_zero, down_others, attend_blocks))
         back_one = orthogonalize(0, pair_one, moment, kept + came)
-
-        up_others, back_one = hold(up_others, back_one)
         up_zero = merge_first(up_zero, up_others)
         up_kept = up_zero[0], up_zero[2]
         up_others = send_second(up_zero)

time: 528 us -> 541 us (1.025)
  waiting for transfers between devices: 114 us -> 127 us
    all_to_all x5, waiting for transfers between devices: 0.01 us -> 12.2 us  [swap_line(): lax.all_to_all(parts, 'dp', split_axis=0, concat_axis=0, axis_index_group...]
  transfers between devices with their start and end apart: 93 -> 93, of which waited for: 37 -> 36; matrix products, arithmetic and copies ran while one was open for 9% -> 8% of each run, Pallas kernels for 37% -> 36%
where the time goes in v6:
time: 541 us; the launch traced here: 531 us
  Pallas kernels  200 us (37%)
  waiting for transfers between devices  127 us (23%)
  starting transfers between devices  111 us (21%)
  local copies, waits for them, and re-layouts  42.4 us (8%)
  blocking collectives  32.1 us (6%)
  other arithmetic  16.7 us (3%)
    ppermute x60, waiting for transfers between devices, swap_head(): lax.ppermute(values, 'head', [(h, h ^ offset) for h in range(lax.axis_siz...  68 us
    ppermute x60, starting transfers between devices, swap_head(): lax.ppermute(values, 'head', [(h, h ^ offset) for h in range(lax.axis_siz...  38 us
    ppermute x23, waiting for transfers between devices, swap_dp(): lax.ppermute(values, 'dp', [(d, d ^ offset) for d in range(lax.axis_size(...  33.8 us
    all_to_all x1, blocking collectives, swap_line(): lax.all_to_all(parts, 'dp', split_axis=0, concat_axis=0, axis_index_group...  32.1 us
    pallas_call x6, Pallas kernels, matrix_grad(): call(partial(grad_kernel, quick, splits), 'matrix_grad', vmem(2 + len(lef...  31.9 us
    pallas_call x12, Pallas kernels, merge(): return call(kernel, 'merge', vmem(len(operands)), outs, [], 1, 1)(*operands)  30.9 us
    pallas_call x2, Pallas kernels, back_project(): call(partial(back_project_kernel, plan), 'back_project', vmem(21) + scala...  29.1 us
    pallas_call x3, Pallas kernels, orthogonalize(): call(partial(ortho_kernel, place, len(terms)), 'ortho', vmem(1 + len(term...  28.9 us
  transfers between devices with their start and end apart: 93, of which 36 were waited for; matrix products, arithmetic and copies ran while one was open for 8% of the time, Pallas kernels for 36%

profile of v6, /device:TPU:0, one launch (start us, length us, event | category | flops | bytes accessed | tf_op | source)
XLA Modules:
  0.0 531.2 jit_solution(15354588896531698273)
XLA Ops:
  4.1 5.1 collective-permute-start.2
  18.1 3.6 collective-permute-done.1
  22.8 4.3 all-to-all-start
  31.1 4.3 collective-permute-done.3
  44.6 5.6 %collective-permute-done.6.rest_6_ = bf16[2,4,96,384]{3,2,1,0:T(8,128)(2,1)S(1)} collective-permute-done((bf16[2,4,96,384]{3,2,1,0:T(8,128)(2,1)S(1)}, bf16[2,4,96,384]{3,2,1,0:T(8,128)(2,1)S(1)}, u32[]{:S(2)}, u32[]{:S(2)}) %collective-permute-start.6) | collective-permute-done | bytes 589856 | tf_op jit(solution)/shard_map/ppermute | solution.py:62
  57.8 4.5 all-to-all-start.1
  68.1 9.3 %project.2 = (bf16[256,384]{1,0:T(8,128)(2,1)}, bf16[256,384]{1,0:T(8,128)(2,1)}, bf16[256,768]{1,0:T(8,128)(2,1)}, f32[8,768]{1,0:T(8,128)}, f32[256,768]{1,0:T...) custom-call(f32[256,768]{1,0:T(8,128)} %convert_element_type.66.resid, f32[5,768]{1,0:T(8,128)} %get-tuple-element.744.vectors, ...), custom_call_target="tpu_custom_call" | custom-call | flops 1358954496 | bytes 4718592 | tf_op jit(solution)/shard_map/project/pallas_call | solution.py:719
  85.2 5.3 all-to-all-start.2
  99.6 15.3 %collective-permute-done.19.recv_three = bf16[400,128]{1,0:T(8,128)(2,1)S(1)} collective-permute-done((bf16[400,128]{1,0:T(8,128)(2,1)}, bf16[400,128]{1,0:T(8,128)(2,1)S(1)}, u32[]{:S(2)}, u32[]{:S(2)}) %collective-permute-start.19) | collective-permute-done | bytes 102432 | tf_op jit(solution)/shard_map/ppermute | solution.py:58
  123.6 6.5 %collective-permute-done.24 = bf16[4,96,384]{2,1,0:T(8,128)(2,1)S(1)} collective-permute-done((bf16[4,96,384]{2,1,0:T(8,128)(2,1)S(1)}, bf16[4,96,384]{2,1,0:T(8,128)(2,1)S(1)}, u32[]{:S(2)}, u32[]{:S(2)}) %collective-permute-start.24) | collective-permute-done | bytes 294944 | tf_op jit(solution)/shard_map/ppermute | solution.py:58
  137.8 13.1 %mix.2 = (f32[256,768]{1,0:T(8,128)}, f32[256,768]{1,0:T(8,128)}, f32[256,768]{1,0:T(8,128)}, bf16[4,256,768]{2,1,0:T(8,128)(2,1)}, bf16[2,256,768]{2,1,0:T(8,12...) custom-call(f32[256,768]{1,0:T(8,128)} %convert_element_type.66.resid, f32[5,768]{1,0:T(8,128)} %get-tuple-element.744.vectors, ...), custom_call_target="tpu_custom_call" | custom-call | flops 3623878656 | bytes 11796480 | tf_op jit(solution)/shard_map/mix/pallas_call | solution.py:755
  151.5 6.9 %collective-permute-done.30 = bf16[4,96,768]{2,1,0:T(8,128)(2,1)S(1)} collective-permute-done((bf16[4,96,768]{2,1,0:T(8,128)(2,1)S(1)}, bf16[4,96,768]{2,1,0:T(8,128)(2,1)S(1)}, u32[]{:S(2)}, u32[]{:S(2)}) %collective-permute-start.30) | collective-permute-done | bytes 589856 | tf_op jit(solution)/shard_map/ppermute | solution.py:58
  165.7 8.8 %project.3 = (bf16[256,384]{1,0:T(8,128)(2,1)}, bf16[256,384]{1,0:T(8,128)(2,1)}, bf16[256,768]{1,0:T(8,128)(2,1)}, f32[8,768]{1,0:T(8,128)}, f32[256,768]{1,0:T...) custom-call(f32[256,768]{1,0:T(8,128)} %get-tuple-element.404.resid, f32[5,768]{1,0:T(8,128)} %get-tuple-element.743.vectors, ...), custom_call_target="tpu_custom_call" | custom-call | flops 1358954496 | bytes 4718592 | tf_op jit(solution)/shard_map/project/pallas_call | solution.py:719
  176.8 11.3 %collective-permute-done.42.rest_14_ = bf16[2,4,96,768]{3,2,1,0:T(8,128)(2,1)} collective-permute-done((bf16[2,4,96,768]{3,2,1,0:T(8,128)(2,1)S(1)}, bf16[2,4,96,768]{3,2,1,0:T(8,128)(2,1)}, u32[]{:S(2)}, u32[]{:S(2)}) %collective-permute-start.42) | collective-permute-done | bytes 1179680 | tf_op jit(solution)/shard_map/ppermute | solution.py:62
  193.2 5.7 %all-to-all-start.3 = ((bf16[8,96,384]{2,1,0:T(8,128)(2,1)}), bf16[8,96,384]{2,1,0:T(8,128)(2,1)S(1)}, u32[]{:S(2)}, u32[]{:S(2)}) async-start(bf16[8,96,384]{2,1,0:T(8,128)(2,1)} %pad_maximum_fusion.4), calls=%async_computation.3 | async-start | bytes 1179648 | tf_op jit(solution)/shard_map/all_to_all | solution.py:79
  201.0 12.6 %mix.3 = (f32[256,768]{1,0:T(8,128)}, f32[256,768]{1,0:T(8,128)}, f32[256,768]{1,0:T(8,128)}, bf16[4,256,768]{2,1,0:T(8,128)(2,1)}, bf16[2,256,768]{2,1,0:T(8,12...) custom-call(f32[256,768]{1,0:T(8,128)} %get-tuple-element.404.resid, f32[5,768]{1,0:T(8,128)} %get-tuple-element.743.vectors, ...), custom_call_target="tpu_custom_call" | custom-call | flops 3623878656 | bytes 11796480 | tf_op jit(solution)/shard_map/mix/pallas_call | solution.py:755
  214.9 3.1 collective-permute-done.45.right_other.rest_1_
  219.0 4.4 matrix_grad.6
  226.3 13.0 %back_mix.2 = (bf16[2,256,768]{2,1,0:T(8,128)(2,1)}, bf16[3,256,768]{2,1,0:T(8,128)(2,1)}, f32[256,768]{1,0:T(8,128)}, bf16[256,768]{1,0:T(8,128)(2,1)}, bf16[25...) custom-call(f32[256,768]{1,0:T(8,128)} %convert_multiply_fusion.grad, ...), custom_call_target="tpu_custom_call" | custom-call | flops 3321888768 | bytes 11796480 | tf_op jit(solution)/shard_map/back_mix/pallas_call | solution.py:786
  247.9 4.9 matrix_grad.7
  252.8 4.3 collective-permute-done.50.back_two
  260.2 4.7 all-to-all-start.4
  264.9 13.7 %back_project.2 = (bf16[2,256,768]{2,1,0:T(8,128)(2,1)}, bf16[4,256,768]{2,1,0:T(8,128)(2,1)}, f32[256,768]{1,0:T(8,128)}, f32[8,768]{1,0:T(8,128)}) custom-call(f32[256,768]{1,0:T(8,128)} %get-tuple-element.404.resid, f32[5,768]{1,0:T(8,128)} %get-tuple-element.743.vectors, f32[256,32]{1,0:T(8,128)} %get-tuple-element.354.cosine_part, ...), custom_call_target="tpu_custom_call" | custom-call | flops 2415919104 | bytes 4718592 | tf_op jit(solution)/shard_map/back_project/pallas_call | solution.py:811
  287.5 6.1 %matrix_grad.8 = (bf16[2,192,768]{2,1,0:T(8,128)(2,1)}, bf16[2,192,768]{2,1,0:T(8,128)(2,1)}, bf16[2,192,768]{2,1,0:T(8,128)(2,1)}, bf16[2,192,768]{2,1,0:T(8,128)(2,1)}) custom-call(bf16[2,256,768]{2,1,0:T(8,128)(2,1)} %get-tuple-element.471.right_own, bf16[4,256,768]{2,1,0:T(8,128)(2,1)} %copy-done.4, bf16[4,256,768]{2,1,0:T(8,128)(2,1)} %get-tuple-element.478.rest_0_, ...), custom_call_target="tpu_custom_call" | custom-call | flops 1207959552 | bytes 4718592 | tf_op jit(solution)/shard_map/matrix_grad/pallas_call | solution.py:831
  296.8 13.2 %back_mix.3 = (bf16[2,256,768]{2,1,0:T(8,128)(2,1)}, bf16[3,256,768]{2,1,0:T(8,128)(2,1)}, f32[256,768]{1,0:T(8,128)}, bf16[256,768]{1,0:T(8,128)(2,1)}, bf16[25...) custom-call(f32[256,768]{1,0:T(8,128)} %get-tuple-element.496.grad, ...), custom_call_target="tpu_custom_call" | custom-call | flops 3321888768 | bytes 11796480 | tf_op jit(solution)/shard_map/back_mix/pallas_call | solution.py:786
  315.5 4.5 all-to-all-start.5
  320.1 2.7 merge.14
  326.9 5.1 matrix_grad.9
  332.1 4.4 collective-permute-done.64.back_two
  339.4 15.4 %back_project.3 = (bf16[2,256,768]{2,1,0:T(8,128)(2,1)}, bf16[4,256,768]{2,1,0:T(8,128)(2,1)}, f32[256,768]{1,0:T(8,128)}, f32[8,768]{1,0:T(8,128)}) custom-call(f32[256,768]{1,0:T(8,128)} %convert_element_type.66.resid, f32[5,768]{1,0:T(8,128)} %get-tuple-element.744.vectors, f32[256,32]{1,0:T(8,128)} %get-tuple-element.354.cosine_part, ...), custom_call_target="tpu_custom_call" | custom-call | flops 2415919104 | bytes 4718592 | tf_op jit(solution)/shard_map/back_project/pallas_call | solution.py:811
  357.2 5.2 matrix_grad.10
  370.8 6.2 %matrix_grad.11 = (bf16[2,192,768]{2,1,0:T(8,128)(2,1)}, bf16[2,192,768]{2,1,0:T(8,128)(2,1)}, bf16[2,192,768]{2,1,0:T(8,128)(2,1)}, bf16[2,192,768]{2,1,0:T(8,128)(2,1)}) custom-call(bf16[2,256,768]{2,1,0:T(8,128)(2,1)} %get-tuple-element.531.right_own, bf16[4,256,768]{2,1,0:T(8,128)(2,1)} %copy-done.20, bf16[4,256,768]{2,1,0:T(8,128)(2,1)} %get-tuple-element.557.rest_0_, ...), custom_call_target="tpu_custom_call" | custom-call | flops 1207959552 | bytes 4718592 | tf_op jit(solution)/shard_map/matrix_grad/pallas_call | solution.py:831
  379.2 8.7 %collective-permute-done.74 = f32[12,768]{1,0:T(8,128)S(1)} collective-permute-done((f32[12,768]{1,0:T(8,128)S(1)}, f32[12,768]{1,0:T(8,128)S(1)}, u32[]{:S(2)}, u32[]{:S(2)}) %collective-permute-start.74) | collective-permute-done | bytes 36896 | tf_op jit(solution)/shard_map/ppermute | solution.py:58
  391.3 5.1 all-to-all-start.6
  399.9 9.6 %ortho.3 = bf16[8,128,384]{2,1,0:T(8,128)(2,1)} custom-call(bf16[8,96,384]{2,1,0:T(8,128)(2,1)} %copy-done.24, bf16[4,192,768]{2,1,0:T(8,128)(2,1)} %copy-done.25, f32[12,768]{1,0:T(8,128)} %maximum_add_fusion.1.rest_1_), custom_call_target="tpu_custom_call" | custom-call | flops 1 | bytes 1 | tf_op jit(solution)/shard_map/ortho/pallas_call | solution.py:883
  412.2 12.2 %all-to-all-done.6.rest_0_ = bf16[4,192,768]{2,1,0:T(8,128)(2,1)S(1)} async-done(((bf16[4,192,768]{2,1,0:T(8,128)(2,1)}), bf16[4,192,768]{2,1,0:T(8,128)(2,1)S(1)}, u32[]{:S(2)}, u32[]{:S(2)}) %all-to-all-start.6) | async-done | bytes 1179680 | tf_op jit(solution)/shard_map/all_to_all | solution.py:71
  424.4 4.0 all-to-all-start.7
  435.3 9.6 %ortho.4 = bf16[8,96,384]{2,1,0:T(8,128)(2,1)} custom-call(bf16[8,96,384]{2,1,0:T(8,128)(2,1)} %copy-done.24, bf16[4,192,768]{2,1,0:T(8,128)(2,1)} %copy-done.26), custom_call_target="tpu_custom_call" | custom-call | flops 1 | bytes 1 | tf_op jit(solution)/shard_map/ortho/pallas_call | solution.py:883
  446.8 4.3 collective-permute-done.79.up_other
  456.1 32.1 %all_to_all.55.rest_0_ = bf16[4,192,768]{2,1,0:T(8,128)(2,1)} all-to-all(bf16[4,192,768]{2,1,0:T(8,128)(2,1)} %merge.23), channel_id=1, replica_groups={{0,8,16,24},{4,12,20,28},{1,9,17,25},{5,13,21,29},{2,10,18,26},{6,14,22..., dimensions={0} | all-to-all | bytes 2359296 | tf_op jit(solution)/shard_map/all_to_all | solution.py:71
  488.2 4.0 all-to-all-start.9
  492.2 9.6 %ortho.5 = bf16[8,96,384]{2,1,0:T(8,128)(2,1)} custom-call(bf16[8,96,192]{2,1,0:T(8,128)(2,1)} %copy-done.40, bf16[4,192,768]{2,1,0:T(8,128)(2,1)} %all_to_all.55.rest_0_), custom_call_target="tpu_custom_call" | custom-call | flops 1 | bytes 1 | tf_op jit(solution)/shard_map/ortho/pallas_call | solution.py:883
  501.8 5.7 %all-to-all-done.9.pieces = bf16[8,96,384]{2,1,0:T(8,128)(2,1)S(1)} async-done(((bf16[8,96,384]{2,1,0:T(8,128)(2,1)}), bf16[8,96,384]{2,1,0:T(8,128)(2,1)S(1)}, u32[]{:S(2)}, u32[]{:S(2)}) %all-to-all-start.9) | async-done | bytes 589856 | tf_op jit(solution)/shard_map/all_to_all | solution.py:79
  507.5 3.6 all-to-all-start.10
  514.0 2.7 update.3
  518.1 3.2 update.4
  521.3 5.6 %all-to-all-done.10.pieces = bf16[8,96,384]{2,1,0:T(8,128)(2,1)S(1)} async-done(((bf16[8,96,384]{2,1,0:T(8,128)(2,1)}), bf16[8,96,384]{2,1,0:T(8,128)(2,1)S(1)}, u32[]{:S(2)}, u32[]{:S(2)}) %all-to-all-start.10) | async-done | bytes 589856 | tf_op jit(solution)/shard_map/all_to_all | solution.py:79
  527.8 3.2 update.5
  (512 shorter events, 172.3 us)
Async XLA Ops:
  22.8 35.0 %all-to-all-start = ((bf16[4,96,1536]{2,1,0:T(8,128)(2,1)}), bf16[4,96,1536]{2,1,0:T(8,128)(2,1)}, u32[]{:S(2)}, u32[]{:S(2)}) async-start(bf16[4,96,1536]{2,1,0:T(8,128)(2,1)} %broadcast_in_dim.6), calls=%async_computation | async-start | bytes 2359296 | tf_op jit(solution)/shard_map/all_to_all | solution.py:71
  57.8 22.2 %all-to-all-start.1 = ((bf16[4,96,768]{2,1,0:T(8,128)(2,1)}), bf16[4,96,768]{2,1,0:T(8,128)(2,1)S(1)}, u32[]{:S(2)}, u32[]{:S(2)}) async-start(bf16[4,96,768]{2,1,0:T(8,128)(2,1)} %broadcast_in_dim.7), calls=%async_computation.1 | async-start | bytes 1179648 | tf_op jit(solution)/shard_map/all_to_all | solution.py:71
  63.7 15.3 %collective-permute-start.12 = (bf16[4,96,768]{2,1,0:T(8,128)(2,1)S(1)}, bf16[4,96,768]{2,1,0:T(8,128)(2,1)}, u32[]{:S(2)}, u32[]{:S(2)}) collective-permute-start(bf16[4,96,768]{2,1,0:T(8,128)(2,1)S(1)} %get-tuple-element.366), channel_id=1, source_target_pairs={{0,2},{1,3},{2,0},{3,1},{4,6},{5,7},{6,4},{7,5},{8,10},{9,11},{10,... | collective-permute-start | bytes 1769480 | tf_op jit(solution)/shard_map/ppermute | solution.py:58
  65.2 14.8 %collective-permute-start.11 = (bf16[4,96,768]{2,1,0:T(8,128)(2,1)S(1)}, bf16[4,96,768]{2,1,0:T(8,128)(2,1)S(1)}, u32[]{:S(2)}, u32[]{:S(2)}) collective-permute-start(bf16[4,96,768]{2,1,0:T(8,128)(2,1)S(1)} %get-tuple-element.364), channel_id=1, source_target_pairs={{0,4},{4,0},{8,12},{12,8},{16,20},{20,16},{24,28},{28,24},{1,5},{5... | collective-permute-start | bytes 1769480 | tf_op jit(solution)/shard_map/ppermute | solution.py:62
  77.5 18.6 %collective-permute-start.18 = (bf16[400,128]{1,0:T(8,128)(2,1)}, bf16[400,128]{1,0:T(8,128)(2,1)}, u32[]{:S(2)}, u32[]{:S(2)}) collective-permute-start(bf16[400,128]{1,0:T(8,128)(2,1)} %get-tuple-element.361), channel_id=1, source_target_pairs={{0,2},{1,3},{2,0},{3,1},{4,6},{5,7},{6,4},{7,5},{8,10},{9,11},{10,... | collective-permute-start | bytes 307208 | tf_op jit(solution)/shard_map/ppermute | solution.py:58
  82.5 34.6 %collective-permute-start.17 = (bf16[2,4,96,768]{3,2,1,0:T(8,128)(2,1)S(1)}, bf16[2,4,96,768]{3,2,1,0:T(8,128)(2,1)}, u32[]{:S(2)}, u32[]{:S(2)}) collective-permute-start(bf16[2,4,96,768]{3,2,1,0:T(8,128)(2,1)S(1)} %pad_maximum_fusion.1.rest_12_), channel_id=1, source_target_pairs={{0,4},{4,0},{8,12},{12,8},{16,20},{20,16},{24,28},{28,24},{1,5},{5... | collective-permute-start | bytes 3538952 | tf_op jit(solution)/shard_map/ppermute | solution.py:62
  84.1 33.0 %collective-permute-start.15 = (bf16[2,4,96,768]{3,2,1,0:T(8,128)(2,1)S(1)}, bf16[2,4,96,768]{3,2,1,0:T(8,128)(2,1)}, u32[]{:S(2)}, u32[]{:S(2)}) collective-permute-start(bf16[2,4,96,768]{3,2,1,0:T(8,128)(2,1)S(1)} %pad_maximum_fusion.1.rest_12_), channel_id=1, source_target_pairs={{0,1},{1,0},{2,3},{3,2},{4,5},{5,4},{6,7},{7,6},{8,9},{9,8},{10,11... | collective-permute-start | bytes 3538952 | tf_op jit(solution)/shard_map/ppermute | solution.py:58
  84.2 32.8 %collective-permute-start.16 = (bf16[2,4,96,768]{3,2,1,0:T(8,128)(2,1)S(1)}, bf16[2,4,96,768]{3,2,1,0:T(8,128)(2,1)}, u32[]{:S(2)}, u32[]{:S(2)}) collective-permute-start(bf16[2,4,96,768]{3,2,1,0:T(8,128)(2,1)S(1)} %pad_maximum_fusion.rest_8_), channel_id=1, source_target_pairs={{0,2},{1,3},{2,0},{3,1},{4,6},{5,7},{6,4},{7,5},{8,10},{9,11},{10,... | collective-permute-start | bytes 3538952 | tf_op jit(solution)/shard_map/ppermute | solution.py:58
  84.8 32.3 %collective-permute-start.14 = (bf16[2,4,96,768]{3,2,1,0:T(8,128)(2,1)S(1)}, bf16[2,4,96,768]{3,2,1,0:T(8,128)(2,1)}, u32[]{:S(2)}, u32[]{:S(2)}) collective-permute-start(bf16[2,4,96,768]{3,2,1,0:T(8,128)(2,1)S(1)} %pad_maximum_fusion.rest_8_), channel_id=1, source_target_pairs={{0,1},{1,0},{2,3},{3,2},{4,5},{5,4},{6,7},{7,6},{8,9},{9,8},{10,11... | collective-permute-start | bytes 3538952 | tf_op jit(solution)/shard_map/ppermute | solution.py:58
  85.2 45.1 %all-to-all-start.2 = ((bf16[4,96,1536]{2,1,0:T(8,128)(2,1)}), bf16[4,96,1536]{2,1,0:T(8,128)(2,1)}, u32[]{:S(2)}, u32[]{:S(2)}) async-start(bf16[4,96,1536]{2,1,0:T(8,128)(2,1)} %broadcast_in_dim.8), calls=%async_computation.2 | async-start | bytes 2359296 | tf_op jit(solution)/shard_map/all_to_all | solution.py:71
  96.1 18.8 %collective-permute-start.19 = (bf16[400,128]{1,0:T(8,128)(2,1)}, bf16[400,128]{1,0:T(8,128)(2,1)S(1)}, u32[]{:S(2)}, u32[]{:S(2)}) collective-permute-start(bf16[400,128]{1,0:T(8,128)(2,1)} %copy-done.58), channel_id=1, source_target_pairs={{0,2},{1,3},{2,0},{3,1},{4,6},{5,7},{6,4},{7,5},{8,10},{9,11},{10,... | collective-permute-start | bytes 307208 | tf_op jit(solution)/shard_map/ppermute | solution.py:58
  130.5 20.4 %collective-permute-start.28 = (bf16[2,4,96,384]{3,2,1,0:T(8,128)(2,1)S(1)}, bf16[2,4,96,384]{3,2,1,0:T(8,128)(2,1)}, u32[]{:S(2)}, u32[]{:S(2)}) collective-permute-start(bf16[2,4,96,384]{3,2,1,0:T(8,128)(2,1)S(1)} %pad_maximum_fusion.8.rest_4_), channel_id=1, source_target_pairs={{0,4},{4,0},{8,12},{12,8},{16,20},{20,16},{24,28},{28,24},{1,5},{5... | collective-permute-start | bytes 1769480 | tf_op jit(solution)/shard_map/ppermute | solution.py:62
  131.8 19.7 %collective-permute-start.27 = (bf16[2,4,96,384]{3,2,1,0:T(8,128)(2,1)S(1)}, bf16[2,4,96,384]{3,2,1,0:T(8,128)(2,1)S(1)}, u32[]{:S(2)}, u32[]{:S(2)}) collective-permute-start(bf16[2,4,96,384]{3,2,1,0:T(8,128)(2,1)S(1)} %pad_maximum_fusion.7.rest_0_), channel_id=1, source_target_pairs={{0,2},{1,3},{2,0},{3,1},{4,6},{5,7},{6,4},{7,5},{8,10},{9,11},{10,... | collective-permute-start | bytes 1769480 | tf_op jit(solution)/shard_map/ppermute | solution.py:58
  134.8 23.6 %collective-permute-start.30 = (bf16[4,96,768]{2,1,0:T(8,128)(2,1)S(1)}, bf16[4,96,768]{2,1,0:T(8,128)(2,1)S(1)}, u32[]{:S(2)}, u32[]{:S(2)}) collective-permute-start(bf16[4,96,768]{2,1,0:T(8,128)(2,1)S(1)} %get-tuple-element.709), channel_id=1, source_target_pairs={{0,2},{1,3},{2,0},{3,1},{4,6},{5,7},{6,4},{7,5},{8,10},{9,11},{10,... | collective-permute-start | bytes 1769480 | tf_op jit(solution)/shard_map/ppermute | solution.py:58
  135.4 22.9 %collective-permute-start.29 = (bf16[4,96,768]{2,1,0:T(8,128)(2,1)S(1)}, bf16[4,96,768]{2,1,0:T(8,128)(2,1)S(1)}, u32[]{:S(2)}, u32[]{:S(2)}) collective-permute-start(bf16[4,96,768]{2,1,0:T(8,128)(2,1)S(1)} %get-tuple-element.710), channel_id=1, source_target_pairs={{0,4},{4,0},{8,12},{12,8},{16,20},{20,16},{24,28},{28,24},{1,5},{5... | collective-permute-start | bytes 1769480 | tf_op jit(solution)/shard_map/ppermute | solution.py:62
  137.8 21.5 %collective-permute-start.26 = (bf16[2,4,96,384]{3,2,1,0:T(8,128)(2,1)S(1)}, bf16[2,4,96,384]{3,2,1,0:T(8,128)(2,1)S(1)}, u32[]{:S(2)}, u32[]{:S(2)}) collective-permute-start(bf16[2,4,96,384]{3,2,1,0:T(8,128)(2,1)S(1)} %pad_maximum_fusion.8.rest_4_), channel_id=1, source_target_pairs={{0,1},{1,0},{2,3},{3,2},{4,5},{5,4},{6,7},{7,6},{8,9},{9,8},{10,11... | collective-permute-start | bytes 1769480 | tf_op jit(solution)/shard_map/ppermute | solution.py:58
  159.6 28.5 %collective-permute-start.42 = (bf16[2,4,96,768]{3,2,1,0:T(8,128)(2,1)S(1)}, bf16[2,4,96,768]{3,2,1,0:T(8,128)(2,1)}, u32[]{:S(2)}, u32[]{:S(2)}) collective-permute-start(bf16[2,4,96,768]{3,2,1,0:T(8,128)(2,1)S(1)} %pad_maximum_fusion.3.rest_12_), channel_id=1, source_target_pairs={{0,4},{4,0},{8,12},{12,8},{16,20},{20,16},{24,28},{28,24},{1,5},{5... | collective-permute-start | bytes 3538952 | tf_op jit(solution)/shard_map/ppermute | solution.py:62
  160.2 28.9 %collective-permute-start.41 = (bf16[2,4,96,768]{3,2,1,0:T(8,128)(2,1)S(1)}, bf16[2,4,96,768]{3,2,1,0:T(8,128)(2,1)}, u32[]{:S(2)}, u32[]{:S(2)}) collective-permute-start(bf16[2,4,96,768]{3,2,1,0:T(8,128)(2,1)S(1)} %pad_maximum_fusion.2.rest_8_), channel_id=1, source_target_pairs={{0,2},{1,3},{2,0},{3,1},{4,6},{5,7},{6,4},{7,5},{8,10},{9,11},{10,... | collective-permute-start | bytes 3538952 | tf_op jit(solution)/shard_map/ppermute | solution.py:58
  174.7 16.5 %collective-permute-start.39 = (bf16[400,128]{1,0:T(8,128)(2,1)}, bf16[400,128]{1,0:T(8,128)(2,1)S(1)}, u32[]{:S(2)}, u32[]{:S(2)}) collective-permute-start(bf16[400,128]{1,0:T(8,128)(2,1)} %get-tuple-element.409), channel_id=1, source_target_pairs={{0,2},{1,3},{2,0},{3,1},{4,6},{5,7},{6,4},{7,5},{8,10},{9,11},{10,... | collective-permute-start | bytes 307208 | tf_op jit(solution)/shard_map/ppermute | solution.py:58
  176.1 16.6 %collective-permute-start.40 = (bf16[400,128]{1,0:T(8,128)(2,1)S(1)}, bf16[400,128]{1,0:T(8,128)(2,1)S(1)}, u32[]{:S(2)}, u32[]{:S(2)}) collective-permute-start(bf16[400,128]{1,0:T(8,128)(2,1)S(1)} %collective-permute-done.38.recv_one), channel_id=1, source_target_pairs={{0,2},{1,3},{2,0},{3,1},{4,6},{5,7},{6,4},{7,5},{8,10},{9,11},{10,... | collective-permute-start | bytes 307208 | tf_op jit(solution)/shard_map/ppermute | solution.py:58
  193.2 21.7 %all-to-all-start.3 = ((bf16[8,96,384]{2,1,0:T(8,128)(2,1)}), bf16[8,96,384]{2,1,0:T(8,128)(2,1)S(1)}, u32[]{:S(2)}, u32[]{:S(2)}) async-start(bf16[8,96,384]{2,1,0:T(8,128)(2,1)} %pad_maximum_fusion.4), calls=%async_computation.3 | async-start | bytes 1179648 | tf_op jit(solution)/shard_map/all_to_all | solution.py:79
  223.4 15.9 %collective-permute-start.46 = (bf16[2,192,768]{2,1,0:T(8,128)(2,1)}, bf16[2,192,768]{2,1,0:T(8,128)(2,1)S(1)}, u32[]{:S(2)}, u32[]{:S(2)}) collective-permute-start(bf16[2,192,768]{2,1,0:T(8,128)(2,1)} %get-tuple-element.445), channel_id=1, source_target_pairs={{0,2},{1,3},{2,0},{3,1},{4,6},{5,7},{6,4},{7,5},{8,10},{9,11},{10,... | collective-permute-start | bytes 1769480 | tf_op jit(solution)/shard_map/ppermute | solution.py:58
  224.8 15.3 %collective-permute-start.47 = (bf16[2,192,768]{2,1,0:T(8,128)(2,1)}, bf16[2,192,768]{2,1,0:T(8,128)(2,1)S(1)}, u32[]{:S(2)}, u32[]{:S(2)}) collective-permute-start(bf16[2,192,768]{2,1,0:T(8,128)(2,1)} %get-tuple-element.446), channel_id=1, source_target_pairs={{0,4},{4,0},{8,12},{12,8},{16,20},{20,16},{24,28},{28,24},{1,5},{5... | collective-permute-start | bytes 1769480 | tf_op jit(solution)/shard_map/ppermute | solution.py:62
  243.7 14.6 %collective-permute-start.52 = (bf16[192,768]{1,0:T(8,128)(2,1)}, bf16[192,768]{1,0:T(8,128)(2,1)S(1)}, u32[]{:S(2)}, u32[]{:S(2)}) collective-permute-start(bf16[192,768]{1,0:T(8,128)(2,1)} %get-tuple-element.466), channel_id=1, source_target_pairs={{0,4},{4,0},{8,12},{12,8},{16,20},{20,16},{24,28},{28,24},{1,5},{5... | collective-permute-start | bytes 884744 | tf_op jit(solution)/shard_map/ppermute | solution.py:62
  259.0 19.6 %collective-permute-start.54 = (bf16[2,192,768]{2,1,0:T(8,128)(2,1)}, bf16[2,192,768]{2,1,0:T(8,128)(2,1)S(1)}, u32[]{:S(2)}, u32[]{:S(2)}) collective-permute-start(bf16[2,192,768]{2,1,0:T(8,128)(2,1)} %get-tuple-element.472), channel_id=1, source_target_pairs={{0,2},{1,3},{2,0},{3,1},{4,6},{5,7},{6,4},{7,5},{8,10},{9,11},{10,... | collective-permute-start | bytes 1769480 | tf_op jit(solution)/shard_map/ppermute | solution.py:58
  259.6 19.0 %collective-permute-start.55 = (bf16[2,192,768]{2,1,0:T(8,128)(2,1)}, bf16[2,192,768]{2,1,0:T(8,128)(2,1)S(1)}, u32[]{:S(2)}, u32[]{:S(2)}) collective-permute-start(bf16[2,192,768]{2,1,0:T(8,128)(2,1)} %get-tuple-element.473), channel_id=1, source_target_pairs={{0,4},{4,0},{8,12},{12,8},{16,20},{20,16},{24,28},{28,24},{1,5},{5... | collective-permute-start | bytes 1769480 | tf_op jit(solution)/shard_map/ppermute | solution.py:62
  260.2 18.4 %all-to-all-start.4 = ((bf16[8,96,192]{2,1,0:T(8,128)(2,1)}), bf16[8,96,192]{2,1,0:T(8,128)(2,1)S(1)}, u32[]{:S(2)}, u32[]{:S(2)}) async-start(bf16[8,96,192]{2,1,0:T(8,128)(2,1)} %fusion.10), calls=%async_computation.4 | async-start | bytes 786432 | tf_op jit(solution)/shard_map/all_to_all | solution.py:79
  295.0 15.0 %collective-permute-start.60 = (bf16[2,192,768]{2,1,0:T(8,128)(2,1)}, bf16[2,192,768]{2,1,0:T(8,128)(2,1)S(1)}, u32[]{:S(2)}, u32[]{:S(2)}) collective-permute-start(bf16[2,192,768]{2,1,0:T(8,128)(2,1)} %get-tuple-element.504), channel_id=1, source_target_pairs={{0,2},{1,3},{2,0},{3,1},{4,6},{5,7},{6,4},{7,5},{8,10},{9,11},{10,... | collective-permute-start | bytes 1769480 | tf_op jit(solution)/shard_map/ppermute | solution.py:58
  296.4 14.1 %collective-permute-start.61 = (bf16[2,192,768]{2,1,0:T(8,128)(2,1)}, bf16[2,192,768]{2,1,0:T(8,128)(2,1)S(1)}, u32[]{:S(2)}, u32[]{:S(2)}) collective-permute-start(bf16[2,192,768]{2,1,0:T(8,128)(2,1)} %get-tuple-element.505), channel_id=1, source_target_pairs={{0,4},{4,0},{8,12},{12,8},{16,20},{20,16},{24,28},{28,24},{1,5},{5... | collective-permute-start | bytes 1769480 | tf_op jit(solution)/shard_map/ppermute | solution.py:62
  315.5 39.3 %all-to-all-start.5 = ((bf16[4,192,768]{2,1,0:T(8,128)(2,1)}), bf16[4,192,768]{2,1,0:T(8,128)(2,1)S(1)}, u32[]{:S(2)}, u32[]{:S(2)}) async-start(bf16[4,192,768]{2,1,0:T(8,128)(2,1)} %merge.16), calls=%async_computation.5 | async-start | bytes 2359296 | tf_op jit(solution)/shard_map/all_to_all | solution.py:71
  322.8 15.2 %collective-permute-start.66 = (bf16[192,768]{1,0:T(8,128)(2,1)}, bf16[192,768]{1,0:T(8,128)(2,1)S(1)}, u32[]{:S(2)}, u32[]{:S(2)}) collective-permute-start(bf16[192,768]{1,0:T(8,128)(2,1)} %get-tuple-element.525), channel_id=1, source_target_pairs={{0,4},{4,0},{8,12},{12,8},{16,20},{20,16},{24,28},{28,24},{1,5},{5... | collective-permute-start | bytes 884744 | tf_op jit(solution)/shard_map/ppermute | solution.py:62
  338.0 16.9 %collective-permute-start.68 = (bf16[2,192,768]{2,1,0:T(8,128)(2,1)}, bf16[2,192,768]{2,1,0:T(8,128)(2,1)S(1)}, u32[]{:S(2)}, u32[]{:S(2)}) collective-permute-start(bf16[2,192,768]{2,1,0:T(8,128)(2,1)} %get-tuple-element.539), channel_id=1, source_target_pairs={{0,2},{1,3},{2,0},{3,1},{4,6},{5,7},{6,4},{7,5},{8,10},{9,11},{10,... | collective-permute-start | bytes 1769480 | tf_op jit(solution)/shard_map/ppermute | solution.py:58
  338.7 16.2 %collective-permute-start.69 = (bf16[2,192,768]{2,1,0:T(8,128)(2,1)}, bf16[2,192,768]{2,1,0:T(8,128)(2,1)S(1)}, u32[]{:S(2)}, u32[]{:S(2)}) collective-permute-start(bf16[2,192,768]{2,1,0:T(8,128)(2,1)} %get-tuple-element.540), channel_id=1, source_target_pairs={{0,4},{4,0},{8,12},{12,8},{16,20},{20,16},{24,28},{28,24},{1,5},{5... | collective-permute-start | bytes 1769480 | tf_op jit(solution)/shard_map/ppermute | solution.py:62
  365.1 23.0 %collective-permute-start.75 = (bf16[2,192,768]{2,1,0:T(8,128)(2,1)}, bf16[2,192,768]{2,1,0:T(8,128)(2,1)S(1)}, u32[]{:S(2)}, u32[]{:S(2)}) collective-permute-start(bf16[2,192,768]{2,1,0:T(8,128)(2,1)} %get-tuple-element.576), channel_id=1, source_target_pairs={{0,2},{1,3},{2,0},{3,1},{4,6},{5,7},{6,4},{7,5},{8,10},{9,11},{10,... | collective-permute-start | bytes 1769480 | tf_op jit(solution)/shard_map/ppermute | solution.py:58
  366.5 21.5 %collective-permute-start.76 = (bf16[2,192,768]{2,1,0:T(8,128)(2,1)}, bf16[2,192,768]{2,1,0:T(8,128)(2,1)S(1)}, u32[]{:S(2)}, u32[]{:S(2)}) collective-permute-start(bf16[2,192,768]{2,1,0:T(8,128)(2,1)} %get-tuple-element.577), channel_id=1, source_target_pairs={{0,4},{4,0},{8,12},{12,8},{16,20},{20,16},{24,28},{28,24},{1,5},{5... | collective-permute-start | bytes 1769480 | tf_op jit(solution)/shard_map/ppermute | solution.py:62
  368.0 20.0 %collective-permute-start.72 = (bf16[192,768]{1,0:T(8,128)(2,1)}, bf16[192,768]{1,0:T(8,128)(2,1)S(1)}, u32[]{:S(2)}, u32[]{:S(2)}) collective-permute-start(bf16[192,768]{1,0:T(8,128)(2,1)} %get-tuple-element.573), channel_id=1, source_target_pairs={{0,4},{4,0},{8,12},{12,8},{16,20},{20,16},{24,28},{28,24},{1,5},{5... | collective-permute-start | bytes 884744 | tf_op jit(solution)/shard_map/ppermute | solution.py:62
  368.7 19.4 %collective-permute-start.73 = (bf16[192,768]{1,0:T(8,128)(2,1)}, bf16[192,768]{1,0:T(8,128)(2,1)}, u32[]{:S(2)}, u32[]{:S(2)}) collective-permute-start(bf16[192,768]{1,0:T(8,128)(2,1)} %get-tuple-element.574), channel_id=1, source_target_pairs={{0,2},{1,3},{2,0},{3,1},{4,6},{5,7},{6,4},{7,5},{8,10},{9,11},{10,... | collective-permute-start | bytes 884744 | tf_op jit(solution)/shard_map/ppermute | solution.py:58
  369.4 18.6 %collective-permute-start.74 = (f32[12,768]{1,0:T(8,128)S(1)}, f32[12,768]{1,0:T(8,128)S(1)}, u32[]{:S(2)}, u32[]{:S(2)}) collective-permute-start(f32[12,768]{1,0:T(8,128)S(1)} %pad_maximum_fusion.17), channel_id=1, source_target_pairs={{0,2},{1,3},{2,0},{3,1},{4,6},{5,7},{6,4},{7,5},{8,10},{9,11},{10,... | collective-permute-start | bytes 110600 | tf_op jit(solution)/shard_map/ppermute | solution.py:58
  391.3 33.0 %all-to-all-start.6 = ((bf16[4,192,768]{2,1,0:T(8,128)(2,1)}), bf16[4,192,768]{2,1,0:T(8,128)(2,1)S(1)}, u32[]{:S(2)}, u32[]{:S(2)}) async-start(bf16[4,192,768]{2,1,0:T(8,128)(2,1)} %merge.19), calls=%async_computation.6 | async-start | bytes 2359296 | tf_op jit(solution)/shard_map/all_to_all | solution.py:71
  396.4 15.7 %collective-permute-start.77 = (bf16[2,192,768]{2,1,0:T(8,128)(2,1)}, bf16[2,192,768]{2,1,0:T(8,128)(2,1)S(1)}, u32[]{:S(2)}, u32[]{:S(2)}) collective-permute-start(bf16[2,192,768]{2,1,0:T(8,128)(2,1)} %get-tuple-element.579), channel_id=1, source_target_pairs={{0,2},{1,3},{2,0},{3,1},{4,6},{5,7},{6,4},{7,5},{8,10},{9,11},{10,... | collective-permute-start | bytes 1769480 | tf_op jit(solution)/shard_map/ppermute | solution.py:58
  397.8 14.4 %collective-permute-start.78 = (bf16[2,192,768]{2,1,0:T(8,128)(2,1)}, bf16[2,192,768]{2,1,0:T(8,128)(2,1)S(1)}, u32[]{:S(2)}, u32[]{:S(2)}) collective-permute-start(bf16[2,192,768]{2,1,0:T(8,128)(2,1)} %get-tuple-element.580), channel_id=1, source_target_pairs={{0,4},{4,0},{8,12},{12,8},{16,20},{20,16},{24,28},{28,24},{1,5},{5... | collective-permute-start | bytes 1769480 | tf_op jit(solution)/shard_map/ppermute | solution.py:62
  424.4 31.8 %all-to-all-start.7 = ((bf16[8,128,384]{2,1,0:T(8,128)(2,1)}), bf16[8,128,384]{2,1,0:T(8,128)(2,1)S(1)}, u32[]{:S(2)}, u32[]{:S(2)}) async-start(bf16[8,128,384]{2,1,0:T(8,128)(2,1)} %ortho.3), calls=%async_computation.7 | async-start | bytes 1572864 | tf_op jit(solution)/shard_map/all_to_all | solution.py:79
  428.4 18.4 %collective-permute-start.81 = (bf16[192,768]{1,0:T(8,128)(2,1)}, bf16[192,768]{1,0:T(8,128)(2,1)S(1)}, u32[]{:S(2)}, u32[]{:S(2)}) collective-permute-start(bf16[192,768]{1,0:T(8,128)(2,1)} %get-tuple-element.604), channel_id=1, source_target_pairs={{0,4},{4,0},{8,12},{12,8},{16,20},{20,16},{24,28},{28,24},{1,5},{5... | collective-permute-start | bytes 884744 | tf_op jit(solution)/shard_map/ppermute | solution.py:62
  430.5 16.3 %collective-permute-start.82 = (bf16[192,768]{1,0:T(8,128)(2,1)S(1)}, bf16[192,768]{1,0:T(8,128)(2,1)S(1)}, u32[]{:S(2)}, u32[]{:S(2)}) collective-permute-start(bf16[192,768]{1,0:T(8,128)(2,1)S(1)} %copy-done.107), channel_id=1, source_target_pairs={{0,2},{1,3},{2,0},{3,1},{4,6},{5,7},{6,4},{7,5},{8,10},{9,11},{10,... | collective-permute-start | bytes 884744 | tf_op jit(solution)/shard_map/ppermute | solution.py:58
  434.6 16.5 %collective-permute-start.79 = (bf16[192,768]{1,0:T(8,128)(2,1)}, bf16[192,768]{1,0:T(8,128)(2,1)S(1)}, u32[]{:S(2)}, u32[]{:S(2)}) collective-permute-start(bf16[192,768]{1,0:T(8,128)(2,1)} %get-tuple-element.602), channel_id=1, source_target_pairs={{0,4},{4,0},{8,12},{12,8},{16,20},{20,16},{24,28},{28,24},{1,5},{5... | collective-permute-start | bytes 884744 | tf_op jit(solution)/shard_map/ppermute | solution.py:62
  434.7 16.5 %collective-permute-start.80 = (bf16[192,768]{1,0:T(8,128)(2,1)}, bf16[192,768]{1,0:T(8,128)(2,1)S(1)}, u32[]{:S(2)}, u32[]{:S(2)}) collective-permute-start(bf16[192,768]{1,0:T(8,128)(2,1)} %get-tuple-element.603), channel_id=1, source_target_pairs={{0,2},{1,3},{2,0},{3,1},{4,6},{5,7},{6,4},{7,5},{8,10},{9,11},{10,... | collective-permute-start | bytes 884744 | tf_op jit(solution)/shard_map/ppermute | solution.py:58
  488.2 19.3 %all-to-all-start.9 = ((bf16[8,96,384]{2,1,0:T(8,128)(2,1)}), bf16[8,96,384]{2,1,0:T(8,128)(2,1)S(1)}, u32[]{:S(2)}, u32[]{:S(2)}) async-start(bf16[8,96,384]{2,1,0:T(8,128)(2,1)} %ortho.4), calls=%async_computation.9 | async-start | bytes 1179648 | tf_op jit(solution)/shard_map/all_to_all | solution.py:79
  507.5 19.4 %all-to-all-start.10 = ((bf16[8,96,384]{2,1,0:T(8,128)(2,1)}), bf16[8,96,384]{2,1,0:T(8,128)(2,1)S(1)}, u32[]{:S(2)}, u32[]{:S(2)}) async-start(bf16[8,96,384]{2,1,0:T(8,128)(2,1)} %ortho.5), calls=%async_computation.10 | async-start | bytes 1179648 | tf_op jit(solution)/shard_map/all_to_all | solution.py:79
  (155 other events, 1240.6 us)
